TPU v7x, 32 devices: a whole 2x2x4 slice. The times are simulated.
32 devices in a mesh: dom: 8 (over z, y), orb: 4 (over x, core).
Axes of the slice: x: 2, y: 2, z: 4, core: 2. Of those that a mesh axis runs over, the one named last changes fastest.
Arguments:
- orbitals: bfloat16 [18816, 1024], P('dom', 'orb'), may hold values from -6 to 6
- potential: float32 [18816], P('dom'), may hold values from 0.5 to 2
- cell_hamiltonian: bfloat16 [64, 343, 343], P('dom'), may hold values from -2 to 2, as said below
- connectivity: int32 [64, 343], P('dom'), may hold values from 0 to 2400, as said below
- face_nodes: int32 [392], P('dom'), may hold values from 0 to 2351, as said below
Outputs:
- residual: float32 [18816, 1024], P(('dom', 'orb'))
- projected: bfloat16 [1024, 1024], replicated
Inputs may be any that keep to these rules, and one draw needn't show every extreme that they name: `connectivity`: cell c of a domain is its c-th layer of cells; each row lists the cell's 343 nodes in the domain's local numbering, where a number 2352 + p stands for entry p of the next domain's face_nodes list. Every local node of a domain belongs to some cell of it, and neighbouring cells of a domain share a face of 49 nodes. `face_nodes`: each domain's 49 entries are distinct local node numbers of that domain: the nodes that the previous domain's last cell shares with it, in the order of that cell's numbers 2352 + p. `cell_hamiltonian`: each cell's matrix is symmetric.
All inputs are finite; a program needn't handle non-finite values.
Results may differ from a plain program's by a relative error of at most 0.0096.
Values may be sent and summed in bfloat16 or wider, within the bound.
No kernel may reach another device: no remote copies, remote signals or barrier semaphores. Data moves between devices by JAX's collectives and lax.ppermute only.
A program may use at most 64 MiB of HBM per device.

v0:
```python
import jax
import jax.numpy as jnp
from jax import lax
from jax.sharding import PartitionSpec as P

DEGREE = 4


filter_center = 1.5
filter_half = 2.0


def from_behind(block, axis, distance):
    devices = range(lax.axis_size(axis))
    route = [(i - distance, i) for i in devices if i - distance in devices]
    return lax.ppermute(block, axis, route)


def apply_hamiltonian(values, potential, cell_hamiltonian, connectivity, face_nodes):
    node_count = values.shape[1]
    face_vals = jnp.take(values, face_nodes, axis=1)
    ghosts = from_behind(face_vals, "dom", -1)
    extended = jnp.concatenate([values, ghosts], axis=1)
    cell_values = jnp.take(extended, connectivity, axis=1)
    products = jnp.einsum(
        "kij,okj->oki", cell_hamiltonian, cell_values, preferred_element_type=jnp.float32
    )
    summed = (
        jnp.zeros((values.shape[0], extended.shape[1]), jnp.float32)
        .at[:, connectivity]
        .add(products)
    )
    returned = from_behind(summed[:, node_count:], "dom", 1)
    assembled = summed[:, :node_count].at[:, face_nodes].add(returned)
    return assembled + potential[None, :] * values.astype(jnp.float32)


def body(orbitals, potential, cell_hamiltonian, connectivity, face_nodes):
    previous = orbitals.T
    image = apply_hamiltonian(previous, potential, cell_hamiltonian, connectivity, face_nodes)
    current = ((image - filter_center * previous.astype(jnp.float32)) / filter_half).astype(
        jnp.bfloat16
    )
    for step in range(DEGREE - 1):
        image = apply_hamiltonian(current, potential, cell_hamiltonian, connectivity, face_nodes)
        following_iter = (
            2.0 * (image - filter_center * current.astype(jnp.float32)) / filter_half
            - previous.astype(jnp.float32)
        ).astype(jnp.bfloat16)
        previous, current = (current, following_iter)
    image = apply_hamiltonian(
        current, potential, cell_hamiltonian, connectivity, face_nodes
    ).astype(jnp.bfloat16)
    node_rows, image_rows = (
        lax.all_to_all(current.T, "orb", split_axis=0, concat_axis=1, tiled=True),
        lax.all_to_all(image.T, "orb", split_axis=0, concat_axis=1, tiled=True),
    )
    node_total = node_rows.shape[0] * lax.axis_size("orb") * lax.axis_size("dom")
    inverse_nodes = 1.0 / node_total
    share = lax.psum_scatter(
        jnp.einsum("ri,rj->ij", node_rows, image_rows, preferred_element_type=jnp.float32)
        * inverse_nodes,
        "orb",
        scatter_dimension=0,
        tiled=True,
    )
    share = lax.psum(share, "dom")
    projected = lax.all_gather(share.astype(jnp.bfloat16), "orb", axis=0, tiled=True)
    residual = image_rows.astype(jnp.float32) - jnp.dot(
        node_rows, projected, preferred_element_type=jnp.float32
    )
    return (residual, projected)


def solution(mesh):
    return jax.shard_map(
        body,
        mesh=mesh,
        in_specs=(P("dom", "orb"), P("dom"), P("dom", None, None), P("dom", None), P("dom")),
        out_specs=(P(("dom", "orb"), None), P()),
        check_vma=False,
    )
```

profile of v0, /device:TPU:0, one launch (start us, length us, event | category | flops | bytes accessed | tf_op | source)
XLA Modules:
  0.0 481.6 jit_solution(2454241895254476116)
XLA Ops:
  8.7 2.1 gather_fusion
  13.7 3.9 collective-permute-done
  18.9 8.9 %gather_fusion.1 = bf16[2744,256]{1,0:T(8,128)(2,1)} fusion(bf16[256,2401]{0,1:T(8,128)(2,1)S(1)} %pad_maximum_fusion, s32[3072]{0:T(1024)S(1)} %pad_clamp_fusion), kind=kCustom, calls=%fused_computation.1.clone | custom fusion | bytes 2820832 | tf_op jit(solution)/shard_map/jit(_take)/gather | solution.py:24
  27.8 1.8 reshape.216
  29.5 2.5 convolution_bitcast_fusion.4
  32.0 3.7 reshape.105
  35.8 17.5 %scatter_custom_fusion = f32[256,2401]{0,1:T(8,128)} fusion(s32[2744]{0:T(1024)} %copy-done.13, f32[2744,256]{1,0:T(8,128)} %reshape.105, f32[]{:T(128)} %constant.23.clone.1), kind=kCustom, calls=%fused_computation.80 | custom fusion | flops 702464 | bytes 2459136 | tf_op jit(solution)/shard_map/scatter-add | solution.py:31
  54.1 4.8 collective-permute-start.1
  58.9 3.5 fusion.2
  62.4 4.0 scatter_custom_fusion.1
  66.4 2.4 fusion.5
  69.6 1.5 collective-permute-start.2
  71.0 4.3 collective-permute-done.2
  76.7 8.9 %gather_fusion.3 = bf16[2744,256]{1,0:T(8,128)(2,1)} fusion(bf16[256,2401]{0,1:T(8,128)(2,1)S(1)} %pad_maximum_fusion.1, s32[3072]{0:T(1024)S(1)} %pad_clamp_fusion), kind=kCustom, calls=%fused_computation.6.clone | custom fusion | bytes 2820832 | tf_op jit(solution)/shard_map/jit(_take)/gather | solution.py:24
  85.5 1.8 reshape.222
  87.3 2.5 convolution_bitcast_fusion.3
  89.8 3.7 reshape.121
  93.5 17.5 %scatter_custom_fusion.2 = f32[256,2401]{0,1:T(8,128)} fusion(s32[2744]{0:T(1024)} %copy-done.13, f32[2744,256]{1,0:T(8,128)} %reshape.121, f32[]{:T(128)} %constant.23.clone.1), kind=kCustom, calls=%fused_computation.78 | custom fusion | flops 702464 | bytes 2459136 | tf_op jit(solution)/shard_map/scatter-add | solution.py:31
  111.9 3.4 collective-permute-start.3
  115.3 3.5 fusion.7
  118.8 4.0 scatter_custom_fusion.3
  122.8 2.8 fusion.6
  127.7 4.5 collective-permute-done.4
  133.5 8.9 %gather_fusion.5 = bf16[2744,256]{1,0:T(8,128)(2,1)} fusion(bf16[256,2401]{0,1:T(8,128)(2,1)S(1)} %pad_maximum_fusion.2, s32[3072]{0:T(1024)S(1)} %pad_clamp_fusion), kind=kCustom, calls=%fused_computation.7.clone | custom fusion | bytes 2820832 | tf_op jit(solution)/shard_map/jit(_take)/gather | solution.py:24
  142.4 1.8 reshape.228
  144.1 2.5 convolution_bitcast_fusion.2
  146.6 3.7 reshape.137
  150.3 17.5 %scatter_custom_fusion.4 = f32[256,2401]{0,1:T(8,128)} fusion(s32[2744]{0:T(1024)} %copy-done.13, f32[2744,256]{1,0:T(8,128)} %reshape.137, f32[]{:T(128)} %constant.23.clone.1), kind=kCustom, calls=%fused_computation.76 | custom fusion | flops 702464 | bytes 2459136 | tf_op jit(solution)/shard_map/scatter-add | solution.py:31
  168.7 4.5 collective-permute-start.5
  173.2 3.5 fusion.10
  176.7 4.0 scatter_custom_fusion.5
  180.7 3.6 fusion.9
  184.3 2.1 gather_fusion.6
  187.8 4.5 collective-permute-done.6
  193.6 8.9 %gather_fusion.7 = bf16[2744,256]{1,0:T(8,128)(2,1)} fusion(bf16[256,2401]{0,1:T(8,128)(2,1)S(1)} %pad_maximum_fusion.3, s32[3072]{0:T(1024)S(1)} %pad_clamp_fusion), kind=kCustom, calls=%fused_computation.8.clone | custom fusion | bytes 2820832 | tf_op jit(solution)/shard_map/jit(_take)/gather | solution.py:24
  202.5 1.8 reshape.234
  204.2 2.5 convolution_bitcast_fusion.1
  206.7 3.7 reshape.153
  210.5 17.5 %scatter_custom_fusion.6 = f32[256,2401]{0,1:T(8,128)} fusion(s32[2744]{0:T(1024)} %copy-done.13, f32[2744,256]{1,0:T(8,128)} %reshape.153, f32[]{:T(128)} %constant.23.clone.1), kind=kCustom, calls=%fused_computation.74 | custom fusion | flops 702464 | bytes 2459136 | tf_op jit(solution)/shard_map/scatter-add | solution.py:31
  228.8 3.5 collective-permute-start.7
  232.3 3.5 fusion
  235.8 4.1 scatter_custom_fusion.7
  239.9 3.6 fusion.12
  243.5 2.1 gather_fusion.8
  247.0 2.2 all_to_all.32
  249.2 4.5 all-to-all-start.1
  253.8 1.4 pad_maximum_fusion.4
  255.1 8.9 %gather_fusion.9 = bf16[2744,256]{1,0:T(8,128)(2,1)} fusion(bf16[256,2401]{0,1:T(8,128)(2,1)S(1)} %pad_maximum_fusion.4, s32[3072]{0:T(1024)S(1)} %pad_clamp_fusion), kind=kCustom, calls=%fused_computation.9.clone | custom fusion | bytes 2820832 | tf_op jit(solution)/shard_map/jit(_take)/gather | solution.py:24
  264.0 1.8 reshape.240
  265.7 2.5 convolution_bitcast_fusion
  268.2 3.7 reshape.169
  272.0 17.5 %scatter_custom_fusion.8 = f32[256,2401]{0,1:T(8,128)} fusion(s32[2744]{0:T(1024)} %copy-done.13, f32[2744,256]{1,0:T(8,128)} %reshape.169, f32[]{:T(128)} %constant.23.clone.1), kind=kCustom, calls=%fused_computation.72 | custom fusion | flops 702464 | bytes 2459136 | tf_op jit(solution)/shard_map/scatter-add | solution.py:31
  290.3 4.5 collective-permute-start.9
  294.9 3.5 slice_add_fusion
  298.4 4.0 scatter_custom_fusion.9
  302.4 1.8 convert_bitcast_fusion
  305.3 3.5 all-to-all-start
  308.9 1.9 copy.19
  312.6 12.5 %all-to-all-done = bf16[4,588,256]{2,1,0:T(8,128)(2,1)S(1)} async-done(((bf16[4,588,256]{2,1,0:T(8,128)(2,1)}), bf16[4,588,256]{2,1,0:T(8,128)(2,1)S(1)}, u32[]{:S(2)}, u32[]{:S(2)}) %all-to-all-start) | async-done | bytes 1204256 | tf_op jit(solution)/shard_map/all_to_all | solution.py:56
  327.5 3.8 convolution_multiply_fusion
  331.3 43.3 %reduce-scatter.2.cloned.1.call-done = f32[256,1024]{1,0:T(8,128)} async-done(((f32[1024,1024]{1,0:T(8,128)}), f32[256,1024]{1,0:T(8,128)}) %reduce-scatter.2.cloned.1.call-update) | async-done | bytes 1048592 | tf_op jit(solution)/shard_map/reduce_scatter | solution.py:60
  374.6 73.3 %all-reduce.1 = bf16[256,1024]{1,0:T(8,128)(2,1)} all-reduce(f32[256,1024]{1,0:T(8,128)} %reduce-scatter.2.cloned.1.call-done), channel_id=1, replica_groups=mesh['dom'=8,'orb'=4] {'dom'}, use_global_device_ids=true, to_apply=%region_11.14 | all-reduce | flops 262144 | bytes 1572864 | tf_op jit(solution)/shard_map/psum | solution.py:67
  447.9 20.2 %all-gather.2.cloned.1.call-done = bf16[1024,1024]{1,0:T(8,128)(2,1)} async-done(((bf16[256,1024]{1,0:T(8,128)(2,1)}), bf16[1024,1024]{1,0:T(8,128)(2,1)}) %all-gather.2.cloned.1.call-update) | async-done | bytes 2097168 | tf_op jit(solution)/shard_map/all_gather | solution.py:68
  468.1 4.9 %convert_subtract_fusion.3 = f32[588,1024]{1,0:T(8,128)} fusion(bf16[588,1024]{1,0:T(8,128)(2,1)} %bitcast.78, bf16[588,1024]{1,0:T(8,128)(2,1)S(1)} %bitcast.76, bf16[1024,1024]{1,0:T(8,128)(2,1)} %all-gather.2.cloned.1.call-done), kind=kOutput, calls=%fused_computation.31 | convolution fusion | flops 1234329600 | bytes 6914048 | tf_op jit(solution)/shard_map/dot_general | solution.py:69
  (75 shorter events, 26.2 us)
Async XLA Ops:
  7.2 22.4 %copy-start = (bf16[8,343,343]{2,0,1:T(8,128)(2,1)S(1)}, bf16[8,343,343]{2,0,1:T(8,128)(2,1)}, u32[]{:S(2)}) copy-start(bf16[8,343,343]{2,0,1:T(8,128)(2,1)} %param.11) | copy-start | bytes 5647156
  8.0 0.7 copy-start.14
  10.8 6.7 %collective-permute-start = (bf16[256,49]{0,1:T(8,128)(2,1)S(1)}, bf16[256,49]{0,1:T(8,128)(2,1)S(1)}, u32[]{:S(2)}, u32[]{:S(2)}) collective-permute-start(bf16[256,49]{0,1:T(8,128)(2,1)S(1)} %select_bitcast_fusion.4), channel_id=1, source_target_pairs={{4,0},{8,4},{12,8},{16,12},{20,16},{24,20},{28,24},{5,1},{9,5},{13... | collective-permute-start | bytes 75272 | tf_op jit(solution)/shard_map/ppermute | solution.py:16
  13.6 14.1 %copy-start.13 = (s32[2744]{0:T(1024)}, s32[2744]{0:T(1024)S(1)}, u32[]{:S(2)}) copy-start(s32[2744]{0:T(1024)S(1)} %reshape.167) | copy-start | bytes 32932
  35.8 23.2 %copy-start.6 = (bf16[2352,256]{1,0:T(8,128)(2,1)S(1)}, bf16[2352,256]{1,0:T(8,128)(2,1)}, u32[]{:S(2)}) copy-start(bf16[2352,256]{1,0:T(8,128)(2,1)} %param.9) | copy-start | bytes 3612676
  35.8 23.2 %copy-start.12 = (f32[2352]{0:T(1024)S(1)}, f32[2352]{0:T(1024)}, u32[]{:S(2)}) copy-start(f32[2352]{0:T(1024)} %param.10) | copy-start | bytes 28228
  54.1 8.3 %collective-permute-start.1 = (f32[256,49]{0,1:T(8,128)S(1)}, f32[256,49]{0,1:T(8,128)S(1)}, u32[]{:S(2)}, u32[]{:S(2)}) collective-permute-start(f32[256,49]{0,1:T(8,128)S(1)} %slice.61), channel_id=1, source_target_pairs={{0,4},{4,8},{8,12},{12,16},{16,20},{20,24},{24,28},{1,5},{5,9},{9,... | collective-permute-start | bytes 150536 | tf_op jit(solution)/shard_map/ppermute | solution.py:16
  68.8 2.2 copy-start.4
  69.6 5.8 %collective-permute-start.2 = (bf16[256,49]{0,1:T(8,128)(2,1)S(1)}, bf16[256,49]{0,1:T(8,128)(2,1)S(1)}, u32[]{:S(2)}, u32[]{:S(2)}) collective-permute-start(bf16[256,49]{0,1:T(8,128)(2,1)S(1)} %select_bitcast_fusion.3), channel_id=1, source_target_pairs={{4,0},{8,4},{12,8},{16,12},{20,16},{24,20},{28,24},{5,1},{9,5},{13... | collective-permute-start | bytes 75272 | tf_op jit(solution)/shard_map/ppermute | solution.py:16
  93.5 21.8 %copy-start.5 = (bf16[256,2352]{0,1:T(8,128)(2,1)S(1)}, bf16[256,2352]{0,1:T(8,128)(2,1)}, u32[]{:S(2)}) copy-start(bf16[256,2352]{0,1:T(8,128)(2,1)} %copy-done.4) | copy-start | bytes 3612676
  111.9 6.9 %collective-permute-start.3 = (f32[256,49]{0,1:T(8,128)S(1)}, f32[256,49]{0,1:T(8,128)S(1)}, u32[]{:S(2)}, u32[]{:S(2)}) collective-permute-start(f32[256,49]{0,1:T(8,128)S(1)} %slice.63), channel_id=1, source_target_pairs={{0,4},{4,8},{8,12},{12,16},{16,20},{20,24},{24,28},{1,5},{5,9},{9,... | collective-permute-start | bytes 150536 | tf_op jit(solution)/shard_map/ppermute | solution.py:16
  125.6 2.1 copy-start.1
  126.4 5.8 %collective-permute-start.4 = (bf16[256,49]{0,1:T(8,128)(2,1)S(1)}, bf16[256,49]{0,1:T(8,128)(2,1)S(1)}, u32[]{:S(2)}, u32[]{:S(2)}) collective-permute-start(bf16[256,49]{0,1:T(8,128)(2,1)S(1)} %select_bitcast_fusion.2), channel_id=1, source_target_pairs={{4,0},{8,4},{12,8},{16,12},{20,16},{24,20},{28,24},{5,1},{9,5},{13... | collective-permute-start | bytes 75272 | tf_op jit(solution)/shard_map/ppermute | solution.py:16
  150.3 22.9 %copy-start.2 = (bf16[256,2352]{0,1:T(8,128)(2,1)S(1)}, bf16[256,2352]{0,1:T(8,128)(2,1)}, u32[]{:S(2)}) copy-start(bf16[256,2352]{0,1:T(8,128)(2,1)} %copy-done.1) | copy-start | bytes 3612676
  168.7 8.0 %collective-permute-start.5 = (f32[256,49]{0,1:T(8,128)S(1)}, f32[256,49]{0,1:T(8,128)S(1)}, u32[]{:S(2)}, u32[]{:S(2)}) collective-permute-start(f32[256,49]{0,1:T(8,128)S(1)} %slice.65), channel_id=1, source_target_pairs={{0,4},{4,8},{8,12},{12,16},{16,20},{20,24},{24,28},{1,5},{5,9},{9,... | collective-permute-start | bytes 150536 | tf_op jit(solution)/shard_map/ppermute | solution.py:16
  186.5 5.8 %collective-permute-start.6 = (bf16[256,49]{0,1:T(8,128)(2,1)S(1)}, bf16[256,49]{0,1:T(8,128)(2,1)S(1)}, u32[]{:S(2)}, u32[]{:S(2)}) collective-permute-start(bf16[256,49]{0,1:T(8,128)(2,1)S(1)} %select_bitcast_fusion.1), channel_id=1, source_target_pairs={{4,0},{8,4},{12,8},{16,12},{20,16},{24,20},{28,24},{5,1},{9,5},{13... | collective-permute-start | bytes 75272 | tf_op jit(solution)/shard_map/ppermute | solution.py:16
  210.5 21.8 %copy-start.8 = (bf16[256,2352]{0,1:T(8,128)(2,1)S(1)}, bf16[256,2352]{0,1:T(8,128)(2,1)}, u32[]{:S(2)}) copy-start(bf16[256,2352]{0,1:T(8,128)(2,1)} %fusion.9) | copy-start | bytes 3612676
  228.8 7.0 %collective-permute-start.7 = (f32[256,49]{0,1:T(8,128)S(1)}, f32[256,49]{0,1:T(8,128)S(1)}, u32[]{:S(2)}, u32[]{:S(2)}) collective-permute-start(f32[256,49]{0,1:T(8,128)S(1)} %slice.67), channel_id=1, source_target_pairs={{0,4},{4,8},{8,12},{12,16},{16,20},{20,24},{24,28},{1,5},{5,9},{9,... | collective-permute-start | bytes 150536 | tf_op jit(solution)/shard_map/ppermute | solution.py:16
  235.8 4.1 copy-start.3
  245.7 8.1 %collective-permute-start.8 = (bf16[256,49]{0,1:T(8,128)(2,1)S(1)}, bf16[256,49]{0,1:T(8,128)(2,1)S(1)}, u32[]{:S(2)}, u32[]{:S(2)}) collective-permute-start(bf16[256,49]{0,1:T(8,128)(2,1)S(1)} %select_bitcast_fusion), channel_id=1, source_target_pairs={{4,0},{8,4},{12,8},{16,12},{20,16},{24,20},{28,24},{5,1},{9,5},{13... | collective-permute-start | bytes 75272 | tf_op jit(solution)/shard_map/ppermute | solution.py:16
  249.2 56.1 %all-to-all-start.1 = ((bf16[4,588,256]{2,1,0:T(8,128)(2,1)}), bf16[4,588,256]{2,1,0:T(8,128)(2,1)}, u32[]{:S(2)}, u32[]{:S(2)}) async-start(bf16[4,588,256]{2,1,0:T(8,128)(2,1)} %all_to_all.32), calls=%async_computation.1 | async-start | bytes 2424832 | tf_op jit(solution)/shard_map/all_to_all | solution.py:55
  272.0 22.9 %copy-start.7 = (bf16[256,2352]{0,1:T(8,128)(2,1)S(1)}, bf16[256,2352]{0,1:T(8,128)(2,1)}, u32[]{:S(2)}) copy-start(bf16[256,2352]{0,1:T(8,128)(2,1)} %fusion.12) | copy-start | bytes 3612676
  290.3 8.0 %collective-permute-start.9 = (f32[256,49]{0,1:T(8,128)S(1)}, f32[256,49]{0,1:T(8,128)S(1)}, u32[]{:S(2)}, u32[]{:S(2)}) collective-permute-start(f32[256,49]{0,1:T(8,128)S(1)} %slice.69), channel_id=1, source_target_pairs={{0,4},{4,8},{8,12},{12,16},{16,20},{20,24},{24,28},{1,5},{5,9},{9,... | collective-permute-start | bytes 150536 | tf_op jit(solution)/shard_map/ppermute | solution.py:16
  305.3 19.7 %all-to-all-start = ((bf16[4,588,256]{2,1,0:T(8,128)(2,1)}), bf16[4,588,256]{2,1,0:T(8,128)(2,1)S(1)}, u32[]{:S(2)}, u32[]{:S(2)}) async-start(bf16[4,588,256]{2,1,0:T(8,128)(2,1)} %all_to_all.28), calls=%async_computation | async-start | bytes 2424832 | tf_op jit(solution)/shard_map/all_to_all | solution.py:56
  308.9 65.8 %reduce-scatter.2.cloned.1.call-start = ((), (), s32[]{:S(2)}) async-start(), calls=%async_computation.3 | async-start | bytes 5242880 | tf_op jit(solution)/shard_map/reduce_scatter | solution.py:60
  325.7 1.8 copy-start.10
  326.4 1.0 copy-start.11
  331.3 136.8 %all-gather.2.cloned.1.call-start = ((), (), s32[]{:S(2)}) async-start(), calls=%async_computation.4 | async-start | bytes 2621440 | tf_op jit(solution)/shard_map/all_gather | solution.py:68
  468.1 4.9 %copy-start.9 = (bf16[1024,1024]{1,0:T(8,128)(2,1)S(1)}, bf16[1024,1024]{1,0:T(8,128)(2,1)}, u32[]{:S(2)}) copy-start(bf16[1024,1024]{1,0:T(8,128)(2,1)} %all-gather.2.cloned.1.call-done) | copy-start | bytes 6291460
Sparse Core Ops, SparseCore 0:
  331.4 43.1 reduce-scatter.1
  448.0 20.0 all-gather.1
where the time goes:
time: 489 us; the launch traced here: 482 us
  other arithmetic  150 us (31%)
  local copies, waits for them, and re-layouts  94.3 us (19%)
  waiting for transfers between devices  93.1 us (19%)
  blocking collectives  73.3 us (15%)
  starting transfers between devices  35.5 us (7%)
  matrix products  21.1 us (4%)
  between operations  14.8 us (3%)
    scatter-add x5, other arithmetic, apply_hamiltonian(): summed = jnp.zeros((values.shape[0], extended.shape[1]), jnp.float32).at[...  87.6 us
    psum x1, blocking collectives, body(): share = lax.psum(share, 'dom')  73.3 us
    gather x10, local copies, waits for them, and re-layouts, apply_hamiltonian(): cell_values = jnp.take(extended, connectivity, axis=1)  53.1 us
    reduce_scatter x1, waiting for transfers between devices, body(): lax.psum_scatter(jnp.einsum('ri,rj->ij', node_rows, image_rows, preferred...  43.3 us
    ppermute x10, starting transfers between devices, from_behind(): return lax.ppermute(block, axis, route)  27.4 us
    all_gather x1, waiting for transfers between devices, body(): lax.all_gather(share.astype(jnp.bfloat16), 'orb', axis=0, tiled=True)  20.2 us
    scatter-add x5, other arithmetic, apply_hamiltonian(): assembled = summed[:, :node_count].at[:, face_nodes].add(returned)  20.1 us
    transpose x5, local copies, waits for them, and re-layouts, apply_hamiltonian(): jnp.einsum('kij,okj->oki', cell_hamiltonian, cell_values, preferred_eleme...  18.7 us
  transfers between devices with their start and end apart: 14, of which 7 were waited for; matrix products, arithmetic and copies ran while one was open for 13% of the time, Pallas kernels for 0%

commit v1 on v0

v1 whole, which is shorter than its diff:
```python
import functools

import jax
import jax.numpy as jnp
from jax import lax
from jax.experimental import pallas as pl
from jax.experimental.pallas import tpu as pltpu
from jax.sharding import PartitionSpec as P

DEGREE = 4
CENTER = 1.5
HALF = 2.0
F32 = jnp.float32
BF16 = jnp.bfloat16
VMEM_LIMIT = 50 * 1024 * 1024


def up16(n):
    return (n + 15) // 16 * 16


def iota(shape, dim):
    return lax.broadcasted_iota(jnp.int32, shape, dim).astype(F32)


def to_col(row, rows):
    n = row.shape[1]
    return jnp.sum(jnp.where(iota((rows, n), 0) == iota((rows, n), 1), row, 0.0), axis=1, keepdims=True)


def to_row(col):
    n = col.shape[0]
    return jnp.sum(jnp.where(iota((n, n), 0) == iota((n, n), 1), col, 0.0), axis=0, keepdims=True)


def params():
    return pltpu.CompilerParams(vmem_limit_bytes=VMEM_LIMIT)


def face_kernel(face_ref, x_ref, pot_ref, fv_ref, fp_ref):
    rows = fv_ref.shape[0]
    nodes = x_ref.shape[0]
    col = to_col(face_ref[...].astype(F32) + 1.0, rows) - 1.0
    hit = col == iota((rows, nodes), 1)
    fv_ref[...] = jnp.dot(hit.astype(BF16), x_ref[...], preferred_element_type=F32).astype(BF16)
    fp_ref[...] = jnp.sum(jnp.where(hit, pot_ref[...], 0.0), axis=1, keepdims=True)


def order_kernel(fp, ip, conn_ref, face_ref, h_ref, x_ref, pot_ref, hcan_ref, v_ref, potc_ref, node_ref):
    cells, npc = conn_ref.shape
    nodes = x_ref.shape[0]
    face = face_ref.shape[1]
    stride = fp + ip
    cp = stride + fp
    c = pl.program_id(0)
    last = cells - 1
    row = conn_ref[pl.ds(c, 1), :].astype(F32)
    row_n = conn_ref[pl.ds(jnp.minimum(c + 1, last), 1), :].astype(F32)
    row_p = conn_ref[pl.ds(jnp.maximum(c - 1, 0), 1), :].astype(F32)
    col, col_n, col_p = to_col(row, npc), to_col(row_n, npc), to_col(row_p, npc)
    less = jnp.where(col < row, 1.0, 0.0).astype(BF16)
    shared_n = jnp.max(jnp.where(col_n == row, 1.0, 0.0), axis=0, keepdims=True)
    shared_p = jnp.max(jnp.where(col_p == row, 1.0, 0.0), axis=0, keepdims=True)
    fcol = to_col(face_ref[...].astype(F32), face)
    fhit = fcol == row
    on_face = jnp.max(jnp.where(fhit, 1.0, 0.0), axis=0, keepdims=True)
    face_slot = jnp.sum(jnp.where(fhit, iota((face, npc), 0), 0.0), axis=0, keepdims=True)
    first_f = jnp.where(c == 0, 1.0, 0.0)
    last_f = jnp.where(c == last, 1.0, 0.0)
    ghost = jnp.where(row >= float(nodes), 1.0, 0.0)
    top = last_f * ghost + (1.0 - last_f) * shared_n
    bot = first_f * on_face + (1.0 - first_f) * shared_p
    mid = 1.0 - top - bot
    ri = lax.broadcasted_iota(jnp.int32, (8, npc), 0)
    flags = jnp.where(ri == 0, top, jnp.where(ri == 1, bot, jnp.where(ri == 2, mid, 0.0)))
    ranks = jnp.dot(flags.astype(BF16), less, preferred_element_type=F32)
    bot_slot = first_f * face_slot + (1.0 - first_f) * ranks[1:2]
    slot = jnp.where(top > 0.5, ranks[0:1] + float(stride), jnp.where(bot > 0.5, bot_slot, ranks[2:3] + float(fp)))
    perm = iota((cp, npc), 0) == slot
    perm_b = jnp.where(perm, 1.0, 0.0).astype(BF16)
    half = jnp.dot(perm_b, h_ref[0], preferred_element_type=F32).astype(BF16)
    hcan_ref[0] = lax.dot_general(half, perm_b, (((1,), (1,)), ((), ())), preferred_element_type=F32).astype(BF16)
    node = jnp.sum(jnp.where(perm, row + 1.0, 0.0), axis=1, keepdims=True) - 1.0
    node = node[:stride]
    node_ref[0] = to_row(node)
    hit = node == iota((stride, nodes), 1)
    v_ref[...] = jnp.dot(jnp.where(hit, 1.0, 0.0).astype(BF16), x_ref[...], preferred_element_type=F32).astype(BF16)
    potc_ref[...] = jnp.sum(jnp.where(hit, pot_ref[...], 0.0), axis=1, keepdims=True)


def advance(image, now, before):
    if before is None:
        return (image - CENTER * now) / HALF
    return 2.0 * (image - CENTER * now) / HALF - before


def edge_kernel(step, fp, *refs):
    if step == 0:
        last_ref, ghost_ref, yb_ref, yt_ref, hb_ref, ht_ref, yf_ref, pb_ref, pt_ref = refs
        yf_ref[:fp] = yb_ref[:fp]
        yf_ref[fp:] = ghost_ref[...]
    else:
        if step == 1:
            last_ref, sb_ref, st_ref, rb_ref, rt_ref, now_ref, potf_ref, *refs = refs
            before = None
        else:
            last_ref, sb_ref, st_ref, rb_ref, rt_ref, now_ref, potf_ref, before_ref, *refs = refs
            before = before_ref[...].astype(F32)
        yb_ref, yt_ref, hb_ref, ht_ref, yf_ref, pb_ref, pt_ref = refs
        now = now_ref[...].astype(F32)
        total = jnp.concatenate([sb_ref[...] + rb_ref[...], st_ref[...] + rt_ref[...]], axis=0)
        value = advance(total + potf_ref[...] * now, now, before)
        dead = (lax.broadcasted_iota(jnp.int32, value.shape, 0) >= fp) & (last_ref[0] == 1)
        yf_ref[...] = jnp.where(dead, 0.0, value).astype(BF16)
    low, high = yf_ref[:fp], yf_ref[fp:]
    pb_ref[...] = jnp.dot(
        hb_ref[0], jnp.concatenate([low, yb_ref[fp:]], axis=0), preferred_element_type=F32
    )
    pt_ref[...] = jnp.dot(
        ht_ref[0], jnp.concatenate([yt_ref[...], high], axis=0), preferred_element_type=F32
    )


def bulk_kernel(step, fp, *refs):
    if step == 0 or step == DEGREE:
        y_ref, yf_ref, h_ref, pot_ref, out_ref = refs
    else:
        y_ref, yf_ref, h_ref, pot_ref, before_ref, out_ref = refs
    cells, cp = h_ref.shape[:2]
    stride = cp - fp
    carry = None
    for c in range(cells):
        if c == 0:
            v = jnp.concatenate([yf_ref[:fp], y_ref[fp:cp]], axis=0)
        elif c == cells - 1:
            v = jnp.concatenate([y_ref[c * stride :], yf_ref[fp:]], axis=0)
        else:
            v = y_ref[c * stride : c * stride + cp]
        prod = jnp.dot(h_ref[c], v, preferred_element_type=F32)
        if c == 0:
            rows, lo = prod[fp:stride], fp
            out_ref[:fp] = jnp.zeros((fp, out_ref.shape[1]), BF16)
        else:
            rows, lo = jnp.concatenate([prod[:fp] + carry, prod[fp:stride]], axis=0), 0
        carry = prod[stride:]
        at = slice(c * stride + lo, (c + 1) * stride)
        now = v[lo:stride].astype(F32)
        image = rows + pot_ref[at] * now
        if step == DEGREE:
            out_ref[at] = image.astype(BF16)
        else:
            before = None if step == 0 else before_ref[at].astype(F32)
            out_ref[at] = advance(image, now, before).astype(BF16)


def back_kernel(fp, node_ref, y_ref, low_ref, out_ref):
    rows = out_ref.shape[1]
    want = (lax.broadcasted_iota(jnp.int32, (rows, 1), 0) + pl.program_id(0) * rows).astype(F32)
    hit = jnp.where(want == node_ref[...], 1.0, 0.0).astype(BF16)
    out = jnp.dot(hit, y_ref[...], preferred_element_type=F32)
    out = out + jnp.dot(hit[:, :fp], low_ref[...], preferred_element_type=F32)
    out_ref[0] = out.astype(BF16)


def back_image_kernel(fp, node_ref, y_ref, sb_ref, rb_ref, now_ref, pot_ref, out_ref):
    rows = out_ref.shape[1]
    low = (sb_ref[...] + rb_ref[...] + pot_ref[...] * now_ref[...].astype(F32)).astype(BF16)
    want = (lax.broadcasted_iota(jnp.int32, (rows, 1), 0) + pl.program_id(0) * rows).astype(F32)
    hit = jnp.where(want == node_ref[...], 1.0, 0.0).astype(BF16)
    out = jnp.dot(hit, y_ref[...], preferred_element_type=F32)
    out = out + jnp.dot(hit[:, :fp], low, preferred_element_type=F32)
    out_ref[0] = out.astype(BF16)


def gram_kernel(scale, x_ref, y_ref, out_ref, rows_ref):
    parts, _, width = y_ref.shape

    @pl.when(pl.program_id(0) == 0)
    def _():
        for j in range(parts):
            rows_ref[:, j * width : (j + 1) * width] = y_ref[j]

    out_ref[0] = (
        lax.dot_general(x_ref[0], rows_ref[...], (((0,), (0,)), ((), ())), preferred_element_type=F32) * scale
    ).astype(BF16)


def residual_kernel(x_ref, y_ref, p_ref, out_ref):
    parts, _, width = x_ref.shape
    x = jnp.concatenate([x_ref[j] for j in range(parts)], axis=1)
    y = jnp.concatenate([y_ref[j] for j in range(parts)], axis=1)
    out_ref[...] = y.astype(F32) - jnp.dot(x, p_ref[...], preferred_element_type=F32)


def full(shape):
    return pl.BlockSpec(shape, lambda i: (0,) * len(shape))


def swap(block, axis, bit):
    return lax.ppermute(block, axis, [(i, i ^ bit) for i in range(lax.axis_size(axis))])


def shift(block, axis, distance):
    n = lax.axis_size(axis)
    return lax.ppermute(block, axis, [(i, i + distance) for i in range(n) if 0 <= i + distance < n])


def body(orbitals, potential, cell_hamiltonian, connectivity, face_nodes):
    nodes, width = orbitals.shape
    cells, npc = connectivity.shape
    face = face_nodes.shape[0]
    fp, ip = up16(face), up16(npc - 2 * face)
    fp = (fp + 63) // 64 * 64
    stride = fp + ip
    cp = stride + fp
    total = cells * stride
    orb, dom = lax.axis_size("orb"), lax.axis_size("dom")
    d = lax.axis_index("dom")
    o = lax.axis_index("orb")
    sds = jax.ShapeDtypeStruct
    pot_row = potential.reshape(1, nodes)
    face_row = face_nodes.reshape(1, face)

    fv, fpot = pl.pallas_call(
        face_kernel,
        out_shape=(sds((fp, width), BF16), sds((fp, 1), F32)),
        compiler_params=params(),
    )(face_row, orbitals, pot_row)
    ghost = shift(fv, "dom", -1)
    ghost_pot = shift(fpot, "dom", -1)

    hcan, y, pot, node = pl.pallas_call(
        functools.partial(order_kernel, fp, ip),
        grid=(cells,),
        in_specs=[
            full((cells, npc)),
            full((1, face)),
            pl.BlockSpec((1, npc, npc), lambda c: (c, 0, 0)),
            full((nodes, width)),
            full((1, nodes)),
        ],
        out_specs=[
            pl.BlockSpec((1, cp, cp), lambda c: (c, 0, 0)),
            pl.BlockSpec((stride, width), lambda c: (c, 0)),
            pl.BlockSpec((stride, 1), lambda c: (c, 0)),
            pl.BlockSpec((1, 1, stride), lambda c: (c, 0, 0)),
        ],
        out_shape=[
            sds((cells, cp, cp), BF16),
            sds((total, width), BF16),
            sds((total, 1), F32),
            sds((cells, 1, stride), F32),
        ],
        compiler_params=params(),
        cost_estimate=pl.CostEstimate(flops=4 * total * nodes * width, bytes_accessed=8 << 20, transcendentals=0),
    )(connectivity, face_row, cell_hamiltonian, orbitals, pot_row)
    node_row = node.reshape(1, total)
    potf = jnp.concatenate([pot[:fp], ghost_pot], axis=0)
    is_last = (d == dom - 1).astype(jnp.int32).reshape(1)

    smem = pl.BlockSpec(memory_space=pltpu.SMEM)
    small = lambda: full((fp, width))
    end_specs = [
        pl.BlockSpec((cp, width), lambda i: (0, 0)),
        pl.BlockSpec((stride, width), lambda i: (cells - 1, 0)),
        pl.BlockSpec((1, fp, cp), lambda i: (0, 0, 0)),
        pl.BlockSpec((1, fp, cp), lambda i: (cells - 1, stride // fp, 0)),
    ]
    edge_out = dict(
        grid=(1,),
        out_specs=[full((2 * fp, width)), small(), small()],
        out_shape=[sds((2 * fp, width), BF16), sds((fp, width), F32), sds((fp, width), F32)],
        compiler_params=params(),
        cost_estimate=pl.CostEstimate(flops=4 * fp * cp * width, bytes_accessed=1 << 20, transcendentals=0),
    )
    bulk_cost = pl.CostEstimate(flops=2 * cells * cp * cp * width, bytes_accessed=6 << 20, transcendentals=0)

    before = yf_before = None
    yf = sums = None
    for step in range(DEGREE + 1):
        ends = [y, y, hcan, hcan]
        if step == 0:
            yf, sb, st = pl.pallas_call(
                functools.partial(edge_kernel, step, fp), in_specs=[smem, small()] + end_specs, **edge_out
            )(is_last, ghost, *ends)
        else:
            args = [sb, st, rb, rt, yf, potf] + ([yf_before] if step > 1 else [])
            specs = [small()] * 4 + [full((2 * fp, width)), full((2 * fp, 1))]
            specs += [full((2 * fp, width))] if step > 1 else []
            yf_new, sb, st = pl.pallas_call(
                functools.partial(edge_kernel, step, fp), in_specs=[smem] + specs + end_specs, **edge_out
            )(is_last, *args, *ends)
            yf_before, yf = yf, yf_new
        rb = shift(st, "dom", 1)
        if step < DEGREE:
            rt = shift(sb, "dom", -1)
        extra = [] if step in (0, DEGREE) else [before]
        out = pl.pallas_call(
            functools.partial(bulk_kernel, step, fp),
            out_shape=sds((total, width), BF16),
            compiler_params=params(),
            cost_estimate=bulk_cost,
        )(y, yf, hcan, pot, *extra)
        if step < DEGREE:
            before, y = y, out
    image = out

    back = dict(
        grid=(orb,),
        out_specs=pl.BlockSpec((1, nodes // orb, width), lambda i: (i, 0, 0)),
        out_shape=sds((orb, nodes // orb, width), BF16),
        compiler_params=params(),
        cost_estimate=pl.CostEstimate(flops=2 * total * nodes * width, bytes_accessed=4 << 20, transcendentals=0),
    )
    x_cols = pl.pallas_call(
        functools.partial(back_kernel, fp), in_specs=[full((1, total)), full((total, width)), small()], **back
    )(node_row, y, yf[:fp])
    x_rows = lax.all_to_all(x_cols, "orb", split_axis=0, concat_axis=0, tiled=True)
    i_cols = pl.pallas_call(
        functools.partial(back_image_kernel, fp),
        in_specs=[full((1, total)), full((total, width)), small(), small(), small(), full((fp, 1))],
        **back,
    )(node_row, image, sb, rb, yf[:fp], pot[:fp])
    i_rows = lax.all_to_all(i_cols, "orb", split_axis=0, concat_axis=0, tiled=True)

    rows = nodes // orb
    cols = orb * width
    share = pl.pallas_call(
        functools.partial(gram_kernel, 1.0 / (nodes * dom)),
        grid=(orb,),
        in_specs=[pl.BlockSpec((1, rows, width), lambda i: (i, 0, 0)), full((orb, rows, width))],
        out_specs=pl.BlockSpec((1, width, cols), lambda i: (i, 0, 0)),
        out_shape=sds((orb, width, cols), BF16),
        scratch_shapes=[pltpu.VMEM((rows, cols), BF16)],
        compiler_params=params(),
    )(x_rows, i_rows)

    hops = []
    for axis, me, size in (("orb", o, orb), ("dom", d, dom)):
        if axis == "dom":
            share = share.reshape(dom, width // dom, cols)
        bit = 1
        while bit < size:
            share = share.reshape((share.shape[0] // 2, 2) + share.shape[1:])
            mine = (me // bit) % 2
            keep = lax.dynamic_index_in_dim(share, mine, 1, keepdims=False)
            give = lax.dynamic_index_in_dim(share, 1 - mine, 1, keepdims=False)
            got = swap(give, axis, bit)
            share = (keep.astype(F32) + got.astype(F32)).astype(BF16)
            hops.append((axis, bit, mine))
            bit *= 2
    for axis, bit, mine in reversed(hops):
        if axis == "orb" and share.shape[0] == dom and bit * 2 == orb:
            share = share.reshape(1, width, cols)
        got = swap(share, axis, bit)
        share = jnp.where(mine == 0, jnp.stack([share, got], axis=1), jnp.stack([got, share], axis=1))
        share = share.reshape((share.shape[0] * 2,) + share.shape[2:])
    projected = share.reshape(cols, cols)

    residual = pl.pallas_call(
        residual_kernel, out_shape=sds((rows, cols), F32), compiler_params=params()
    )(x_rows, i_rows, projected)
    return (residual, projected)


def solution(mesh):
    return jax.shard_map(
        body,
        mesh=mesh,
        in_specs=(P("dom", "orb"), P("dom"), P("dom", None, None), P("dom", None), P("dom")),
        out_specs=(P(("dom", "orb"), None), P()),
        check_vma=False,
    )
```

time: 489 us -> 214 us (0.44); the launches traced: 482 us -> 212 us
  other arithmetic: 150 us -> 7.04 us
  local copies, waits for them, and re-layouts: 94.3 us -> 14 us
  blocking collectives: 73.3 us -> 0 us
  Pallas kernels: 0 us -> 58 us
  matrix products: 21.1 us -> 0 us
  starting transfers between devices: 35.5 us -> 55.2 us
  waiting for transfers between devices: 93.1 us -> 76.9 us
  between operations: 14.8 us -> 1.11 us
    scatter-add x10 -> x0, other arithmetic: 108 us -> none  [the longest x5 87.6 us: apply_hamiltonian(): summed = jnp.zeros((values.shape[0], extended.shape[1]), jnp.float32).at[...]
    psum x1 -> x0, blocking collectives: 73.3 us -> none  [body(): share = lax.psum(share, 'dom')]
    gather x15 -> x0, local copies, waits for them, and re-layouts: 60.7 us -> none  [the longest x10 53.1 us: apply_hamiltonian(): cell_values = jnp.take(extended, connectivity, axis=1)]
    pallas_call x0 -> x16, Pallas kernels: none -> 58 us  [the longest x1 19.1 us: body(): pl.pallas_call(functools.partial(order_kernel, fp, ip), grid=(cells,), in...]
    reduce_scatter x1 -> x0, waiting for transfers between devices: 43.3 us -> none  [body(): lax.psum_scatter(jnp.einsum('ri,rj->ij', node_rows, image_rows, preferred...]
    ppermute x10 -> x21, waiting for transfers between devices: 17.1 us -> 56.8 us  [the longest x10 50.4 us: swap(): lax.ppermute(block, axis, [(i, i ^ bit) for i in range(lax.axis_size(axis...]
    dot_general x7 -> x0, matrix products: 21.1 us -> none  [the longest x5 12.4 us: apply_hamiltonian(): jnp.einsum('kij,okj->oki', cell_hamiltonian, cell_values, preferred_eleme...]
    all_gather x1 -> x0, waiting for transfers between devices: 20.2 us -> none  [body(): lax.all_gather(share.astype(jnp.bfloat16), 'orb', axis=0, tiled=True)]
  transfers between devices with their start and end apart: 14 -> 23, of which waited for: 7 -> 16; matrix products, arithmetic and copies ran while one was open for 13% -> 2% of each run, Pallas kernels for 0% -> 19%
where the time goes in v1:
time: 214 us; the launch traced here: 212 us
  waiting for transfers between devices  76.9 us (36%)
  Pallas kernels  58 us (27%)
  starting transfers between devices  55.2 us (26%)
  local copies, waits for them, and re-layouts  14 us (7%)
  other arithmetic  7.04 us (3%)
    ppermute x10, waiting for transfers between devices, swap(): lax.ppermute(block, axis, [(i, i ^ bit) for i in range(lax.axis_size(axis...  50.4 us
    ppermute x11, starting transfers between devices, shift(): lax.ppermute(block, axis, [(i, i + distance) for i in range(n) if 0 <= i...  31.4 us
    pallas_call x1, Pallas kernels, body(): pl.pallas_call(functools.partial(order_kernel, fp, ip), grid=(cells,), in...  19.1 us
    all_to_all x1, waiting for transfers between devices, body(): lax.all_to_all(i_cols, 'orb', split_axis=0, concat_axis=0, tiled=True)  16 us
    ppermute x10, starting transfers between devices, swap(): lax.ppermute(block, axis, [(i, i ^ bit) for i in range(lax.axis_size(axis...  15.8 us
    pallas_call x5, Pallas kernels, body(): pl.pallas_call(functools.partial(bulk_kernel, step, fp), out_shape=sds((t...  15 us
    unnamed x27, local copies, waits for them, and re-layouts  9.67 us
    ppermute x11, waiting for transfers between devices, shift(): lax.ppermute(block, axis, [(i, i + distance) for i in range(n) if 0 <= i...  6.42 us
  transfers between devices with their start and end apart: 23, of which 16 were waited for; matrix products, arithmetic and copies ran while one was open for 2% of the time, Pallas kernels for 19%

profile of v1, /device:TPU:0, one launch (start us, length us, event | category | flops | bytes accessed | tf_op | source)
XLA Modules:
  0.0 212.3 jit_solution(10056249637575204317)
XLA Ops:
  0.6 0.7 reshape.263.pot_ref
  1.3 1.3 copy-done.7
  2.6 0.7 copy-done.9
  3.3 0.4 shard_map.69
  3.7 1.3 collective-permute-start
  5.0 1.4 collective-permute-start.3
  6.5 3.2 %copy.17.h_ref = bf16[8,343,343]{2,1,0:T(8,128)(2,1)} copy(bf16[8,343,343]{2,0,1:T(8,128)(2,1)} %param.7) | data formatting | bytes 3764768 | tf_op args[2]
  9.7 19.1 %shard_map.68 = (bf16[8,384,384]{2,1,0:T(8,128)(2,1)}, bf16[2560,256]{1,0:T(8,128)(2,1)S(1)}, f32[2560,1]{1,0:T(8,128)S(1)}, f32[8,1,320]{2,1,0:T(1,128)S(1)}) custom-call(s32[8,343]{1,0:T(8,128)S(1)} %copy-done.11, s32[1,49]{1,0:T(1,128)S(1)} %bitcast.34, bf16[8,343,343]{2,1,0:T(8,128)(2,1)} %copy.17.h_ref, bf16[2352,256]{1,0:T(8,128)(2,1)S(1)} %copy-done.8, ...), custom_call_target="tpu_custom_call" | custom-call | flops 6165626880 | bytes 8388608 | tf_op jit(solution)/shard_map/pallas_call | solution.py:232
  28.9 2.1 %copy-done = bf16[8,384,384]{2,1,0:T(8,128)(2,1)S(1)} copy-done((bf16[8,384,384]{2,1,0:T(8,128)(2,1)S(1)}, bf16[8,384,384]{2,1,0:T(8,128)(2,1)}, u32[]{:S(2)}) %copy-start) | copy-done | bytes 2359320
  31.2 6.1 %collective-permute-start.1 = (f32[64,256]{1,0:T(8,128)S(1)}, f32[64,256]{1,0:T(8,128)S(1)}, u32[]{:S(2)}, u32[]{:S(2)}) collective-permute-start(f32[64,256]{1,0:T(8,128)S(1)} %get-tuple-element.30.refs_2_), channel_id=1, source_target_pairs={{0,4},{4,8},{8,12},{12,16},{16,20},{20,24},{24,28},{1,5},{5,9},{9,... | collective-permute-start | bytes 196616 | tf_op jit(solution)/shard_map/ppermute | solution.py:205
  37.3 1.3 collective-permute-start.2
  38.7 2.7 %shard_map.71.refs_7_.refs_8_.refs_0_.refs_4_ = bf16[2560,256]{1,0:T(8,128)(2,1)S(1)} custom-call(bf16[2560,256]{1,0:T(8,128)(2,1)S(1)} %get-tuple-element.24.refs_2_.refs_3_.refs_0_.refs_4_, bf16[128,256]{1,0:T(8,128)(2,1)S(1)} %get-tuple-element.27.refs_1_.refs_5_.refs_7_, ...), custom_call_target="tpu_custom_call" | custom-call | flops 603979776 | bytes 6291456 | tf_op jit(solution)/shard_map/pallas_call | solution.py:298
  41.4 3.0 %collective-permute-done.2.refs_4_ = f32[64,256]{1,0:T(8,128)S(1)} collective-permute-done((f32[64,256]{1,0:T(8,128)S(1)}, f32[64,256]{1,0:T(8,128)S(1)}, u32[]{:S(2)}, u32[]{:S(2)}) %collective-permute-start.2) | collective-permute-done | bytes 65568 | tf_op jit(solution)/shard_map/ppermute | solution.py:205
  44.4 1.1 shard_map.72
  45.5 4.8 %collective-permute-start.4 = (f32[64,256]{1,0:T(8,128)S(1)}, f32[64,256]{1,0:T(8,128)S(1)}, u32[]{:S(2)}, u32[]{:S(2)}) collective-permute-start(f32[64,256]{1,0:T(8,128)S(1)} %get-tuple-element.34.refs_2_), channel_id=1, source_target_pairs={{0,4},{4,8},{8,12},{12,16},{16,20},{20,24},{24,28},{1,5},{5,9},{9,... | collective-permute-start | bytes 196616 | tf_op jit(solution)/shard_map/ppermute | solution.py:205
  50.3 1.3 collective-permute-start.5
  51.6 3.2 %shard_map.73.refs_8_.refs_9_.refs_0_.refs_4_ = bf16[2560,256]{1,0:T(8,128)(2,1)S(1)} custom-call(bf16[2560,256]{1,0:T(8,128)(2,1)S(1)} %shard_map.71.refs_7_.refs_8_.refs_0_.refs_4_, bf16[128,256]{1,0:T(8,128)(2,1)S(1)} %get-tuple-element.32.refs_1_.refs_5_.refs_7_, bf16[8,384,384]{2,1,0:T(8,128)(2,1)} %get-tuple-element.26.refs_4_.refs_5_.refs_2_.refs_9_.refs_10_.refs_11_, ...), custom_call_target="tpu_custom_call" | custom-call | flops 603979776 | bytes 6291456 | tf_op jit(solution)/shard_map/pallas_call | solution.py:298
  54.8 1.6 collective-permute-done.5.refs_4_
  56.5 1.1 shard_map.74
  57.6 3.9 %collective-permute-start.6 = (f32[64,256]{1,0:T(8,128)S(1)}, f32[64,256]{1,0:T(8,128)S(1)}, u32[]{:S(2)}, u32[]{:S(2)}) collective-permute-start(f32[64,256]{1,0:T(8,128)S(1)} %get-tuple-element.37.refs_2_), channel_id=1, source_target_pairs={{0,4},{4,8},{8,12},{12,16},{16,20},{20,24},{24,28},{1,5},{5,9},{9,... | collective-permute-start | bytes 196616 | tf_op jit(solution)/shard_map/ppermute | solution.py:205
  61.5 1.3 collective-permute-start.7
  62.8 3.2 %shard_map.75.refs_8_.refs_9_.refs_0_ = bf16[2560,256]{1,0:T(8,128)(2,1)S(1)} custom-call(bf16[2560,256]{1,0:T(8,128)(2,1)S(1)} %shard_map.73.refs_8_.refs_9_.refs_0_.refs_4_, bf16[128,256]{1,0:T(8,128)(2,1)S(1)} %get-tuple-element.35.refs_1_.refs_5_.refs_7_, bf16[8,384,384]{2,1,0:T(8,128)(2,1)} %get-tuple-element.26.refs_4_.refs_5_.refs_2_.refs_9_.refs_10_.refs_11_, ...), custom_call_target="tpu_custom_call" | custom-call | flops 603979776 | bytes 6291456 | tf_op jit(solution)/shard_map/pallas_call | solution.py:298
  66.1 1.6 collective-permute-done.7.refs_4_
  67.7 1.1 shard_map.76
  68.8 4.3 %collective-permute-start.8 = (f32[64,256]{1,0:T(8,128)S(1)}, f32[64,256]{1,0:T(8,128)S(1)}, u32[]{:S(2)}, u32[]{:S(2)}) collective-permute-start(f32[64,256]{1,0:T(8,128)S(1)} %get-tuple-element.40.refs_2_), channel_id=1, source_target_pairs={{0,4},{4,8},{8,12},{12,16},{16,20},{20,24},{24,28},{1,5},{5,9},{9,... | collective-permute-start | bytes 196616 | tf_op jit(solution)/shard_map/ppermute | solution.py:205
  73.1 1.3 collective-permute-start.9
  74.6 1.3 copy-done.5
  75.9 3.2 %shard_map.77.refs_8_.refs_9_.y_ref.refs_0_ = bf16[2560,256]{1,0:T(8,128)(2,1)S(1)} custom-call(bf16[2560,256]{1,0:T(8,128)(2,1)S(1)} %copy-done.5, bf16[128,256]{1,0:T(8,128)(2,1)S(1)} %get-tuple-element.38.refs_1_.refs_5_, bf16[8,384,384]{2,1,0:T(8,128)(2,1)} %get-tuple-element.26.refs_4_.refs_5_.refs_2_.refs_9_.refs_10_.refs_11_, ...), custom_call_target="tpu_custom_call" | custom-call | flops 603979776 | bytes 6291456 | tf_op jit(solution)/shard_map/pallas_call | solution.py:298
  79.3 1.1 shard_map.78
  80.4 4.1 %shard_map.79 = bf16[4,588,256]{2,1,0:T(8,128)(2,1)S(1)} custom-call(f32[1,2560]{1,0:T(1,128)S(1)} %reshape.264.node_ref, bf16[2560,256]{1,0:T(8,128)(2,1)S(1)} %shard_map.77.refs_8_.refs_9_.y_ref.refs_0_, bf16[64,256]{1,0:T(8,128)(2,1)S(1)} %slice.9.low_ref.now_ref), custom_call_target="tpu_custom_call" | custom-call | flops 3082813440 | bytes 4194304 | tf_op jit(solution)/shard_map/pallas_call | solution.py:315
  84.5 1.0 copy-done.6
  85.6 4.3 %all-to-all-start = ((bf16[4,588,256]{2,1,0:T(8,128)(2,1)}), bf16[4,588,256]{2,1,0:T(8,128)(2,1)}, u32[]{:S(2)}, u32[]{:S(2)}) async-start(bf16[4,588,256]{2,1,0:T(8,128)(2,1)} %copy-done.6), calls=%async_computation | async-start | bytes 2424832 | tf_op jit(solution)/shard_map/all_to_all | solution.py:318
  89.8 4.3 %collective-permute-start.10 = (f32[64,256]{1,0:T(8,128)S(1)}, f32[64,256]{1,0:T(8,128)S(1)}, u32[]{:S(2)}, u32[]{:S(2)}) collective-permute-start(f32[64,256]{1,0:T(8,128)S(1)} %get-tuple-element.43), channel_id=1, source_target_pairs={{0,4},{4,8},{8,12},{12,16},{16,20},{20,24},{24,28},{1,5},{5,9},{9,... | collective-permute-start | bytes 196616 | tf_op jit(solution)/shard_map/ppermute | solution.py:205
  94.2 2.6 %shard_map.80.y_ref = bf16[2560,256]{1,0:T(8,128)(2,1)S(1)} custom-call(bf16[2560,256]{1,0:T(8,128)(2,1)S(1)} %shard_map.77.refs_8_.refs_9_.y_ref.refs_0_, bf16[128,256]{1,0:T(8,128)(2,1)S(1)} %get-tuple-element.41.refs_1_, bf16[8,384,384]{2,1,0:T(8,128)(2,1)} %get-tuple-element.26.refs_4_.refs_5_.refs_2_.refs_9_.refs_10_.refs_11_, ...), custom_call_target="tpu_custom_call" | custom-call | flops 603979776 | bytes 6291456 | tf_op jit(solution)/shard_map/pallas_call | solution.py:298
  96.8 5.1 %shard_map.81 = bf16[4,588,256]{2,1,0:T(8,128)(2,1)} custom-call(f32[1,2560]{1,0:T(1,128)S(1)} %reshape.264.node_ref, bf16[2560,256]{1,0:T(8,128)(2,1)S(1)} %shard_map.80.y_ref, f32[64,256]{1,0:T(8,128)S(1)} %get-tuple-element.42.sb_ref, f32[64,256]{1,0:T(8,128)S(1)} %collective-permute-done.10.rb_ref, bf16[64,256]{1,0:T(8,128)(2,1)S(1)} %slice.9.low_ref.now_ref, ...), custom_call_target="tpu_custom_call" | custom-call | flops 3082813440 | bytes 4194304 | tf_op jit(solution)/shard_map/pallas_call | solution.py:319
  102.0 4.1 %all-to-all-done.x_ref = bf16[4,588,256]{2,1,0:T(8,128)(2,1)} async-done(((bf16[4,588,256]{2,1,0:T(8,128)(2,1)}), bf16[4,588,256]{2,1,0:T(8,128)(2,1)}, u32[]{:S(2)}, u32[]{:S(2)}) %all-to-all-start) | async-done | bytes 1204256 | tf_op jit(solution)/shard_map/all_to_all | solution.py:318
  106.1 3.7 %all-to-all-start.1 = ((bf16[4,588,256]{2,1,0:T(8,128)(2,1)}), bf16[4,588,256]{2,1,0:T(8,128)(2,1)S(1)}, u32[]{:S(2)}, u32[]{:S(2)}) async-start(bf16[4,588,256]{2,1,0:T(8,128)(2,1)} %shard_map.81), calls=%async_computation.1 | async-start | bytes 2424832 | tf_op jit(solution)/shard_map/all_to_all | solution.py:324
  109.9 16.0 %all-to-all-done.1.y_ref = bf16[4,588,256]{2,1,0:T(8,128)(2,1)S(1)} async-done(((bf16[4,588,256]{2,1,0:T(8,128)(2,1)}), bf16[4,588,256]{2,1,0:T(8,128)(2,1)S(1)}, u32[]{:S(2)}, u32[]{:S(2)}) %all-to-all-start.1) | async-done | bytes 1204256 | tf_op jit(solution)/shard_map/all_to_all | solution.py:324
  125.8 4.9 %shard_map.82 = bf16[4,256,1024]{2,1,0:T(8,128)(2,1)} custom-call(bf16[4,588,256]{2,1,0:T(8,128)(2,1)} %all-to-all-done.x_ref, bf16[4,588,256]{2,1,0:T(8,128)(2,1)S(1)} %all-to-all-done.1.y_ref), custom_call_target="tpu_custom_call" | custom-call | tf_op jit(solution)/shard_map/pallas_call | solution.py:328
  130.8 2.4 %dynamic-slice_bitcast_fusion = bf16[2,256,1024]{2,1,0:T(8,128)(2,1)} fusion(bf16[2,2,256,1024]{3,2,1,0:T(8,128)(2,1)} %bitcast.35, s32[]{:T(128)S(6)} %select_n.192), kind=kLoop, calls=%fused_computation.6 | loop fusion | bytes 2097156 | tf_op jit(solution)/shard_map/jit(dynamic_index_in_dim)/squeeze | solution.py:347
  133.2 3.0 %collective-permute-done.11 = bf16[2,256,1024]{2,1,0:T(8,128)(2,1)} collective-permute-done((bf16[2,256,1024]{2,1,0:T(8,128)(2,1)}, bf16[2,256,1024]{2,1,0:T(8,128)(2,1)}, u32[]{:S(2)}, u32[]{:S(2)}) %collective-permute-start.11) | collective-permute-done | bytes 1048608 | tf_op jit(solution)/shard_map/ppermute | solution.py:200
  136.2 2.6 %fusion = bf16[2,256,1024]{2,1,0:T(8,128)(2,1)} fusion(bf16[2,256,1024]{2,1,0:T(8,128)(2,1)} %collective-permute-done.11, bf16[2,2,256,1024]{3,2,1,0:T(8,128)(2,1)S(1)} %bitcast.36, s32[]{:T(128)S(6)} %select_n.191), kind=kLoop, calls=%fused_computation.2 | loop fusion | flops 2097152 | bytes 3145732 | tf_op jit(solution)/shard_map/convert_element_type | solution.py:349
  138.8 1.1 constant_dynamic-slice_fusion.1
  139.8 0.4 collective-permute-start.12
  140.3 13.6 %collective-permute-done.12 = bf16[1,256,1024]{2,1,0:T(8,128)(2,1)S(1)} collective-permute-done((bf16[1,256,1024]{2,1,0:T(8,128)(2,1)S(1)}, bf16[1,256,1024]{2,1,0:T(8,128)(2,1)S(1)}, u32[]{:S(2)}, u32[]{:S(2)}) %collective-permute-start.12) | collective-permute-done | bytes 524320 | tf_op jit(solution)/shard_map/ppermute | solution.py:200
  153.9 1.2 add_convert_fusion
  155.1 2.5 %collective-permute-start.13 = (bf16[4,32,1024]{2,1,0:T(8,128)(2,1)S(1)}, bf16[4,32,1024]{2,1,0:T(8,128)(2,1)S(1)}, u32[]{:S(2)}, u32[]{:S(2)}) collective-permute-start(bf16[4,32,1024]{2,1,0:T(8,128)(2,1)S(1)} %dynamic-slice_bitcast_fusion.1), channel_id=1, source_target_pairs={{0,4},{4,0},{8,12},{12,8},{16,20},{20,16},{24,28},{28,24},{1,5},{5... | collective-permute-start | bytes 786440 | tf_op jit(solution)/shard_map/ppermute | solution.py:200
  157.6 5.8 %collective-permute-done.13 = bf16[4,32,1024]{2,1,0:T(8,128)(2,1)S(1)} collective-permute-done((bf16[4,32,1024]{2,1,0:T(8,128)(2,1)S(1)}, bf16[4,32,1024]{2,1,0:T(8,128)(2,1)S(1)}, u32[]{:S(2)}, u32[]{:S(2)}) %collective-permute-start.13) | collective-permute-done | bytes 262176 | tf_op jit(solution)/shard_map/ppermute | solution.py:200
  163.5 2.4 %collective-permute-start.14 = (bf16[2,32,1024]{2,1,0:T(8,128)(2,1)S(1)}, bf16[2,32,1024]{2,1,0:T(8,128)(2,1)S(1)}, u32[]{:S(2)}, u32[]{:S(2)}) collective-permute-start(bf16[2,32,1024]{2,1,0:T(8,128)(2,1)S(1)} %dynamic-slice_bitcast_fusion.2), channel_id=1, source_target_pairs={{0,8},{4,12},{8,0},{12,4},{16,24},{20,28},{24,16},{28,20},{1,9},{5... | collective-permute-start | bytes 393224 | tf_op jit(solution)/shard_map/ppermute | solution.py:200
  165.9 2.9 %collective-permute-done.14 = bf16[2,32,1024]{2,1,0:T(8,128)(2,1)S(1)} collective-permute-done((bf16[2,32,1024]{2,1,0:T(8,128)(2,1)S(1)}, bf16[2,32,1024]{2,1,0:T(8,128)(2,1)S(1)}, u32[]{:S(2)}, u32[]{:S(2)}) %collective-permute-start.14) | collective-permute-done | bytes 131104 | tf_op jit(solution)/shard_map/ppermute | solution.py:200
  168.9 3.4 %collective-permute-start.15 = (bf16[1,32,1024]{2,1,0:T(8,128)(2,1)S(1)}, bf16[1,32,1024]{2,1,0:T(8,128)(2,1)S(1)}, u32[]{:S(2)}, u32[]{:S(2)}) collective-permute-start(bf16[1,32,1024]{2,1,0:T(8,128)(2,1)S(1)} %constant_dynamic-slice_fusion), channel_id=1, source_target_pairs={{0,16},{4,20},{8,24},{12,28},{16,0},{20,4},{24,8},{28,12},{1,17},{... | collective-permute-start | bytes 196616 | tf_op jit(solution)/shard_map/ppermute | solution.py:200
  172.3 2.5 %collective-permute-done.15 = bf16[1,32,1024]{2,1,0:T(8,128)(2,1)S(1)} collective-permute-done((bf16[1,32,1024]{2,1,0:T(8,128)(2,1)S(1)}, bf16[1,32,1024]{2,1,0:T(8,128)(2,1)S(1)}, u32[]{:S(2)}, u32[]{:S(2)}) %collective-permute-start.15) | collective-permute-done | bytes 65568 | tf_op jit(solution)/shard_map/ppermute | solution.py:200
  174.9 3.3 %collective-permute-start.16 = (bf16[1,32,1024]{2,1,0:T(8,128)(2,1)S(1)}, bf16[1,32,1024]{2,1,0:T(8,128)(2,1)S(1)}, u32[]{:S(2)}, u32[]{:S(2)}) collective-permute-start(bf16[1,32,1024]{2,1,0:T(8,128)(2,1)S(1)} %add_convert_fusion.1), channel_id=1, source_target_pairs={{0,16},{4,20},{8,24},{12,28},{16,0},{20,4},{24,8},{28,12},{1,17},{... | collective-permute-start | bytes 196616 | tf_op jit(solution)/shard_map/ppermute | solution.py:200
  178.2 2.3 %collective-permute-done.16 = bf16[1,32,1024]{2,1,0:T(8,128)(2,1)S(1)} collective-permute-done((bf16[1,32,1024]{2,1,0:T(8,128)(2,1)S(1)}, bf16[1,32,1024]{2,1,0:T(8,128)(2,1)S(1)}, u32[]{:S(2)}, u32[]{:S(2)}) %collective-permute-start.16) | collective-permute-done | bytes 65568 | tf_op jit(solution)/shard_map/ppermute | solution.py:200
  180.5 2.6 %collective-permute-start.17 = (bf16[2,32,1024]{2,1,0:T(8,128)(2,1)S(1)}, bf16[2,32,1024]{2,1,0:T(8,128)(2,1)S(1)}, u32[]{:S(2)}, u32[]{:S(2)}) collective-permute-start(bf16[2,32,1024]{2,1,0:T(8,128)(2,1)S(1)} %maximum_select_fusion.6), channel_id=1, source_target_pairs={{0,8},{4,12},{8,0},{12,4},{16,24},{20,28},{24,16},{28,20},{1,9},{5... | collective-permute-start | bytes 393224 | tf_op jit(solution)/shard_map/ppermute | solution.py:200
  183.2 2.9 %collective-permute-done.17 = bf16[2,32,1024]{2,1,0:T(8,128)(2,1)S(1)} collective-permute-done((bf16[2,32,1024]{2,1,0:T(8,128)(2,1)S(1)}, bf16[2,32,1024]{2,1,0:T(8,128)(2,1)S(1)}, u32[]{:S(2)}, u32[]{:S(2)}) %collective-permute-start.17) | collective-permute-done | bytes 131104 | tf_op jit(solution)/shard_map/ppermute | solution.py:200
  186.1 0.7 collective-permute-start.18
  186.8 5.8 %collective-permute-done.18 = bf16[4,32,1024]{2,1,0:T(8,128)(2,1)S(1)} collective-permute-done((bf16[4,32,1024]{2,1,0:T(8,128)(2,1)S(1)}, bf16[4,32,1024]{2,1,0:T(8,128)(2,1)S(1)}, u32[]{:S(2)}, u32[]{:S(2)}) %collective-permute-start.18) | collective-permute-done | bytes 262176 | tf_op jit(solution)/shard_map/ppermute | solution.py:200
  192.6 0.4 collective-permute-start.19
  193.1 8.8 %collective-permute-done.19 = bf16[1,256,1024]{2,1,0:T(8,128)(2,1)S(1)} collective-permute-done((bf16[1,256,1024]{2,1,0:T(8,128)(2,1)S(1)}, bf16[1,256,1024]{2,1,0:T(8,128)(2,1)S(1)}, u32[]{:S(2)}, u32[]{:S(2)}) %collective-permute-start.19) | collective-permute-done | bytes 524320 | tf_op jit(solution)/shard_map/ppermute | solution.py:200
  201.9 1.1 maximum_select_fusion.2
  203.2 2.7 %collective-permute-done.20 = bf16[2,256,1024]{2,1,0:T(8,128)(2,1)S(1)} collective-permute-done((bf16[2,256,1024]{2,1,0:T(8,128)(2,1)}, bf16[2,256,1024]{2,1,0:T(8,128)(2,1)S(1)}, u32[]{:S(2)}, u32[]{:S(2)}) %collective-permute-start.20) | collective-permute-done | bytes 1048608 | tf_op jit(solution)/shard_map/ppermute | solution.py:200
  205.9 1.6 maximum_select_fusion
  207.5 4.8 %shard_map.83 = f32[588,1024]{1,0:T(8,128)} custom-call(bf16[4,588,256]{2,1,0:T(8,128)(2,1)} %all-to-all-done.x_ref, bf16[4,588,256]{2,1,0:T(8,128)(2,1)S(1)} %all-to-all-done.1.y_ref, bf16[1024,1024]{1,0:T(8,128)(2,1)} %bitcast.37), custom_call_target="tpu_custom_call" | custom-call | tf_op jit(solution)/shard_map/pallas_call | solution.py:360
  (48 shorter events, 1.1 us)
Async XLA Ops:
  1.3 1.3 copy-start.7
  2.6 0.7 copy-start.9
  3.7 25.1 %collective-permute-start = (bf16[64,256]{1,0:T(8,128)(2,1)S(1)}, bf16[64,256]{1,0:T(8,128)(2,1)S(1)}, u32[]{:S(2)}, u32[]{:S(2)}) collective-permute-start(bf16[64,256]{1,0:T(8,128)(2,1)S(1)} %get-tuple-element.25), channel_id=1, source_target_pairs={{4,0},{8,4},{12,8},{16,12},{20,16},{24,20},{28,24},{5,1},{9,5},{13... | collective-permute-start | bytes 98312 | tf_op jit(solution)/shard_map/ppermute | solution.py:205
  5.0 4.7 %copy-start.8 = (bf16[2352,256]{1,0:T(8,128)(2,1)S(1)}, bf16[2352,256]{1,0:T(8,128)(2,1)}, u32[]{:S(2)}) copy-start(bf16[2352,256]{1,0:T(8,128)(2,1)} %x_ref.3) | copy-start | bytes 3612676
  5.0 4.7 %copy-start.10 = (s32[49]{0:T(128)S(1)}, s32[49]{0:T(128)}, u32[]{:S(2)}) copy-start(s32[49]{0:T(128)} %param.9) | copy-start | bytes 592
  5.0 4.7 %copy-start.11 = (s32[8,343]{1,0:T(8,128)S(1)}, s32[8,343]{1,0:T(8,128)}, u32[]{:S(2)}) copy-start(s32[8,343]{1,0:T(8,128)} %conn_ref.1) | copy-start | bytes 32932
  5.0 33.6 %collective-permute-start.3 = (f32[64,1]{1,0:T(8,128)S(1)}, f32[64,1]{1,0:T(8,128)S(1)}, u32[]{:S(2)}, u32[]{:S(2)}) collective-permute-start(f32[64,1]{1,0:T(8,128)S(1)} %get-tuple-element.31), channel_id=1, source_target_pairs={{4,0},{8,4},{12,8},{16,12},{20,16},{24,20},{28,24},{5,1},{9,5},{13... | collective-permute-start | bytes 776 | tf_op jit(solution)/shard_map/ppermute | solution.py:205
  28.8 9.8 %copy-start.3 = (bf16[2560,256]{1,0:T(8,128)(2,1)}, bf16[2560,256]{1,0:T(8,128)(2,1)S(1)}, u32[]{:S(2)}) copy-start(bf16[2560,256]{1,0:T(8,128)(2,1)S(1)} %get-tuple-element.24.refs_2_.refs_3_.refs_0_.refs_4_) | copy-start | bytes 3932164
  28.9 2.1 %copy-start = (bf16[8,384,384]{2,1,0:T(8,128)(2,1)S(1)}, bf16[8,384,384]{2,1,0:T(8,128)(2,1)}, u32[]{:S(2)}) copy-start(bf16[8,384,384]{2,1,0:T(8,128)(2,1)} %get-tuple-element.26.refs_4_.refs_5_.refs_2_.refs_9_.refs_10_.refs_11_) | copy-start | bytes 7077892
  31.2 10.2 %collective-permute-start.1 = (f32[64,256]{1,0:T(8,128)S(1)}, f32[64,256]{1,0:T(8,128)S(1)}, u32[]{:S(2)}, u32[]{:S(2)}) collective-permute-start(f32[64,256]{1,0:T(8,128)S(1)} %get-tuple-element.30.refs_2_), channel_id=1, source_target_pairs={{0,4},{4,8},{8,12},{12,16},{16,20},{20,24},{24,28},{1,5},{5,9},{9,... | collective-permute-start | bytes 196616 | tf_op jit(solution)/shard_map/ppermute | solution.py:205
  37.3 7.0 %collective-permute-start.2 = (f32[64,256]{1,0:T(8,128)S(1)}, f32[64,256]{1,0:T(8,128)S(1)}, u32[]{:S(2)}, u32[]{:S(2)}) collective-permute-start(f32[64,256]{1,0:T(8,128)S(1)} %get-tuple-element.29.refs_1_), channel_id=1, source_target_pairs={{4,0},{8,4},{12,8},{16,12},{20,16},{24,20},{28,24},{5,1},{9,5},{13... | collective-permute-start | bytes 196616 | tf_op jit(solution)/shard_map/ppermute | solution.py:205
  41.4 10.2 %copy-start.1 = (bf16[2560,256]{1,0:T(8,128)(2,1)}, bf16[2560,256]{1,0:T(8,128)(2,1)S(1)}, u32[]{:S(2)}) copy-start(bf16[2560,256]{1,0:T(8,128)(2,1)S(1)} %shard_map.71.refs_7_.refs_8_.refs_0_.refs_4_) | copy-start | bytes 3932164
  45.5 9.4 %collective-permute-start.4 = (f32[64,256]{1,0:T(8,128)S(1)}, f32[64,256]{1,0:T(8,128)S(1)}, u32[]{:S(2)}, u32[]{:S(2)}) collective-permute-start(f32[64,256]{1,0:T(8,128)S(1)} %get-tuple-element.34.refs_2_), channel_id=1, source_target_pairs={{0,4},{4,8},{8,12},{12,16},{16,20},{20,24},{24,28},{1,5},{5,9},{9,... | collective-permute-start | bytes 196616 | tf_op jit(solution)/shard_map/ppermute | solution.py:205
  50.3 6.2 %collective-permute-start.5 = (f32[64,256]{1,0:T(8,128)S(1)}, f32[64,256]{1,0:T(8,128)S(1)}, u32[]{:S(2)}, u32[]{:S(2)}) collective-permute-start(f32[64,256]{1,0:T(8,128)S(1)} %get-tuple-element.33.refs_1_), channel_id=1, source_target_pairs={{4,0},{8,4},{12,8},{16,12},{20,16},{24,20},{28,24},{5,1},{9,5},{13... | collective-permute-start | bytes 196616 | tf_op jit(solution)/shard_map/ppermute | solution.py:205
  54.8 8.0 %copy-start.2 = (bf16[2560,256]{1,0:T(8,128)(2,1)}, bf16[2560,256]{1,0:T(8,128)(2,1)S(1)}, u32[]{:S(2)}) copy-start(bf16[2560,256]{1,0:T(8,128)(2,1)S(1)} %shard_map.73.refs_8_.refs_9_.refs_0_.refs_4_) | copy-start | bytes 3932164
  57.6 8.5 %collective-permute-start.6 = (f32[64,256]{1,0:T(8,128)S(1)}, f32[64,256]{1,0:T(8,128)S(1)}, u32[]{:S(2)}, u32[]{:S(2)}) collective-permute-start(f32[64,256]{1,0:T(8,128)S(1)} %get-tuple-element.37.refs_2_), channel_id=1, source_target_pairs={{0,4},{4,8},{8,12},{12,16},{16,20},{20,24},{24,28},{1,5},{5,9},{9,... | collective-permute-start | bytes 196616 | tf_op jit(solution)/shard_map/ppermute | solution.py:205
  61.5 6.2 %collective-permute-start.7 = (f32[64,256]{1,0:T(8,128)S(1)}, f32[64,256]{1,0:T(8,128)S(1)}, u32[]{:S(2)}, u32[]{:S(2)}) collective-permute-start(f32[64,256]{1,0:T(8,128)S(1)} %get-tuple-element.36.refs_1_), channel_id=1, source_target_pairs={{4,0},{8,4},{12,8},{16,12},{20,16},{24,20},{28,24},{5,1},{9,5},{13... | collective-permute-start | bytes 196616 | tf_op jit(solution)/shard_map/ppermute | solution.py:205
  66.0 2.8 %copy-start.4 = (bf16[2560,256]{1,0:T(8,128)(2,1)}, bf16[2560,256]{1,0:T(8,128)(2,1)S(1)}, u32[]{:S(2)}) copy-start(bf16[2560,256]{1,0:T(8,128)(2,1)S(1)} %shard_map.75.refs_8_.refs_9_.refs_0_) | copy-start | bytes 3932164
  68.8 10.3 %collective-permute-start.8 = (f32[64,256]{1,0:T(8,128)S(1)}, f32[64,256]{1,0:T(8,128)S(1)}, u32[]{:S(2)}, u32[]{:S(2)}) collective-permute-start(f32[64,256]{1,0:T(8,128)S(1)} %get-tuple-element.40.refs_2_), channel_id=1, source_target_pairs={{0,4},{4,8},{8,12},{12,16},{16,20},{20,24},{24,28},{1,5},{5,9},{9,... | collective-permute-start | bytes 196616 | tf_op jit(solution)/shard_map/ppermute | solution.py:205
  73.1 6.2 %collective-permute-start.9 = (f32[64,256]{1,0:T(8,128)S(1)}, f32[64,256]{1,0:T(8,128)S(1)}, u32[]{:S(2)}, u32[]{:S(2)}) collective-permute-start(f32[64,256]{1,0:T(8,128)S(1)} %get-tuple-element.39.refs_1_), channel_id=1, source_target_pairs={{4,0},{8,4},{12,8},{16,12},{20,16},{24,20},{28,24},{5,1},{9,5},{13... | collective-permute-start | bytes 196616 | tf_op jit(solution)/shard_map/ppermute | solution.py:205
  74.5 1.3 copy-start.5
  84.5 1.0 copy-start.6
  85.6 20.6 %all-to-all-start = ((bf16[4,588,256]{2,1,0:T(8,128)(2,1)}), bf16[4,588,256]{2,1,0:T(8,128)(2,1)}, u32[]{:S(2)}, u32[]{:S(2)}) async-start(bf16[4,588,256]{2,1,0:T(8,128)(2,1)} %copy-done.6), calls=%async_computation | async-start | bytes 2424832 | tf_op jit(solution)/shard_map/all_to_all | solution.py:318
  89.8 7.0 %collective-permute-start.10 = (f32[64,256]{1,0:T(8,128)S(1)}, f32[64,256]{1,0:T(8,128)S(1)}, u32[]{:S(2)}, u32[]{:S(2)}) collective-permute-start(f32[64,256]{1,0:T(8,128)S(1)} %get-tuple-element.43), channel_id=1, source_target_pairs={{0,4},{4,8},{8,12},{12,16},{16,20},{20,24},{24,28},{1,5},{5,9},{9,... | collective-permute-start | bytes 196616 | tf_op jit(solution)/shard_map/ppermute | solution.py:205
  106.1 19.7 %all-to-all-start.1 = ((bf16[4,588,256]{2,1,0:T(8,128)(2,1)}), bf16[4,588,256]{2,1,0:T(8,128)(2,1)S(1)}, u32[]{:S(2)}, u32[]{:S(2)}) async-start(bf16[4,588,256]{2,1,0:T(8,128)(2,1)} %shard_map.81), calls=%async_computation.1 | async-start | bytes 2424832 | tf_op jit(solution)/shard_map/all_to_all | solution.py:324
  130.8 5.4 %copy-start.12 = (bf16[4,256,1024]{2,1,0:T(8,128)(2,1)S(1)}, bf16[4,256,1024]{2,1,0:T(8,128)(2,1)}, u32[]{:S(2)}) copy-start(bf16[4,256,1024]{2,1,0:T(8,128)(2,1)} %shard_map.82) | copy-start | bytes 6291460
  133.2 3.0 %collective-permute-start.11 = (bf16[2,256,1024]{2,1,0:T(8,128)(2,1)}, bf16[2,256,1024]{2,1,0:T(8,128)(2,1)}, u32[]{:S(2)}, u32[]{:S(2)}) collective-permute-start(bf16[2,256,1024]{2,1,0:T(8,128)(2,1)} %dynamic-slice_bitcast_fusion), channel_id=1, source_target_pairs={{0,1},{1,0},{2,3},{3,2},{4,5},{5,4},{6,7},{7,6},{8,9},{9,8},{10,11... | collective-permute-start | bytes 3145736 | tf_op jit(solution)/shard_map/ppermute | solution.py:200
  139.8 14.0 %collective-permute-start.12 = (bf16[1,256,1024]{2,1,0:T(8,128)(2,1)S(1)}, bf16[1,256,1024]{2,1,0:T(8,128)(2,1)S(1)}, u32[]{:S(2)}, u32[]{:S(2)}) collective-permute-start(bf16[1,256,1024]{2,1,0:T(8,128)(2,1)S(1)} %constant_dynamic-slice_fusion.1), channel_id=1, source_target_pairs={{0,2},{1,3},{2,0},{3,1},{4,6},{5,7},{6,4},{7,5},{8,10},{9,11},{10,... | collective-permute-start | bytes 1572872 | tf_op jit(solution)/shard_map/ppermute | solution.py:200
  155.1 8.3 %collective-permute-start.13 = (bf16[4,32,1024]{2,1,0:T(8,128)(2,1)S(1)}, bf16[4,32,1024]{2,1,0:T(8,128)(2,1)S(1)}, u32[]{:S(2)}, u32[]{:S(2)}) collective-permute-start(bf16[4,32,1024]{2,1,0:T(8,128)(2,1)S(1)} %dynamic-slice_bitcast_fusion.1), channel_id=1, source_target_pairs={{0,4},{4,0},{8,12},{12,8},{16,20},{20,16},{24,28},{28,24},{1,5},{5... | collective-permute-start | bytes 786440 | tf_op jit(solution)/shard_map/ppermute | solution.py:200
  163.5 5.3 %collective-permute-start.14 = (bf16[2,32,1024]{2,1,0:T(8,128)(2,1)S(1)}, bf16[2,32,1024]{2,1,0:T(8,128)(2,1)S(1)}, u32[]{:S(2)}, u32[]{:S(2)}) collective-permute-start(bf16[2,32,1024]{2,1,0:T(8,128)(2,1)S(1)} %dynamic-slice_bitcast_fusion.2), channel_id=1, source_target_pairs={{0,8},{4,12},{8,0},{12,4},{16,24},{20,28},{24,16},{28,20},{1,9},{5... | collective-permute-start | bytes 393224 | tf_op jit(solution)/shard_map/ppermute | solution.py:200
  168.9 5.9 %collective-permute-start.15 = (bf16[1,32,1024]{2,1,0:T(8,128)(2,1)S(1)}, bf16[1,32,1024]{2,1,0:T(8,128)(2,1)S(1)}, u32[]{:S(2)}, u32[]{:S(2)}) collective-permute-start(bf16[1,32,1024]{2,1,0:T(8,128)(2,1)S(1)} %constant_dynamic-slice_fusion), channel_id=1, source_target_pairs={{0,16},{4,20},{8,24},{12,28},{16,0},{20,4},{24,8},{28,12},{1,17},{... | collective-permute-start | bytes 196616 | tf_op jit(solution)/shard_map/ppermute | solution.py:200
  174.9 5.6 %collective-permute-start.16 = (bf16[1,32,1024]{2,1,0:T(8,128)(2,1)S(1)}, bf16[1,32,1024]{2,1,0:T(8,128)(2,1)S(1)}, u32[]{:S(2)}, u32[]{:S(2)}) collective-permute-start(bf16[1,32,1024]{2,1,0:T(8,128)(2,1)S(1)} %add_convert_fusion.1), channel_id=1, source_target_pairs={{0,16},{4,20},{8,24},{12,28},{16,0},{20,4},{24,8},{28,12},{1,17},{... | collective-permute-start | bytes 196616 | tf_op jit(solution)/shard_map/ppermute | solution.py:200
  180.5 5.6 %collective-permute-start.17 = (bf16[2,32,1024]{2,1,0:T(8,128)(2,1)S(1)}, bf16[2,32,1024]{2,1,0:T(8,128)(2,1)S(1)}, u32[]{:S(2)}, u32[]{:S(2)}) collective-permute-start(bf16[2,32,1024]{2,1,0:T(8,128)(2,1)S(1)} %maximum_select_fusion.6), channel_id=1, source_target_pairs={{0,8},{4,12},{8,0},{12,4},{16,24},{20,28},{24,16},{28,20},{1,9},{5... | collective-permute-start | bytes 393224 | tf_op jit(solution)/shard_map/ppermute | solution.py:200
  186.1 6.4 %collective-permute-start.18 = (bf16[4,32,1024]{2,1,0:T(8,128)(2,1)S(1)}, bf16[4,32,1024]{2,1,0:T(8,128)(2,1)S(1)}, u32[]{:S(2)}, u32[]{:S(2)}) collective-permute-start(bf16[4,32,1024]{2,1,0:T(8,128)(2,1)S(1)} %bitcast.46), channel_id=1, source_target_pairs={{0,4},{4,0},{8,12},{12,8},{16,20},{20,16},{24,28},{28,24},{1,5},{5... | collective-permute-start | bytes 786440 | tf_op jit(solution)/shard_map/ppermute | solution.py:200
  192.6 9.2 %collective-permute-start.19 = (bf16[1,256,1024]{2,1,0:T(8,128)(2,1)S(1)}, bf16[1,256,1024]{2,1,0:T(8,128)(2,1)S(1)}, u32[]{:S(2)}, u32[]{:S(2)}) collective-permute-start(bf16[1,256,1024]{2,1,0:T(8,128)(2,1)S(1)} %bitcast.39), channel_id=1, source_target_pairs={{0,2},{1,3},{2,0},{3,1},{4,6},{5,7},{6,4},{7,5},{8,10},{9,11},{10,... | collective-permute-start | bytes 1572872 | tf_op jit(solution)/shard_map/ppermute | solution.py:200
  203.0 2.9 %collective-permute-start.20 = (bf16[2,256,1024]{2,1,0:T(8,128)(2,1)}, bf16[2,256,1024]{2,1,0:T(8,128)(2,1)S(1)}, u32[]{:S(2)}, u32[]{:S(2)}) collective-permute-start(bf16[2,256,1024]{2,1,0:T(8,128)(2,1)} %maximum_select_fusion.2), channel_id=1, source_target_pairs={{0,1},{1,0},{2,3},{3,2},{4,5},{5,4},{6,7},{7,6},{8,9},{9,8},{10,11... | collective-permute-start | bytes 3145736 | tf_op jit(solution)/shard_map/ppermute | solution.py:200

commit v2 on v1

--- a/solution.py
+++ b/solution.py
@@ -94,82 +94,207 @@
     return 2.0 * (image - CENTER * now) / HALF - before
 
 
-def edge_kernel(step, fp, *refs):
-    if step == 0:
-        last_ref, ghost_ref, yb_ref, yt_ref, hb_ref, ht_ref, yf_ref, pb_ref, pt_ref = refs
-        yf_ref[:fp] = yb_ref[:fp]
-        yf_ref[fp:] = ghost_ref[...]
-    else:
-        if step == 1:
-            last_ref, sb_ref, st_ref, rb_ref, rt_ref, now_ref, potf_ref, *refs = refs
-            before = None
-        else:
-            last_ref, sb_ref, st_ref, rb_ref, rt_ref, now_ref, potf_ref, before_ref, *refs = refs
-            before = before_ref[...].astype(F32)
-        yb_ref, yt_ref, hb_ref, ht_ref, yf_ref, pb_ref, pt_ref = refs
-        now = now_ref[...].astype(F32)
-        total = jnp.concatenate([sb_ref[...] + rb_ref[...], st_ref[...] + rt_ref[...]], axis=0)
-        value = advance(total + potf_ref[...] * now, now, before)
-        dead = (lax.broadcasted_iota(jnp.int32, value.shape, 0) >= fp) & (last_ref[0] == 1)
-        yf_ref[...] = jnp.where(dead, 0.0, value).astype(BF16)
-    low, high = yf_ref[:fp], yf_ref[fp:]
-    pb_ref[...] = jnp.dot(
-        hb_ref[0], jnp.concatenate([low, yb_ref[fp:]], axis=0), preferred_element_type=F32
-    )
-    pt_ref[...] = jnp.dot(
-        ht_ref[0], jnp.concatenate([yt_ref[...], high], axis=0), preferred_element_type=F32
-    )
-
-
-def bulk_kernel(step, fp, *refs):
-    if step == 0 or step == DEGREE:
-        y_ref, yf_ref, h_ref, pot_ref, out_ref = refs
-    else:
-        y_ref, yf_ref, h_ref, pot_ref, before_ref, out_ref = refs
+def split(a):
+    high = a.astype(BF16)
+    return high, (a - high.astype(F32)).astype(BF16)
+
+
+def mul(a, b):
+    return jnp.dot(a, b, preferred_element_type=F32)
+
+
+def mul_r(a, b):
+    high, low = split(b)
+    return mul(a, high) + mul(a, low)
+
+
+def sweep(h_ref, y_ref, fp, emit):
     cells, cp = h_ref.shape[:2]
     stride = cp - fp
     carry = None
     for c in range(cells):
-        if c == 0:
-            v = jnp.concatenate([yf_ref[:fp], y_ref[fp:cp]], axis=0)
-        elif c == cells - 1:
-            v = jnp.concatenate([y_ref[c * stride :], yf_ref[fp:]], axis=0)
-        else:
-            v = y_ref[c * stride : c * stride + cp]
-        prod = jnp.dot(h_ref[c], v, preferred_element_type=F32)
-        if c == 0:
-            rows, lo = prod[fp:stride], fp
-            out_ref[:fp] = jnp.zeros((fp, out_ref.shape[1]), BF16)
-        else:
-            rows, lo = jnp.concatenate([prod[:fp] + carry, prod[fp:stride]], axis=0), 0
+        prod = mul(h_ref[c], y_ref[c * stride : c * stride + cp])
+        rows = prod[:stride]
+        if c > 0:
+            rows = jnp.concatenate([rows[:fp] + carry, rows[fp:]], axis=0)
         carry = prod[stride:]
-        at = slice(c * stride + lo, (c + 1) * stride)
-        now = v[lo:stride].astype(F32)
-        image = rows + pot_ref[at] * now
-        if step == DEGREE:
-            out_ref[at] = image.astype(BF16)
-        else:
-            before = None if step == 0 else before_ref[at].astype(F32)
-            out_ref[at] = advance(image, now, before).astype(BF16)
-
-
-def back_kernel(fp, node_ref, y_ref, low_ref, out_ref):
+        emit(c, rows)
+    return carry
+
+
+def response(hc, hn, potc, fp, upper):
+    cp = hc.shape[0]
+    stride = cp - fp
+    if upper:
+        f, r, s, g = slice(stride, cp), slice(0, stride), slice(0, fp), slice(stride, cp)
+        rest = slice(0, stride)
+    else:
+        f, r, s, g = slice(0, fp), slice(fp, cp), slice(stride - fp, stride), slice(0, fp)
+        rest = slice(fp, cp)
+    gain = 2.0 / HALF
+    out = [hc[f, f].astype(F32)]
+    one = gain * hc[r, f].astype(F32)
+    out.append(mul_r(hc[f, r], one))
+
+    def pad_next(face_rows):
+        zero = jnp.zeros((stride, fp), F32)
+        return jnp.concatenate([zero, face_rows] if upper else [face_rows, zero], axis=0)
+
+    def near(value, next_value):
+        got = mul_r(hc[r, r], value) + (potc - CENTER) * value
+        add = mul_r(hn[g, :], next_value)
+        if upper:
+            return jnp.concatenate([got[:fp] + add, got[fp:]], axis=0)
+        return jnp.concatenate([got[: stride - fp], got[stride - fp :] + add], axis=0)
+
+    two = gain * near(one, pad_next(one[s]))
+    out.append(mul_r(hc[f, r], two))
+    two_next = gain * mul_r(hn, pad_next(one[s]))
+    if upper:
+        two_next = jnp.concatenate([two_next[:stride], two[s]], axis=0)
+    else:
+        two_next = jnp.concatenate([two[s], two_next[fp:]], axis=0)
+    three = gain * near(two, two_next) - one
+    out.append(mul_r(hc[f, r], three))
+    return out
+
+
+def store_matrices(mats, out_ref, at, fp, width):
+    for part in range(2):
+        for j, m in enumerate(mats):
+            block, lane = divmod((part * len(mats) + j) * fp, width)
+            out_ref[at + block, :, lane : lane + fp] = split(m)[part]
+
+
+def load_matrices(ref, at, count, fp, width):
+    out = []
+    for j in range(count):
+        pieces = []
+        for part in range(2):
+            block, lane = divmod((part * count + j) * fp, width)
+            pieces.append(ref[at + block, :, lane : lane + fp].astype(F32))
+        out.append(pieces[0] + pieces[1])
+    return out
+
+
+def free_kernel(fp, v_ref, ghost_ref, h_ref, pot_ref, first_ref, own_ref, up_ref, down_ref, a_ref, b_ref):
+    cells, cp = h_ref.shape[:2]
+    stride = cp - fp
+    total = cells * stride
+    width = v_ref.shape[1]
+    a_ref[:total] = v_ref[...]
+    a_ref[total:] = ghost_ref[...]
+    b_ref[total:] = jnp.zeros((fp, width), BF16)
+
+    def keep(k, low, high):
+        own_ref[0, k] = low
+        own_ref[1, k] = high
+        down_ref[k] = low.astype(BF16)
+        up_ref[k] = high.astype(BF16)
+
+    now_ref, other_ref = a_ref, b_ref
+    for k in range(DEGREE):
+        ends = {}
+
+        def emit(c, rows, k=k, now_ref=now_ref, other_ref=other_ref, ends=ends):
+            at = slice(c * stride, (c + 1) * stride)
+            if c == 0:
+                ends["low"] = rows[:fp]
+            now = now_ref[at].astype(F32)
+            before = None if k == 0 else other_ref[at].astype(F32)
+            if k == 1:
+                before = v_ref[at].astype(F32)
+            value = advance(rows + pot_ref[at] * now, now, before).astype(BF16)
+            if c == 0:
+                value = jnp.concatenate([jnp.zeros((fp, width), BF16), value[fp:]], axis=0)
+            if k == 0:
+                first_ref[at] = value
+            other_ref[at] = value
+
+        high = sweep(h_ref, now_ref, fp, emit)
+        keep(k, ends["low"], high)
+        if k == 0:
+            a_ref[total:] = jnp.zeros((fp, width), BF16)
+        now_ref, other_ref = other_ref, now_ref
+    keep(DEGREE, mul(h_ref[0, :fp], now_ref[:cp]), mul(h_ref[cells - 1, stride:], now_ref[total - stride :]))
+    low = response(h_ref[0], h_ref[1], pot_ref[fp:cp], fp, False)
+    high = response(h_ref[cells - 1], h_ref[cells - 2], pot_ref[total - stride :], fp, True)
+    store_matrices(low, down_ref, DEGREE + 1, fp, width)
+    store_matrices(high, up_ref, DEGREE + 1, fp, width)
+    count = len(low)
+    for side, mats in enumerate((low, high)):
+        for j, m in enumerate(mats):
+            own_ref_at = (DEGREE + 1) * 0
+            block, lane = divmod(j * fp, width)
+            own_ref[side, DEGREE + 1 + block + own_ref_at, :, lane : lane + fp] = m
+
+
+def forced_kernel(fp, dead_ref, v_ref, ghost_ref, first_ref, own_ref, fromleft_ref, fromright_ref, h_ref, pot_ref, potg_ref, x_ref, image_ref, a_ref, b_ref, c_ref):
+    cells, cp = h_ref.shape[:2]
+    stride = cp - fp
+    total = cells * stride
+    width = v_ref.shape[1]
+    histories = []
+    last_image = None
+    for side, (got_ref, pot, start) in enumerate(
+        ((fromleft_ref, pot_ref[:fp], v_ref[:fp]), (fromright_ref, potg_ref[...], ghost_ref[...]))
+    ):
+        mats = load_matrices(got_ref, DEGREE + 1, DEGREE, fp, width)
+        for j in range(DEGREE):
+            block, lane = divmod(j * fp, width)
+            mats[j] = mats[j] + own_ref[side, DEGREE + 1 + block, :, lane : lane + fp]
+        mats = [split(m) for m in mats]
+        values = [start]
+        for k in range(DEGREE + 1 if side == 0 else DEGREE):
+            h = own_ref[side, k] + got_ref[k].astype(F32)
+            for m in range(1, k + 1):
+                h = h + mul(mats[k - m][0], values[m]) + mul(mats[k - m][1], values[m])
+            now = values[k].astype(F32)
+            h = h + pot * now
+            if k == DEGREE:
+                last_image = h
+                break
+            value = advance(h, now, None if k == 0 else values[k - 1].astype(F32))
+            if side == 1:
+                value = jnp.where(dead_ref[0] == 1, 0.0, value)
+            values.append(value.astype(BF16))
+        histories.append(values)
+    low, high = histories
+    a_ref[:fp] = low[1]
+    a_ref[fp:total] = first_ref[fp:]
+    a_ref[total:] = high[1]
+    refs = [None, a_ref, b_ref, c_ref, a_ref]
+    for k in range(1, DEGREE + 1):
+        now_ref = refs[k]
+
+        def emit(c, rows, k=k, now_ref=now_ref):
+            at = slice(c * stride, (c + 1) * stride)
+            now = now_ref[at].astype(F32)
+            image = rows + pot_ref[at] * now
+            if k == DEGREE:
+                out = image.astype(BF16)
+                if c == 0:
+                    out = jnp.concatenate([last_image.astype(BF16), out[fp:]], axis=0)
+                image_ref[at] = out
+                return
+            before = (v_ref if k == 1 else refs[k - 1])[at].astype(F32)
+            value = advance(image, now, before).astype(BF16)
+            if c == 0:
+                value = jnp.concatenate([low[k + 1], value[fp:]], axis=0)
+            refs[k + 1][at] = value
+            if k + 1 == DEGREE:
+                x_ref[at] = value
+
+        sweep(h_ref, now_ref, fp, emit)
+        if k < DEGREE:
+            refs[k + 1][total:] = high[k + 1]
+
+
+def back_kernel(node_ref, y_ref, out_ref):
     rows = out_ref.shape[1]
     want = (lax.broadcasted_iota(jnp.int32, (rows, 1), 0) + pl.program_id(0) * rows).astype(F32)
     hit = jnp.where(want == node_ref[...], 1.0, 0.0).astype(BF16)
-    out = jnp.dot(hit, y_ref[...], preferred_element_type=F32)
-    out = out + jnp.dot(hit[:, :fp], low_ref[...], preferred_element_type=F32)
-    out_ref[0] = out.astype(BF16)
-
-
-def back_image_kernel(fp, node_ref, y_ref, sb_ref, rb_ref, now_ref, pot_ref, out_ref):
-    rows = out_ref.shape[1]
-    low = (sb_ref[...] + rb_ref[...] + pot_ref[...] * now_ref[...].astype(F32)).astype(BF16)
-    want = (lax.broadcasted_iota(jnp.int32, (rows, 1), 0) + pl.program_id(0) * rows).astype(F32)
-    hit = jnp.where(want == node_ref[...], 1.0, 0.0).astype(BF16)
-    out = jnp.dot(hit, y_ref[...], preferred_element_type=F32)
-    out = out + jnp.dot(hit[:, :fp], low, preferred_element_type=F32)
-    out_ref[0] = out.astype(BF16)
+    out_ref[0] = mul(hit, y_ref[...]).astype(BF16)
 
 
 def gram_kernel(scale, x_ref, y_ref, out_ref, rows_ref):
@@ -182,7 +307,7 @@
 
     out_ref[0] = (
         lax.dot_general(x_ref[0], rows_ref[...], (((0,), (0,)), ((), ())), preferred_element_type=F32) * scale
-    ).astype(BF16)
+    )
 
 
 def residual_kernel(x_ref, y_ref, p_ref, out_ref):
@@ -255,73 +380,49 @@
         cost_estimate=pl.CostEstimate(flops=4 * total * nodes * width, bytes_accessed=8 << 20, transcendentals=0),
     )(connectivity, face_row, cell_hamiltonian, orbitals, pot_row)
     node_row = node.reshape(1, total)
-    potf = jnp.concatenate([pot[:fp], ghost_pot], axis=0)
-    is_last = (d == dom - 1).astype(jnp.int32).reshape(1)
-
-    smem = pl.BlockSpec(memory_space=pltpu.SMEM)
-    small = lambda: full((fp, width))
-    end_specs = [
-        pl.BlockSpec((cp, width), lambda i: (0, 0)),
-        pl.BlockSpec((stride, width), lambda i: (cells - 1, 0)),
-        pl.BlockSpec((1, fp, cp), lambda i: (0, 0, 0)),
-        pl.BlockSpec((1, fp, cp), lambda i: (cells - 1, stride // fp, 0)),
-    ]
-    edge_out = dict(
-        grid=(1,),
-        out_specs=[full((2 * fp, width)), small(), small()],
-        out_shape=[sds((2 * fp, width), BF16), sds((fp, width), F32), sds((fp, width), F32)],
-        compiler_params=params(),
-        cost_estimate=pl.CostEstimate(flops=4 * fp * cp * width, bytes_accessed=1 << 20, transcendentals=0),
+    dead = (d == dom - 1).astype(jnp.int32).reshape(1)
+
+    extra = -(-DEGREE * fp // width)
+    sent = DEGREE + 1 + -(-2 * DEGREE * fp // width)
+    ext = pltpu.VMEM((total + fp, width), BF16)
+    cost = pl.CostEstimate(
+        flops=2 * DEGREE * cells * cp * cp * width, bytes_accessed=8 << 20, transcendentals=0
     )
-    bulk_cost = pl.CostEstimate(flops=2 * cells * cp * cp * width, bytes_accessed=6 << 20, transcendentals=0)
-
-    before = yf_before = None
-    yf = sums = None
-    for step in range(DEGREE + 1):
-        ends = [y, y, hcan, hcan]
-        if step == 0:
-            yf, sb, st = pl.pallas_call(
-                functools.partial(edge_kernel, step, fp), in_specs=[smem, small()] + end_specs, **edge_out
-            )(is_last, ghost, *ends)
-        else:
-            args = [sb, st, rb, rt, yf, potf] + ([yf_before] if step > 1 else [])
-            specs = [small()] * 4 + [full((2 * fp, width)), full((2 * fp, 1))]
-            specs += [full((2 * fp, width))] if step > 1 else []
-            yf_new, sb, st = pl.pallas_call(
-                functools.partial(edge_kernel, step, fp), in_specs=[smem] + specs + end_specs, **edge_out
-            )(is_last, *args, *ends)
-            yf_before, yf = yf, yf_new
-        rb = shift(st, "dom", 1)
-        if step < DEGREE:
-            rt = shift(sb, "dom", -1)
-        extra = [] if step in (0, DEGREE) else [before]
-        out = pl.pallas_call(
-            functools.partial(bulk_kernel, step, fp),
-            out_shape=sds((total, width), BF16),
-            compiler_params=params(),
-            cost_estimate=bulk_cost,
-        )(y, yf, hcan, pot, *extra)
-        if step < DEGREE:
-            before, y = y, out
-    image = out
-
-    back = dict(
+    first, own, up, down = pl.pallas_call(
+        functools.partial(free_kernel, fp),
+        out_shape=[
+            sds((total, width), BF16),
+            sds((2, DEGREE + 1 + extra, fp, width), F32),
+            sds((sent, fp, width), BF16),
+            sds((sent, fp, width), BF16),
+        ],
+        scratch_shapes=[ext, ext],
+        compiler_params=params(),
+        cost_estimate=cost,
+    )(y, ghost, hcan, pot)
+    from_left = shift(up, "dom", 1)
+    from_right = shift(down, "dom", -1)
+    vmem = pl.BlockSpec(memory_space=pltpu.VMEM)
+    x_own, image = pl.pallas_call(
+        functools.partial(forced_kernel, fp),
+        in_specs=[pl.BlockSpec(memory_space=pltpu.SMEM)] + [vmem] * 9,
+        out_shape=[sds((total, width), BF16)] * 2,
+        scratch_shapes=[ext, ext, ext],
+        compiler_params=params(),
+        cost_estimate=cost,
+    )(dead, y, ghost, first, own, from_left, from_right, hcan, pot, ghost_pot)
+
+    back = pl.pallas_call(
+        back_kernel,
         grid=(orb,),
+        in_specs=[full((1, total)), full((total, width))],
         out_specs=pl.BlockSpec((1, nodes // orb, width), lambda i: (i, 0, 0)),
         out_shape=sds((orb, nodes // orb, width), BF16),
         compiler_params=params(),
         cost_estimate=pl.CostEstimate(flops=2 * total * nodes * width, bytes_accessed=4 << 20, transcendentals=0),
     )
-    x_cols = pl.pallas_call(
-        functools.partial(back_kernel, fp), in_specs=[full((1, total)), full((total, width)), small()], **back
-    )(node_row, y, yf[:fp])
-    x_rows = lax.all_to_all(x_cols, "orb", split_axis=0, concat_axis=0, tiled=True)
-    i_cols = pl.pallas_call(
-        functools.partial(back_image_kernel, fp),
-        in_specs=[full((1, total)), full((total, width)), small(), small(), small(), full((fp, 1))],
-        **back,
-    )(node_row, image, sb, rb, yf[:fp], pot[:fp])
-    i_rows = lax.all_to_all(i_cols, "orb", split_axis=0, concat_axis=0, tiled=True)
+    x_rows = lax.all_to_all(back(node_row, x_own), "orb", split_axis=0, concat_axis=0, tiled=True)
+    i_rows = lax.all_to_all(back(node_row, image), "orb", split_axis=0, concat_axis=0, tiled=True)
 
     rows = nodes // orb
     cols = orb * width
@@ -330,7 +431,7 @@
         grid=(orb,),
         in_specs=[pl.BlockSpec((1, rows, width), lambda i: (i, 0, 0)), full((orb, rows, width))],
         out_specs=pl.BlockSpec((1, width, cols), lambda i: (i, 0, 0)),
-        out_shape=sds((orb, width, cols), BF16),
+        out_shape=sds((orb, width, cols), F32),
         scratch_shapes=[pltpu.VMEM((rows, cols), BF16)],
         compiler_params=params(),
     )(x_rows, i_rows)
@@ -345,10 +446,11 @@
             mine = (me // bit) % 2
             keep = lax.dynamic_index_in_dim(share, mine, 1, keepdims=False)
             give = lax.dynamic_index_in_dim(share, 1 - mine, 1, keepdims=False)
-            got = swap(give, axis, bit)
-            share = (keep.astype(F32) + got.astype(F32)).astype(BF16)
+            got = swap(give.astype(BF16), axis, bit)
+            share = keep + got.astype(F32)
             hops.append((axis, bit, mine))
             bit *= 2
+    share = share.astype(BF16)
     for axis, bit, mine in reversed(hops):
         if axis == "orb" and share.shape[0] == dom and bit * 2 == orb:
             share = share.reshape(1, width, cols)

time: 214 us -> 200 us (0.935)
  starting transfers between devices: 55.2 us -> 34.4 us
  waiting for transfers between devices: 76.9 us -> 84.6 us
  Pallas kernels: 58 us -> 51.9 us
  other arithmetic: 7.04 us -> 10.4 us
  local copies, waits for them, and re-layouts: 14 us -> 17.2 us
    ppermute x11 -> x4, starting transfers between devices: 31.4 us -> 9.69 us  [shift(): lax.ppermute(block, axis, [(i, i + distance) for i in range(n) if 0 <= i...]
    all_to_all x2, waiting for transfers between devices: 20.1 us -> 26.2 us  [the longest x1 16.2 us: body(): lax.all_to_all(back(node_row, image), 'orb', split_axis=0, concat_axis=0,...]
    add x0 -> x4, other arithmetic: none -> 5.73 us  [body(): share = keep + got.astype(F32)]
    pallas_call x12 -> x4, Pallas kernels: 28.8 us -> 24 us  [the longest x1 8.55 us: body(): pl.pallas_call(functools.partial(free_kernel, fp), out_shape=[sds((total,...]
    unnamed x27 -> x29, local copies, waits for them, and re-layouts: 9.67 us -> 13.8 us
    convert_element_type x5 -> x1, other arithmetic: 3.95 us -> 0.01 us  [body(): share = share.astype(BF16)]
    squeeze x5 -> x0, local copies, waits for them, and re-layouts: 3.54 us -> none  [body(): give = lax.dynamic_index_in_dim(share, 1 - mine, 1, keepdims=False)]
    convert_element_type x0 -> x5, local copies, waits for them, and re-layouts: none -> 2.59 us  [body(): got = swap(give.astype(BF16), axis, bit)]
  transfers between devices with their start and end apart: 23 -> 16, of which waited for: 16 -> 13; matrix products, arithmetic and copies ran while one was open for 2% -> 2% of each run, Pallas kernels for 19% -> 12%
where the time goes in v2:
time: 200 us
  waiting for transfers between devices  84.6 us (42%)
  Pallas kernels  51.9 us (26%)
  starting transfers between devices  34.4 us (17%)
  local copies, waits for them, and re-layouts  17.2 us (9%)
  other arithmetic  10.4 us (5%)
    ppermute x10, waiting for transfers between devices, swap(): lax.ppermute(block, axis, [(i, i ^ bit) for i in range(lax.axis_size(axis...  50.8 us
    pallas_call x1, Pallas kernels, body(): pl.pallas_call(functools.partial(order_kernel, fp, ip), grid=(cells,), in...  19.1 us
    ppermute x10, starting transfers between devices, swap(): lax.ppermute(block, axis, [(i, i ^ bit) for i in range(lax.axis_size(axis...  17.7 us
    all_to_all x1, waiting for transfers between devices, body(): lax.all_to_all(back(node_row, image), 'orb', split_axis=0, concat_axis=0,...  16.2 us
    unnamed x29, local copies, waits for them, and re-layouts  13.8 us
    all_to_all x1, waiting for transfers between devices, body(): lax.all_to_all(back(node_row, x_own), 'orb', split_axis=0, concat_axis=0,...  10 us
    ppermute x4, starting transfers between devices, shift(): lax.ppermute(block, axis, [(i, i + distance) for i in range(n) if 0 <= i...  9.69 us
    pallas_call x1, Pallas kernels, body(): pl.pallas_call(functools.partial(free_kernel, fp), out_shape=[sds((total,...  8.55 us
  transfers between devices with their start and end apart: 16, of which 13 were waited for; matrix products, arithmetic and copies ran while one was open for 2% of the time, Pallas kernels for 12%

profile of v2, /device:TPU:0, one launch (start us, length us, event | category | flops | bytes accessed | tf_op | source)
XLA Modules:
  0.0 199.5 jit_solution(7718842895738230951)
XLA Ops:
  0.6 0.7 reshape.260.pot_ref
  1.3 1.3 copy-done.2
  2.6 0.7 copy-done.4
  3.3 0.4 shard_map.69
  3.7 0.0 copy-start.6
  3.7 1.4 collective-permute-start
  5.2 3.2 %copy.7.h_ref = bf16[8,343,343]{2,1,0:T(8,128)(2,1)} copy(bf16[8,343,343]{2,0,1:T(8,128)(2,1)} %param.7) | data formatting | bytes 3764768 | tf_op args[2]
  8.4 19.1 %shard_map.68 = (bf16[8,384,384]{2,1,0:T(8,128)(2,1)}, bf16[2560,256]{1,0:T(8,128)(2,1)S(1)}, f32[2560,1]{1,0:T(8,128)S(1)}, f32[8,1,320]{2,1,0:T(1,128)S(1)}) custom-call(s32[8,343]{1,0:T(8,128)S(1)} %copy-done.6, s32[1,49]{1,0:T(1,128)S(1)} %bitcast.33, bf16[8,343,343]{2,1,0:T(8,128)(2,1)} %copy.7.h_ref, bf16[2352,256]{1,0:T(8,128)(2,1)S(1)} %copy-done.3, ...), custom_call_target="tpu_custom_call" | custom-call | flops 6165626880 | bytes 8388608 | tf_op jit(solution)/shard_map/pallas_call | solution.py:357
  27.6 1.1 copy-done.8
  28.6 8.5 %shard_map.70 = (bf16[2560,256]{1,0:T(8,128)(2,1)S(1)}, f32[2,6,64,256]{3,2,1,0:T(8,128)S(1)}, bf16[7,64,256]{2,1,0:T(8,128)(2,1)S(1)}, bf16[7,64,256]{2,1,0:T(8,128)(2,1)S(1)}) custom-call(bf16[2560,256]{1,0:T(8,128)(2,1)S(1)} %get-tuple-element.15.v_ref, bf16[64,256]{1,0:T(8,128)(2,1)S(1)} %collective-permute-done.ghost_ref, ...), custom_call_target="tpu_custom_call" | custom-call | flops 2415919104 | bytes 8388608 | tf_op jit(solution)/shard_map/pallas_call | solution.py:391
  37.2 1.1 copy-done.9
  38.3 5.5 %collective-permute-start.1 = (bf16[7,64,256]{2,1,0:T(8,128)(2,1)S(1)}, bf16[7,64,256]{2,1,0:T(8,128)(2,1)S(1)}, u32[]{:S(2)}, u32[]{:S(2)}) collective-permute-start(bf16[7,64,256]{2,1,0:T(8,128)(2,1)S(1)} %get-tuple-element.21), channel_id=1, source_target_pairs={{0,4},{4,8},{8,12},{12,16},{16,20},{20,24},{24,28},{1,5},{5,9},{9,... | collective-permute-start | bytes 688136 | tf_op jit(solution)/shard_map/ppermute | solution.py:330
  43.8 1.3 collective-permute-start.2
  45.1 1.5 collective-permute-start.3
  46.6 0.1 reshape.261.node_ref
  46.7 7.6 %collective-permute-done.3.potg_ref = f32[64,1]{1,0:T(8,128)S(1)} collective-permute-done((f32[64,1]{1,0:T(8,128)S(1)}, f32[64,1]{1,0:T(8,128)S(1)}, u32[]{:S(2)}, u32[]{:S(2)}) %collective-permute-start.3) | collective-permute-done | bytes 288 | tf_op jit(solution)/shard_map/ppermute | solution.py:330
  54.3 7.8 %shard_map.71 = (bf16[2560,256]{1,0:T(8,128)(2,1)S(1)}, bf16[2560,256]{1,0:T(8,128)(2,1)S(1)}) custom-call(s32[1]{0:T(128)} %bitcast.1.dead_ref, bf16[2560,256]{1,0:T(8,128)(2,1)} %copy-done.7, bf16[64,256]{1,0:T(8,128)(2,1)S(1)} %collective-permute-done.ghost_ref, bf16[2560,256]{1,0:T(8,128)(2,1)} %copy-done.9, ...), custom_call_target="tpu_custom_call" | custom-call | flops 2415919104 | bytes 8388608 | tf_op jit(solution)/shard_map/pallas_call | solution.py:406
  62.2 0.0 copy-start.10
  62.2 1.0 copy-done.10
  63.2 3.8 %shard_map.72 = bf16[4,588,256]{2,1,0:T(8,128)(2,1)S(1)} custom-call(f32[1,2560]{1,0:T(1,128)S(1)} %reshape.261.node_ref, bf16[2560,256]{1,0:T(8,128)(2,1)S(1)} %get-tuple-element.24.y_ref), custom_call_target="tpu_custom_call" | custom-call | flops 3082813440 | bytes 4194304 | tf_op jit(solution)/shard_map/pallas_call | solution.py:424
  67.1 0.0 copy-start.1
  67.1 1.0 copy-done.1
  68.1 3.5 %all-to-all-start = ((bf16[4,588,256]{2,1,0:T(8,128)(2,1)}), bf16[4,588,256]{2,1,0:T(8,128)(2,1)S(1)}, u32[]{:S(2)}, u32[]{:S(2)}) async-start(bf16[4,588,256]{2,1,0:T(8,128)(2,1)} %copy-done.1), calls=%async_computation | async-start | bytes 2424832 | tf_op jit(solution)/shard_map/all_to_all | solution.py:424
  71.6 0.0 copy-start.11
  71.6 1.3 copy-done.11
  72.9 3.8 %shard_map.73 = bf16[4,588,256]{2,1,0:T(8,128)(2,1)S(1)} custom-call(f32[1,2560]{1,0:T(1,128)S(1)} %reshape.261.node_ref, bf16[2560,256]{1,0:T(8,128)(2,1)S(1)} %copy-done.11), custom_call_target="tpu_custom_call" | custom-call | flops 3082813440 | bytes 4194304 | tf_op jit(solution)/shard_map/pallas_call | solution.py:425
  76.8 1.0 copy-done
  77.8 10.0 %all-to-all-done.x_ref = bf16[4,588,256]{2,1,0:T(8,128)(2,1)S(1)} async-done(((bf16[4,588,256]{2,1,0:T(8,128)(2,1)}), bf16[4,588,256]{2,1,0:T(8,128)(2,1)S(1)}, u32[]{:S(2)}, u32[]{:S(2)}) %all-to-all-start) | async-done | bytes 1204256 | tf_op jit(solution)/shard_map/all_to_all | solution.py:424
  87.8 3.5 %all-to-all-start.1 = ((bf16[4,588,256]{2,1,0:T(8,128)(2,1)}), bf16[4,588,256]{2,1,0:T(8,128)(2,1)S(1)}, u32[]{:S(2)}, u32[]{:S(2)}) async-start(bf16[4,588,256]{2,1,0:T(8,128)(2,1)} %copy-done), calls=%async_computation.1 | async-start | bytes 2424832 | tf_op jit(solution)/shard_map/all_to_all | solution.py:425
  91.4 16.2 %all-to-all-done.1.y_ref = bf16[4,588,256]{2,1,0:T(8,128)(2,1)S(1)} async-done(((bf16[4,588,256]{2,1,0:T(8,128)(2,1)}), bf16[4,588,256]{2,1,0:T(8,128)(2,1)S(1)}, u32[]{:S(2)}, u32[]{:S(2)}) %all-to-all-start.1) | async-done | bytes 1204256 | tf_op jit(solution)/shard_map/all_to_all | solution.py:425
  107.5 3.9 %shard_map.74 = f32[4,256,1024]{2,1,0:T(8,128)} custom-call(bf16[4,588,256]{2,1,0:T(8,128)(2,1)S(1)} %all-to-all-done.x_ref, bf16[4,588,256]{2,1,0:T(8,128)(2,1)S(1)} %all-to-all-done.1.y_ref), custom_call_target="tpu_custom_call" | custom-call | tf_op jit(solution)/shard_map/pallas_call | solution.py:429
  111.5 1.7 fusion
  113.2 0.1 collective-permute-start.4
  113.3 2.7 %collective-permute-done.4 = bf16[2,256,1024]{2,1,0:T(8,128)(2,1)} collective-permute-done((bf16[2,256,1024]{2,1,0:T(8,128)(2,1)S(1)}, bf16[2,256,1024]{2,1,0:T(8,128)(2,1)}, u32[]{:S(2)}, u32[]{:S(2)}) %collective-permute-start.4) | collective-permute-done | bytes 1048608 | tf_op jit(solution)/shard_map/ppermute | solution.py:325
  116.1 2.2 %bitcast_add_fusion = f32[2,256,1024]{2,1,0:T(8,128)S(1)} fusion(bf16[2,256,1024]{2,1,0:T(8,128)(2,1)} %collective-permute-done.4, f32[2,2,256,1024]{3,2,1,0:T(8,128)} %bitcast.35, s32[]{:T(128)S(6)} %select_n.191), kind=kLoop, calls=%fused_computation.1 | loop fusion | flops 1048576 | bytes 5242884 | tf_op jit(solution)/shard_map/add | solution.py:450
  118.3 0.0 copy-start.12
  118.3 1.3 copy-done.12
  119.6 0.1 dynamic-slice_convert_fusion.1
  119.7 0.4 collective-permute-start.5
  120.1 13.7 %collective-permute-done.5 = bf16[1,256,1024]{2,1,0:T(8,128)(2,1)} collective-permute-done((bf16[1,256,1024]{2,1,0:T(8,128)(2,1)S(1)}, bf16[1,256,1024]{2,1,0:T(8,128)(2,1)}, u32[]{:S(2)}, u32[]{:S(2)}) %collective-permute-start.5) | collective-permute-done | bytes 524320 | tf_op jit(solution)/shard_map/ppermute | solution.py:325
  133.8 1.5 convert_add_fusion
  135.4 0.7 fusion.1
  136.1 2.6 %collective-permute-start.6 = (bf16[4,32,1024]{2,1,0:T(8,128)(2,1)}, bf16[4,32,1024]{2,1,0:T(8,128)(2,1)}, u32[]{:S(2)}, u32[]{:S(2)}) collective-permute-start(bf16[4,32,1024]{2,1,0:T(8,128)(2,1)} %fusion.1), channel_id=1, source_target_pairs={{0,4},{4,0},{8,12},{12,8},{16,20},{20,16},{24,28},{28,24},{1,5},{5... | collective-permute-start | bytes 786440 | tf_op jit(solution)/shard_map/ppermute | solution.py:325
  138.7 6.1 %collective-permute-done.6 = bf16[4,32,1024]{2,1,0:T(8,128)(2,1)} collective-permute-done((bf16[4,32,1024]{2,1,0:T(8,128)(2,1)}, bf16[4,32,1024]{2,1,0:T(8,128)(2,1)}, u32[]{:S(2)}, u32[]{:S(2)}) %collective-permute-start.6) | collective-permute-done | bytes 262176 | tf_op jit(solution)/shard_map/ppermute | solution.py:325
  144.8 1.0 bitcast_add_fusion.1
  145.9 0.8 copy-done.13
  146.7 3.6 %collective-permute-start.7 = (bf16[2,32,1024]{2,1,0:T(8,128)(2,1)S(1)}, bf16[2,32,1024]{2,1,0:T(8,128)(2,1)S(1)}, u32[]{:S(2)}, u32[]{:S(2)}) collective-permute-start(bf16[2,32,1024]{2,1,0:T(8,128)(2,1)S(1)} %fusion.2), channel_id=1, source_target_pairs={{0,8},{4,12},{8,0},{12,4},{16,24},{20,28},{24,16},{28,20},{1,9},{5... | collective-permute-start | bytes 393224 | tf_op jit(solution)/shard_map/ppermute | solution.py:325
  150.3 2.9 %collective-permute-done.7 = bf16[2,32,1024]{2,1,0:T(8,128)(2,1)S(1)} collective-permute-done((bf16[2,32,1024]{2,1,0:T(8,128)(2,1)S(1)}, bf16[2,32,1024]{2,1,0:T(8,128)(2,1)S(1)}, u32[]{:S(2)}, u32[]{:S(2)}) %collective-permute-start.7) | collective-permute-done | bytes 131104 | tf_op jit(solution)/shard_map/ppermute | solution.py:325
  153.2 1.0 bitcast_add_fusion.2
  154.2 3.1 %collective-permute-start.8 = (bf16[1,32,1024]{2,1,0:T(8,128)(2,1)S(1)}, bf16[1,32,1024]{2,1,0:T(8,128)(2,1)S(1)}, u32[]{:S(2)}, u32[]{:S(2)}) collective-permute-start(bf16[1,32,1024]{2,1,0:T(8,128)(2,1)S(1)} %dynamic-slice_convert_fusion.3), channel_id=1, source_target_pairs={{0,16},{4,20},{8,24},{12,28},{16,0},{20,4},{24,8},{28,12},{1,17},{... | collective-permute-start | bytes 196616 | tf_op jit(solution)/shard_map/ppermute | solution.py:325
  157.3 2.2 %collective-permute-done.8 = bf16[1,32,1024]{2,1,0:T(8,128)(2,1)S(1)} collective-permute-done((bf16[1,32,1024]{2,1,0:T(8,128)(2,1)S(1)}, bf16[1,32,1024]{2,1,0:T(8,128)(2,1)S(1)}, u32[]{:S(2)}, u32[]{:S(2)}) %collective-permute-start.8) | collective-permute-done | bytes 65568 | tf_op jit(solution)/shard_map/ppermute | solution.py:325
  159.6 3.4 %collective-permute-start.9 = (bf16[1,32,1024]{2,1,0:T(8,128)(2,1)S(1)}, bf16[1,32,1024]{2,1,0:T(8,128)(2,1)S(1)}, u32[]{:S(2)}, u32[]{:S(2)}) collective-permute-start(bf16[1,32,1024]{2,1,0:T(8,128)(2,1)S(1)} %add_convert_fusion), channel_id=1, source_target_pairs={{0,16},{4,20},{8,24},{12,28},{16,0},{20,4},{24,8},{28,12},{1,17},{... | collective-permute-start | bytes 196616 | tf_op jit(solution)/shard_map/ppermute | solution.py:325
  163.0 2.4 %collective-permute-done.9 = bf16[1,32,1024]{2,1,0:T(8,128)(2,1)S(1)} collective-permute-done((bf16[1,32,1024]{2,1,0:T(8,128)(2,1)S(1)}, bf16[1,32,1024]{2,1,0:T(8,128)(2,1)S(1)}, u32[]{:S(2)}, u32[]{:S(2)}) %collective-permute-start.9) | collective-permute-done | bytes 65568 | tf_op jit(solution)/shard_map/ppermute | solution.py:325
  165.4 3.6 %collective-permute-start.10 = (bf16[2,32,1024]{2,1,0:T(8,128)(2,1)S(1)}, bf16[2,32,1024]{2,1,0:T(8,128)(2,1)S(1)}, u32[]{:S(2)}, u32[]{:S(2)}) collective-permute-start(bf16[2,32,1024]{2,1,0:T(8,128)(2,1)S(1)} %maximum_select_fusion.6), channel_id=1, source_target_pairs={{0,8},{4,12},{8,0},{12,4},{16,24},{20,28},{24,16},{28,20},{1,9},{5... | collective-permute-start | bytes 393224 | tf_op jit(solution)/shard_map/ppermute | solution.py:325
  169.0 2.9 %collective-permute-done.10 = bf16[2,32,1024]{2,1,0:T(8,128)(2,1)S(1)} collective-permute-done((bf16[2,32,1024]{2,1,0:T(8,128)(2,1)S(1)}, bf16[2,32,1024]{2,1,0:T(8,128)(2,1)S(1)}, u32[]{:S(2)}, u32[]{:S(2)}) %collective-permute-start.10) | collective-permute-done | bytes 131104 | tf_op jit(solution)/shard_map/ppermute | solution.py:325
  172.0 0.3 collective-permute-start.11
  172.3 6.1 %collective-permute-done.11 = bf16[4,32,1024]{2,1,0:T(8,128)(2,1)S(1)} collective-permute-done((bf16[4,32,1024]{2,1,0:T(8,128)(2,1)S(1)}, bf16[4,32,1024]{2,1,0:T(8,128)(2,1)S(1)}, u32[]{:S(2)}, u32[]{:S(2)}) %collective-permute-start.11) | collective-permute-done | bytes 262176 | tf_op jit(solution)/shard_map/ppermute | solution.py:325
  178.5 0.4 collective-permute-start.12
  178.9 8.8 %collective-permute-done.12 = bf16[1,256,1024]{2,1,0:T(8,128)(2,1)S(1)} collective-permute-done((bf16[1,256,1024]{2,1,0:T(8,128)(2,1)S(1)}, bf16[1,256,1024]{2,1,0:T(8,128)(2,1)S(1)}, u32[]{:S(2)}, u32[]{:S(2)}) %collective-permute-start.12) | collective-permute-done | bytes 524320 | tf_op jit(solution)/shard_map/ppermute | solution.py:325
  187.7 1.1 maximum_select_fusion.2
  188.9 0.2 maximum_select_fusion.1
  189.0 2.8 %collective-permute-done.13 = bf16[2,256,1024]{2,1,0:T(8,128)(2,1)} collective-permute-done((bf16[2,256,1024]{2,1,0:T(8,128)(2,1)}, bf16[2,256,1024]{2,1,0:T(8,128)(2,1)}, u32[]{:S(2)}, u32[]{:S(2)}) %collective-permute-start.13) | collective-permute-done | bytes 1048608 | tf_op jit(solution)/shard_map/ppermute | solution.py:325
  191.9 3.2 %maximum_select_fusion = bf16[2,2,256,1024]{3,2,1,0:T(8,128)(2,1)} fusion(bf16[2,1,256,1024]{3,2,1,0:T(8,128)(2,1)} %bitcast.20, bf16[2,1,256,1024]{3,2,1,0:T(8,128)(2,1)S(1)} %maximum_select_fusion.1, pred[]{:T(512)S(6)} %eq.25), kind=kLoop, calls=%fused_computation | loop fusion | flops 3145728 | bytes 4194305 | tf_op jit(solution)/shard_map/jit(_where)/select_n | solution.py:458
  195.1 4.4 %shard_map.75 = f32[588,1024]{1,0:T(8,128)} custom-call(bf16[4,588,256]{2,1,0:T(8,128)(2,1)S(1)} %all-to-all-done.x_ref, bf16[4,588,256]{2,1,0:T(8,128)(2,1)S(1)} %all-to-all-done.1.y_ref, bf16[1024,1024]{1,0:T(8,128)(2,1)} %bitcast.36), custom_call_target="tpu_custom_call" | custom-call | tf_op jit(solution)/shard_map/pallas_call | solution.py:462
  (25 shorter events, 0.2 us)
Async XLA Ops:
  1.3 1.3 copy-start.2
  2.6 0.7 copy-start.4
  3.7 4.7 %copy-start.3 = (bf16[2352,256]{1,0:T(8,128)(2,1)S(1)}, bf16[2352,256]{1,0:T(8,128)(2,1)}, u32[]{:S(2)}) copy-start(bf16[2352,256]{1,0:T(8,128)(2,1)} %x_ref.3) | copy-start | bytes 3612676
  3.7 4.7 %copy-start.5 = (s32[49]{0:T(128)S(1)}, s32[49]{0:T(128)}, u32[]{:S(2)}) copy-start(s32[49]{0:T(128)} %param.9) | copy-start | bytes 592
  3.7 4.7 %copy-start.6 = (s32[8,343]{1,0:T(8,128)S(1)}, s32[8,343]{1,0:T(8,128)}, u32[]{:S(2)}) copy-start(s32[8,343]{1,0:T(8,128)} %conn_ref.1) | copy-start | bytes 32932
  3.7 24.9 %collective-permute-start = (bf16[64,256]{1,0:T(8,128)(2,1)S(1)}, bf16[64,256]{1,0:T(8,128)(2,1)S(1)}, u32[]{:S(2)}, u32[]{:S(2)}) collective-permute-start(bf16[64,256]{1,0:T(8,128)(2,1)S(1)} %get-tuple-element.16), channel_id=1, source_target_pairs={{4,0},{8,4},{12,8},{16,12},{20,16},{24,20},{28,24},{5,1},{9,5},{13... | collective-permute-start | bytes 98312 | tf_op jit(solution)/shard_map/ppermute | solution.py:330
  27.6 1.1 copy-start.8
  28.6 8.6 %copy-start.7 = (bf16[2560,256]{1,0:T(8,128)(2,1)}, bf16[2560,256]{1,0:T(8,128)(2,1)S(1)}, u32[]{:S(2)}) copy-start(bf16[2560,256]{1,0:T(8,128)(2,1)S(1)} %get-tuple-element.15.v_ref) | copy-start | bytes 3932164
  37.2 1.1 copy-start.9
  38.3 16.1 %collective-permute-start.1 = (bf16[7,64,256]{2,1,0:T(8,128)(2,1)S(1)}, bf16[7,64,256]{2,1,0:T(8,128)(2,1)S(1)}, u32[]{:S(2)}, u32[]{:S(2)}) collective-permute-start(bf16[7,64,256]{2,1,0:T(8,128)(2,1)S(1)} %get-tuple-element.21), channel_id=1, source_target_pairs={{0,4},{4,8},{8,12},{12,16},{16,20},{20,24},{24,28},{1,5},{5,9},{9,... | collective-permute-start | bytes 688136 | tf_op jit(solution)/shard_map/ppermute | solution.py:330
  43.8 10.6 %collective-permute-start.2 = (bf16[7,64,256]{2,1,0:T(8,128)(2,1)S(1)}, bf16[7,64,256]{2,1,0:T(8,128)(2,1)S(1)}, u32[]{:S(2)}, u32[]{:S(2)}) collective-permute-start(bf16[7,64,256]{2,1,0:T(8,128)(2,1)S(1)} %get-tuple-element.22), channel_id=1, source_target_pairs={{4,0},{8,4},{12,8},{16,12},{20,16},{24,20},{28,24},{5,1},{9,5},{13... | collective-permute-start | bytes 688136 | tf_op jit(solution)/shard_map/ppermute | solution.py:330
  45.1 9.3 %collective-permute-start.3 = (f32[64,1]{1,0:T(8,128)S(1)}, f32[64,1]{1,0:T(8,128)S(1)}, u32[]{:S(2)}, u32[]{:S(2)}) collective-permute-start(f32[64,1]{1,0:T(8,128)S(1)} %get-tuple-element.23), channel_id=1, source_target_pairs={{4,0},{8,4},{12,8},{16,12},{20,16},{24,20},{28,24},{5,1},{9,5},{13... | collective-permute-start | bytes 776 | tf_op jit(solution)/shard_map/ppermute | solution.py:330
  62.2 1.1 copy-start.10
  67.1 1.0 copy-start.1
  68.1 19.7 %all-to-all-start = ((bf16[4,588,256]{2,1,0:T(8,128)(2,1)}), bf16[4,588,256]{2,1,0:T(8,128)(2,1)S(1)}, u32[]{:S(2)}, u32[]{:S(2)}) async-start(bf16[4,588,256]{2,1,0:T(8,128)(2,1)} %copy-done.1), calls=%async_computation | async-start | bytes 2424832 | tf_op jit(solution)/shard_map/all_to_all | solution.py:424
  71.6 1.3 copy-start.11
  76.8 1.0 copy-start
  87.8 19.7 %all-to-all-start.1 = ((bf16[4,588,256]{2,1,0:T(8,128)(2,1)}), bf16[4,588,256]{2,1,0:T(8,128)(2,1)S(1)}, u32[]{:S(2)}, u32[]{:S(2)}) async-start(bf16[4,588,256]{2,1,0:T(8,128)(2,1)} %copy-done), calls=%async_computation.1 | async-start | bytes 2424832 | tf_op jit(solution)/shard_map/all_to_all | solution.py:425
  113.2 2.9 %collective-permute-start.4 = (bf16[2,256,1024]{2,1,0:T(8,128)(2,1)S(1)}, bf16[2,256,1024]{2,1,0:T(8,128)(2,1)}, u32[]{:S(2)}, u32[]{:S(2)}) collective-permute-start(bf16[2,256,1024]{2,1,0:T(8,128)(2,1)S(1)} %fusion), channel_id=1, source_target_pairs={{0,1},{1,0},{2,3},{3,2},{4,5},{5,4},{6,7},{7,6},{8,9},{9,8},{10,11... | collective-permute-start | bytes 3145736 | tf_op jit(solution)/shard_map/ppermute | solution.py:325
  118.3 1.3 copy-start.12
  119.7 14.1 %collective-permute-start.5 = (bf16[1,256,1024]{2,1,0:T(8,128)(2,1)S(1)}, bf16[1,256,1024]{2,1,0:T(8,128)(2,1)}, u32[]{:S(2)}, u32[]{:S(2)}) collective-permute-start(bf16[1,256,1024]{2,1,0:T(8,128)(2,1)S(1)} %dynamic-slice_convert_fusion.1), channel_id=1, source_target_pairs={{0,2},{1,3},{2,0},{3,1},{4,6},{5,7},{6,4},{7,5},{8,10},{9,11},{10,... | collective-permute-start | bytes 1572872 | tf_op jit(solution)/shard_map/ppermute | solution.py:325
  136.1 8.7 %collective-permute-start.6 = (bf16[4,32,1024]{2,1,0:T(8,128)(2,1)}, bf16[4,32,1024]{2,1,0:T(8,128)(2,1)}, u32[]{:S(2)}, u32[]{:S(2)}) collective-permute-start(bf16[4,32,1024]{2,1,0:T(8,128)(2,1)} %fusion.1), channel_id=1, source_target_pairs={{0,4},{4,0},{8,12},{12,8},{16,20},{20,16},{24,28},{28,24},{1,5},{5... | collective-permute-start | bytes 786440 | tf_op jit(solution)/shard_map/ppermute | solution.py:325
  145.8 0.8 copy-start.13
  146.7 6.6 %collective-permute-start.7 = (bf16[2,32,1024]{2,1,0:T(8,128)(2,1)S(1)}, bf16[2,32,1024]{2,1,0:T(8,128)(2,1)S(1)}, u32[]{:S(2)}, u32[]{:S(2)}) collective-permute-start(bf16[2,32,1024]{2,1,0:T(8,128)(2,1)S(1)} %fusion.2), channel_id=1, source_target_pairs={{0,8},{4,12},{8,0},{12,4},{16,24},{20,28},{24,16},{28,20},{1,9},{5... | collective-permute-start | bytes 393224 | tf_op jit(solution)/shard_map/ppermute | solution.py:325
  154.2 5.3 %collective-permute-start.8 = (bf16[1,32,1024]{2,1,0:T(8,128)(2,1)S(1)}, bf16[1,32,1024]{2,1,0:T(8,128)(2,1)S(1)}, u32[]{:S(2)}, u32[]{:S(2)}) collective-permute-start(bf16[1,32,1024]{2,1,0:T(8,128)(2,1)S(1)} %dynamic-slice_convert_fusion.3), channel_id=1, source_target_pairs={{0,16},{4,20},{8,24},{12,28},{16,0},{20,4},{24,8},{28,12},{1,17},{... | collective-permute-start | bytes 196616 | tf_op jit(solution)/shard_map/ppermute | solution.py:325
  159.6 5.8 %collective-permute-start.9 = (bf16[1,32,1024]{2,1,0:T(8,128)(2,1)S(1)}, bf16[1,32,1024]{2,1,0:T(8,128)(2,1)S(1)}, u32[]{:S(2)}, u32[]{:S(2)}) collective-permute-start(bf16[1,32,1024]{2,1,0:T(8,128)(2,1)S(1)} %add_convert_fusion), channel_id=1, source_target_pairs={{0,16},{4,20},{8,24},{12,28},{16,0},{20,4},{24,8},{28,12},{1,17},{... | collective-permute-start | bytes 196616 | tf_op jit(solution)/shard_map/ppermute | solution.py:325
  165.4 6.6 %collective-permute-start.10 = (bf16[2,32,1024]{2,1,0:T(8,128)(2,1)S(1)}, bf16[2,32,1024]{2,1,0:T(8,128)(2,1)S(1)}, u32[]{:S(2)}, u32[]{:S(2)}) collective-permute-start(bf16[2,32,1024]{2,1,0:T(8,128)(2,1)S(1)} %maximum_select_fusion.6), channel_id=1, source_target_pairs={{0,8},{4,12},{8,0},{12,4},{16,24},{20,28},{24,16},{28,20},{1,9},{5... | collective-permute-start | bytes 393224 | tf_op jit(solution)/shard_map/ppermute | solution.py:325
  172.0 6.4 %collective-permute-start.11 = (bf16[4,32,1024]{2,1,0:T(8,128)(2,1)S(1)}, bf16[4,32,1024]{2,1,0:T(8,128)(2,1)S(1)}, u32[]{:S(2)}, u32[]{:S(2)}) collective-permute-start(bf16[4,32,1024]{2,1,0:T(8,128)(2,1)S(1)} %bitcast.46), channel_id=1, source_target_pairs={{0,4},{4,0},{8,12},{12,8},{16,20},{20,16},{24,28},{28,24},{1,5},{5... | collective-permute-start | bytes 786440 | tf_op jit(solution)/shard_map/ppermute | solution.py:325
  178.5 9.2 %collective-permute-start.12 = (bf16[1,256,1024]{2,1,0:T(8,128)(2,1)S(1)}, bf16[1,256,1024]{2,1,0:T(8,128)(2,1)S(1)}, u32[]{:S(2)}, u32[]{:S(2)}) collective-permute-start(bf16[1,256,1024]{2,1,0:T(8,128)(2,1)S(1)} %bitcast.38), channel_id=1, source_target_pairs={{0,2},{1,3},{2,0},{3,1},{4,6},{5,7},{6,4},{7,5},{8,10},{9,11},{10,... | collective-permute-start | bytes 1572872 | tf_op jit(solution)/shard_map/ppermute | solution.py:325
  188.9 3.0 %collective-permute-start.13 = (bf16[2,256,1024]{2,1,0:T(8,128)(2,1)}, bf16[2,256,1024]{2,1,0:T(8,128)(2,1)}, u32[]{:S(2)}, u32[]{:S(2)}) collective-permute-start(bf16[2,256,1024]{2,1,0:T(8,128)(2,1)} %maximum_select_fusion.2), channel_id=1, source_target_pairs={{0,1},{1,0},{2,3},{3,2},{4,5},{5,4},{6,7},{7,6},{8,9},{9,8},{10,11... | collective-permute-start | bytes 3145736 | tf_op jit(solution)/shard_map/ppermute | solution.py:325

commit v3 on v2

--- a/solution.py
+++ b/solution.py
@@ -117,8 +117,8 @@
         rows = prod[:stride]
         if c > 0:
             rows = jnp.concatenate([rows[:fp] + carry, rows[fp:]], axis=0)
+        emit(c, rows, prod[:fp], carry)
         carry = prod[stride:]
-        emit(c, rows)
     return carry
 
 
@@ -196,7 +196,7 @@
     for k in range(DEGREE):
         ends = {}
 
-        def emit(c, rows, k=k, now_ref=now_ref, other_ref=other_ref, ends=ends):
+        def emit(c, rows, lower, carry, k=k, now_ref=now_ref, other_ref=other_ref, ends=ends):
             at = slice(c * stride, (c + 1) * stride)
             if c == 0:
                 ends["low"] = rows[:fp]
@@ -229,11 +229,12 @@
             own_ref[side, DEGREE + 1 + block + own_ref_at, :, lane : lane + fp] = m
 
 
-def forced_kernel(fp, dead_ref, v_ref, ghost_ref, first_ref, own_ref, fromleft_ref, fromright_ref, h_ref, pot_ref, potg_ref, x_ref, image_ref, a_ref, b_ref, c_ref):
+def forced_kernel(fp, dead_ref, v_ref, ghost_ref, first_ref, own_ref, fromleft_ref, fromright_ref, h_ref, pot_ref, potg_ref, x_ref, image_ref, w_ref, a_ref, b_ref, c_ref):
     cells, cp = h_ref.shape[:2]
     stride = cp - fp
     total = cells * stride
     width = v_ref.shape[1]
+    half = cells // 2
     histories = []
     last_image = None
     for side, (got_ref, pot, start) in enumerate(
@@ -267,12 +268,17 @@
     for k in range(1, DEGREE + 1):
         now_ref = refs[k]
 
-        def emit(c, rows, k=k, now_ref=now_ref):
+        def emit(c, rows, lower, carry, k=k, now_ref=now_ref):
             at = slice(c * stride, (c + 1) * stride)
             now = now_ref[at].astype(F32)
             image = rows + pot_ref[at] * now
             if k == DEGREE:
                 out = image.astype(BF16)
+                part, at_w = divmod(c, half)
+                w_ref[part, at_w * stride : (at_w + 1) * stride] = out
+                if c == half:
+                    w_ref[0, half * stride :] = carry.astype(BF16)
+                    w_ref[1, :fp] = (lower + pot_ref[c * stride : c * stride + fp] * now[:fp]).astype(BF16)
                 if c == 0:
                     out = jnp.concatenate([last_image.astype(BF16), out[fp:]], axis=0)
                 image_ref[at] = out
@@ -285,9 +291,12 @@
             if k + 1 == DEGREE:
                 x_ref[at] = value
 
-        sweep(h_ref, now_ref, fp, emit)
+        end = sweep(h_ref, now_ref, fp, emit)
         if k < DEGREE:
             refs[k + 1][total:] = high[k + 1]
+        else:
+            w_ref[1, half * stride :] = end.astype(BF16)
+    x_ref[total:] = high[DEGREE]
 
 
 def back_kernel(node_ref, y_ref, out_ref):
@@ -328,6 +337,134 @@
 def shift(block, axis, distance):
     n = lax.axis_size(axis)
     return lax.ppermute(block, axis, [(i, i + distance) for i in range(n) if 0 <= i + distance < n])
+
+
+def tmul(a, b):
+    return lax.dot_general(a, b, (((0,), (0,)), ((), ())), preferred_element_type=F32)
+
+
+def near_gram_kernel(scale, core_ref, x_ref, w_ref, other_ref, out_ref):
+    slab, width = w_ref.shape[1:]
+    at = (slice(0, slab), slice(x_ref.shape[0] - slab, x_ref.shape[0]))
+    own = [x_ref[a] for a in at]
+    out_ref[:width] = (tmul(own[0], w_ref[0]) + tmul(own[1], w_ref[1])) * scale
+    half = width // 2
+
+    @pl.when(core_ref[0] == 0)
+    def _():
+        out_ref[width:] = sum(tmul(own[i][:, :half], other_ref[i]) for i in range(2)) * scale
+
+    @pl.when(core_ref[0] == 1)
+    def _():
+        out_ref[width:] = sum(tmul(other_ref[i, :, half:], own[i]) for i in range(2)) * scale
+
+
+def far_gram_kernel(scale, place_ref, w_ref, other_ref, far_ref, near_ref, out_ref):
+    width = w_ref.shape[2]
+    near = near_ref.shape[0]
+    side, core = place_ref[0], place_ref[1]
+    out_ref[:near] = near_ref[...]
+    far = far_ref[...]
+    mine = pl.multiple_of(near + core * width, width // 2)
+    other = pl.multiple_of(near + (1 - core) * width, width // 2)
+    out_ref[pl.ds(mine, width)] = tmul(w_ref[side], far) * scale
+    out_ref[pl.ds(other, width)] = tmul(other_ref[side], far) * scale
+
+
+def paired_residual_kernel(place_ref, q0_ref, q1_ref, q2_ref, q3_ref, x_ref, y_ref, out_ref, p_ref, q_ref):
+    parts, _, width = x_ref.shape
+    half = width // 2
+    for k, ref in enumerate((q0_ref, q1_ref, q2_ref, q3_ref)):
+        q_ref[k] = ref[...]
+    me = place_ref[0]
+    eye = (lax.broadcasted_iota(jnp.int32, (width, width), 0) == lax.broadcasted_iota(jnp.int32, (width, width), 1)).astype(
+        F32
+    ).astype(BF16)
+
+    def turned(a):
+        return lax.dot_general(eye, a, (((1,), (1,)), ((), ())), preferred_element_type=F32)
+
+    def piece(i, lo, hi):
+        return q_ref[jnp.bitwise_xor(me, i), lo:hi]
+
+    def put(i, j, value):
+        p_ref[i * width : (i + 1) * width, j * width : (j + 1) * width] = value
+
+    near = width + half
+    for i in range(parts):
+        put(i, i, piece(i, 0, width))
+    for i in range(0, parts, 2):
+        block = jnp.concatenate([piece(i, width, near), piece(i + 1, width, near)], axis=0)
+        put(i, i + 1, block)
+        put(i + 1, i, turned(block).astype(BF16))
+    for i in (0, 1):
+        for j in (2, 3):
+            one = piece(j ^ 2, near + i * width, near + (i + 1) * width)
+            two = piece(i ^ 2, near + (j - 2) * width, near + (j - 1) * width)
+            block = (one.astype(F32) + turned(two)).astype(BF16)
+            put(i, j, block)
+            put(j, i, turned(block).astype(BF16))
+    x = jnp.concatenate([x_ref[j] for j in range(parts)], axis=1)
+    for j in range(parts):
+        at = slice(j * width, (j + 1) * width)
+        out_ref[:, at] = y_ref[j].astype(F32) - mul(x, p_ref[:, at])
+
+
+def paired_tail(x_own, w_own, x_cols, i_cols, o, d, dom, nodes):
+    slab, width = w_own.shape[1:]
+    orb, rows = x_cols.shape[:2]
+    side, core = o // 2, o % 2
+    scale = 1.0 / (nodes * dom)
+    sds = jax.ShapeDtypeStruct
+    smem = pl.BlockSpec(memory_space=pltpu.SMEM)
+    vmem = pl.BlockSpec(memory_space=pltpu.VMEM)
+    start = (1 - side) * (x_own.shape[0] - slab)
+    far = swap(lax.dynamic_slice_in_dim(x_own, start, slab, 0), "orb", 2)
+    w_other = swap(w_own, "orb", 1)
+    near_rows = width + width // 2
+    near = pl.pallas_call(
+        functools.partial(near_gram_kernel, scale),
+        in_specs=[smem] + [vmem] * 3,
+        out_shape=sds((near_rows, width), F32),
+        compiler_params=params(),
+        cost_estimate=pl.CostEstimate(flops=12 * slab * width * width, bytes_accessed=4 << 20, transcendentals=0),
+    )(core.reshape(1), x_own, w_own, w_other)
+    x_cols, i_cols, far = lax.optimization_barrier((x_cols, i_cols, far))
+    x_rows = lax.all_to_all(x_cols, "orb", split_axis=0, concat_axis=0, tiled=True)
+    i_rows = lax.all_to_all(i_cols, "orb", split_axis=0, concat_axis=0, tiled=True)
+    share = pl.pallas_call(
+        functools.partial(far_gram_kernel, scale),
+        in_specs=[smem] + [vmem] * 4,
+        out_shape=sds((near_rows + 2 * width, width), F32),
+        compiler_params=params(),
+        cost_estimate=pl.CostEstimate(flops=8 * slab * width * width, bytes_accessed=4 << 20, transcendentals=0),
+    )(jnp.stack([side, core]), w_own, w_other, far, near)
+
+    bits = []
+    bit = 1
+    while bit < dom:
+        mine = (d // bit) % 2
+        share = share.reshape(2, share.shape[0] // 2, width)
+        keep = lax.dynamic_index_in_dim(share, mine, 0, keepdims=False)
+        give = lax.dynamic_index_in_dim(share, 1 - mine, 0, keepdims=False)
+        share = keep + swap(give.astype(BF16), "dom", bit).astype(F32)
+        bits.append((bit, mine))
+        bit *= 2
+    share = share.astype(BF16)
+    for bit, mine in reversed(bits):
+        got = swap(share, "dom", bit)
+        share = jnp.where(mine == 0, jnp.concatenate([share, got], axis=0), jnp.concatenate([got, share], axis=0))
+    q2 = swap(share, "orb", 2)
+    q1 = swap(share, "orb", 1)
+    q3 = swap(q2, "orb", 1)
+    cols = orb * width
+    return pl.pallas_call(
+        paired_residual_kernel,
+        in_specs=[smem] + [vmem] * 6,
+        out_shape=(sds((rows, cols), F32), sds((cols, cols), BF16)),
+        scratch_shapes=[pltpu.VMEM((orb,) + share.shape, BF16)],
+        compiler_params=params(),
+    )(o.reshape(1), share, q1, q2, q3, x_rows, i_rows)
 
 
 def body(orbitals, potential, cell_hamiltonian, connectivity, face_nodes):
@@ -403,10 +540,11 @@
     from_left = shift(up, "dom", 1)
     from_right = shift(down, "dom", -1)
     vmem = pl.BlockSpec(memory_space=pltpu.VMEM)
-    x_own, image = pl.pallas_call(
+    slab = cells // 2 * stride + fp
+    x_own, image, w_own = pl.pallas_call(
         functools.partial(forced_kernel, fp),
         in_specs=[pl.BlockSpec(memory_space=pltpu.SMEM)] + [vmem] * 9,
-        out_shape=[sds((total, width), BF16)] * 2,
+        out_shape=[sds((total + fp, width), BF16), sds((total, width), BF16), sds((2, slab, width), BF16)],
         scratch_shapes=[ext, ext, ext],
         compiler_params=params(),
         cost_estimate=cost,
@@ -421,8 +559,11 @@
         compiler_params=params(),
         cost_estimate=pl.CostEstimate(flops=2 * total * nodes * width, bytes_accessed=4 << 20, transcendentals=0),
     )
-    x_rows = lax.all_to_all(back(node_row, x_own), "orb", split_axis=0, concat_axis=0, tiled=True)
-    i_rows = lax.all_to_all(back(node_row, image), "orb", split_axis=0, concat_axis=0, tiled=True)
+    x_cols, i_cols = back(node_row, x_own), back(node_row, image)
+    if orb == 4 and dom % 8 == 0:
+        return paired_tail(x_own, w_own, x_cols, i_cols, o, d, dom, nodes)
+    x_rows = lax.all_to_all(x_cols, "orb", split_axis=0, concat_axis=0, tiled=True)
+    i_rows = lax.all_to_all(i_cols, "orb", split_axis=0, concat_axis=0, tiled=True)
 
     rows = nodes // orb
     cols = orb * width

time: 200 us -> 156 us (0.78)
  waiting for transfers between devices: 84.6 us -> 53.9 us
  other arithmetic: 10.4 us -> 0.49 us
  local copies, waits for them, and re-layouts: 17.2 us -> 10.8 us
  Pallas kernels: 51.9 us -> 55.6 us
    ppermute x10 -> x11, waiting for transfers between devices: 50.8 us -> 32.8 us  [swap(): lax.ppermute(block, axis, [(i, i ^ bit) for i in range(lax.axis_size(axis...]
    all_to_all x2, waiting for transfers between devices: 26.2 us -> 13.3 us  [the longest x1 13.3 us: paired_tail(): lax.all_to_all(i_cols, 'orb', split_axis=0, concat_axis=0, tiled=True)]
    add x4 -> x2, other arithmetic: 5.73 us -> 0.07 us  [paired_tail(): share = keep + swap(give.astype(BF16), 'dom', bit).astype(F32)]
    unnamed x29 -> x23, local copies, waits for them, and re-layouts: 13.8 us -> 8.67 us
    select_n x7 -> x3, other arithmetic: 4.65 us -> 0.3 us  [paired_tail(): jnp.where(mine == 0, jnp.concatenate([share, got], axis=0), jnp.concatena...]
    pallas_call x4 -> x5, Pallas kernels: 16 us -> 18.8 us  [the longest x2 9.1 us: body(): x_cols, i_cols = (back(node_row, x_own), back(node_row, image))]
    convert_element_type x5 -> x3, local copies, waits for them, and re-layouts: 2.59 us -> 0.07 us  [paired_tail(): share = keep + swap(give.astype(BF16), 'dom', bit).astype(F32)]
    ppermute x10 -> x11, starting transfers between devices: 17.7 us -> 15.9 us  [swap(): lax.ppermute(block, axis, [(i, i ^ bit) for i in range(lax.axis_size(axis...]
  transfers between devices with their start and end apart: 16 -> 17, of which waited for: 13 -> 9; matrix products, arithmetic and copies ran while one was open for 2% -> 3% of each run, Pallas kernels for 12% -> 18%
where the time goes in v3:
time: 156 us; the launch traced here: 155 us
  Pallas kernels  55.6 us (36%)
  waiting for transfers between devices  53.9 us (35%)
  starting transfers between devices  33.4 us (21%)
  local copies, waits for them, and re-layouts  10.8 us (7%)
    ppermute x11, waiting for transfers between devices, swap(): lax.ppermute(block, axis, [(i, i ^ bit) for i in range(lax.axis_size(axis...  32.8 us
    pallas_call x1, Pallas kernels, body(): pl.pallas_call(functools.partial(order_kernel, fp, ip), grid=(cells,), in...  19.1 us
    ppermute x11, starting transfers between devices, swap(): lax.ppermute(block, axis, [(i, i ^ bit) for i in range(lax.axis_size(axis...  15.9 us
    all_to_all x1, waiting for transfers between devices, paired_tail(): lax.all_to_all(i_cols, 'orb', split_axis=0, concat_axis=0, tiled=True)  13.3 us
    ppermute x4, starting transfers between devices, shift(): lax.ppermute(block, axis, [(i, i + distance) for i in range(n) if 0 <= i...  9.69 us
    pallas_call x2, Pallas kernels, body(): x_cols, i_cols = (back(node_row, x_own), back(node_row, image))  9.1 us
    pallas_call x1, Pallas kernels, body(): pl.pallas_call(functools.partial(free_kernel, fp), out_shape=[sds((total,...  8.7 us
    unnamed x23, local copies, waits for them, and re-layouts  8.67 us
  transfers between devices with their start and end apart: 17, of which 9 were waited for; matrix products, arithmetic and copies ran while one was open for 3% of the time, Pallas kernels for 18%

profile of v3, /device:TPU:0, one launch (start us, length us, event | category | flops | bytes accessed | tf_op | source)
XLA Modules:
  0.0 155.0 jit_solution(11916195634820531627)
XLA Ops:
  0.6 0.7 reshape.38.pot_ref
  1.3 1.3 copy-done.2
  2.6 0.7 copy-done.4
  3.3 0.4 shard_map.69
  3.7 0.0 copy-start.3
  3.7 0.0 copy-start.5
  3.7 0.0 copy-start.6
  3.7 1.4 collective-permute-start
  5.2 3.2 %copy.7.h_ref = bf16[8,343,343]{2,1,0:T(8,128)(2,1)} copy(bf16[8,343,343]{2,0,1:T(8,128)(2,1)} %param.7) | data formatting | bytes 3764768 | tf_op args[2]
  8.4 0.0 copy-done.3
  8.4 0.0 copy-done.5
  8.4 0.0 copy-done.6
  8.4 19.1 %shard_map.68 = (bf16[8,384,384]{2,1,0:T(8,128)(2,1)}, bf16[2560,256]{1,0:T(8,128)(2,1)S(1)}, f32[2560,1]{1,0:T(8,128)S(1)}, f32[8,1,320]{2,1,0:T(1,128)S(1)}) custom-call(s32[8,343]{1,0:T(8,128)S(1)} %copy-done.6, s32[1,49]{1,0:T(1,128)S(1)} %bitcast.25, bf16[8,343,343]{2,1,0:T(8,128)(2,1)} %copy.7.h_ref, bf16[2352,256]{1,0:T(8,128)(2,1)S(1)} %copy-done.3, ...), custom_call_target="tpu_custom_call" | custom-call | flops 6165626880 | bytes 8388608 | tf_op jit(solution)/shard_map/pallas_call | solution.py:494
  27.5 1.1 copy-done.9
  28.6 0.0 collective-permute-done.ghost_ref
  28.6 8.7 %shard_map.70 = (bf16[2560,256]{1,0:T(8,128)(2,1)S(1)}, f32[2,6,64,256]{3,2,1,0:T(8,128)S(1)}, bf16[7,64,256]{2,1,0:T(8,128)(2,1)S(1)}, bf16[7,64,256]{2,1,0:T(8,128)(2,1)S(1)}) custom-call(bf16[2560,256]{1,0:T(8,128)(2,1)S(1)} %get-tuple-element.18.v_ref, bf16[64,256]{1,0:T(8,128)(2,1)S(1)} %collective-permute-done.ghost_ref, ...), custom_call_target="tpu_custom_call" | custom-call | flops 2415919104 | bytes 8388608 | tf_op jit(solution)/shard_map/pallas_call | solution.py:528
  37.3 0.0 copy-done.7
  37.3 0.0 copy-start.10
  37.3 1.1 copy-done.10
  38.4 5.5 %collective-permute-start.1 = (bf16[7,64,256]{2,1,0:T(8,128)(2,1)S(1)}, bf16[7,64,256]{2,1,0:T(8,128)(2,1)S(1)}, u32[]{:S(2)}, u32[]{:S(2)}) collective-permute-start(bf16[7,64,256]{2,1,0:T(8,128)(2,1)S(1)} %get-tuple-element.24), channel_id=1, source_target_pairs={{0,4},{4,8},{8,12},{12,16},{16,20},{20,24},{24,28},{1,5},{5,9},{9,... | collective-permute-start | bytes 688136 | tf_op jit(solution)/shard_map/ppermute | solution.py:339
  43.9 1.3 collective-permute-start.2
  45.2 1.5 collective-permute-start.3
  46.7 7.8 %collective-permute-done.3.potg_ref = f32[64,1]{1,0:T(8,128)S(1)} collective-permute-done((f32[64,1]{1,0:T(8,128)S(1)}, f32[64,1]{1,0:T(8,128)S(1)}, u32[]{:S(2)}, u32[]{:S(2)}) %collective-permute-start.3) | collective-permute-done | bytes 288 | tf_op jit(solution)/shard_map/ppermute | solution.py:339
  54.5 0.0 collective-permute-done.1.fromleft_ref
  54.5 0.0 collective-permute-done.2.fromright_ref
  54.5 1.3 copy-done.8
  55.8 8.6 %shard_map.71 = (bf16[2624,256]{1,0:T(8,128)(2,1)}, bf16[2560,256]{1,0:T(8,128)(2,1)S(1)}, bf16[2,1344,256]{2,1,0:T(8,128)(2,1)}) custom-call(s32[1]{0:T(128)} %bitcast.3.dead_ref, bf16[2560,256]{1,0:T(8,128)(2,1)S(1)} %copy-done.8, bf16[64,256]{1,0:T(8,128)(2,1)S(1)} %collective-permute-done.ghost_ref, bf16[2560,256]{1,0:T(8,128)(2,1)} %copy-done.10, ...), custom_call_target="tpu_custom_call" | custom-call | flops 2415919104 | bytes 8388608 | tf_op jit(solution)/shard_map/pallas_call | solution.py:544
  64.4 0.0 collective-permute-start.4
  64.5 0.1 reshape.39.node_ref
  64.5 1.2 constant_dynamic-slice_fusion
  65.8 1.6 %collective-permute-start.5 = (bf16[1344,256]{1,0:T(8,128)(2,1)S(1)}, bf16[1344,256]{1,0:T(8,128)(2,1)S(1)}, u32[]{:S(2)}, u32[]{:S(2)}) collective-permute-start(bf16[1344,256]{1,0:T(8,128)(2,1)S(1)} %constant_dynamic-slice_fusion), channel_id=1, source_target_pairs={{0,2},{1,3},{2,0},{3,1},{4,6},{5,7},{6,4},{7,5},{8,10},{9,11},{10,... | collective-permute-start | bytes 2064392 | tf_op jit(solution)/shard_map/ppermute | solution.py:334
  67.3 0.1 pad_add_fusion.place_ref
  67.4 0.0 copy-done.1
  67.4 4.5 %shard_map.72 = bf16[4,588,256]{2,1,0:T(8,128)(2,1)} custom-call(f32[1,2560]{1,0:T(1,128)S(1)} %reshape.39.node_ref, bf16[2624,256]{1,0:T(8,128)(2,1)S(1)} %copy-done.1), custom_call_target="tpu_custom_call" | custom-call | flops 3082813440 | bytes 4194304 | tf_op jit(solution)/shard_map/pallas_call | solution.py:562
  72.0 4.6 %shard_map.73 = bf16[4,588,256]{2,1,0:T(8,128)(2,1)} custom-call(f32[1,2560]{1,0:T(1,128)S(1)} %reshape.39.node_ref, bf16[2560,256]{1,0:T(8,128)(2,1)S(1)} %get-tuple-element.30.y_ref), custom_call_target="tpu_custom_call" | custom-call | flops 3082813440 | bytes 4194304 | tf_op jit(solution)/shard_map/pallas_call | solution.py:562
  76.5 7.1 %collective-permute-done.5.far_ref = bf16[1344,256]{1,0:T(8,128)(2,1)S(1)} collective-permute-done((bf16[1344,256]{1,0:T(8,128)(2,1)S(1)}, bf16[1344,256]{1,0:T(8,128)(2,1)S(1)}, u32[]{:S(2)}, u32[]{:S(2)}) %collective-permute-start.5) | collective-permute-done | bytes 688160 | tf_op jit(solution)/shard_map/ppermute | solution.py:334
  83.6 0.0 collective-permute-done.4.other_ref
  83.6 2.3 %shard_map.74.near_ref = f32[384,256]{1,0:T(8,128)S(1)} custom-call(s32[1]{0:T(128)} %bitcast.2.core_ref, bf16[2624,256]{1,0:T(8,128)(2,1)S(1)} %copy-done.1, bf16[2,1344,256]{2,1,0:T(8,128)(2,1)S(1)} %copy-done, bf16[2,1344,256]{2,1,0:T(8,128)(2,1)} %collective-permute-done.4.other_ref), custom_call_target="tpu_custom_call" | custom-call | flops 1056964608 | bytes 4194304 | tf_op jit(solution)/shard_map/pallas_call | solution.py:425
  86.0 2.0 %shard_map.75 = f32[896,256]{1,0:T(8,128)S(1)} custom-call(s32[2]{0:T(128)S(1)} %pad_add_fusion.place_ref, bf16[2,1344,256]{2,1,0:T(8,128)(2,1)S(1)} %copy-done, bf16[2,1344,256]{2,1,0:T(8,128)(2,1)} %collective-permute-done.4.other_ref, bf16[1344,256]{1,0:T(8,128)(2,1)S(1)} %collective-permute-done.5.far_ref, f32[384,256]{1,0:T(8,128)S(1)} %shard_map.74.near_ref), custom_call_target="tpu_custom_call" | custom-call | flops 704643072 | bytes 4194304 | tf_op jit(solution)/shard_map/pallas_call | solution.py:435
  88.0 2.7 %collective-permute-start.6 = (bf16[448,256]{1,0:T(8,128)(2,1)S(1)}, bf16[448,256]{1,0:T(8,128)(2,1)S(1)}, u32[]{:S(2)}, u32[]{:S(2)}) collective-permute-start(bf16[448,256]{1,0:T(8,128)(2,1)S(1)} %fusion), channel_id=1, source_target_pairs={{0,4},{4,0},{8,12},{12,8},{16,20},{20,16},{24,28},{28,24},{1,5},{5... | collective-permute-start | bytes 688136 | tf_op jit(solution)/shard_map/ppermute | solution.py:334
  90.7 5.5 %collective-permute-done.6 = bf16[448,256]{1,0:T(8,128)(2,1)S(1)} collective-permute-done((bf16[448,256]{1,0:T(8,128)(2,1)S(1)}, bf16[448,256]{1,0:T(8,128)(2,1)S(1)}, u32[]{:S(2)}, u32[]{:S(2)}) %collective-permute-start.6) | collective-permute-done | bytes 229408 | tf_op jit(solution)/shard_map/ppermute | solution.py:334
  96.2 3.6 %collective-permute-start.7 = (bf16[224,256]{1,0:T(8,128)(2,1)S(1)}, bf16[224,256]{1,0:T(8,128)(2,1)S(1)}, u32[]{:S(2)}, u32[]{:S(2)}) collective-permute-start(bf16[224,256]{1,0:T(8,128)(2,1)S(1)} %fusion.1), channel_id=1, source_target_pairs={{0,8},{4,12},{8,0},{12,4},{16,24},{20,28},{24,16},{28,20},{1,9},{5... | collective-permute-start | bytes 344072 | tf_op jit(solution)/shard_map/ppermute | solution.py:334
  99.8 2.8 %collective-permute-done.7 = bf16[224,256]{1,0:T(8,128)(2,1)S(1)} collective-permute-done((bf16[224,256]{1,0:T(8,128)(2,1)S(1)}, bf16[224,256]{1,0:T(8,128)(2,1)S(1)}, u32[]{:S(2)}, u32[]{:S(2)}) %collective-permute-start.7) | collective-permute-done | bytes 114720 | tf_op jit(solution)/shard_map/ppermute | solution.py:334
  102.7 3.1 %collective-permute-start.8 = (bf16[112,256]{1,0:T(8,128)(2,1)S(1)}, bf16[112,256]{1,0:T(8,128)(2,1)S(1)}, u32[]{:S(2)}, u32[]{:S(2)}) collective-permute-start(bf16[112,256]{1,0:T(8,128)(2,1)S(1)} %fusion.3), channel_id=1, source_target_pairs={{0,16},{4,20},{8,24},{12,28},{16,0},{20,4},{24,8},{28,12},{1,17},{... | collective-permute-start | bytes 172040 | tf_op jit(solution)/shard_map/ppermute | solution.py:334
  105.8 3.5 %all-to-all-start = ((bf16[4,588,256]{2,1,0:T(8,128)(2,1)}), bf16[4,588,256]{2,1,0:T(8,128)(2,1)S(1)}, u32[]{:S(2)}, u32[]{:S(2)}) async-start(bf16[4,588,256]{2,1,0:T(8,128)(2,1)} %shard_map.72), calls=%async_computation | async-start | bytes 2424832 | tf_op jit(solution)/shard_map/all_to_all | solution.py:433
  109.3 0.0 collective-permute-done.8
  109.3 1.6 %collective-permute-start.9 = (bf16[112,256]{1,0:T(8,128)(2,1)S(1)}, bf16[112,256]{1,0:T(8,128)(2,1)S(1)}, u32[]{:S(2)}, u32[]{:S(2)}) collective-permute-start(bf16[112,256]{1,0:T(8,128)(2,1)S(1)} %fusion.2), channel_id=1, source_target_pairs={{0,16},{4,20},{8,24},{12,28},{16,0},{20,4},{24,8},{28,12},{1,17},{... | collective-permute-start | bytes 172040 | tf_op jit(solution)/shard_map/ppermute | solution.py:334
  111.0 4.8 %collective-permute-done.9 = bf16[112,256]{1,0:T(8,128)(2,1)S(1)} collective-permute-done((bf16[112,256]{1,0:T(8,128)(2,1)S(1)}, bf16[112,256]{1,0:T(8,128)(2,1)S(1)}, u32[]{:S(2)}, u32[]{:S(2)}) %collective-permute-start.9) | collective-permute-done | bytes 57376 | tf_op jit(solution)/shard_map/ppermute | solution.py:334
  115.8 0.5 collective-permute-start.10
  116.3 4.3 %collective-permute-done.10 = bf16[224,256]{1,0:T(8,128)(2,1)S(1)} collective-permute-done((bf16[224,256]{1,0:T(8,128)(2,1)S(1)}, bf16[224,256]{1,0:T(8,128)(2,1)S(1)}, u32[]{:S(2)}, u32[]{:S(2)}) %collective-permute-start.10) | collective-permute-done | bytes 114720 | tf_op jit(solution)/shard_map/ppermute | solution.py:334
  120.7 0.1 maximum_select_fusion.1
  120.8 0.4 collective-permute-start.11
  121.1 5.7 %collective-permute-done.11 = bf16[448,256]{1,0:T(8,128)(2,1)S(1)} collective-permute-done((bf16[448,256]{1,0:T(8,128)(2,1)S(1)}, bf16[448,256]{1,0:T(8,128)(2,1)S(1)}, u32[]{:S(2)}, u32[]{:S(2)}) %collective-permute-start.11) | collective-permute-done | bytes 229408 | tf_op jit(solution)/shard_map/ppermute | solution.py:334
  126.9 0.2 maximum_select_fusion.q0_ref
  127.1 1.9 %collective-permute-start.13 = (bf16[896,256]{1,0:T(8,128)(2,1)S(1)}, bf16[896,256]{1,0:T(8,128)(2,1)S(1)}, u32[]{:S(2)}, u32[]{:S(2)}) collective-permute-start(bf16[896,256]{1,0:T(8,128)(2,1)S(1)} %maximum_select_fusion.q0_ref), channel_id=1, source_target_pairs={{0,2},{1,3},{2,0},{3,1},{4,6},{5,7},{6,4},{7,5},{8,10},{9,11},{10,... | collective-permute-start | bytes 1376264 | tf_op jit(solution)/shard_map/ppermute | solution.py:334
  129.0 0.0 all-to-all-done.x_ref
  129.0 4.3 %all-to-all-start.1 = ((bf16[4,588,256]{2,1,0:T(8,128)(2,1)}), bf16[4,588,256]{2,1,0:T(8,128)(2,1)}, u32[]{:S(2)}, u32[]{:S(2)}) async-start(bf16[4,588,256]{2,1,0:T(8,128)(2,1)} %shard_map.73), calls=%async_computation.1 | async-start | bytes 2424832 | tf_op jit(solution)/shard_map/all_to_all | solution.py:434
  133.3 0.5 collective-permute-start.12
  133.7 2.5 %collective-permute-done.13.q2_ref = bf16[896,256]{1,0:T(8,128)(2,1)S(1)} collective-permute-done((bf16[896,256]{1,0:T(8,128)(2,1)S(1)}, bf16[896,256]{1,0:T(8,128)(2,1)S(1)}, u32[]{:S(2)}, u32[]{:S(2)}) %collective-permute-start.13) | collective-permute-done | bytes 458784 | tf_op jit(solution)/shard_map/ppermute | solution.py:334
  136.3 0.0 collective-permute-start.14
  136.3 13.3 %all-to-all-done.1.y_ref = bf16[4,588,256]{2,1,0:T(8,128)(2,1)} async-done(((bf16[4,588,256]{2,1,0:T(8,128)(2,1)}), bf16[4,588,256]{2,1,0:T(8,128)(2,1)}, u32[]{:S(2)}, u32[]{:S(2)}) %all-to-all-start.1) | async-done | bytes 1204256 | tf_op jit(solution)/shard_map/all_to_all | solution.py:434
  149.6 0.0 collective-permute-done.12.q1_ref
  149.6 0.0 collective-permute-done.14.q3_ref
  149.6 5.4 %shard_map.76 = (f32[588,1024]{1,0:T(8,128)}, bf16[1024,1024]{1,0:T(8,128)(2,1)}) custom-call(s32[1]{0:T(128)} %bitcast.place_ref, bf16[896,256]{1,0:T(8,128)(2,1)S(1)} %maximum_select_fusion.q0_ref, bf16[896,256]{1,0:T(8,128)(2,1)S(1)} %collective-permute-done.12.q1_ref, bf16[896,256]{1,0:T(8,128)(2,1)S(1)} %collective-permute-done.13.q2_ref, ...), custom_call_target="tpu_custom_call" | custom-call | tf_op jit(solution)/shard_map/pallas_call | solution.py:461
  (16 shorter events, 0.2 us)
Async XLA Ops:
  1.3 1.3 copy-start.2
  2.6 0.7 copy-start.4
  3.7 4.7 %copy-start.3 = (bf16[2352,256]{1,0:T(8,128)(2,1)S(1)}, bf16[2352,256]{1,0:T(8,128)(2,1)}, u32[]{:S(2)}) copy-start(bf16[2352,256]{1,0:T(8,128)(2,1)} %x_ref.3) | copy-start | bytes 3612676
  3.7 4.7 %copy-start.5 = (s32[49]{0:T(128)S(1)}, s32[49]{0:T(128)}, u32[]{:S(2)}) copy-start(s32[49]{0:T(128)} %param.9) | copy-start | bytes 592
  3.7 4.7 %copy-start.6 = (s32[8,343]{1,0:T(8,128)S(1)}, s32[8,343]{1,0:T(8,128)}, u32[]{:S(2)}) copy-start(s32[8,343]{1,0:T(8,128)} %conn_ref.1) | copy-start | bytes 32932
  3.7 24.8 %collective-permute-start = (bf16[64,256]{1,0:T(8,128)(2,1)S(1)}, bf16[64,256]{1,0:T(8,128)(2,1)S(1)}, u32[]{:S(2)}, u32[]{:S(2)}) collective-permute-start(bf16[64,256]{1,0:T(8,128)(2,1)S(1)} %get-tuple-element.19), channel_id=1, source_target_pairs={{4,0},{8,4},{12,8},{16,12},{20,16},{24,20},{28,24},{5,1},{9,5},{13... | collective-permute-start | bytes 98312 | tf_op jit(solution)/shard_map/ppermute | solution.py:339
  27.5 1.1 copy-start.9
  28.6 8.7 %copy-start.7 = (bf16[2560,256]{1,0:T(8,128)(2,1)}, bf16[2560,256]{1,0:T(8,128)(2,1)S(1)}, u32[]{:S(2)}) copy-start(bf16[2560,256]{1,0:T(8,128)(2,1)S(1)} %get-tuple-element.18.v_ref) | copy-start | bytes 3932164
  37.3 1.1 copy-start.10
  38.4 16.1 %collective-permute-start.1 = (bf16[7,64,256]{2,1,0:T(8,128)(2,1)S(1)}, bf16[7,64,256]{2,1,0:T(8,128)(2,1)S(1)}, u32[]{:S(2)}, u32[]{:S(2)}) collective-permute-start(bf16[7,64,256]{2,1,0:T(8,128)(2,1)S(1)} %get-tuple-element.24), channel_id=1, source_target_pairs={{0,4},{4,8},{8,12},{12,16},{16,20},{20,24},{24,28},{1,5},{5,9},{9,... | collective-permute-start | bytes 688136 | tf_op jit(solution)/shard_map/ppermute | solution.py:339
  43.9 10.6 %collective-permute-start.2 = (bf16[7,64,256]{2,1,0:T(8,128)(2,1)S(1)}, bf16[7,64,256]{2,1,0:T(8,128)(2,1)S(1)}, u32[]{:S(2)}, u32[]{:S(2)}) collective-permute-start(bf16[7,64,256]{2,1,0:T(8,128)(2,1)S(1)} %get-tuple-element.25), channel_id=1, source_target_pairs={{4,0},{8,4},{12,8},{16,12},{20,16},{24,20},{28,24},{5,1},{9,5},{13... | collective-permute-start | bytes 688136 | tf_op jit(solution)/shard_map/ppermute | solution.py:339
  45.2 9.3 %collective-permute-start.3 = (f32[64,1]{1,0:T(8,128)S(1)}, f32[64,1]{1,0:T(8,128)S(1)}, u32[]{:S(2)}, u32[]{:S(2)}) collective-permute-start(f32[64,1]{1,0:T(8,128)S(1)} %get-tuple-element.26), channel_id=1, source_target_pairs={{4,0},{8,4},{12,8},{16,12},{20,16},{24,20},{28,24},{5,1},{9,5},{13... | collective-permute-start | bytes 776 | tf_op jit(solution)/shard_map/ppermute | solution.py:339
  54.5 1.3 copy-start.8
  64.4 3.0 %copy-start.1 = (bf16[2624,256]{1,0:T(8,128)(2,1)S(1)}, bf16[2624,256]{1,0:T(8,128)(2,1)}, u32[]{:S(2)}) copy-start(bf16[2624,256]{1,0:T(8,128)(2,1)} %get-tuple-element.29.y_ref.x_ref) | copy-start | bytes 4030468
  64.4 19.2 %collective-permute-start.4 = (bf16[2,1344,256]{2,1,0:T(8,128)(2,1)}, bf16[2,1344,256]{2,1,0:T(8,128)(2,1)}, u32[]{:S(2)}, u32[]{:S(2)}) collective-permute-start(bf16[2,1344,256]{2,1,0:T(8,128)(2,1)} %get-tuple-element.27.w_ref), channel_id=1, source_target_pairs={{0,1},{1,0},{2,3},{3,2},{4,5},{5,4},{6,7},{7,6},{8,9},{9,8},{10,11... | collective-permute-start | bytes 4128776 | tf_op jit(solution)/shard_map/ppermute | solution.py:334
  65.8 17.8 %collective-permute-start.5 = (bf16[1344,256]{1,0:T(8,128)(2,1)S(1)}, bf16[1344,256]{1,0:T(8,128)(2,1)S(1)}, u32[]{:S(2)}, u32[]{:S(2)}) collective-permute-start(bf16[1344,256]{1,0:T(8,128)(2,1)S(1)} %constant_dynamic-slice_fusion), channel_id=1, source_target_pairs={{0,2},{1,3},{2,0},{3,1},{4,6},{5,7},{6,4},{7,5},{8,10},{9,11},{10,... | collective-permute-start | bytes 2064392 | tf_op jit(solution)/shard_map/ppermute | solution.py:334
  72.0 11.7 %copy-start = (bf16[2,1344,256]{2,1,0:T(8,128)(2,1)S(1)}, bf16[2,1344,256]{2,1,0:T(8,128)(2,1)}, u32[]{:S(2)}) copy-start(bf16[2,1344,256]{2,1,0:T(8,128)(2,1)} %get-tuple-element.27.w_ref) | copy-start | bytes 4128772
  88.0 8.2 %collective-permute-start.6 = (bf16[448,256]{1,0:T(8,128)(2,1)S(1)}, bf16[448,256]{1,0:T(8,128)(2,1)S(1)}, u32[]{:S(2)}, u32[]{:S(2)}) collective-permute-start(bf16[448,256]{1,0:T(8,128)(2,1)S(1)} %fusion), channel_id=1, source_target_pairs={{0,4},{4,0},{8,12},{12,8},{16,20},{20,16},{24,28},{28,24},{1,5},{5... | collective-permute-start | bytes 688136 | tf_op jit(solution)/shard_map/ppermute | solution.py:334
  96.2 6.4 %collective-permute-start.7 = (bf16[224,256]{1,0:T(8,128)(2,1)S(1)}, bf16[224,256]{1,0:T(8,128)(2,1)S(1)}, u32[]{:S(2)}, u32[]{:S(2)}) collective-permute-start(bf16[224,256]{1,0:T(8,128)(2,1)S(1)} %fusion.1), channel_id=1, source_target_pairs={{0,8},{4,12},{8,0},{12,4},{16,24},{20,28},{24,16},{28,20},{1,9},{5... | collective-permute-start | bytes 344072 | tf_op jit(solution)/shard_map/ppermute | solution.py:334
  102.7 6.6 %collective-permute-start.8 = (bf16[112,256]{1,0:T(8,128)(2,1)S(1)}, bf16[112,256]{1,0:T(8,128)(2,1)S(1)}, u32[]{:S(2)}, u32[]{:S(2)}) collective-permute-start(bf16[112,256]{1,0:T(8,128)(2,1)S(1)} %fusion.3), channel_id=1, source_target_pairs={{0,16},{4,20},{8,24},{12,28},{16,0},{20,4},{24,8},{28,12},{1,17},{... | collective-permute-start | bytes 172040 | tf_op jit(solution)/shard_map/ppermute | solution.py:334
  105.8 23.2 %all-to-all-start = ((bf16[4,588,256]{2,1,0:T(8,128)(2,1)}), bf16[4,588,256]{2,1,0:T(8,128)(2,1)S(1)}, u32[]{:S(2)}, u32[]{:S(2)}) async-start(bf16[4,588,256]{2,1,0:T(8,128)(2,1)} %shard_map.72), calls=%async_computation | async-start | bytes 2424832 | tf_op jit(solution)/shard_map/all_to_all | solution.py:433
  109.3 6.5 %collective-permute-start.9 = (bf16[112,256]{1,0:T(8,128)(2,1)S(1)}, bf16[112,256]{1,0:T(8,128)(2,1)S(1)}, u32[]{:S(2)}, u32[]{:S(2)}) collective-permute-start(bf16[112,256]{1,0:T(8,128)(2,1)S(1)} %fusion.2), channel_id=1, source_target_pairs={{0,16},{4,20},{8,24},{12,28},{16,0},{20,4},{24,8},{28,12},{1,17},{... | collective-permute-start | bytes 172040 | tf_op jit(solution)/shard_map/ppermute | solution.py:334
  115.8 4.9 %collective-permute-start.10 = (bf16[224,256]{1,0:T(8,128)(2,1)S(1)}, bf16[224,256]{1,0:T(8,128)(2,1)S(1)}, u32[]{:S(2)}, u32[]{:S(2)}) collective-permute-start(bf16[224,256]{1,0:T(8,128)(2,1)S(1)} %maximum_select_fusion.2), channel_id=1, source_target_pairs={{0,8},{4,12},{8,0},{12,4},{16,24},{20,28},{24,16},{28,20},{1,9},{5... | collective-permute-start | bytes 344072 | tf_op jit(solution)/shard_map/ppermute | solution.py:334
  120.8 6.1 %collective-permute-start.11 = (bf16[448,256]{1,0:T(8,128)(2,1)S(1)}, bf16[448,256]{1,0:T(8,128)(2,1)S(1)}, u32[]{:S(2)}, u32[]{:S(2)}) collective-permute-start(bf16[448,256]{1,0:T(8,128)(2,1)S(1)} %maximum_select_fusion.1), channel_id=1, source_target_pairs={{0,4},{4,0},{8,12},{12,8},{16,20},{20,16},{24,28},{28,24},{1,5},{5... | collective-permute-start | bytes 688136 | tf_op jit(solution)/shard_map/ppermute | solution.py:334
  127.1 9.2 %collective-permute-start.13 = (bf16[896,256]{1,0:T(8,128)(2,1)S(1)}, bf16[896,256]{1,0:T(8,128)(2,1)S(1)}, u32[]{:S(2)}, u32[]{:S(2)}) collective-permute-start(bf16[896,256]{1,0:T(8,128)(2,1)S(1)} %maximum_select_fusion.q0_ref), channel_id=1, source_target_pairs={{0,2},{1,3},{2,0},{3,1},{4,6},{5,7},{6,4},{7,5},{8,10},{9,11},{10,... | collective-permute-start | bytes 1376264 | tf_op jit(solution)/shard_map/ppermute | solution.py:334
  129.0 20.6 %all-to-all-start.1 = ((bf16[4,588,256]{2,1,0:T(8,128)(2,1)}), bf16[4,588,256]{2,1,0:T(8,128)(2,1)}, u32[]{:S(2)}, u32[]{:S(2)}) async-start(bf16[4,588,256]{2,1,0:T(8,128)(2,1)} %shard_map.73), calls=%async_computation.1 | async-start | bytes 2424832 | tf_op jit(solution)/shard_map/all_to_all | solution.py:434
  133.3 16.3 %collective-permute-start.12 = (bf16[896,256]{1,0:T(8,128)(2,1)S(1)}, bf16[896,256]{1,0:T(8,128)(2,1)S(1)}, u32[]{:S(2)}, u32[]{:S(2)}) collective-permute-start(bf16[896,256]{1,0:T(8,128)(2,1)S(1)} %maximum_select_fusion.q0_ref), channel_id=1, source_target_pairs={{0,1},{1,0},{2,3},{3,2},{4,5},{5,4},{6,7},{7,6},{8,9},{9,8},{10,11... | collective-permute-start | bytes 1376264 | tf_op jit(solution)/shard_map/ppermute | solution.py:334
  136.3 13.3 %collective-permute-start.14 = (bf16[896,256]{1,0:T(8,128)(2,1)S(1)}, bf16[896,256]{1,0:T(8,128)(2,1)S(1)}, u32[]{:S(2)}, u32[]{:S(2)}) collective-permute-start(bf16[896,256]{1,0:T(8,128)(2,1)S(1)} %collective-permute-done.13.q2_ref), channel_id=1, source_target_pairs={{0,1},{1,0},{2,3},{3,2},{4,5},{5,4},{6,7},{7,6},{8,9},{9,8},{10,11... | collective-permute-start | bytes 1376264 | tf_op jit(solution)/shard_map/ppermute | solution.py:334

commit v4 on v3

--- a/solution.py
+++ b/solution.py
@@ -37,55 +37,86 @@
     return pltpu.CompilerParams(vmem_limit_bytes=VMEM_LIMIT)
 
 
-def face_kernel(face_ref, x_ref, pot_ref, fv_ref, fp_ref):
-    rows = fv_ref.shape[0]
+def thirds(a):
+    one = a.astype(BF16)
+    rest = a - one.astype(F32)
+    two = rest.astype(BF16)
+    return one, two, (rest - two.astype(F32)).astype(BF16)
+
+
+def face_kernel(face_ref, x_ref, pot_ref, out_ref):
+    width = x_ref.shape[1]
+    fp = out_ref.shape[0] - 16
     nodes = x_ref.shape[0]
-    col = to_col(face_ref[...].astype(F32) + 1.0, rows) - 1.0
-    hit = col == iota((rows, nodes), 1)
-    fv_ref[...] = jnp.dot(hit.astype(BF16), x_ref[...], preferred_element_type=F32).astype(BF16)
-    fp_ref[...] = jnp.sum(jnp.where(hit, pot_ref[...], 0.0), axis=1, keepdims=True)
-
-
-def order_kernel(fp, ip, conn_ref, face_ref, h_ref, x_ref, pot_ref, hcan_ref, v_ref, potc_ref, node_ref):
+    col = to_col(face_ref[...].astype(F32) + 1.0, fp) - 1.0
+    hit = jnp.where(col == iota((fp, nodes), 1), 1.0, 0.0).astype(BF16)
+    out_ref[:fp] = mul(hit, x_ref[...]).astype(BF16)
+    ri = lax.broadcasted_iota(jnp.int32, (16, nodes), 0)
+    parts = [p.astype(F32) for p in thirds(pot_ref[...])]
+    rows = jnp.where(ri == 0, parts[0], jnp.where(ri == 1, parts[1], jnp.where(ri == 2, parts[2], 0.0))).astype(BF16)
+    got = lax.dot_general(rows, hit, (((1,), (1,)), ((), ())), preferred_element_type=F32).astype(BF16)
+    if width > fp:
+        got = jnp.concatenate([got, jnp.zeros((16, width - fp), BF16)], axis=1)
+    out_ref[fp:] = got
+
+
+def turn(a, b):
+    return lax.dot_general(a, b, (((1,), (1,)), ((), ())), preferred_element_type=F32)
+
+
+def halves(a):
+    high = jnp.floor(a * (1.0 / 64.0))
+    return high.astype(BF16), (a - 64.0 * high).astype(BF16)
+
+
+def flat(mask):
+    return jnp.where(mask, 1.0, 0.0).astype(BF16)
+
+
+def order(fp, ip, conn_ref, face_ref, h_ref, x_ref, pot_ref, hcan_ref, v_ref, potc_ref, node_ref):
     cells, npc = conn_ref.shape
     nodes = x_ref.shape[0]
     face = face_ref.shape[1]
     stride = fp + ip
     cp = stride + fp
-    c = pl.program_id(0)
-    last = cells - 1
-    row = conn_ref[pl.ds(c, 1), :].astype(F32)
-    row_n = conn_ref[pl.ds(jnp.minimum(c + 1, last), 1), :].astype(F32)
-    row_p = conn_ref[pl.ds(jnp.maximum(c - 1, 0), 1), :].astype(F32)
-    col, col_n, col_p = to_col(row, npc), to_col(row_n, npc), to_col(row_p, npc)
-    less = jnp.where(col < row, 1.0, 0.0).astype(BF16)
-    shared_n = jnp.max(jnp.where(col_n == row, 1.0, 0.0), axis=0, keepdims=True)
-    shared_p = jnp.max(jnp.where(col_p == row, 1.0, 0.0), axis=0, keepdims=True)
-    fcol = to_col(face_ref[...].astype(F32), face)
-    fhit = fcol == row
-    on_face = jnp.max(jnp.where(fhit, 1.0, 0.0), axis=0, keepdims=True)
-    face_slot = jnp.sum(jnp.where(fhit, iota((face, npc), 0), 0.0), axis=0, keepdims=True)
-    first_f = jnp.where(c == 0, 1.0, 0.0)
-    last_f = jnp.where(c == last, 1.0, 0.0)
-    ghost = jnp.where(row >= float(nodes), 1.0, 0.0)
-    top = last_f * ghost + (1.0 - last_f) * shared_n
-    bot = first_f * on_face + (1.0 - first_f) * shared_p
-    mid = 1.0 - top - bot
-    ri = lax.broadcasted_iota(jnp.int32, (8, npc), 0)
-    flags = jnp.where(ri == 0, top, jnp.where(ri == 1, bot, jnp.where(ri == 2, mid, 0.0)))
-    ranks = jnp.dot(flags.astype(BF16), less, preferred_element_type=F32)
-    bot_slot = first_f * face_slot + (1.0 - first_f) * ranks[1:2]
-    slot = jnp.where(top > 0.5, ranks[0:1] + float(stride), jnp.where(bot > 0.5, bot_slot, ranks[2:3] + float(fp)))
-    perm = iota((cp, npc), 0) == slot
-    perm_b = jnp.where(perm, 1.0, 0.0).astype(BF16)
-    half = jnp.dot(perm_b, h_ref[0], preferred_element_type=F32).astype(BF16)
-    hcan_ref[0] = lax.dot_general(half, perm_b, (((1,), (1,)), ((), ())), preferred_element_type=F32).astype(BF16)
-    node = jnp.sum(jnp.where(perm, row + 1.0, 0.0), axis=1, keepdims=True) - 1.0
-    node = node[:stride]
-    node_ref[0] = to_row(node)
-    hit = node == iota((stride, nodes), 1)
-    v_ref[...] = jnp.dot(jnp.where(hit, 1.0, 0.0).astype(BF16), x_ref[...], preferred_element_type=F32).astype(BF16)
-    potc_ref[...] = jnp.sum(jnp.where(hit, pot_ref[...], 0.0), axis=1, keepdims=True)
+    conn = conn_ref[...].astype(F32)
+    eye = flat(iota((npc, npc), 0) == iota((npc, npc), 1))
+    below = flat(iota((npc, npc), 0) < iota((npc, npc), 1))
+    high, low = halves(conn)
+    cols = 64.0 * turn(eye, high) + turn(eye, low)
+    rows = [conn[c : c + 1] for c in range(cells)]
+    ones = jnp.ones((cells, npc), BF16)
+    same = [flat(cols[:, c : c + 1] == rows[c + 1]) for c in range(cells - 1)]
+    ri = lax.broadcasted_iota(jnp.int32, (cells, npc), 0)
+    top = jnp.where(conn >= float(nodes), 1.0, 0.0)
+    for c in range(cells - 1):
+        top = jnp.where(ri == c, turn(ones, same[c]), top)
+    rank_top = mul(top.astype(BF16), below)
+    rank_b = rank_top.astype(BF16)
+    top_slot = jnp.where(ri == cells - 1, conn - float(nodes), rank_top)
+    fhit = to_col(face_ref[...].astype(F32), face) == rows[0]
+    bot = jnp.where(ri == 0, jnp.max(jnp.where(fhit, 1.0, 0.0), axis=0, keepdims=True), 0.0)
+    bot_slot = jnp.where(ri == 0, jnp.sum(jnp.where(fhit, iota((face, npc), 0), 0.0), axis=0, keepdims=True), 0.0)
+    for c in range(cells - 1):
+        both = jnp.concatenate([ones, rank_b], axis=0)
+        got = mul(both, same[c])
+        bot = jnp.where(ri == c + 1, got[:1], bot)
+        bot_slot = jnp.where(ri == c + 1, got[cells + c : cells + c + 1], bot_slot)
+    mid_rank = mul((1.0 - top - bot).astype(BF16), below)
+    slot = jnp.where(top > 0.5, top_slot + float(stride), jnp.where(bot > 0.5, bot_slot, mid_rank + float(fp)))
+    high, low = halves(conn + 1.0)
+    number = iota((8, nodes), 1)[:1]
+    for c in range(cells):
+        perm = flat(iota((cp, npc), 0) == slot[c : c + 1])
+        half = mul(perm, h_ref[c]).astype(BF16)
+        hcan_ref[c] = turn(half, perm).astype(BF16)
+        lead = perm[:stride]
+        node = 64.0 * turn(lead, high)[:, c : c + 1] + turn(lead, low)[:, c : c + 1] - 1.0
+        node_ref[c] = 64.0 * turn(high, lead)[c : c + 1] + turn(low, lead)[c : c + 1] - 1.0
+        at = slice(c * stride, (c + 1) * stride)
+        hit = node == number
+        v_ref[at] = mul(flat(hit), x_ref[...]).astype(BF16)
+        potc_ref[at] = jnp.sum(jnp.where(hit, pot_ref[...], 0.0), axis=1, keepdims=True)
 
 
 def advance(image, now, before):
@@ -177,13 +208,17 @@
     return out
 
 
-def free_kernel(fp, v_ref, ghost_ref, h_ref, pot_ref, first_ref, own_ref, up_ref, down_ref, a_ref, b_ref):
+def free_kernel(
+    fp, ip, conn_ref, face_ref, hraw_ref, raw_ref, potraw_ref, ghost_ref,
+    h_ref, v_ref, pot_ref, node_ref, first_ref, own_ref, up_ref, down_ref, a_ref, b_ref,
+):
+    order(fp, ip, conn_ref, face_ref, hraw_ref, raw_ref, potraw_ref, h_ref, v_ref, pot_ref, node_ref)
     cells, cp = h_ref.shape[:2]
     stride = cp - fp
     total = cells * stride
     width = v_ref.shape[1]
     a_ref[:total] = v_ref[...]
-    a_ref[total:] = ghost_ref[...]
+    a_ref[total:] = ghost_ref[:fp]
     b_ref[total:] = jnp.zeros((fp, width), BF16)
 
     def keep(k, low, high):
@@ -229,16 +264,20 @@
             own_ref[side, DEGREE + 1 + block + own_ref_at, :, lane : lane + fp] = m
 
 
-def forced_kernel(fp, dead_ref, v_ref, ghost_ref, first_ref, own_ref, fromleft_ref, fromright_ref, h_ref, pot_ref, potg_ref, x_ref, image_ref, w_ref, a_ref, b_ref, c_ref):
+def forced_kernel(
+    fp, place_ref, v_ref, ghost_ref, first_ref, own_ref, fromleft_ref, fromright_ref, h_ref, pot_ref,
+    x_ref, image_ref, w_ref, slab_ref, a_ref, b_ref, c_ref,
+):
     cells, cp = h_ref.shape[:2]
     stride = cp - fp
     total = cells * stride
     width = v_ref.shape[1]
     half = cells // 2
+    potg = to_col(jnp.sum(ghost_ref[fp:].astype(F32), axis=0, keepdims=True)[:, :fp], fp)
     histories = []
     last_image = None
     for side, (got_ref, pot, start) in enumerate(
-        ((fromleft_ref, pot_ref[:fp], v_ref[:fp]), (fromright_ref, potg_ref[...], ghost_ref[...]))
+        ((fromleft_ref, pot_ref[:fp], v_ref[:fp]), (fromright_ref, potg, ghost_ref[:fp]))
     ):
         mats = load_matrices(got_ref, DEGREE + 1, DEGREE, fp, width)
         for j in range(DEGREE):
@@ -257,7 +296,7 @@
                 break
             value = advance(h, now, None if k == 0 else values[k - 1].astype(F32))
             if side == 1:
-                value = jnp.where(dead_ref[0] == 1, 0.0, value)
+                value = jnp.where(place_ref[0] == 1, 0.0, value)
             values.append(value.astype(BF16))
         histories.append(values)
     low, high = histories
@@ -298,12 +337,22 @@
             w_ref[1, half * stride :] = end.astype(BF16)
     x_ref[total:] = high[DEGREE]
 
-
-def back_kernel(node_ref, y_ref, out_ref):
+    @pl.when(place_ref[1] == 0)
+    def _():
+        slab_ref[...] = x_ref[half * stride :]
+
+    @pl.when(place_ref[1] == 1)
+    def _():
+        slab_ref[...] = x_ref[: half * stride + fp]
+
+
+def back_kernel(node_ref, x_ref, image_ref, out_ref):
     rows = out_ref.shape[1]
+    width = x_ref.shape[1]
     want = (lax.broadcasted_iota(jnp.int32, (rows, 1), 0) + pl.program_id(0) * rows).astype(F32)
-    hit = jnp.where(want == node_ref[...], 1.0, 0.0).astype(BF16)
-    out_ref[0] = mul(hit, y_ref[...]).astype(BF16)
+    hit = flat(want == node_ref[...])
+    out_ref[0, :, :width] = mul(hit, x_ref[...]).astype(BF16)
+    out_ref[0, :, width:] = mul(hit, image_ref[...]).astype(BF16)
 
 
 def gram_kernel(scale, x_ref, y_ref, out_ref, rows_ref):
@@ -371,8 +420,9 @@
     out_ref[pl.ds(other, width)] = tmul(other_ref[side], far) * scale
 
 
-def paired_residual_kernel(place_ref, q0_ref, q1_ref, q2_ref, q3_ref, x_ref, y_ref, out_ref, p_ref, q_ref):
-    parts, _, width = x_ref.shape
+def paired_residual_kernel(place_ref, q0_ref, q1_ref, q2_ref, q3_ref, both_ref, out_ref, p_ref, q_ref):
+    parts, _, width = both_ref.shape
+    width = width // 2
     half = width // 2
     for k, ref in enumerate((q0_ref, q1_ref, q2_ref, q3_ref)):
         q_ref[k] = ref[...]
@@ -404,22 +454,22 @@
             block = (one.astype(F32) + turned(two)).astype(BF16)
             put(i, j, block)
             put(j, i, turned(block).astype(BF16))
-    x = jnp.concatenate([x_ref[j] for j in range(parts)], axis=1)
+    x = jnp.concatenate([both_ref[j, :, :width] for j in range(parts)], axis=1)
     for j in range(parts):
         at = slice(j * width, (j + 1) * width)
-        out_ref[:, at] = y_ref[j].astype(F32) - mul(x, p_ref[:, at])
-
-
-def paired_tail(x_own, w_own, x_cols, i_cols, o, d, dom, nodes):
+        out_ref[:, at] = both_ref[j, :, width:].astype(F32) - mul(x, p_ref[:, at])
+
+
+def paired_tail(x_own, w_own, give, cut, o, d, dom, nodes):
     slab, width = w_own.shape[1:]
-    orb, rows = x_cols.shape[:2]
+    orb, rows = cut.shape[:2]
     side, core = o // 2, o % 2
     scale = 1.0 / (nodes * dom)
     sds = jax.ShapeDtypeStruct
     smem = pl.BlockSpec(memory_space=pltpu.SMEM)
     vmem = pl.BlockSpec(memory_space=pltpu.VMEM)
-    start = (1 - side) * (x_own.shape[0] - slab)
-    far = swap(lax.dynamic_slice_in_dim(x_own, start, slab, 0), "orb", 2)
+    far = swap(give, "orb", 2)
+    cut, w_own = lax.optimization_barrier((cut, w_own))
     w_other = swap(w_own, "orb", 1)
     near_rows = width + width // 2
     near = pl.pallas_call(
@@ -429,9 +479,6 @@
         compiler_params=params(),
         cost_estimate=pl.CostEstimate(flops=12 * slab * width * width, bytes_accessed=4 << 20, transcendentals=0),
     )(core.reshape(1), x_own, w_own, w_other)
-    x_cols, i_cols, far = lax.optimization_barrier((x_cols, i_cols, far))
-    x_rows = lax.all_to_all(x_cols, "orb", split_axis=0, concat_axis=0, tiled=True)
-    i_rows = lax.all_to_all(i_cols, "orb", split_axis=0, concat_axis=0, tiled=True)
     share = pl.pallas_call(
         functools.partial(far_gram_kernel, scale),
         in_specs=[smem] + [vmem] * 4,
@@ -447,7 +494,11 @@
         share = share.reshape(2, share.shape[0] // 2, width)
         keep = lax.dynamic_index_in_dim(share, mine, 0, keepdims=False)
         give = lax.dynamic_index_in_dim(share, 1 - mine, 0, keepdims=False)
-        share = keep + swap(give.astype(BF16), "dom", bit).astype(F32)
+        give = give.astype(BF16)
+        if bit == 1:
+            cut, give = lax.optimization_barrier((cut, give))
+            both = lax.all_to_all(cut, "orb", split_axis=0, concat_axis=0, tiled=True)
+        share = keep + swap(give, "dom", bit).astype(F32)
         bits.append((bit, mine))
         bit *= 2
     share = share.astype(BF16)
@@ -460,11 +511,11 @@
     cols = orb * width
     return pl.pallas_call(
         paired_residual_kernel,
-        in_specs=[smem] + [vmem] * 6,
+        in_specs=[smem] + [vmem] * 5,
         out_shape=(sds((rows, cols), F32), sds((cols, cols), BF16)),
         scratch_shapes=[pltpu.VMEM((orb,) + share.shape, BF16)],
         compiler_params=params(),
-    )(o.reshape(1), share, q1, q2, q3, x_rows, i_rows)
+    )(o.reshape(1), share, q1, q2, q3, both)
 
 
 def body(orbitals, potential, cell_hamiltonian, connectivity, face_nodes):
@@ -483,41 +534,10 @@
     pot_row = potential.reshape(1, nodes)
     face_row = face_nodes.reshape(1, face)
 
-    fv, fpot = pl.pallas_call(
-        face_kernel,
-        out_shape=(sds((fp, width), BF16), sds((fp, 1), F32)),
-        compiler_params=params(),
+    face_values = pl.pallas_call(
+        face_kernel, out_shape=sds((fp + 16, width), BF16), compiler_params=params()
     )(face_row, orbitals, pot_row)
-    ghost = shift(fv, "dom", -1)
-    ghost_pot = shift(fpot, "dom", -1)
-
-    hcan, y, pot, node = pl.pallas_call(
-        functools.partial(order_kernel, fp, ip),
-        grid=(cells,),
-        in_specs=[
-            full((cells, npc)),
-            full((1, face)),
-            pl.BlockSpec((1, npc, npc), lambda c: (c, 0, 0)),
-            full((nodes, width)),
-            full((1, nodes)),
-        ],
-        out_specs=[
-            pl.BlockSpec((1, cp, cp), lambda c: (c, 0, 0)),
-            pl.BlockSpec((stride, width), lambda c: (c, 0)),
-            pl.BlockSpec((stride, 1), lambda c: (c, 0)),
-            pl.BlockSpec((1, 1, stride), lambda c: (c, 0, 0)),
-        ],
-        out_shape=[
-            sds((cells, cp, cp), BF16),
-            sds((total, width), BF16),
-            sds((total, 1), F32),
-            sds((cells, 1, stride), F32),
-        ],
-        compiler_params=params(),
-        cost_estimate=pl.CostEstimate(flops=4 * total * nodes * width, bytes_accessed=8 << 20, transcendentals=0),
-    )(connectivity, face_row, cell_hamiltonian, orbitals, pot_row)
-    node_row = node.reshape(1, total)
-    dead = (d == dom - 1).astype(jnp.int32).reshape(1)
+    ghost = shift(face_values, "dom", -1)
 
     extra = -(-DEGREE * fp // width)
     sent = DEGREE + 1 + -(-2 * DEGREE * fp // width)
@@ -525,9 +545,13 @@
     cost = pl.CostEstimate(
         flops=2 * DEGREE * cells * cp * cp * width, bytes_accessed=8 << 20, transcendentals=0
     )
-    first, own, up, down = pl.pallas_call(
-        functools.partial(free_kernel, fp),
+    hcan, y, pot, node, first, own, up, down = pl.pallas_call(
+        functools.partial(free_kernel, fp, ip),
         out_shape=[
+            sds((cells, cp, cp), BF16),
+            sds((total, width), BF16),
+            sds((total, 1), F32),
+            sds((cells, 1, stride), F32),
             sds((total, width), BF16),
             sds((2, DEGREE + 1 + extra, fp, width), F32),
             sds((sent, fp, width), BF16),
@@ -536,34 +560,40 @@
         scratch_shapes=[ext, ext],
         compiler_params=params(),
         cost_estimate=cost,
-    )(y, ghost, hcan, pot)
+    )(connectivity, face_row, cell_hamiltonian, orbitals, pot_row, ghost)
+    node_row = node.reshape(1, total)
     from_left = shift(up, "dom", 1)
     from_right = shift(down, "dom", -1)
     vmem = pl.BlockSpec(memory_space=pltpu.VMEM)
     slab = cells // 2 * stride + fp
-    x_own, image, w_own = pl.pallas_call(
+    place = jnp.stack([(d == dom - 1).astype(jnp.int32), (o // 2) % 2])
+    x_own, image, w_own, give = pl.pallas_call(
         functools.partial(forced_kernel, fp),
-        in_specs=[pl.BlockSpec(memory_space=pltpu.SMEM)] + [vmem] * 9,
-        out_shape=[sds((total + fp, width), BF16), sds((total, width), BF16), sds((2, slab, width), BF16)],
+        in_specs=[pl.BlockSpec(memory_space=pltpu.SMEM)] + [vmem] * 8,
+        out_shape=[
+            sds((total + fp, width), BF16),
+            sds((total, width), BF16),
+            sds((2, slab, width), BF16),
+            sds((slab, width), BF16),
+        ],
         scratch_shapes=[ext, ext, ext],
         compiler_params=params(),
         cost_estimate=cost,
-    )(dead, y, ghost, first, own, from_left, from_right, hcan, pot, ghost_pot)
-
-    back = pl.pallas_call(
+    )(place, y, ghost, first, own, from_left, from_right, hcan, pot)
+
+    cut = pl.pallas_call(
         back_kernel,
         grid=(orb,),
-        in_specs=[full((1, total)), full((total, width))],
-        out_specs=pl.BlockSpec((1, nodes // orb, width), lambda i: (i, 0, 0)),
-        out_shape=sds((orb, nodes // orb, width), BF16),
+        in_specs=[full((1, total)), full((total, width)), full((total, width))],
+        out_specs=pl.BlockSpec((1, nodes // orb, 2 * width), lambda i: (i, 0, 0)),
+        out_shape=sds((orb, nodes // orb, 2 * width), BF16),
         compiler_params=params(),
-        cost_estimate=pl.CostEstimate(flops=2 * total * nodes * width, bytes_accessed=4 << 20, transcendentals=0),
-    )
-    x_cols, i_cols = back(node_row, x_own), back(node_row, image)
+        cost_estimate=pl.CostEstimate(flops=4 * total * nodes * width, bytes_accessed=4 << 20, transcendentals=0),
+    )(node_row, x_own, image)
     if orb == 4 and dom % 8 == 0:
-        return paired_tail(x_own, w_own, x_cols, i_cols, o, d, dom, nodes)
-    x_rows = lax.all_to_all(x_cols, "orb", split_axis=0, concat_axis=0, tiled=True)
-    i_rows = lax.all_to_all(i_cols, "orb", split_axis=0, concat_axis=0, tiled=True)
+        return paired_tail(x_own, w_own, give, cut, o, d, dom, nodes)
+    both = lax.all_to_all(cut, "orb", split_axis=0, concat_axis=0, tiled=True)
+    x_rows, i_rows = both[:, :, :width], both[:, :, width:]
 
     rows = nodes // orb
     cols = orb * width

time: 156 us -> 152 us (0.974)
  waiting for transfers between devices: 53.9 us -> 68.2 us
  Pallas kernels: 55.6 us -> 47.3 us
  starting transfers between devices: 33.4 us -> 26.3 us
  local copies, waits for them, and re-layouts: 10.8 us -> 8.42 us
    ppermute x11, waiting for transfers between devices: 32.8 us -> 59.2 us  [swap(): lax.ppermute(block, axis, [(i, i ^ bit) for i in range(lax.axis_size(axis...]
    all_to_all x2 -> x1, waiting for transfers between devices: 13.3 us -> 0.01 us  [paired_tail(): both = lax.all_to_all(cut, 'orb', split_axis=0, concat_axis=0, tiled=True)]
    pallas_call x6 -> x4, Pallas kernels: 42.7 us -> 33.2 us  [the longest x1 19.3 us: body(): pl.pallas_call(functools.partial(free_kernel, fp, ip), out_shape=[sds((ce...]
    all_to_all x2 -> x1, starting transfers between devices: 7.81 us -> 4.52 us  [paired_tail(): both = lax.all_to_all(cut, 'orb', split_axis=0, concat_axis=0, tiled=True)]
    ppermute x4 -> x3, starting transfers between devices: 9.69 us -> 7.41 us  [shift(): lax.ppermute(block, axis, [(i, i + distance) for i in range(n) if 0 <= i...]
    ppermute x4 -> x3, waiting for transfers between devices: 7.77 us -> 9 us  [shift(): lax.ppermute(block, axis, [(i, i + distance) for i in range(n) if 0 <= i...]
    unnamed x23 -> x15, local copies, waits for them, and re-layouts: 8.67 us -> 7.55 us
  transfers between devices with their start and end apart: 17 -> 15, of which waited for: 9 -> 12; matrix products, arithmetic and copies ran while one was open for 3% -> 3% of each run, Pallas kernels for 18% -> 2%
where the time goes in v4:
time: 152 us
  waiting for transfers between devices  68.2 us (45%)
  Pallas kernels  47.3 us (31%)
  starting transfers between devices  26.3 us (17%)
  local copies, waits for them, and re-layouts  8.42 us (6%)
    ppermute x11, waiting for transfers between devices, swap(): lax.ppermute(block, axis, [(i, i ^ bit) for i in range(lax.axis_size(axis...  59.2 us
    pallas_call x1, Pallas kernels, body(): pl.pallas_call(functools.partial(free_kernel, fp, ip), out_shape=[sds((ce...  19.3 us
    ppermute x11, starting transfers between devices, swap(): lax.ppermute(block, axis, [(i, i ^ bit) for i in range(lax.axis_size(axis...  14.4 us
    pallas_call x1, Pallas kernels, body(): pl.pallas_call(functools.partial(forced_kernel, fp), in_specs=[pl.BlockSp...  9.67 us
    ppermute x3, waiting for transfers between devices, shift(): lax.ppermute(block, axis, [(i, i + distance) for i in range(n) if 0 <= i...  9 us
    pallas_call x1, Pallas kernels, body(): pl.pallas_call(back_kernel, grid=(orb,), in_specs=[full((1, total)), full...  7.81 us
    unnamed x15, local copies, waits for them, and re-layouts  7.55 us
    ppermute x3, starting transfers between devices, shift(): lax.ppermute(block, axis, [(i, i + distance) for i in range(n) if 0 <= i...  7.41 us
  transfers between devices with their start and end apart: 15, of which 12 were waited for; matrix products, arithmetic and copies ran while one was open for 3% of the time, Pallas kernels for 2%

profile of v4, /device:TPU:0, one launch (start us, length us, event | category | flops | bytes accessed | tf_op | source)
XLA Modules:
  0.0 151.7 jit_solution(17821078340768183938)
XLA Ops:
  0.6 0.7 reshape.31.pot_ref.potraw_ref
  1.3 0.0 copy-start.3
  1.3 1.3 copy-done.3
  2.6 0.0 copy-start.4
  2.6 0.7 copy-done.4
  3.3 0.5 shard_map.68
  3.8 0.0 copy-start.5
  3.8 1.3 collective-permute-start
  5.1 3.2 %copy.7.hraw_ref = bf16[8,343,343]{2,1,0:T(8,128)(2,1)} copy(bf16[8,343,343]{2,0,1:T(8,128)(2,1)} %param.7) | data formatting | bytes 3764768 | tf_op args[2]
  8.3 2.3 %collective-permute-done.ghost_ref = bf16[80,256]{1,0:T(8,128)(2,1)S(1)} collective-permute-done((bf16[80,256]{1,0:T(8,128)(2,1)S(1)}, bf16[80,256]{1,0:T(8,128)(2,1)S(1)}, u32[]{:S(2)}, u32[]{:S(2)}) %collective-permute-start) | collective-permute-done | bytes 40992 | tf_op jit(solution)/shard_map/ppermute | solution.py:388
  10.6 0.0 copy-done.5
  10.6 19.3 %shard_map.69 = (bf16[8,384,384]{2,1,0:T(8,128)(2,1)}, bf16[2560,256]{1,0:T(8,128)(2,1)S(1)}, f32[2560,1]{1,0:T(8,128)}, f32[8,1,320]{2,1,0:T(1,128)S(1)}, bf16[...) custom-call(s32[8,343]{1,0:T(8,128)S(1)} %copy-done.5, ...), custom_call_target="tpu_custom_call" | custom-call | flops 2415919104 | bytes 8388608 | tf_op jit(solution)/shard_map/pallas_call | solution.py:548
  30.0 0.0 copy-start.6
  30.0 1.1 copy-done.6
  31.1 4.8 %collective-permute-start.1 = (bf16[7,64,256]{2,1,0:T(8,128)(2,1)S(1)}, bf16[7,64,256]{2,1,0:T(8,128)(2,1)S(1)}, u32[]{:S(2)}, u32[]{:S(2)}) collective-permute-start(bf16[7,64,256]{2,1,0:T(8,128)(2,1)S(1)} %get-tuple-element.22), channel_id=1, source_target_pairs={{0,4},{4,8},{8,12},{12,16},{16,20},{20,24},{24,28},{1,5},{5,9},{9,... | collective-permute-start | bytes 688136 | tf_op jit(solution)/shard_map/ppermute | solution.py:388
  35.9 1.3 collective-permute-start.2
  37.2 0.1 pad_add_fusion.1.place_ref
  37.3 0.1 reshape.32.node_ref
  37.4 2.2 %collective-permute-done.1.fromleft_ref = bf16[7,64,256]{2,1,0:T(8,128)(2,1)S(1)} collective-permute-done((bf16[7,64,256]{2,1,0:T(8,128)(2,1)S(1)}, bf16[7,64,256]{2,1,0:T(8,128)(2,1)S(1)}, u32[]{:S(2)}, u32[]{:S(2)}) %collective-permute-start.1) | collective-permute-done | bytes 229408 | tf_op jit(solution)/shard_map/ppermute | solution.py:388
  39.6 4.5 %collective-permute-done.2.fromright_ref = bf16[7,64,256]{2,1,0:T(8,128)(2,1)S(1)} collective-permute-done((bf16[7,64,256]{2,1,0:T(8,128)(2,1)S(1)}, bf16[7,64,256]{2,1,0:T(8,128)(2,1)S(1)}, u32[]{:S(2)}, u32[]{:S(2)}) %collective-permute-start.2) | collective-permute-done | bytes 229408 | tf_op jit(solution)/shard_map/ppermute | solution.py:388
  44.1 9.7 %shard_map.70 = (bf16[2624,256]{1,0:T(8,128)(2,1)}, bf16[2560,256]{1,0:T(8,128)(2,1)S(1)}, bf16[2,1344,256]{2,1,0:T(8,128)(2,1)}, bf16[1344,256]{1,0:T(8,128)(2,1)}) custom-call(s32[2]{0:T(128)S(1)} %pad_add_fusion.1.place_ref, bf16[2560,256]{1,0:T(8,128)(2,1)} %copy-done.6, bf16[80,256]{1,0:T(8,128)(2,1)S(1)} %collective-permute-done.ghost_ref, ...), custom_call_target="tpu_custom_call" | custom-call | flops 2415919104 | bytes 8388608 | tf_op jit(solution)/shard_map/pallas_call | solution.py:570
  53.8 0.0 copy-start.1
  53.8 1.3 copy-done.1
  55.1 0.0 copy-start
  55.1 0.0 copy-start.2
  55.1 7.8 %shard_map.71 = bf16[4,588,512]{2,1,0:T(8,128)(2,1)} custom-call(f32[1,2560]{1,0:T(1,128)S(1)} %reshape.32.node_ref, bf16[2624,256]{1,0:T(8,128)(2,1)S(1)} %copy-done.1, bf16[2560,256]{1,0:T(8,128)(2,1)S(1)} %get-tuple-element.27.image_ref), custom_call_target="tpu_custom_call" | custom-call | flops 6165626880 | bytes 4194304 | tf_op jit(solution)/shard_map/pallas_call | solution.py:584
  62.9 0.0 copy-done
  62.9 0.0 collective-permute-start.3
  62.9 1.5 %collective-permute-start.4 = (bf16[1344,256]{1,0:T(8,128)(2,1)}, bf16[1344,256]{1,0:T(8,128)(2,1)S(1)}, u32[]{:S(2)}, u32[]{:S(2)}) collective-permute-start(bf16[1344,256]{1,0:T(8,128)(2,1)} %get-tuple-element.30), channel_id=1, source_target_pairs={{0,2},{1,3},{2,0},{3,1},{4,6},{5,7},{6,4},{7,5},{8,10},{9,11},{10,... | collective-permute-start | bytes 2064392 | tf_op jit(solution)/shard_map/ppermute | solution.py:383
  64.4 0.1 pad_add_fusion.place_ref
  64.5 1.7 %collective-permute-done.3.other_ref = bf16[2,1344,256]{2,1,0:T(8,128)(2,1)} collective-permute-done((bf16[2,1344,256]{2,1,0:T(8,128)(2,1)S(1)}, bf16[2,1344,256]{2,1,0:T(8,128)(2,1)}, u32[]{:S(2)}, u32[]{:S(2)}) %collective-permute-start.3) | collective-permute-done | bytes 1376288 | tf_op jit(solution)/shard_map/ppermute | solution.py:383
  66.2 0.0 copy-done.2
  66.2 2.5 %shard_map.72.near_ref = f32[384,256]{1,0:T(8,128)S(1)} custom-call(s32[1]{0:T(128)} %bitcast.2.core_ref, bf16[2624,256]{1,0:T(8,128)(2,1)S(1)} %copy-done.2, bf16[2,1344,256]{2,1,0:T(8,128)(2,1)S(1)} %copy-done, bf16[2,1344,256]{2,1,0:T(8,128)(2,1)} %collective-permute-done.3.other_ref), custom_call_target="tpu_custom_call" | custom-call | flops 1056964608 | bytes 4194304 | tf_op jit(solution)/shard_map/pallas_call | solution.py:475
  68.7 12.3 %collective-permute-done.4.far_ref = bf16[1344,256]{1,0:T(8,128)(2,1)S(1)} collective-permute-done((bf16[1344,256]{1,0:T(8,128)(2,1)}, bf16[1344,256]{1,0:T(8,128)(2,1)S(1)}, u32[]{:S(2)}, u32[]{:S(2)}) %collective-permute-start.4) | collective-permute-done | bytes 688160 | tf_op jit(solution)/shard_map/ppermute | solution.py:383
  81.0 2.0 %shard_map.73 = f32[896,256]{1,0:T(8,128)S(1)} custom-call(s32[2]{0:T(128)S(1)} %pad_add_fusion.place_ref, bf16[2,1344,256]{2,1,0:T(8,128)(2,1)S(1)} %copy-done, bf16[2,1344,256]{2,1,0:T(8,128)(2,1)} %collective-permute-done.3.other_ref, bf16[1344,256]{1,0:T(8,128)(2,1)S(1)} %collective-permute-done.4.far_ref, f32[384,256]{1,0:T(8,128)S(1)} %shard_map.72.near_ref), custom_call_target="tpu_custom_call" | custom-call | flops 704643072 | bytes 4194304 | tf_op jit(solution)/shard_map/pallas_call | solution.py:482
  83.0 2.9 %collective-permute-start.5 = (bf16[448,256]{1,0:T(8,128)(2,1)S(1)}, bf16[448,256]{1,0:T(8,128)(2,1)S(1)}, u32[]{:S(2)}, u32[]{:S(2)}) collective-permute-start(bf16[448,256]{1,0:T(8,128)(2,1)S(1)} %fusion), channel_id=1, source_target_pairs={{0,4},{4,0},{8,12},{12,8},{16,20},{20,16},{24,28},{28,24},{1,5},{5... | collective-permute-start | bytes 688136 | tf_op jit(solution)/shard_map/ppermute | solution.py:383
  85.9 5.5 %collective-permute-done.5 = bf16[448,256]{1,0:T(8,128)(2,1)S(1)} collective-permute-done((bf16[448,256]{1,0:T(8,128)(2,1)S(1)}, bf16[448,256]{1,0:T(8,128)(2,1)S(1)}, u32[]{:S(2)}, u32[]{:S(2)}) %collective-permute-start.5) | collective-permute-done | bytes 229408 | tf_op jit(solution)/shard_map/ppermute | solution.py:383
  91.5 3.4 %collective-permute-start.6 = (bf16[224,256]{1,0:T(8,128)(2,1)S(1)}, bf16[224,256]{1,0:T(8,128)(2,1)S(1)}, u32[]{:S(2)}, u32[]{:S(2)}) collective-permute-start(bf16[224,256]{1,0:T(8,128)(2,1)S(1)} %fusion.1), channel_id=1, source_target_pairs={{0,8},{4,12},{8,0},{12,4},{16,24},{20,28},{24,16},{28,20},{1,9},{5... | collective-permute-start | bytes 344072 | tf_op jit(solution)/shard_map/ppermute | solution.py:383
  94.9 2.8 %collective-permute-done.6 = bf16[224,256]{1,0:T(8,128)(2,1)S(1)} collective-permute-done((bf16[224,256]{1,0:T(8,128)(2,1)S(1)}, bf16[224,256]{1,0:T(8,128)(2,1)S(1)}, u32[]{:S(2)}, u32[]{:S(2)}) %collective-permute-start.6) | collective-permute-done | bytes 114720 | tf_op jit(solution)/shard_map/ppermute | solution.py:383
  97.7 3.1 %collective-permute-start.7 = (bf16[112,256]{1,0:T(8,128)(2,1)S(1)}, bf16[112,256]{1,0:T(8,128)(2,1)S(1)}, u32[]{:S(2)}, u32[]{:S(2)}) collective-permute-start(bf16[112,256]{1,0:T(8,128)(2,1)S(1)} %fusion.3), channel_id=1, source_target_pairs={{0,16},{4,20},{8,24},{12,28},{16,0},{20,4},{24,8},{28,12},{1,17},{... | collective-permute-start | bytes 172040 | tf_op jit(solution)/shard_map/ppermute | solution.py:383
  100.8 4.5 %all-to-all-start = ((bf16[4,588,512]{2,1,0:T(8,128)(2,1)}), bf16[4,588,512]{2,1,0:T(8,128)(2,1)}, u32[]{:S(2)}, u32[]{:S(2)}) async-start(bf16[4,588,512]{2,1,0:T(8,128)(2,1)} %shard_map.71), calls=%async_computation | async-start | bytes 4849664 | tf_op jit(solution)/shard_map/all_to_all | solution.py:500
  105.3 0.0 collective-permute-done.7
  105.4 0.6 collective-permute-start.8
  106.0 5.8 %collective-permute-done.8 = bf16[112,256]{1,0:T(8,128)(2,1)S(1)} collective-permute-done((bf16[112,256]{1,0:T(8,128)(2,1)S(1)}, bf16[112,256]{1,0:T(8,128)(2,1)S(1)}, u32[]{:S(2)}, u32[]{:S(2)}) %collective-permute-start.8) | collective-permute-done | bytes 57376 | tf_op jit(solution)/shard_map/ppermute | solution.py:383
  111.9 0.5 collective-permute-start.9
  112.4 4.3 %collective-permute-done.9 = bf16[224,256]{1,0:T(8,128)(2,1)S(1)} collective-permute-done((bf16[224,256]{1,0:T(8,128)(2,1)S(1)}, bf16[224,256]{1,0:T(8,128)(2,1)S(1)}, u32[]{:S(2)}, u32[]{:S(2)}) %collective-permute-start.9) | collective-permute-done | bytes 114720 | tf_op jit(solution)/shard_map/ppermute | solution.py:383
  116.7 0.1 maximum_select_fusion.1
  116.8 0.4 collective-permute-start.10
  117.2 5.7 %collective-permute-done.10 = bf16[448,256]{1,0:T(8,128)(2,1)S(1)} collective-permute-done((bf16[448,256]{1,0:T(8,128)(2,1)S(1)}, bf16[448,256]{1,0:T(8,128)(2,1)S(1)}, u32[]{:S(2)}, u32[]{:S(2)}) %collective-permute-start.10) | collective-permute-done | bytes 229408 | tf_op jit(solution)/shard_map/ppermute | solution.py:383
  122.9 0.2 maximum_select_fusion.q0_ref
  123.1 1.9 %collective-permute-start.12 = (bf16[896,256]{1,0:T(8,128)(2,1)S(1)}, bf16[896,256]{1,0:T(8,128)(2,1)S(1)}, u32[]{:S(2)}, u32[]{:S(2)}) collective-permute-start(bf16[896,256]{1,0:T(8,128)(2,1)S(1)} %maximum_select_fusion.q0_ref), channel_id=1, source_target_pairs={{0,2},{1,3},{2,0},{3,1},{4,6},{5,7},{6,4},{7,5},{8,10},{9,11},{10,... | collective-permute-start | bytes 1376264 | tf_op jit(solution)/shard_map/ppermute | solution.py:383
  125.0 0.0 collective-permute-start.11
  125.0 19.3 %collective-permute-done.12.q2_ref = bf16[896,256]{1,0:T(8,128)(2,1)S(1)} collective-permute-done((bf16[896,256]{1,0:T(8,128)(2,1)S(1)}, bf16[896,256]{1,0:T(8,128)(2,1)S(1)}, u32[]{:S(2)}, u32[]{:S(2)}) %collective-permute-start.12) | collective-permute-done | bytes 458784 | tf_op jit(solution)/shard_map/ppermute | solution.py:383
  144.3 0.0 collective-permute-start.13
  144.3 0.0 collective-permute-done.11.q1_ref
  144.3 1.8 %collective-permute-done.13.q3_ref = bf16[896,256]{1,0:T(8,128)(2,1)S(1)} collective-permute-done((bf16[896,256]{1,0:T(8,128)(2,1)S(1)}, bf16[896,256]{1,0:T(8,128)(2,1)S(1)}, u32[]{:S(2)}, u32[]{:S(2)}) %collective-permute-start.13) | collective-permute-done | bytes 458784 | tf_op jit(solution)/shard_map/ppermute | solution.py:383
  146.1 0.0 all-to-all-done.both_ref
  146.2 5.5 %shard_map.74 = (f32[588,1024]{1,0:T(8,128)}, bf16[1024,1024]{1,0:T(8,128)(2,1)}) custom-call(s32[1]{0:T(128)} %bitcast.place_ref, bf16[896,256]{1,0:T(8,128)(2,1)S(1)} %maximum_select_fusion.q0_ref, bf16[896,256]{1,0:T(8,128)(2,1)S(1)} %collective-permute-done.11.q1_ref, bf16[896,256]{1,0:T(8,128)(2,1)S(1)} %collective-permute-done.12.q2_ref, ...), custom_call_target="tpu_custom_call" | custom-call | tf_op jit(solution)/shard_map/pallas_call | solution.py:512
  (8 shorter events, 0.2 us)
Async XLA Ops:
  1.3 1.3 copy-start.3
  2.6 0.7 copy-start.4
  3.8 6.9 %copy-start.5 = (s32[8,343]{1,0:T(8,128)S(1)}, s32[8,343]{1,0:T(8,128)}, u32[]{:S(2)}) copy-start(s32[8,343]{1,0:T(8,128)} %conn_ref.1) | copy-start | bytes 32932
  3.8 6.8 %collective-permute-start = (bf16[80,256]{1,0:T(8,128)(2,1)S(1)}, bf16[80,256]{1,0:T(8,128)(2,1)S(1)}, u32[]{:S(2)}, u32[]{:S(2)}) collective-permute-start(bf16[80,256]{1,0:T(8,128)(2,1)S(1)} %shard_map.68), channel_id=1, source_target_pairs={{4,0},{8,4},{12,8},{16,12},{20,16},{24,20},{28,24},{5,1},{9,5},{13... | collective-permute-start | bytes 122888 | tf_op jit(solution)/shard_map/ppermute | solution.py:388
  30.0 1.1 copy-start.6
  31.1 8.6 %collective-permute-start.1 = (bf16[7,64,256]{2,1,0:T(8,128)(2,1)S(1)}, bf16[7,64,256]{2,1,0:T(8,128)(2,1)S(1)}, u32[]{:S(2)}, u32[]{:S(2)}) collective-permute-start(bf16[7,64,256]{2,1,0:T(8,128)(2,1)S(1)} %get-tuple-element.22), channel_id=1, source_target_pairs={{0,4},{4,8},{8,12},{12,16},{16,20},{20,24},{24,28},{1,5},{5,9},{9,... | collective-permute-start | bytes 688136 | tf_op jit(solution)/shard_map/ppermute | solution.py:388
  35.9 8.2 %collective-permute-start.2 = (bf16[7,64,256]{2,1,0:T(8,128)(2,1)S(1)}, bf16[7,64,256]{2,1,0:T(8,128)(2,1)S(1)}, u32[]{:S(2)}, u32[]{:S(2)}) collective-permute-start(bf16[7,64,256]{2,1,0:T(8,128)(2,1)S(1)} %get-tuple-element.23), channel_id=1, source_target_pairs={{4,0},{8,4},{12,8},{16,12},{20,16},{24,20},{28,24},{5,1},{9,5},{13... | collective-permute-start | bytes 688136 | tf_op jit(solution)/shard_map/ppermute | solution.py:388
  53.8 1.3 copy-start.1
  55.1 7.8 %copy-start = (bf16[2,1344,256]{2,1,0:T(8,128)(2,1)S(1)}, bf16[2,1344,256]{2,1,0:T(8,128)(2,1)}, u32[]{:S(2)}) copy-start(bf16[2,1344,256]{2,1,0:T(8,128)(2,1)} %get-tuple-element.29.w_ref) | copy-start | bytes 4128772
  55.1 11.1 %copy-start.2 = (bf16[2624,256]{1,0:T(8,128)(2,1)S(1)}, bf16[2624,256]{1,0:T(8,128)(2,1)}, u32[]{:S(2)}) copy-start(bf16[2624,256]{1,0:T(8,128)(2,1)} %get-tuple-element.26.x_ref) | copy-start | bytes 4030468
  62.9 3.3 %collective-permute-start.3 = (bf16[2,1344,256]{2,1,0:T(8,128)(2,1)S(1)}, bf16[2,1344,256]{2,1,0:T(8,128)(2,1)}, u32[]{:S(2)}, u32[]{:S(2)}) collective-permute-start(bf16[2,1344,256]{2,1,0:T(8,128)(2,1)S(1)} %copy-done), channel_id=1, source_target_pairs={{0,1},{1,0},{2,3},{3,2},{4,5},{5,4},{6,7},{7,6},{8,9},{9,8},{10,11... | collective-permute-start | bytes 4128776 | tf_op jit(solution)/shard_map/ppermute | solution.py:383
  62.9 18.1 %collective-permute-start.4 = (bf16[1344,256]{1,0:T(8,128)(2,1)}, bf16[1344,256]{1,0:T(8,128)(2,1)S(1)}, u32[]{:S(2)}, u32[]{:S(2)}) collective-permute-start(bf16[1344,256]{1,0:T(8,128)(2,1)} %get-tuple-element.30), channel_id=1, source_target_pairs={{0,2},{1,3},{2,0},{3,1},{4,6},{5,7},{6,4},{7,5},{8,10},{9,11},{10,... | collective-permute-start | bytes 2064392 | tf_op jit(solution)/shard_map/ppermute | solution.py:383
  83.0 8.4 %collective-permute-start.5 = (bf16[448,256]{1,0:T(8,128)(2,1)S(1)}, bf16[448,256]{1,0:T(8,128)(2,1)S(1)}, u32[]{:S(2)}, u32[]{:S(2)}) collective-permute-start(bf16[448,256]{1,0:T(8,128)(2,1)S(1)} %fusion), channel_id=1, source_target_pairs={{0,4},{4,0},{8,12},{12,8},{16,20},{20,16},{24,28},{28,24},{1,5},{5... | collective-permute-start | bytes 688136 | tf_op jit(solution)/shard_map/ppermute | solution.py:383
  91.5 6.1 %collective-permute-start.6 = (bf16[224,256]{1,0:T(8,128)(2,1)S(1)}, bf16[224,256]{1,0:T(8,128)(2,1)S(1)}, u32[]{:S(2)}, u32[]{:S(2)}) collective-permute-start(bf16[224,256]{1,0:T(8,128)(2,1)S(1)} %fusion.1), channel_id=1, source_target_pairs={{0,8},{4,12},{8,0},{12,4},{16,24},{20,28},{24,16},{28,20},{1,9},{5... | collective-permute-start | bytes 344072 | tf_op jit(solution)/shard_map/ppermute | solution.py:383
  97.7 7.6 %collective-permute-start.7 = (bf16[112,256]{1,0:T(8,128)(2,1)S(1)}, bf16[112,256]{1,0:T(8,128)(2,1)S(1)}, u32[]{:S(2)}, u32[]{:S(2)}) collective-permute-start(bf16[112,256]{1,0:T(8,128)(2,1)S(1)} %fusion.3), channel_id=1, source_target_pairs={{0,16},{4,20},{8,24},{12,28},{16,0},{20,4},{24,8},{28,12},{1,17},{... | collective-permute-start | bytes 172040 | tf_op jit(solution)/shard_map/ppermute | solution.py:383
  100.8 45.3 %all-to-all-start = ((bf16[4,588,512]{2,1,0:T(8,128)(2,1)}), bf16[4,588,512]{2,1,0:T(8,128)(2,1)}, u32[]{:S(2)}, u32[]{:S(2)}) async-start(bf16[4,588,512]{2,1,0:T(8,128)(2,1)} %shard_map.71), calls=%async_computation | async-start | bytes 4849664 | tf_op jit(solution)/shard_map/all_to_all | solution.py:500
  105.4 6.5 %collective-permute-start.8 = (bf16[112,256]{1,0:T(8,128)(2,1)S(1)}, bf16[112,256]{1,0:T(8,128)(2,1)S(1)}, u32[]{:S(2)}, u32[]{:S(2)}) collective-permute-start(bf16[112,256]{1,0:T(8,128)(2,1)S(1)} %fusion.2), channel_id=1, source_target_pairs={{0,16},{4,20},{8,24},{12,28},{16,0},{20,4},{24,8},{28,12},{1,17},{... | collective-permute-start | bytes 172040 | tf_op jit(solution)/shard_map/ppermute | solution.py:383
  111.9 4.9 %collective-permute-start.9 = (bf16[224,256]{1,0:T(8,128)(2,1)S(1)}, bf16[224,256]{1,0:T(8,128)(2,1)S(1)}, u32[]{:S(2)}, u32[]{:S(2)}) collective-permute-start(bf16[224,256]{1,0:T(8,128)(2,1)S(1)} %maximum_select_fusion.2), channel_id=1, source_target_pairs={{0,8},{4,12},{8,0},{12,4},{16,24},{20,28},{24,16},{28,20},{1,9},{5... | collective-permute-start | bytes 344072 | tf_op jit(solution)/shard_map/ppermute | solution.py:383
  116.8 6.1 %collective-permute-start.10 = (bf16[448,256]{1,0:T(8,128)(2,1)S(1)}, bf16[448,256]{1,0:T(8,128)(2,1)S(1)}, u32[]{:S(2)}, u32[]{:S(2)}) collective-permute-start(bf16[448,256]{1,0:T(8,128)(2,1)S(1)} %maximum_select_fusion.1), channel_id=1, source_target_pairs={{0,4},{4,0},{8,12},{12,8},{16,20},{20,16},{24,28},{28,24},{1,5},{5... | collective-permute-start | bytes 688136 | tf_op jit(solution)/shard_map/ppermute | solution.py:383
  123.1 21.2 %collective-permute-start.12 = (bf16[896,256]{1,0:T(8,128)(2,1)S(1)}, bf16[896,256]{1,0:T(8,128)(2,1)S(1)}, u32[]{:S(2)}, u32[]{:S(2)}) collective-permute-start(bf16[896,256]{1,0:T(8,128)(2,1)S(1)} %maximum_select_fusion.q0_ref), channel_id=1, source_target_pairs={{0,2},{1,3},{2,0},{3,1},{4,6},{5,7},{6,4},{7,5},{8,10},{9,11},{10,... | collective-permute-start | bytes 1376264 | tf_op jit(solution)/shard_map/ppermute | solution.py:383
  125.0 19.3 %collective-permute-start.11 = (bf16[896,256]{1,0:T(8,128)(2,1)S(1)}, bf16[896,256]{1,0:T(8,128)(2,1)S(1)}, u32[]{:S(2)}, u32[]{:S(2)}) collective-permute-start(bf16[896,256]{1,0:T(8,128)(2,1)S(1)} %maximum_select_fusion.q0_ref), channel_id=1, source_target_pairs={{0,1},{1,0},{2,3},{3,2},{4,5},{5,4},{6,7},{7,6},{8,9},{9,8},{10,11... | collective-permute-start | bytes 1376264 | tf_op jit(solution)/shard_map/ppermute | solution.py:383
  144.3 1.8 %collective-permute-start.13 = (bf16[896,256]{1,0:T(8,128)(2,1)S(1)}, bf16[896,256]{1,0:T(8,128)(2,1)S(1)}, u32[]{:S(2)}, u32[]{:S(2)}) collective-permute-start(bf16[896,256]{1,0:T(8,128)(2,1)S(1)} %collective-permute-done.12.q2_ref), channel_id=1, source_target_pairs={{0,1},{1,0},{2,3},{3,2},{4,5},{5,4},{6,7},{7,6},{8,9},{9,8},{10,11... | collective-permute-start | bytes 1376264 | tf_op jit(solution)/shard_map/ppermute | solution.py:383

commit v5 on v4

--- a/solution.py
+++ b/solution.py
@@ -355,6 +355,15 @@
     out_ref[0, :, width:] = mul(hit, image_ref[...]).astype(BF16)
 
 
+def back_pair_kernel(at_ref, node_ref, x_ref, image_ref, *out_refs):
+    rows = out_refs[0].shape[0]
+    for i in range(2):
+        want = (lax.broadcasted_iota(jnp.int32, (rows, 1), 0) + at_ref[i] * rows).astype(F32)
+        hit = flat(want == node_ref[...])
+        out_refs[2 * i][...] = mul(hit, x_ref[...]).astype(BF16)
+        out_refs[2 * i + 1][...] = mul(hit, image_ref[...]).astype(BF16)
+
+
 def gram_kernel(scale, x_ref, y_ref, out_ref, rows_ref):
     parts, _, width = y_ref.shape
 
@@ -420,9 +429,10 @@
     out_ref[pl.ds(other, width)] = tmul(other_ref[side], far) * scale
 
 
-def paired_residual_kernel(place_ref, q0_ref, q1_ref, q2_ref, q3_ref, both_ref, out_ref, p_ref, q_ref):
-    parts, _, width = both_ref.shape
-    width = width // 2
+def paired_residual_kernel(place_ref, q0_ref, q1_ref, q2_ref, q3_ref, *refs):
+    parts = 4
+    x_refs, y_refs, (out_ref, p_ref, q_ref) = refs[: 2 * parts : 2], refs[1 : 2 * parts : 2], refs[2 * parts :]
+    width = x_refs[0].shape[1]
     half = width // 2
     for k, ref in enumerate((q0_ref, q1_ref, q2_ref, q3_ref)):
         q_ref[k] = ref[...]
@@ -454,40 +464,60 @@
             block = (one.astype(F32) + turned(two)).astype(BF16)
             put(i, j, block)
             put(j, i, turned(block).astype(BF16))
-    x = jnp.concatenate([both_ref[j, :, :width] for j in range(parts)], axis=1)
-    for j in range(parts):
-        at = slice(j * width, (j + 1) * width)
-        out_ref[:, at] = both_ref[j, :, width:].astype(F32) - mul(x, p_ref[:, at])
-
-
-def paired_tail(x_own, w_own, give, cut, o, d, dom, nodes):
+    x = jnp.concatenate([ref[...] for ref in x_refs], axis=1)
+    spots = [pl.ds(pl.multiple_of(jnp.bitwise_xor(me, k) * width, width), width) for k in range(parts)]
+    for k in range(parts):
+        at = spots[k]
+        p = jnp.concatenate([p_ref[spots[m], at] for m in range(parts)], axis=0)
+        out_ref[:, at] = y_refs[k][...].astype(F32) - mul(x, p)
+
+
+def paired_tail(x_own, image, w_own, give, node_row, o, d, dom, nodes):
     slab, width = w_own.shape[1:]
-    orb, rows = cut.shape[:2]
+    orb = 4
+    rows = nodes // orb
     side, core = o // 2, o % 2
     scale = 1.0 / (nodes * dom)
     sds = jax.ShapeDtypeStruct
     smem = pl.BlockSpec(memory_space=pltpu.SMEM)
     vmem = pl.BlockSpec(memory_space=pltpu.VMEM)
     far = swap(give, "orb", 2)
-    cut, w_own = lax.optimization_barrier((cut, w_own))
+    total = image.shape[0]
+
+    def back(first, second, x_own, image):
+        whole = lambda *shape: pl.BlockSpec(shape, lambda i: (0,) * len(shape))
+        return pl.pallas_call(
+            back_pair_kernel,
+            grid=(1,),
+            in_specs=[smem, whole(1, total), whole(total, width), whole(total, width)],
+            out_specs=[whole(rows, width)] * 4,
+            out_shape=[sds((rows, width), BF16)] * 4,
+            compiler_params=params(),
+            cost_estimate=pl.CostEstimate(flops=1 << 20, bytes_accessed=1 << 10, transcendentals=0),
+        )(jnp.stack([jnp.bitwise_xor(o, first), jnp.bitwise_xor(o, second)]), node_row, x_own, image)
+
+    cuts = back(2, 3, x_own, image)
     w_other = swap(w_own, "orb", 1)
-    near_rows = width + width // 2
+    top = width + width // 2
     near = pl.pallas_call(
         functools.partial(near_gram_kernel, scale),
         in_specs=[smem] + [vmem] * 3,
-        out_shape=sds((near_rows, width), F32),
+        out_shape=sds((top, width), F32),
         compiler_params=params(),
-        cost_estimate=pl.CostEstimate(flops=12 * slab * width * width, bytes_accessed=4 << 20, transcendentals=0),
+        cost_estimate=pl.CostEstimate(flops=1 << 20, bytes_accessed=1 << 10, transcendentals=0),
     )(core.reshape(1), x_own, w_own, w_other)
+    far, near, *cuts = lax.optimization_barrier((far, near, *cuts))
+    rows_far = [swap(cut, "orb", 2 + i // 2) for i, cut in enumerate(cuts)]
     share = pl.pallas_call(
         functools.partial(far_gram_kernel, scale),
         in_specs=[smem] + [vmem] * 4,
-        out_shape=sds((near_rows + 2 * width, width), F32),
+        out_shape=sds((top + 2 * width, width), F32),
         compiler_params=params(),
         cost_estimate=pl.CostEstimate(flops=8 * slab * width * width, bytes_accessed=4 << 20, transcendentals=0),
     )(jnp.stack([side, core]), w_own, w_other, far, near)
 
     bits = []
+    pending, rows_got = list(rows_far), []
     bit = 1
     while bit < dom:
         mine = (d // bit) % 2
@@ -496,26 +526,34 @@
         give = lax.dynamic_index_in_dim(share, 1 - mine, 0, keepdims=False)
         give = give.astype(BF16)
         if bit == 1:
-            cut, give = lax.optimization_barrier((cut, give))
-            both = lax.all_to_all(cut, "orb", split_axis=0, concat_axis=0, tiled=True)
+            x_own, image, give = lax.optimization_barrier((x_own, image, give))
+            near_rows = back(0, 1, x_own, image)
+            rows_near = list(near_rows[:2]) + [swap(cut, "orb", 1) for cut in near_rows[2:]]
         share = keep + swap(give, "dom", bit).astype(F32)
+        if pending:
+            share, got = lax.optimization_barrier((share, pending.pop(0)))
+            rows_got.append(got)
         bits.append((bit, mine))
         bit *= 2
     share = share.astype(BF16)
     for bit, mine in reversed(bits):
         got = swap(share, "dom", bit)
         share = jnp.where(mine == 0, jnp.concatenate([share, got], axis=0), jnp.concatenate([got, share], axis=0))
+        if pending:
+            share, got = lax.optimization_barrier((share, pending.pop(0)))
+            rows_got.append(got)
+    rows_got += pending
     q2 = swap(share, "orb", 2)
     q1 = swap(share, "orb", 1)
     q3 = swap(q2, "orb", 1)
     cols = orb * width
     return pl.pallas_call(
         paired_residual_kernel,
-        in_specs=[smem] + [vmem] * 5,
+        in_specs=[smem] + [vmem] * 12,
         out_shape=(sds((rows, cols), F32), sds((cols, cols), BF16)),
         scratch_shapes=[pltpu.VMEM((orb,) + share.shape, BF16)],
         compiler_params=params(),
-    )(o.reshape(1), share, q1, q2, q3, both)
+    )(o.reshape(1), share, q1, q2, q3, *rows_near, *rows_got)
 
 
 def body(orbitals, potential, cell_hamiltonian, connectivity, face_nodes):
@@ -581,6 +619,8 @@
         cost_estimate=cost,
     )(place, y, ghost, first, own, from_left, from_right, hcan, pot)
 
+    if orb == 4 and dom % 8 == 0:
+        return paired_tail(x_own, image, w_own, give, node_row, o, d, dom, nodes)
     cut = pl.pallas_call(
         back_kernel,
         grid=(orb,),
@@ -590,8 +630,6 @@
         compiler_params=params(),
         cost_estimate=pl.CostEstimate(flops=4 * total * nodes * width, bytes_accessed=4 << 20, transcendentals=0),
     )(node_row, x_own, image)
-    if orb == 4 and dom % 8 == 0:
-        return paired_tail(x_own, w_own, give, cut, o, d, dom, nodes)
     both = lax.all_to_all(cut, "orb", split_axis=0, concat_axis=0, tiled=True)
     x_rows, i_rows = both[:, :, :width], both[:, :, width:]
 

time: 152 us -> 150 us (0.987)
  waiting for transfers between devices: 68.2 us -> 55.5 us
  other arithmetic: 0.57 us -> 6.99 us
  local copies, waits for them, and re-layouts: 8.42 us -> 12.7 us
    ppermute x11 -> x17, waiting for transfers between devices: 59.2 us -> 46.4 us  [swap(): lax.ppermute(block, axis, [(i, i ^ bit) for i in range(lax.axis_size(axis...]
    all_to_all x1 -> x0, starting transfers between devices: 4.52 us -> none  [paired_tail(): both = lax.all_to_all(cut, 'orb', split_axis=0, concat_axis=0, tiled=True)]
    ppermute x11 -> x17, starting transfers between devices: 14.4 us -> 18.5 us  [swap(): lax.ppermute(block, axis, [(i, i ^ bit) for i in range(lax.axis_size(axis...]
    add x2 -> x3, other arithmetic: 0.07 us -> 3.28 us  [paired_tail(): share = keep + swap(give, 'dom', bit).astype(F32)]
    select_n x3, other arithmetic: 0.3 us -> 3.45 us  [paired_tail(): jnp.where(mine == 0, jnp.concatenate([share, got], axis=0), jnp.concatena...]
    unnamed x15 -> x33, local copies, waits for them, and re-layouts: 7.55 us -> 10.2 us
    convert_element_type x3, local copies, waits for them, and re-layouts: 0.07 us -> 1.77 us  [paired_tail(): give = give.astype(BF16)]
    pallas_call x2 -> x3, Pallas kernels: 13.3 us -> 13 us  [the longest x2 7.67 us: back(): pl.pallas_call(back_pair_kernel, grid=(1,), in_specs=[smem, whole(1, tota...]
  transfers between devices with their start and end apart: 15 -> 20, of which waited for: 12 -> 15; matrix products, arithmetic and copies ran while one was open for 3% -> 6% of each run, Pallas kernels for 2% -> 7%
where the time goes in v5:
time: 150 us; the launch traced here: 149 us
  waiting for transfers between devices  55.5 us (37%)
  Pallas kernels  47 us (31%)
  starting transfers between devices  25.9 us (17%)
  local copies, waits for them, and re-layouts  12.7 us (8%)
  other arithmetic  6.99 us (5%)
    ppermute x17, waiting for transfers between devices, swap(): lax.ppermute(block, axis, [(i, i ^ bit) for i in range(lax.axis_size(axis...  46.4 us
    pallas_call x1, Pallas kernels, body(): pl.pallas_call(functools.partial(free_kernel, fp, ip), out_shape=[sds((ce...  19.3 us
    ppermute x17, starting transfers between devices, swap(): lax.ppermute(block, axis, [(i, i ^ bit) for i in range(lax.axis_size(axis...  18.5 us
    unnamed x33, local copies, waits for them, and re-layouts  10.2 us
    pallas_call x1, Pallas kernels, body(): pl.pallas_call(functools.partial(forced_kernel, fp), in_specs=[pl.BlockSp...  9.64 us
    ppermute x3, waiting for transfers between devices, shift(): lax.ppermute(block, axis, [(i, i + distance) for i in range(n) if 0 <= i...  9.12 us
    pallas_call x2, Pallas kernels, back(): pl.pallas_call(back_pair_kernel, grid=(1,), in_specs=[smem, whole(1, tota...  7.67 us
    ppermute x3, starting transfers between devices, shift(): lax.ppermute(block, axis, [(i, i + distance) for i in range(n) if 0 <= i...  7.4 us
  transfers between devices with their start and end apart: 20, of which 15 were waited for; matrix products, arithmetic and copies ran while one was open for 6% of the time, Pallas kernels for 7%

profile of v5, /device:TPU:0, one launch (start us, length us, event | category | flops | bytes accessed | tf_op | source)
XLA Modules:
  0.0 149.1 jit_solution(991634671527089095)
XLA Ops:
  0.6 0.7 reshape.31.pot_ref.potraw_ref
  1.3 1.3 copy-done.3
  2.6 0.7 copy-done.6
  3.3 0.5 shard_map.68
  3.8 0.0 copy-start.10
  3.8 1.3 collective-permute-start
  5.1 3.2 %copy.7.hraw_ref = bf16[8,343,343]{2,1,0:T(8,128)(2,1)} copy(bf16[8,343,343]{2,0,1:T(8,128)(2,1)} %param.7) | data formatting | bytes 3764768 | tf_op args[2]
  8.3 2.3 %collective-permute-done.ghost_ref = bf16[80,256]{1,0:T(8,128)(2,1)S(1)} collective-permute-done((bf16[80,256]{1,0:T(8,128)(2,1)S(1)}, bf16[80,256]{1,0:T(8,128)(2,1)S(1)}, u32[]{:S(2)}, u32[]{:S(2)}) %collective-permute-start) | collective-permute-done | bytes 40992 | tf_op jit(solution)/shard_map/ppermute | solution.py:397
  10.6 19.3 %shard_map.69 = (bf16[8,384,384]{2,1,0:T(8,128)(2,1)}, bf16[2560,256]{1,0:T(8,128)(2,1)S(1)}, f32[2560,1]{1,0:T(8,128)}, f32[8,1,320]{2,1,0:T(1,128)S(1)}, bf16[...) custom-call(s32[8,343]{1,0:T(8,128)S(1)} %copy-done.10, ...), custom_call_target="tpu_custom_call" | custom-call | flops 2415919104 | bytes 8388608 | tf_op jit(solution)/shard_map/pallas_call | solution.py:586
  30.0 1.1 copy-done.11
  31.0 0.9 copy-done.12
  31.9 4.8 %collective-permute-start.1 = (bf16[7,64,256]{2,1,0:T(8,128)(2,1)S(1)}, bf16[7,64,256]{2,1,0:T(8,128)(2,1)S(1)}, u32[]{:S(2)}, u32[]{:S(2)}) collective-permute-start(bf16[7,64,256]{2,1,0:T(8,128)(2,1)S(1)} %get-tuple-element.42), channel_id=1, source_target_pairs={{0,4},{4,8},{8,12},{12,16},{16,20},{20,24},{24,28},{1,5},{5,9},{9,... | collective-permute-start | bytes 688136 | tf_op jit(solution)/shard_map/ppermute | solution.py:397
  36.7 1.3 collective-permute-start.2
  38.1 0.1 pad_add_fusion.1
  38.2 2.3 %collective-permute-done.1.fromleft_ref = bf16[7,64,256]{2,1,0:T(8,128)(2,1)S(1)} collective-permute-done((bf16[7,64,256]{2,1,0:T(8,128)(2,1)S(1)}, bf16[7,64,256]{2,1,0:T(8,128)(2,1)S(1)}, u32[]{:S(2)}, u32[]{:S(2)}) %collective-permute-start.1) | collective-permute-done | bytes 229408 | tf_op jit(solution)/shard_map/ppermute | solution.py:397
  40.5 4.5 %collective-permute-done.2.fromright_ref = bf16[7,64,256]{2,1,0:T(8,128)(2,1)S(1)} collective-permute-done((bf16[7,64,256]{2,1,0:T(8,128)(2,1)S(1)}, bf16[7,64,256]{2,1,0:T(8,128)(2,1)S(1)}, u32[]{:S(2)}, u32[]{:S(2)}) %collective-permute-start.2) | collective-permute-done | bytes 229408 | tf_op jit(solution)/shard_map/ppermute | solution.py:397
  45.0 1.1 copy-done.13
  46.1 9.6 %shard_map.70 = (bf16[2624,256]{1,0:T(8,128)(2,1)}, bf16[2560,256]{1,0:T(8,128)(2,1)S(1)}, bf16[2,1344,256]{2,1,0:T(8,128)(2,1)}, bf16[1344,256]{1,0:T(8,128)(2,1)S(1)}) custom-call(s32[2]{0:T(128)S(1)} %get-tuple-element.76.place_ref, bf16[2560,256]{1,0:T(8,128)(2,1)} %copy-done.11, bf16[80,256]{1,0:T(8,128)(2,1)S(1)} %collective-permute-done.ghost_ref, ...), custom_call_target="tpu_custom_call" | custom-call | flops 2415919104 | bytes 8388608 | tf_op jit(solution)/shard_map/pallas_call | solution.py:608
  55.7 1.5 %collective-permute-start.4 = (bf16[1344,256]{1,0:T(8,128)(2,1)S(1)}, bf16[1344,256]{1,0:T(8,128)(2,1)S(1)}, u32[]{:S(2)}, u32[]{:S(2)}) collective-permute-start(bf16[1344,256]{1,0:T(8,128)(2,1)S(1)} %get-tuple-element.47), channel_id=1, source_target_pairs={{0,2},{1,3},{2,0},{3,1},{4,6},{5,7},{6,4},{7,5},{8,10},{9,11},{10,... | collective-permute-start | bytes 2064392 | tf_op jit(solution)/shard_map/ppermute | solution.py:392
  57.3 0.1 pad_add_fusion.place_ref
  57.4 0.1 reshape.32.node_ref
  57.5 1.3 copy-done
  58.8 3.8 %shard_map.72 = (bf16[588,256]{1,0:T(8,128)(2,1)S(1)}, bf16[588,256]{1,0:T(8,128)(2,1)S(1)}, bf16[588,256]{1,0:T(8,128)(2,1)S(1)}, bf16[588,256]{1,0:T(8,128)(2,1)S(1)}) custom-call(s32[2]{0:T(128)S(1)} %get-tuple-element.77.at_ref, f32[1,2560]{1,0:T(1,128)S(1)} %reshape.32.node_ref, bf16[2624,256]{1,0:T(8,128)(2,1)S(1)} %copy-done, ...), custom_call_target="tpu_custom_call" | custom-call | flops 1048576 | bytes 1024 | tf_op jit(solution)/shard_map/pallas_call | solution.py:489
  62.6 0.0 copy-start.9
  62.7 2.6 %shard_map.71.near_ref = f32[384,256]{1,0:T(8,128)S(1)} custom-call(s32[1]{0:T(128)} %bitcast.2.core_ref, bf16[2624,256]{1,0:T(8,128)(2,1)S(1)} %copy-done, bf16[2,1344,256]{2,1,0:T(8,128)(2,1)S(1)} %copy-done.2, bf16[2,1344,256]{2,1,0:T(8,128)(2,1)} %collective-permute-done.3.other_ref), custom_call_target="tpu_custom_call" | custom-call | flops 1048576 | bytes 1024 | tf_op jit(solution)/shard_map/pallas_call | solution.py:502
  65.3 8.3 %collective-permute-done.4.far_ref = bf16[1344,256]{1,0:T(8,128)(2,1)S(1)} collective-permute-done((bf16[1344,256]{1,0:T(8,128)(2,1)S(1)}, bf16[1344,256]{1,0:T(8,128)(2,1)S(1)}, u32[]{:S(2)}, u32[]{:S(2)}) %collective-permute-start.4) | collective-permute-done | bytes 688160 | tf_op jit(solution)/shard_map/ppermute | solution.py:392
  73.6 2.0 %shard_map.73 = f32[896,256]{1,0:T(8,128)S(1)} custom-call(s32[2]{0:T(128)S(1)} %pad_add_fusion.place_ref, bf16[2,1344,256]{2,1,0:T(8,128)(2,1)S(1)} %copy-done.2, bf16[2,1344,256]{2,1,0:T(8,128)(2,1)} %collective-permute-done.3.other_ref, bf16[1344,256]{1,0:T(8,128)(2,1)S(1)} %collective-permute-done.4.far_ref, f32[384,256]{1,0:T(8,128)S(1)} %shard_map.71.near_ref), custom_call_target="tpu_custom_call" | custom-call | flops 704643072 | bytes 4194304 | tf_op jit(solution)/shard_map/pallas_call | solution.py:511
  75.6 2.9 %collective-permute-start.5 = (bf16[448,256]{1,0:T(8,128)(2,1)S(1)}, bf16[448,256]{1,0:T(8,128)(2,1)S(1)}, u32[]{:S(2)}, u32[]{:S(2)}) collective-permute-start(bf16[448,256]{1,0:T(8,128)(2,1)S(1)} %fusion), channel_id=1, source_target_pairs={{0,4},{4,0},{8,12},{12,8},{16,20},{20,16},{24,28},{28,24},{1,5},{5... | collective-permute-start | bytes 688136 | tf_op jit(solution)/shard_map/ppermute | solution.py:392
  78.5 1.5 %collective-permute-start.6 = (bf16[588,256]{1,0:T(8,128)(2,1)S(1)}, bf16[588,256]{1,0:T(8,128)(2,1)S(1)}, u32[]{:S(2)}, u32[]{:S(2)}) collective-permute-start(bf16[588,256]{1,0:T(8,128)(2,1)S(1)} %get-tuple-element.58), channel_id=1, source_target_pairs={{0,2},{1,3},{2,0},{3,1},{4,6},{5,7},{6,4},{7,5},{8,10},{9,11},{10,... | collective-permute-start | bytes 903176 | tf_op jit(solution)/shard_map/ppermute | solution.py:392
  80.0 4.0 %collective-permute-done.5 = bf16[448,256]{1,0:T(8,128)(2,1)S(1)} collective-permute-done((bf16[448,256]{1,0:T(8,128)(2,1)S(1)}, bf16[448,256]{1,0:T(8,128)(2,1)S(1)}, u32[]{:S(2)}, u32[]{:S(2)}) %collective-permute-start.5) | collective-permute-done | bytes 229408 | tf_op jit(solution)/shard_map/ppermute | solution.py:392
  84.0 0.8 bitcast_add_fusion
  84.8 2.2 %collective-permute-done.6.refs_4_ = bf16[588,256]{1,0:T(8,128)(2,1)S(1)} collective-permute-done((bf16[588,256]{1,0:T(8,128)(2,1)S(1)}, bf16[588,256]{1,0:T(8,128)(2,1)S(1)}, u32[]{:S(2)}, u32[]{:S(2)}) %collective-permute-start.6) | collective-permute-done | bytes 301088 | tf_op jit(solution)/shard_map/ppermute | solution.py:392
  87.1 1.1 fusion.1
  88.1 2.0 %collective-permute-start.7 = (bf16[224,256]{1,0:T(8,128)(2,1)S(1)}, bf16[224,256]{1,0:T(8,128)(2,1)}, u32[]{:S(2)}, u32[]{:S(2)}) collective-permute-start(bf16[224,256]{1,0:T(8,128)(2,1)S(1)} %fusion.1), channel_id=1, source_target_pairs={{0,8},{4,12},{8,0},{12,4},{16,24},{20,28},{24,16},{28,20},{1,9},{5... | collective-permute-start | bytes 344072 | tf_op jit(solution)/shard_map/ppermute | solution.py:392
  90.1 1.5 %collective-permute-start.8 = (bf16[588,256]{1,0:T(8,128)(2,1)}, bf16[588,256]{1,0:T(8,128)(2,1)S(1)}, u32[]{:S(2)}, u32[]{:S(2)}) collective-permute-start(bf16[588,256]{1,0:T(8,128)(2,1)} %copy-done.9), channel_id=1, source_target_pairs={{0,2},{1,3},{2,0},{3,1},{4,6},{5,7},{6,4},{7,5},{8,10},{9,11},{10,... | collective-permute-start | bytes 903176 | tf_op jit(solution)/shard_map/ppermute | solution.py:392
  91.6 1.4 collective-permute-done.7
  93.1 1.0 bitcast_add_fusion.1
  94.1 6.3 %collective-permute-done.8.refs_5_ = bf16[588,256]{1,0:T(8,128)(2,1)S(1)} collective-permute-done((bf16[588,256]{1,0:T(8,128)(2,1)}, bf16[588,256]{1,0:T(8,128)(2,1)S(1)}, u32[]{:S(2)}, u32[]{:S(2)}) %collective-permute-start.8) | collective-permute-done | bytes 301088 | tf_op jit(solution)/shard_map/ppermute | solution.py:392
  100.5 0.7 fusion.2
  101.1 2.6 %collective-permute-start.9 = (bf16[112,256]{1,0:T(8,128)(2,1)}, bf16[112,256]{1,0:T(8,128)(2,1)}, u32[]{:S(2)}, u32[]{:S(2)}) collective-permute-start(bf16[112,256]{1,0:T(8,128)(2,1)} %fusion.2), channel_id=1, source_target_pairs={{0,16},{4,20},{8,24},{12,28},{16,0},{20,4},{24,8},{28,12},{1,17},{... | collective-permute-start | bytes 172040 | tf_op jit(solution)/shard_map/ppermute | solution.py:392
  103.7 3.0 %collective-permute-done.9 = bf16[112,256]{1,0:T(8,128)(2,1)} collective-permute-done((bf16[112,256]{1,0:T(8,128)(2,1)}, bf16[112,256]{1,0:T(8,128)(2,1)}, u32[]{:S(2)}, u32[]{:S(2)}) %collective-permute-start.9) | collective-permute-done | bytes 57376 | tf_op jit(solution)/shard_map/ppermute | solution.py:392
  106.7 1.5 bitcast_add_fusion.2
  108.2 2.4 %collective-permute-start.11 = (bf16[112,256]{1,0:T(8,128)(2,1)}, bf16[112,256]{1,0:T(8,128)(2,1)S(1)}, u32[]{:S(2)}, u32[]{:S(2)}) collective-permute-start(bf16[112,256]{1,0:T(8,128)(2,1)} %bitcast_add_fusion.2), channel_id=1, source_target_pairs={{0,16},{4,20},{8,24},{12,28},{16,0},{20,4},{24,8},{28,12},{1,17},{... | collective-permute-start | bytes 172040 | tf_op jit(solution)/shard_map/ppermute | solution.py:392
  110.6 2.9 %collective-permute-done.11 = bf16[112,256]{1,0:T(8,128)(2,1)S(1)} collective-permute-done((bf16[112,256]{1,0:T(8,128)(2,1)}, bf16[112,256]{1,0:T(8,128)(2,1)S(1)}, u32[]{:S(2)}, u32[]{:S(2)}) %collective-permute-start.11) | collective-permute-done | bytes 57376 | tf_op jit(solution)/shard_map/ppermute | solution.py:392
  113.5 0.9 maximum_select_fusion.2
  114.4 0.0 copy-start.15
  114.4 0.1 collective-permute-start.13
  114.5 0.5 copy-done.15
  115.0 4.3 %collective-permute-done.13 = bf16[224,256]{1,0:T(8,128)(2,1)} collective-permute-done((bf16[224,256]{1,0:T(8,128)(2,1)S(1)}, bf16[224,256]{1,0:T(8,128)(2,1)}, u32[]{:S(2)}, u32[]{:S(2)}) %collective-permute-start.13) | collective-permute-done | bytes 114720 | tf_op jit(solution)/shard_map/ppermute | solution.py:392
  119.4 1.1 maximum_select_fusion.1
  120.5 0.0 copy-start.14
  120.5 1.7 %collective-permute-start.14 = (bf16[448,256]{1,0:T(8,128)(2,1)S(1)}, bf16[448,256]{1,0:T(8,128)(2,1)}, u32[]{:S(2)}, u32[]{:S(2)}) collective-permute-start(bf16[448,256]{1,0:T(8,128)(2,1)S(1)} %maximum_select_fusion.1), channel_id=1, source_target_pairs={{0,4},{4,0},{8,12},{12,8},{16,20},{20,16},{24,28},{28,24},{1,5},{5... | collective-permute-start | bytes 688136 | tf_op jit(solution)/shard_map/ppermute | solution.py:392
  122.3 4.5 %collective-permute-done.14 = bf16[448,256]{1,0:T(8,128)(2,1)} collective-permute-done((bf16[448,256]{1,0:T(8,128)(2,1)S(1)}, bf16[448,256]{1,0:T(8,128)(2,1)}, u32[]{:S(2)}, u32[]{:S(2)}) %collective-permute-start.14) | collective-permute-done | bytes 229408 | tf_op jit(solution)/shard_map/ppermute | solution.py:392
  126.7 1.4 maximum_select_fusion.q0_ref
  128.1 1.6 %collective-permute-start.16 = (bf16[896,256]{1,0:T(8,128)(2,1)S(1)}, bf16[896,256]{1,0:T(8,128)(2,1)}, u32[]{:S(2)}, u32[]{:S(2)}) collective-permute-start(bf16[896,256]{1,0:T(8,128)(2,1)S(1)} %maximum_select_fusion.q0_ref), channel_id=1, source_target_pairs={{0,2},{1,3},{2,0},{3,1},{4,6},{5,7},{6,4},{7,5},{8,10},{9,11},{10,... | collective-permute-start | bytes 1376264 | tf_op jit(solution)/shard_map/ppermute | solution.py:392
  129.7 0.0 collective-permute-start.15
  129.7 7.8 %collective-permute-done.16.q2_ref = bf16[896,256]{1,0:T(8,128)(2,1)} collective-permute-done((bf16[896,256]{1,0:T(8,128)(2,1)S(1)}, bf16[896,256]{1,0:T(8,128)(2,1)}, u32[]{:S(2)}, u32[]{:S(2)}) %collective-permute-start.16) | collective-permute-done | bytes 458784 | tf_op jit(solution)/shard_map/ppermute | solution.py:392
  137.5 0.1 pad_add_fusion.3.at_ref
  137.6 3.8 %shard_map.74 = (bf16[588,256]{1,0:T(8,128)(2,1)S(1)}, bf16[588,256]{1,0:T(8,128)(2,1)S(1)}, bf16[588,256]{1,0:T(8,128)(2,1)S(1)}, bf16[588,256]{1,0:T(8,128)(2,1)S(1)}) custom-call(s32[2]{0:T(128)S(1)} %pad_add_fusion.3.at_ref, f32[1,2560]{1,0:T(1,128)S(1)} %reshape.32.node_ref, bf16[2624,256]{1,0:T(8,128)(2,1)S(1)} %copy-done.1, ...), custom_call_target="tpu_custom_call" | custom-call | flops 1048576 | bytes 1024 | tf_op jit(solution)/shard_map/pallas_call | solution.py:489
  141.5 0.6 collective-permute-start.18
  142.0 0.1 collective-permute-start.19
  142.1 1.1 collective-permute-done.18.refs_2_
  143.3 0.4 collective-permute-done.19.refs_3_
  143.7 5.4 %shard_map.75 = (f32[588,1024]{1,0:T(8,128)}, bf16[1024,1024]{1,0:T(8,128)(2,1)}) custom-call(s32[1]{0:T(128)} %bitcast.place_ref, bf16[896,256]{1,0:T(8,128)(2,1)S(1)} %maximum_select_fusion.q0_ref, bf16[896,256]{1,0:T(8,128)(2,1)} %collective-permute-done.15.q1_ref, bf16[896,256]{1,0:T(8,128)(2,1)} %collective-permute-done.16.q2_ref, ...), custom_call_target="tpu_custom_call" | custom-call | tf_op jit(solution)/shard_map/pallas_call | solution.py:550
  (32 shorter events, 0.1 us)
Async XLA Ops:
  1.3 1.3 copy-start.3
  2.6 0.7 copy-start.6
  3.8 6.9 %copy-start.10 = (s32[8,343]{1,0:T(8,128)S(1)}, s32[8,343]{1,0:T(8,128)}, u32[]{:S(2)}) copy-start(s32[8,343]{1,0:T(8,128)} %conn_ref.1) | copy-start | bytes 32932
  3.8 6.8 %collective-permute-start = (bf16[80,256]{1,0:T(8,128)(2,1)S(1)}, bf16[80,256]{1,0:T(8,128)(2,1)S(1)}, u32[]{:S(2)}, u32[]{:S(2)}) collective-permute-start(bf16[80,256]{1,0:T(8,128)(2,1)S(1)} %shard_map.68), channel_id=1, source_target_pairs={{4,0},{8,4},{12,8},{16,12},{20,16},{24,20},{28,24},{5,1},{9,5},{13... | collective-permute-start | bytes 122888 | tf_op jit(solution)/shard_map/ppermute | solution.py:397
  30.0 1.1 copy-start.11
  31.0 0.9 copy-start.12
  31.9 8.6 %collective-permute-start.1 = (bf16[7,64,256]{2,1,0:T(8,128)(2,1)S(1)}, bf16[7,64,256]{2,1,0:T(8,128)(2,1)S(1)}, u32[]{:S(2)}, u32[]{:S(2)}) collective-permute-start(bf16[7,64,256]{2,1,0:T(8,128)(2,1)S(1)} %get-tuple-element.42), channel_id=1, source_target_pairs={{0,4},{4,8},{8,12},{12,16},{16,20},{20,24},{24,28},{1,5},{5,9},{9,... | collective-permute-start | bytes 688136 | tf_op jit(solution)/shard_map/ppermute | solution.py:397
  36.7 8.2 %collective-permute-start.2 = (bf16[7,64,256]{2,1,0:T(8,128)(2,1)S(1)}, bf16[7,64,256]{2,1,0:T(8,128)(2,1)S(1)}, u32[]{:S(2)}, u32[]{:S(2)}) collective-permute-start(bf16[7,64,256]{2,1,0:T(8,128)(2,1)S(1)} %get-tuple-element.43), channel_id=1, source_target_pairs={{4,0},{8,4},{12,8},{16,12},{20,16},{24,20},{28,24},{5,1},{9,5},{13... | collective-permute-start | bytes 688136 | tf_op jit(solution)/shard_map/ppermute | solution.py:397
  45.0 1.1 copy-start.13
  55.7 6.9 %collective-permute-start.3 = (bf16[2,1344,256]{2,1,0:T(8,128)(2,1)}, bf16[2,1344,256]{2,1,0:T(8,128)(2,1)}, u32[]{:S(2)}, u32[]{:S(2)}) collective-permute-start(bf16[2,1344,256]{2,1,0:T(8,128)(2,1)} %get-tuple-element.46.w_ref), channel_id=1, source_target_pairs={{0,1},{1,0},{2,3},{3,2},{4,5},{5,4},{6,7},{7,6},{8,9},{9,8},{10,11... | collective-permute-start | bytes 4128776 | tf_op jit(solution)/shard_map/ppermute | solution.py:392
  55.7 17.8 %collective-permute-start.4 = (bf16[1344,256]{1,0:T(8,128)(2,1)S(1)}, bf16[1344,256]{1,0:T(8,128)(2,1)S(1)}, u32[]{:S(2)}, u32[]{:S(2)}) collective-permute-start(bf16[1344,256]{1,0:T(8,128)(2,1)S(1)} %get-tuple-element.47), channel_id=1, source_target_pairs={{0,2},{1,3},{2,0},{3,1},{4,6},{5,7},{6,4},{7,5},{8,10},{9,11},{10,... | collective-permute-start | bytes 2064392 | tf_op jit(solution)/shard_map/ppermute | solution.py:392
  57.4 1.3 copy-start
  58.8 3.9 %copy-start.2 = (bf16[2,1344,256]{2,1,0:T(8,128)(2,1)S(1)}, bf16[2,1344,256]{2,1,0:T(8,128)(2,1)}, u32[]{:S(2)}) copy-start(bf16[2,1344,256]{2,1,0:T(8,128)(2,1)} %get-tuple-element.46.w_ref) | copy-start | bytes 4128772
  62.6 2.7 %copy-start.7 = (bf16[588,256]{1,0:T(8,128)(2,1)}, bf16[588,256]{1,0:T(8,128)(2,1)S(1)}, u32[]{:S(2)}) copy-start(bf16[588,256]{1,0:T(8,128)(2,1)S(1)} %get-tuple-element.64) | copy-start | bytes 903172
  62.6 2.7 %copy-start.8 = (bf16[588,256]{1,0:T(8,128)(2,1)}, bf16[588,256]{1,0:T(8,128)(2,1)S(1)}, u32[]{:S(2)}) copy-start(bf16[588,256]{1,0:T(8,128)(2,1)S(1)} %get-tuple-element.62) | copy-start | bytes 903172
  62.6 2.7 %copy-start.9 = (bf16[588,256]{1,0:T(8,128)(2,1)}, bf16[588,256]{1,0:T(8,128)(2,1)S(1)}, u32[]{:S(2)}) copy-start(bf16[588,256]{1,0:T(8,128)(2,1)S(1)} %get-tuple-element.60) | copy-start | bytes 903172
  75.6 8.4 %collective-permute-start.5 = (bf16[448,256]{1,0:T(8,128)(2,1)S(1)}, bf16[448,256]{1,0:T(8,128)(2,1)S(1)}, u32[]{:S(2)}, u32[]{:S(2)}) collective-permute-start(bf16[448,256]{1,0:T(8,128)(2,1)S(1)} %fusion), channel_id=1, source_target_pairs={{0,4},{4,0},{8,12},{12,8},{16,20},{20,16},{24,28},{28,24},{1,5},{5... | collective-permute-start | bytes 688136 | tf_op jit(solution)/shard_map/ppermute | solution.py:392
  78.5 8.5 %collective-permute-start.6 = (bf16[588,256]{1,0:T(8,128)(2,1)S(1)}, bf16[588,256]{1,0:T(8,128)(2,1)S(1)}, u32[]{:S(2)}, u32[]{:S(2)}) collective-permute-start(bf16[588,256]{1,0:T(8,128)(2,1)S(1)} %get-tuple-element.58), channel_id=1, source_target_pairs={{0,2},{1,3},{2,0},{3,1},{4,6},{5,7},{6,4},{7,5},{8,10},{9,11},{10,... | collective-permute-start | bytes 903176 | tf_op jit(solution)/shard_map/ppermute | solution.py:392
  87.1 50.5 %copy-start.1 = (bf16[2624,256]{1,0:T(8,128)(2,1)S(1)}, bf16[2624,256]{1,0:T(8,128)(2,1)}, u32[]{:S(2)}) copy-start(bf16[2624,256]{1,0:T(8,128)(2,1)} %get-tuple-element.66.x_ref) | copy-start | bytes 4030468
  88.1 5.0 %collective-permute-start.7 = (bf16[224,256]{1,0:T(8,128)(2,1)S(1)}, bf16[224,256]{1,0:T(8,128)(2,1)}, u32[]{:S(2)}, u32[]{:S(2)}) collective-permute-start(bf16[224,256]{1,0:T(8,128)(2,1)S(1)} %fusion.1), channel_id=1, source_target_pairs={{0,8},{4,12},{8,0},{12,4},{16,24},{20,28},{24,16},{28,20},{1,9},{5... | collective-permute-start | bytes 344072 | tf_op jit(solution)/shard_map/ppermute | solution.py:392
  90.1 10.3 %collective-permute-start.8 = (bf16[588,256]{1,0:T(8,128)(2,1)}, bf16[588,256]{1,0:T(8,128)(2,1)S(1)}, u32[]{:S(2)}, u32[]{:S(2)}) collective-permute-start(bf16[588,256]{1,0:T(8,128)(2,1)} %copy-done.9), channel_id=1, source_target_pairs={{0,2},{1,3},{2,0},{3,1},{4,6},{5,7},{6,4},{7,5},{8,10},{9,11},{10,... | collective-permute-start | bytes 903176 | tf_op jit(solution)/shard_map/ppermute | solution.py:392
  91.6 16.5 %collective-permute-start.10 = (bf16[588,256]{1,0:T(8,128)(2,1)}, bf16[588,256]{1,0:T(8,128)(2,1)}, u32[]{:S(2)}, u32[]{:S(2)}) collective-permute-start(bf16[588,256]{1,0:T(8,128)(2,1)} %copy-done.8), channel_id=1, source_target_pairs={{0,3},{1,2},{2,1},{3,0},{4,7},{5,6},{6,5},{7,4},{8,11},{9,10},{10,... | collective-permute-start | bytes 903176 | tf_op jit(solution)/shard_map/ppermute | solution.py:392
  100.5 21.8 %copy-start.4 = (bf16[588,256]{1,0:T(8,128)(2,1)}, bf16[588,256]{1,0:T(8,128)(2,1)S(1)}, u32[]{:S(2)}) copy-start(bf16[588,256]{1,0:T(8,128)(2,1)S(1)} %collective-permute-done.8.refs_5_) | copy-start | bytes 903172
  101.1 5.6 %collective-permute-start.9 = (bf16[112,256]{1,0:T(8,128)(2,1)}, bf16[112,256]{1,0:T(8,128)(2,1)}, u32[]{:S(2)}, u32[]{:S(2)}) collective-permute-start(bf16[112,256]{1,0:T(8,128)(2,1)} %fusion.2), channel_id=1, source_target_pairs={{0,16},{4,20},{8,24},{12,28},{16,0},{20,4},{24,8},{28,12},{1,17},{... | collective-permute-start | bytes 172040 | tf_op jit(solution)/shard_map/ppermute | solution.py:392
  103.7 10.7 %collective-permute-start.12 = (bf16[588,256]{1,0:T(8,128)(2,1)}, bf16[588,256]{1,0:T(8,128)(2,1)}, u32[]{:S(2)}, u32[]{:S(2)}) collective-permute-start(bf16[588,256]{1,0:T(8,128)(2,1)} %copy-done.7), channel_id=1, source_target_pairs={{0,3},{1,2},{2,1},{3,0},{4,7},{5,6},{6,5},{7,4},{8,11},{9,10},{10,... | collective-permute-start | bytes 903176 | tf_op jit(solution)/shard_map/ppermute | solution.py:392
  108.2 5.3 %collective-permute-start.11 = (bf16[112,256]{1,0:T(8,128)(2,1)}, bf16[112,256]{1,0:T(8,128)(2,1)S(1)}, u32[]{:S(2)}, u32[]{:S(2)}) collective-permute-start(bf16[112,256]{1,0:T(8,128)(2,1)} %bitcast_add_fusion.2), channel_id=1, source_target_pairs={{0,16},{4,20},{8,24},{12,28},{16,0},{20,4},{24,8},{28,12},{1,17},{... | collective-permute-start | bytes 172040 | tf_op jit(solution)/shard_map/ppermute | solution.py:392
  114.4 0.6 copy-start.15
  114.4 5.0 %collective-permute-start.13 = (bf16[224,256]{1,0:T(8,128)(2,1)S(1)}, bf16[224,256]{1,0:T(8,128)(2,1)}, u32[]{:S(2)}, u32[]{:S(2)}) collective-permute-start(bf16[224,256]{1,0:T(8,128)(2,1)S(1)} %maximum_select_fusion.2), channel_id=1, source_target_pairs={{0,8},{4,12},{8,0},{12,4},{16,24},{20,28},{24,16},{28,20},{1,9},{5... | collective-permute-start | bytes 344072 | tf_op jit(solution)/shard_map/ppermute | solution.py:392
  120.5 1.8 %copy-start.14 = (bf16[448,256]{1,0:T(8,128)(2,1)}, bf16[448,256]{1,0:T(8,128)(2,1)S(1)}, u32[]{:S(2)}) copy-start(bf16[448,256]{1,0:T(8,128)(2,1)S(1)} %maximum_select_fusion.1) | copy-start | bytes 688132
  120.5 6.2 %collective-permute-start.14 = (bf16[448,256]{1,0:T(8,128)(2,1)S(1)}, bf16[448,256]{1,0:T(8,128)(2,1)}, u32[]{:S(2)}, u32[]{:S(2)}) collective-permute-start(bf16[448,256]{1,0:T(8,128)(2,1)S(1)} %maximum_select_fusion.1), channel_id=1, source_target_pairs={{0,4},{4,0},{8,12},{12,8},{16,20},{20,16},{24,28},{28,24},{1,5},{5... | collective-permute-start | bytes 688136 | tf_op jit(solution)/shard_map/ppermute | solution.py:392
  128.1 9.4 %collective-permute-start.16 = (bf16[896,256]{1,0:T(8,128)(2,1)S(1)}, bf16[896,256]{1,0:T(8,128)(2,1)}, u32[]{:S(2)}, u32[]{:S(2)}) collective-permute-start(bf16[896,256]{1,0:T(8,128)(2,1)S(1)} %maximum_select_fusion.q0_ref), channel_id=1, source_target_pairs={{0,2},{1,3},{2,0},{3,1},{4,6},{5,7},{6,4},{7,5},{8,10},{9,11},{10,... | collective-permute-start | bytes 1376264 | tf_op jit(solution)/shard_map/ppermute | solution.py:392
  129.7 14.0 %collective-permute-start.15 = (bf16[896,256]{1,0:T(8,128)(2,1)S(1)}, bf16[896,256]{1,0:T(8,128)(2,1)}, u32[]{:S(2)}, u32[]{:S(2)}) collective-permute-start(bf16[896,256]{1,0:T(8,128)(2,1)S(1)} %maximum_select_fusion.q0_ref), channel_id=1, source_target_pairs={{0,1},{1,0},{2,3},{3,2},{4,5},{5,4},{6,7},{7,6},{8,9},{9,8},{10,11... | collective-permute-start | bytes 1376264 | tf_op jit(solution)/shard_map/ppermute | solution.py:392
  137.5 6.2 %collective-permute-start.17 = (bf16[896,256]{1,0:T(8,128)(2,1)}, bf16[896,256]{1,0:T(8,128)(2,1)}, u32[]{:S(2)}, u32[]{:S(2)}) collective-permute-start(bf16[896,256]{1,0:T(8,128)(2,1)} %collective-permute-done.16.q2_ref), channel_id=1, source_target_pairs={{0,1},{1,0},{2,3},{3,2},{4,5},{5,4},{6,7},{7,6},{8,9},{9,8},{10,11... | collective-permute-start | bytes 1376264 | tf_op jit(solution)/shard_map/ppermute | solution.py:392
  137.5 6.2 %copy-start.5 = (bf16[588,256]{1,0:T(8,128)(2,1)S(1)}, bf16[588,256]{1,0:T(8,128)(2,1)}, u32[]{:S(2)}) copy-start(bf16[588,256]{1,0:T(8,128)(2,1)} %copy-done.4) | copy-start | bytes 903172
  141.5 1.8 %collective-permute-start.18 = (bf16[588,256]{1,0:T(8,128)(2,1)S(1)}, bf16[588,256]{1,0:T(8,128)(2,1)S(1)}, u32[]{:S(2)}, u32[]{:S(2)}) collective-permute-start(bf16[588,256]{1,0:T(8,128)(2,1)S(1)} %get-tuple-element.70), channel_id=1, source_target_pairs={{0,1},{1,0},{2,3},{3,2},{4,5},{5,4},{6,7},{7,6},{8,9},{9,8},{10,11... | collective-permute-start | bytes 903176 | tf_op jit(solution)/shard_map/ppermute | solution.py:392
  142.0 1.7 %collective-permute-start.19 = (bf16[588,256]{1,0:T(8,128)(2,1)S(1)}, bf16[588,256]{1,0:T(8,128)(2,1)S(1)}, u32[]{:S(2)}, u32[]{:S(2)}) collective-permute-start(bf16[588,256]{1,0:T(8,128)(2,1)S(1)} %get-tuple-element.71), channel_id=1, source_target_pairs={{0,1},{1,0},{2,3},{3,2},{4,5},{5,4},{6,7},{7,6},{8,9},{9,8},{10,11... | collective-permute-start | bytes 903176 | tf_op jit(solution)/shard_map/ppermute | solution.py:392

commit v6 on v5

--- a/solution.py
+++ b/solution.py
@@ -191,21 +191,14 @@
 
 
 def store_matrices(mats, out_ref, at, fp, width):
-    for part in range(2):
-        for j, m in enumerate(mats):
-            block, lane = divmod((part * len(mats) + j) * fp, width)
-            out_ref[at + block, :, lane : lane + fp] = split(m)[part]
+    for j, m in enumerate(mats):
+        block, lane = divmod(j * fp, width)
+        out_ref[at + block, :, lane : lane + fp] = m.astype(out_ref.dtype)
 
 
 def load_matrices(ref, at, count, fp, width):
-    out = []
-    for j in range(count):
-        pieces = []
-        for part in range(2):
-            block, lane = divmod((part * count + j) * fp, width)
-            pieces.append(ref[at + block, :, lane : lane + fp].astype(F32))
-        out.append(pieces[0] + pieces[1])
-    return out
+    spots = [divmod(j * fp, width) for j in range(count)]
+    return [ref[at + block, :, lane : lane + fp].astype(F32) for block, lane in spots]
 
 
 def free_kernel(
@@ -224,7 +217,8 @@
     def keep(k, low, high):
         own_ref[0, k] = low
         own_ref[1, k] = high
-        down_ref[k] = low.astype(BF16)
+        if k < DEGREE:
+            down_ref[k] = low.astype(BF16)
         up_ref[k] = high.astype(BF16)
 
     now_ref, other_ref = a_ref, b_ref
@@ -254,14 +248,10 @@
     keep(DEGREE, mul(h_ref[0, :fp], now_ref[:cp]), mul(h_ref[cells - 1, stride:], now_ref[total - stride :]))
     low = response(h_ref[0], h_ref[1], pot_ref[fp:cp], fp, False)
     high = response(h_ref[cells - 1], h_ref[cells - 2], pot_ref[total - stride :], fp, True)
-    store_matrices(low, down_ref, DEGREE + 1, fp, width)
+    store_matrices(low, down_ref, DEGREE, fp, width)
     store_matrices(high, up_ref, DEGREE + 1, fp, width)
-    count = len(low)
     for side, mats in enumerate((low, high)):
-        for j, m in enumerate(mats):
-            own_ref_at = (DEGREE + 1) * 0
-            block, lane = divmod(j * fp, width)
-            own_ref[side, DEGREE + 1 + block + own_ref_at, :, lane : lane + fp] = m
+        store_matrices(mats, own_ref.at[side], DEGREE + 1, fp, width)
 
 
 def forced_kernel(
@@ -273,16 +263,16 @@
     total = cells * stride
     width = v_ref.shape[1]
     half = cells // 2
+    extra = own_ref.shape[1] - DEGREE - 1
     potg = to_col(jnp.sum(ghost_ref[fp:].astype(F32), axis=0, keepdims=True)[:, :fp], fp)
     histories = []
     last_image = None
     for side, (got_ref, pot, start) in enumerate(
         ((fromleft_ref, pot_ref[:fp], v_ref[:fp]), (fromright_ref, potg, ghost_ref[:fp]))
     ):
-        mats = load_matrices(got_ref, DEGREE + 1, DEGREE, fp, width)
-        for j in range(DEGREE):
-            block, lane = divmod(j * fp, width)
-            mats[j] = mats[j] + own_ref[side, DEGREE + 1 + block, :, lane : lane + fp]
+        theirs = load_matrices(got_ref, got_ref.shape[0] - extra, DEGREE, fp, width)
+        ours = load_matrices(own_ref.at[side], DEGREE + 1, DEGREE, fp, width)
+        mats = [a + b for a, b in zip(theirs, ours)]
         mats = [split(m) for m in mats]
         values = [start]
         for k in range(DEGREE + 1 if side == 0 else DEGREE):
@@ -357,11 +347,12 @@
 
 def back_pair_kernel(at_ref, node_ref, x_ref, image_ref, *out_refs):
     rows = out_refs[0].shape[0]
-    for i in range(2):
+    width = x_ref.shape[1]
+    for i, out_ref in enumerate(out_refs):
         want = (lax.broadcasted_iota(jnp.int32, (rows, 1), 0) + at_ref[i] * rows).astype(F32)
         hit = flat(want == node_ref[...])
-        out_refs[2 * i][...] = mul(hit, x_ref[...]).astype(BF16)
-        out_refs[2 * i + 1][...] = mul(hit, image_ref[...]).astype(BF16)
+        out_ref[:, :width] = mul(hit, x_ref[...]).astype(BF16)
+        out_ref[:, width:] = mul(hit, image_ref[...]).astype(BF16)
 
 
 def gram_kernel(scale, x_ref, y_ref, out_ref, rows_ref):
@@ -431,8 +422,8 @@
 
 def paired_residual_kernel(place_ref, q0_ref, q1_ref, q2_ref, q3_ref, *refs):
     parts = 4
-    x_refs, y_refs, (out_ref, p_ref, q_ref) = refs[: 2 * parts : 2], refs[1 : 2 * parts : 2], refs[2 * parts :]
-    width = x_refs[0].shape[1]
+    row_refs, (out_ref, p_ref, q_ref) = refs[:parts], refs[parts:]
+    width = row_refs[0].shape[1] // 2
     half = width // 2
     for k, ref in enumerate((q0_ref, q1_ref, q2_ref, q3_ref)):
         q_ref[k] = ref[...]
@@ -464,12 +455,12 @@
             block = (one.astype(F32) + turned(two)).astype(BF16)
             put(i, j, block)
             put(j, i, turned(block).astype(BF16))
-    x = jnp.concatenate([ref[...] for ref in x_refs], axis=1)
+    x = jnp.concatenate([ref[:, :width] for ref in row_refs], axis=1)
     spots = [pl.ds(pl.multiple_of(jnp.bitwise_xor(me, k) * width, width), width) for k in range(parts)]
     for k in range(parts):
         at = spots[k]
         p = jnp.concatenate([p_ref[spots[m], at] for m in range(parts)], axis=0)
-        out_ref[:, at] = y_refs[k][...].astype(F32) - mul(x, p)
+        out_ref[:, at] = row_refs[k][:, width:].astype(F32) - mul(x, p)
 
 
 def paired_tail(x_own, image, w_own, give, node_row, o, d, dom, nodes):
@@ -490,8 +481,8 @@
             back_pair_kernel,
             grid=(1,),
             in_specs=[smem, whole(1, total), whole(total, width), whole(total, width)],
-            out_specs=[whole(rows, width)] * 4,
-            out_shape=[sds((rows, width), BF16)] * 4,
+            out_specs=[whole(rows, 2 * width)] * 2,
+            out_shape=[sds((rows, 2 * width), BF16)] * 2,
             compiler_params=params(),
             cost_estimate=pl.CostEstimate(flops=1 << 20, bytes_accessed=1 << 10, transcendentals=0),
         )(jnp.stack([jnp.bitwise_xor(o, first), jnp.bitwise_xor(o, second)]), node_row, x_own, image)
@@ -507,7 +498,8 @@
         cost_estimate=pl.CostEstimate(flops=1 << 20, bytes_accessed=1 << 10, transcendentals=0),
     )(core.reshape(1), x_own, w_own, w_other)
     far, near, *cuts = lax.optimization_barrier((far, near, *cuts))
-    rows_far = [swap(cut, "orb", 2 + i // 2) for i, cut in enumerate(cuts)]
+    row2 = swap(cuts[0], "orb", 2)
+    cut3 = cuts[1]
     share = pl.pallas_call(
         functools.partial(far_gram_kernel, scale),
         in_specs=[smem] + [vmem] * 4,
@@ -517,7 +509,6 @@
     )(jnp.stack([side, core]), w_own, w_other, far, near)
 
     bits = []
-    pending, rows_got = list(rows_far), []
     bit = 1
     while bit < dom:
         mine = (d // bit) % 2
@@ -527,33 +518,29 @@
         give = give.astype(BF16)
         if bit == 1:
             x_own, image, give = lax.optimization_barrier((x_own, image, give))
-            near_rows = back(0, 1, x_own, image)
-            rows_near = list(near_rows[:2]) + [swap(cut, "orb", 1) for cut in near_rows[2:]]
+            row0, cut1 = back(0, 1, x_own, image)
         share = keep + swap(give, "dom", bit).astype(F32)
-        if pending:
-            share, got = lax.optimization_barrier((share, pending.pop(0)))
-            rows_got.append(got)
         bits.append((bit, mine))
         bit *= 2
-    share = share.astype(BF16)
+    share, row2, cut3 = lax.optimization_barrier((share.astype(BF16), row2, cut3))
+    row3 = swap(cut3, "orb", 3)
     for bit, mine in reversed(bits):
         got = swap(share, "dom", bit)
         share = jnp.where(mine == 0, jnp.concatenate([share, got], axis=0), jnp.concatenate([got, share], axis=0))
-        if pending:
-            share, got = lax.optimization_barrier((share, pending.pop(0)))
-            rows_got.append(got)
-    rows_got += pending
+    share, row2, row3 = lax.optimization_barrier((share, row2, row3))
     q2 = swap(share, "orb", 2)
     q1 = swap(share, "orb", 1)
+    row1 = swap(cut1, "orb", 1)
+    q2, row1 = lax.optimization_barrier((q2, row1))
     q3 = swap(q2, "orb", 1)
     cols = orb * width
     return pl.pallas_call(
         paired_residual_kernel,
-        in_specs=[smem] + [vmem] * 12,
+        in_specs=[smem] + [vmem] * 8,
         out_shape=(sds((rows, cols), F32), sds((cols, cols), BF16)),
         scratch_shapes=[pltpu.VMEM((orb,) + share.shape, BF16)],
         compiler_params=params(),
-    )(o.reshape(1), share, q1, q2, q3, *rows_near, *rows_got)
+    )(o.reshape(1), share, q1, q2, q3, row0, row1, row2, row3)
 
 
 def body(orbitals, potential, cell_hamiltonian, connectivity, face_nodes):
@@ -578,7 +565,6 @@
     ghost = shift(face_values, "dom", -1)
 
     extra = -(-DEGREE * fp // width)
-    sent = DEGREE + 1 + -(-2 * DEGREE * fp // width)
     ext = pltpu.VMEM((total + fp, width), BF16)
     cost = pl.CostEstimate(
         flops=2 * DEGREE * cells * cp * cp * width, bytes_accessed=8 << 20, transcendentals=0
@@ -592,8 +578,8 @@
             sds((cells, 1, stride), F32),
             sds((total, width), BF16),
             sds((2, DEGREE + 1 + extra, fp, width), F32),
-            sds((sent, fp, width), BF16),
-            sds((sent, fp, width), BF16),
+            sds((DEGREE + 1 + extra, fp, width), BF16),
+            sds((DEGREE + extra, fp, width), BF16),
         ],
         scratch_shapes=[ext, ext],
         compiler_params=params(),

time: 150 us -> 142 us (0.947)
  waiting for transfers between devices: 55.5 us -> 49 us
  starting transfers between devices: 25.9 us -> 23.8 us
    ppermute x17 -> x14, waiting for transfers between devices: 46.4 us -> 40.9 us  [swap(): lax.ppermute(block, axis, [(i, i ^ bit) for i in range(lax.axis_size(axis...]
    ppermute x17 -> x14, starting transfers between devices: 18.5 us -> 16.3 us  [swap(): lax.ppermute(block, axis, [(i, i ^ bit) for i in range(lax.axis_size(axis...]
    unnamed x33, local copies, waits for them, and re-layouts: 10.2 us -> 11.7 us
    add x3 -> x2, other arithmetic: 3.28 us -> 2.08 us  [paired_tail(): share = keep + swap(give, 'dom', bit).astype(F32)]
  transfers between devices with their start and end apart: 20 -> 17, of which waited for: 15 -> 11; matrix products, arithmetic and copies ran while one was open for 6% -> 7% of each run, Pallas kernels for 7% -> 8%
where the time goes in v6:
time: 142 us; the launch traced here: 141 us
  waiting for transfers between devices  49 us (35%)
  Pallas kernels  47.4 us (33%)
  starting transfers between devices  23.8 us (17%)
  local copies, waits for them, and re-layouts  13.2 us (9%)
  other arithmetic  7.05 us (5%)
    ppermute x14, waiting for transfers between devices, swap(): lax.ppermute(block, axis, [(i, i ^ bit) for i in range(lax.axis_size(axis...  40.9 us
    pallas_call x1, Pallas kernels, body(): pl.pallas_call(functools.partial(free_kernel, fp, ip), out_shape=[sds((ce...  19.2 us
    ppermute x14, starting transfers between devices, swap(): lax.ppermute(block, axis, [(i, i ^ bit) for i in range(lax.axis_size(axis...  16.3 us
    unnamed x33, local copies, waits for them, and re-layouts  11.7 us
    pallas_call x1, Pallas kernels, body(): pl.pallas_call(functools.partial(forced_kernel, fp), in_specs=[pl.BlockSp...  9.64 us
    pallas_call x2, Pallas kernels, back(): pl.pallas_call(back_pair_kernel, grid=(1,), in_specs=[smem, whole(1, tota...  8.49 us
    ppermute x3, waiting for transfers between devices, shift(): lax.ppermute(block, axis, [(i, i + distance) for i in range(n) if 0 <= i...  8.13 us
    ppermute x3, starting transfers between devices, shift(): lax.ppermute(block, axis, [(i, i + distance) for i in range(n) if 0 <= i...  7.53 us
  transfers between devices with their start and end apart: 17, of which 11 were waited for; matrix products, arithmetic and copies ran while one was open for 7% of the time, Pallas kernels for 8%

profile of v6, /device:TPU:0, one launch (start us, length us, event | category | flops | bytes accessed | tf_op | source)
XLA Modules:
  0.0 141.4 jit_solution(16255311207802549848)
XLA Ops:
  0.6 0.7 reshape.31.pot_ref.potraw_ref
  1.3 1.3 copy-done.4
  2.6 0.7 copy-done.8
  3.3 0.5 shard_map.68
  3.8 0.0 copy-start.5
  3.8 0.0 copy-start.9
  3.8 0.0 copy-start.12
  3.8 1.4 %collective-permute-start = (bf16[80,256]{1,0:T(8,128)(2,1)S(1)}, bf16[80,256]{1,0:T(8,128)(2,1)S(1)}, u32[]{:S(2)}, u32[]{:S(2)}) collective-permute-start(bf16[80,256]{1,0:T(8,128)(2,1)S(1)} %shard_map.68), channel_id=1, source_target_pairs={{4,0},{8,4},{12,8},{16,12},{20,16},{24,20},{28,24},{5,1},{9,5},{13... | collective-permute-start | bytes 122888 | tf_op jit(solution)/shard_map/ppermute | solution.py:388
  5.2 3.2 %copy.7.hraw_ref = bf16[8,343,343]{2,1,0:T(8,128)(2,1)} copy(bf16[8,343,343]{2,0,1:T(8,128)(2,1)} %param.7) | data formatting | bytes 3764768 | tf_op args[2]
  8.5 2.3 %collective-permute-done.ghost_ref = bf16[80,256]{1,0:T(8,128)(2,1)S(1)} collective-permute-done((bf16[80,256]{1,0:T(8,128)(2,1)S(1)}, bf16[80,256]{1,0:T(8,128)(2,1)S(1)}, u32[]{:S(2)}, u32[]{:S(2)}) %collective-permute-start) | collective-permute-done | bytes 40992 | tf_op jit(solution)/shard_map/ppermute | solution.py:388
  10.8 19.2 %shard_map.69 = (bf16[8,384,384]{2,1,0:T(8,128)(2,1)}, bf16[2560,256]{1,0:T(8,128)(2,1)S(1)}, f32[2560,1]{1,0:T(8,128)}, f32[8,1,320]{2,1,0:T(1,128)S(1)}, bf16[...) custom-call(s32[8,343]{1,0:T(8,128)S(1)} %copy-done.12, ...), custom_call_target="tpu_custom_call" | custom-call | flops 2415919104 | bytes 8388608 | tf_op jit(solution)/shard_map/pallas_call | solution.py:572
  30.0 1.1 copy-done.13
  31.1 4.8 %collective-permute-start.1 = (bf16[6,64,256]{2,1,0:T(8,128)(2,1)S(1)}, bf16[6,64,256]{2,1,0:T(8,128)(2,1)S(1)}, u32[]{:S(2)}, u32[]{:S(2)}) collective-permute-start(bf16[6,64,256]{2,1,0:T(8,128)(2,1)S(1)} %get-tuple-element.36), channel_id=1, source_target_pairs={{0,4},{4,8},{8,12},{12,16},{16,20},{20,24},{24,28},{1,5},{5,9},{9,... | collective-permute-start | bytes 589832 | tf_op jit(solution)/shard_map/ppermute | solution.py:388
  35.9 1.3 collective-permute-start.2
  37.2 0.1 pad_add_fusion.1
  37.3 5.8 %collective-permute-done.2.fromright_ref = bf16[5,64,256]{2,1,0:T(8,128)(2,1)S(1)} collective-permute-done((bf16[5,64,256]{2,1,0:T(8,128)(2,1)S(1)}, bf16[5,64,256]{2,1,0:T(8,128)(2,1)S(1)}, u32[]{:S(2)}, u32[]{:S(2)}) %collective-permute-start.2) | collective-permute-done | bytes 163872 | tf_op jit(solution)/shard_map/ppermute | solution.py:388
  43.1 0.0 collective-permute-done.1.fromleft_ref
  43.1 9.6 %shard_map.70 = (bf16[2624,256]{1,0:T(8,128)(2,1)}, bf16[2560,256]{1,0:T(8,128)(2,1)S(1)}, bf16[2,1344,256]{2,1,0:T(8,128)(2,1)}, bf16[1344,256]{1,0:T(8,128)(2,1)S(1)}) custom-call(s32[2]{0:T(128)S(1)} %get-tuple-element.64.place_ref, bf16[2560,256]{1,0:T(8,128)(2,1)} %copy-done.13, bf16[80,256]{1,0:T(8,128)(2,1)S(1)} %collective-permute-done.ghost_ref, ...), custom_call_target="tpu_custom_call" | custom-call | flops 2415919104 | bytes 8388608 | tf_op jit(solution)/shard_map/pallas_call | solution.py:594
  52.7 1.5 %collective-permute-start.4 = (bf16[1344,256]{1,0:T(8,128)(2,1)S(1)}, bf16[1344,256]{1,0:T(8,128)(2,1)S(1)}, u32[]{:S(2)}, u32[]{:S(2)}) collective-permute-start(bf16[1344,256]{1,0:T(8,128)(2,1)S(1)} %get-tuple-element.41), channel_id=1, source_target_pairs={{0,2},{1,3},{2,0},{3,1},{4,6},{5,7},{6,4},{7,5},{8,10},{9,11},{10,... | collective-permute-start | bytes 2064392 | tf_op jit(solution)/shard_map/ppermute | solution.py:383
  54.2 0.1 pad_add_fusion.place_ref
  54.4 0.1 reshape.32.node_ref
  54.4 1.3 copy-done
  55.8 3.8 %shard_map.72 = (bf16[588,512]{1,0:T(8,128)(2,1)S(1)}, bf16[588,512]{1,0:T(8,128)(2,1)S(1)}) custom-call(s32[2]{0:T(128)S(1)} %get-tuple-element.65.at_ref, f32[1,2560]{1,0:T(1,128)S(1)} %reshape.32.node_ref, bf16[2624,256]{1,0:T(8,128)(2,1)S(1)} %copy-done, bf16[2560,256]{1,0:T(8,128)(2,1)S(1)} %get-tuple-element.57.image_ref), custom_call_target="tpu_custom_call" | custom-call | flops 1048576 | bytes 1024 | tf_op jit(solution)/shard_map/pallas_call | solution.py:480
  59.6 0.0 copy-start.11
  59.6 2.7 %shard_map.71.near_ref = f32[384,256]{1,0:T(8,128)S(1)} custom-call(s32[1]{0:T(128)} %bitcast.2.core_ref, bf16[2624,256]{1,0:T(8,128)(2,1)S(1)} %copy-done, bf16[2,1344,256]{2,1,0:T(8,128)(2,1)S(1)} %copy-done.2, bf16[2,1344,256]{2,1,0:T(8,128)(2,1)} %collective-permute-done.3.other_ref), custom_call_target="tpu_custom_call" | custom-call | flops 1048576 | bytes 1024 | tf_op jit(solution)/shard_map/pallas_call | solution.py:493
  62.4 8.2 %collective-permute-done.4.far_ref = bf16[1344,256]{1,0:T(8,128)(2,1)S(1)} collective-permute-done((bf16[1344,256]{1,0:T(8,128)(2,1)S(1)}, bf16[1344,256]{1,0:T(8,128)(2,1)S(1)}, u32[]{:S(2)}, u32[]{:S(2)}) %collective-permute-start.4) | collective-permute-done | bytes 688160 | tf_op jit(solution)/shard_map/ppermute | solution.py:383
  70.6 2.0 %shard_map.73 = f32[896,256]{1,0:T(8,128)S(1)} custom-call(s32[2]{0:T(128)S(1)} %pad_add_fusion.place_ref, bf16[2,1344,256]{2,1,0:T(8,128)(2,1)S(1)} %copy-done.2, bf16[2,1344,256]{2,1,0:T(8,128)(2,1)} %collective-permute-done.3.other_ref, bf16[1344,256]{1,0:T(8,128)(2,1)S(1)} %collective-permute-done.4.far_ref, f32[384,256]{1,0:T(8,128)S(1)} %shard_map.71.near_ref), custom_call_target="tpu_custom_call" | custom-call | flops 704643072 | bytes 4194304 | tf_op jit(solution)/shard_map/pallas_call | solution.py:503
  72.5 0.0 copy-start.3
  72.6 0.9 copy-done.3
  73.5 2.3 %collective-permute-start.5 = (bf16[448,256]{1,0:T(8,128)(2,1)S(1)}, bf16[448,256]{1,0:T(8,128)(2,1)S(1)}, u32[]{:S(2)}, u32[]{:S(2)}) collective-permute-start(bf16[448,256]{1,0:T(8,128)(2,1)S(1)} %fusion), channel_id=1, source_target_pairs={{0,4},{4,0},{8,12},{12,8},{16,20},{20,16},{24,28},{28,24},{1,5},{5... | collective-permute-start | bytes 688136 | tf_op jit(solution)/shard_map/ppermute | solution.py:383
  75.8 5.5 %collective-permute-done.5 = bf16[448,256]{1,0:T(8,128)(2,1)S(1)} collective-permute-done((bf16[448,256]{1,0:T(8,128)(2,1)S(1)}, bf16[448,256]{1,0:T(8,128)(2,1)S(1)}, u32[]{:S(2)}, u32[]{:S(2)}) %collective-permute-start.5) | collective-permute-done | bytes 229408 | tf_op jit(solution)/shard_map/ppermute | solution.py:383
  81.3 1.1 bitcast_add_fusion
  82.3 0.0 copy-start.14
  82.4 0.8 copy-done.14
  83.1 2.9 %collective-permute-start.6 = (bf16[224,256]{1,0:T(8,128)(2,1)S(1)}, bf16[224,256]{1,0:T(8,128)(2,1)}, u32[]{:S(2)}, u32[]{:S(2)}) collective-permute-start(bf16[224,256]{1,0:T(8,128)(2,1)S(1)} %fusion.1), channel_id=1, source_target_pairs={{0,8},{4,12},{8,0},{12,4},{16,24},{20,28},{24,16},{28,20},{1,9},{5... | collective-permute-start | bytes 344072 | tf_op jit(solution)/shard_map/ppermute | solution.py:383
  86.0 1.5 %collective-permute-start.8 = (bf16[588,512]{1,0:T(8,128)(2,1)}, bf16[588,512]{1,0:T(8,128)(2,1)S(1)}, u32[]{:S(2)}, u32[]{:S(2)}) collective-permute-start(bf16[588,512]{1,0:T(8,128)(2,1)} %copy-done.11), channel_id=1, source_target_pairs={{0,2},{1,3},{2,0},{3,1},{4,6},{5,7},{6,4},{7,5},{8,10},{9,11},{10,... | collective-permute-start | bytes 1806344 | tf_op jit(solution)/shard_map/ppermute | solution.py:383
  87.6 1.4 collective-permute-done.6
  88.9 1.0 bitcast_add_fusion.1
  89.9 0.6 fusion.3
  90.6 3.0 %collective-permute-start.7 = (bf16[112,256]{1,0:T(8,128)(2,1)}, bf16[112,256]{1,0:T(8,128)(2,1)}, u32[]{:S(2)}, u32[]{:S(2)}) collective-permute-start(bf16[112,256]{1,0:T(8,128)(2,1)} %fusion.3), channel_id=1, source_target_pairs={{0,16},{4,20},{8,24},{12,28},{16,0},{20,4},{24,8},{28,12},{1,17},{... | collective-permute-start | bytes 172040 | tf_op jit(solution)/shard_map/ppermute | solution.py:383
  93.6 2.5 %collective-permute-done.7 = bf16[112,256]{1,0:T(8,128)(2,1)} collective-permute-done((bf16[112,256]{1,0:T(8,128)(2,1)}, bf16[112,256]{1,0:T(8,128)(2,1)}, u32[]{:S(2)}, u32[]{:S(2)}) %collective-permute-start.7) | collective-permute-done | bytes 57376 | tf_op jit(solution)/shard_map/ppermute | solution.py:383
  96.1 1.5 %fusion.2 = bf16[112,256]{1,0:T(8,128)(2,1)} fusion(bf16[112,256]{1,0:T(8,128)(2,1)} %collective-permute-done.7, f32[2,112,256]{2,1,0:T(8,128)S(1)} %bitcast.33, s32[]{:T(128)S(6)} %select_n.95), kind=kLoop, calls=%fused_computation.10 | loop fusion | flops 86016 | bytes 229380 | tf_op jit(solution)/shard_map/convert_element_type | solution.py:525
  97.5 2.8 %collective-permute-done.8.refs_2_ = bf16[588,512]{1,0:T(8,128)(2,1)S(1)} collective-permute-done((bf16[588,512]{1,0:T(8,128)(2,1)}, bf16[588,512]{1,0:T(8,128)(2,1)S(1)}, u32[]{:S(2)}, u32[]{:S(2)}) %collective-permute-start.8) | collective-permute-done | bytes 602144 | tf_op jit(solution)/shard_map/ppermute | solution.py:383
  100.4 2.6 %collective-permute-start.9 = (bf16[112,256]{1,0:T(8,128)(2,1)}, bf16[112,256]{1,0:T(8,128)(2,1)S(1)}, u32[]{:S(2)}, u32[]{:S(2)}) collective-permute-start(bf16[112,256]{1,0:T(8,128)(2,1)} %fusion.2), channel_id=1, source_target_pairs={{0,16},{4,20},{8,24},{12,28},{16,0},{20,4},{24,8},{28,12},{1,17},{... | collective-permute-start | bytes 172040 | tf_op jit(solution)/shard_map/ppermute | solution.py:383
  103.0 3.1 %collective-permute-done.9 = bf16[112,256]{1,0:T(8,128)(2,1)S(1)} collective-permute-done((bf16[112,256]{1,0:T(8,128)(2,1)}, bf16[112,256]{1,0:T(8,128)(2,1)S(1)}, u32[]{:S(2)}, u32[]{:S(2)}) %collective-permute-start.9) | collective-permute-done | bytes 57376 | tf_op jit(solution)/shard_map/ppermute | solution.py:383
  106.1 0.9 maximum_select_fusion.2
  107.0 0.0 copy-start.15
  107.1 0.1 collective-permute-start.10
  107.1 0.6 copy-done.15
  107.7 4.3 %collective-permute-done.10 = bf16[224,256]{1,0:T(8,128)(2,1)} collective-permute-done((bf16[224,256]{1,0:T(8,128)(2,1)S(1)}, bf16[224,256]{1,0:T(8,128)(2,1)}, u32[]{:S(2)}, u32[]{:S(2)}) %collective-permute-start.10) | collective-permute-done | bytes 114720 | tf_op jit(solution)/shard_map/ppermute | solution.py:383
  112.0 1.1 maximum_select_fusion.1
  113.1 0.6 collective-permute-start.11
  113.7 0.1 pad_add_fusion.3.at_ref
  113.8 4.7 %shard_map.74 = (bf16[588,512]{1,0:T(8,128)(2,1)S(1)}, bf16[588,512]{1,0:T(8,128)(2,1)}) custom-call(s32[2]{0:T(128)S(1)} %pad_add_fusion.3.at_ref, f32[1,2560]{1,0:T(1,128)S(1)} %reshape.32.node_ref, bf16[2624,256]{1,0:T(8,128)(2,1)S(1)} %copy-done.1, bf16[2560,256]{1,0:T(8,128)(2,1)S(1)} %get-tuple-element.57.image_ref), custom_call_target="tpu_custom_call" | custom-call | flops 1048576 | bytes 1024 | tf_op jit(solution)/shard_map/pallas_call | solution.py:480
  118.5 0.8 copy-done.6
  119.3 0.0 collective-permute-start.15
  119.3 0.0 collective-permute-done.11
  119.3 1.2 maximum_select_fusion.q0_ref
  120.6 1.6 %collective-permute-start.14 = (bf16[896,256]{1,0:T(8,128)(2,1)S(1)}, bf16[896,256]{1,0:T(8,128)(2,1)S(1)}, u32[]{:S(2)}, u32[]{:S(2)}) collective-permute-start(bf16[896,256]{1,0:T(8,128)(2,1)S(1)} %maximum_select_fusion.q0_ref), channel_id=1, source_target_pairs={{0,2},{1,3},{2,0},{3,1},{4,6},{5,7},{6,4},{7,5},{8,10},{9,11},{10,... | collective-permute-start | bytes 1376264 | tf_op jit(solution)/shard_map/ppermute | solution.py:383
  122.1 0.2 collective-permute-start.13
  122.4 11.2 %collective-permute-done.14.q2_ref = bf16[896,256]{1,0:T(8,128)(2,1)S(1)} collective-permute-done((bf16[896,256]{1,0:T(8,128)(2,1)S(1)}, bf16[896,256]{1,0:T(8,128)(2,1)S(1)}, u32[]{:S(2)}, u32[]{:S(2)}) %collective-permute-start.14) | collective-permute-done | bytes 458784 | tf_op jit(solution)/shard_map/ppermute | solution.py:383
  133.6 1.8 %collective-permute-done.16.q3_ref = bf16[896,256]{1,0:T(8,128)(2,1)S(1)} collective-permute-done((bf16[896,256]{1,0:T(8,128)(2,1)S(1)}, bf16[896,256]{1,0:T(8,128)(2,1)S(1)}, u32[]{:S(2)}, u32[]{:S(2)}) %collective-permute-start.16) | collective-permute-done | bytes 458784 | tf_op jit(solution)/shard_map/ppermute | solution.py:383
  135.4 1.1 copy-done.7
  136.4 4.9 %shard_map.75 = (f32[588,1024]{1,0:T(8,128)}, bf16[1024,1024]{1,0:T(8,128)(2,1)}) custom-call(s32[1]{0:T(128)} %bitcast.place_ref, bf16[896,256]{1,0:T(8,128)(2,1)S(1)} %maximum_select_fusion.q0_ref, bf16[896,256]{1,0:T(8,128)(2,1)S(1)} %collective-permute-done.13.q1_ref, bf16[896,256]{1,0:T(8,128)(2,1)S(1)} %collective-permute-done.14.q2_ref, ...), custom_call_target="tpu_custom_call" | custom-call | tf_op jit(solution)/shard_map/pallas_call | solution.py:537
  (26 shorter events, 0.1 us)
Async XLA Ops:
  1.3 1.3 copy-start.4
  2.6 0.7 copy-start.8
  3.8 7.0 %copy-start.5 = (bf16[2352,256]{1,0:T(8,128)(2,1)S(1)}, bf16[2352,256]{1,0:T(8,128)(2,1)}, u32[]{:S(2)}) copy-start(bf16[2352,256]{1,0:T(8,128)(2,1)} %raw_ref.1) | copy-start | bytes 3612676
  3.8 7.0 %copy-start.9 = (s32[49]{0:T(128)S(1)}, s32[49]{0:T(128)}, u32[]{:S(2)}) copy-start(s32[49]{0:T(128)} %param.9) | copy-start | bytes 592
  3.8 7.0 %copy-start.12 = (s32[8,343]{1,0:T(8,128)S(1)}, s32[8,343]{1,0:T(8,128)}, u32[]{:S(2)}) copy-start(s32[8,343]{1,0:T(8,128)} %conn_ref.1) | copy-start | bytes 32932
  3.8 7.0 %collective-permute-start = (bf16[80,256]{1,0:T(8,128)(2,1)S(1)}, bf16[80,256]{1,0:T(8,128)(2,1)S(1)}, u32[]{:S(2)}, u32[]{:S(2)}) collective-permute-start(bf16[80,256]{1,0:T(8,128)(2,1)S(1)} %shard_map.68), channel_id=1, source_target_pairs={{4,0},{8,4},{12,8},{16,12},{20,16},{24,20},{28,24},{5,1},{9,5},{13... | collective-permute-start | bytes 122888 | tf_op jit(solution)/shard_map/ppermute | solution.py:388
  30.0 1.1 copy-start.13
  31.1 12.0 %collective-permute-start.1 = (bf16[6,64,256]{2,1,0:T(8,128)(2,1)S(1)}, bf16[6,64,256]{2,1,0:T(8,128)(2,1)S(1)}, u32[]{:S(2)}, u32[]{:S(2)}) collective-permute-start(bf16[6,64,256]{2,1,0:T(8,128)(2,1)S(1)} %get-tuple-element.36), channel_id=1, source_target_pairs={{0,4},{4,8},{8,12},{12,16},{16,20},{20,24},{24,28},{1,5},{5,9},{9,... | collective-permute-start | bytes 589832 | tf_op jit(solution)/shard_map/ppermute | solution.py:388
  35.9 7.2 %collective-permute-start.2 = (bf16[5,64,256]{2,1,0:T(8,128)(2,1)S(1)}, bf16[5,64,256]{2,1,0:T(8,128)(2,1)S(1)}, u32[]{:S(2)}, u32[]{:S(2)}) collective-permute-start(bf16[5,64,256]{2,1,0:T(8,128)(2,1)S(1)} %get-tuple-element.37), channel_id=1, source_target_pairs={{4,0},{8,4},{12,8},{16,12},{20,16},{24,20},{28,24},{5,1},{9,5},{13... | collective-permute-start | bytes 491528 | tf_op jit(solution)/shard_map/ppermute | solution.py:388
  52.7 6.9 %collective-permute-start.3 = (bf16[2,1344,256]{2,1,0:T(8,128)(2,1)}, bf16[2,1344,256]{2,1,0:T(8,128)(2,1)}, u32[]{:S(2)}, u32[]{:S(2)}) collective-permute-start(bf16[2,1344,256]{2,1,0:T(8,128)(2,1)} %get-tuple-element.40.w_ref), channel_id=1, source_target_pairs={{0,1},{1,0},{2,3},{3,2},{4,5},{5,4},{6,7},{7,6},{8,9},{9,8},{10,11... | collective-permute-start | bytes 4128776 | tf_op jit(solution)/shard_map/ppermute | solution.py:383
  52.7 17.8 %collective-permute-start.4 = (bf16[1344,256]{1,0:T(8,128)(2,1)S(1)}, bf16[1344,256]{1,0:T(8,128)(2,1)S(1)}, u32[]{:S(2)}, u32[]{:S(2)}) collective-permute-start(bf16[1344,256]{1,0:T(8,128)(2,1)S(1)} %get-tuple-element.41), channel_id=1, source_target_pairs={{0,2},{1,3},{2,0},{3,1},{4,6},{5,7},{6,4},{7,5},{8,10},{9,11},{10,... | collective-permute-start | bytes 2064392 | tf_op jit(solution)/shard_map/ppermute | solution.py:383
  54.4 1.3 copy-start
  55.8 3.9 %copy-start.2 = (bf16[2,1344,256]{2,1,0:T(8,128)(2,1)S(1)}, bf16[2,1344,256]{2,1,0:T(8,128)(2,1)}, u32[]{:S(2)}) copy-start(bf16[2,1344,256]{2,1,0:T(8,128)(2,1)} %get-tuple-element.40.w_ref) | copy-start | bytes 4128772
  59.6 2.8 %copy-start.10 = (bf16[588,512]{1,0:T(8,128)(2,1)}, bf16[588,512]{1,0:T(8,128)(2,1)S(1)}, u32[]{:S(2)}) copy-start(bf16[588,512]{1,0:T(8,128)(2,1)S(1)} %get-tuple-element.54) | copy-start | bytes 1806340
  59.6 2.8 %copy-start.11 = (bf16[588,512]{1,0:T(8,128)(2,1)}, bf16[588,512]{1,0:T(8,128)(2,1)S(1)}, u32[]{:S(2)}) copy-start(bf16[588,512]{1,0:T(8,128)(2,1)S(1)} %get-tuple-element.50) | copy-start | bytes 1806340
  72.5 0.9 copy-start.3
  73.5 7.8 %collective-permute-start.5 = (bf16[448,256]{1,0:T(8,128)(2,1)S(1)}, bf16[448,256]{1,0:T(8,128)(2,1)S(1)}, u32[]{:S(2)}, u32[]{:S(2)}) collective-permute-start(bf16[448,256]{1,0:T(8,128)(2,1)S(1)} %fusion), channel_id=1, source_target_pairs={{0,4},{4,0},{8,12},{12,8},{16,20},{20,16},{24,28},{28,24},{1,5},{5... | collective-permute-start | bytes 688136 | tf_op jit(solution)/shard_map/ppermute | solution.py:383
  75.8 38.0 %copy-start.1 = (bf16[2624,256]{1,0:T(8,128)(2,1)S(1)}, bf16[2624,256]{1,0:T(8,128)(2,1)}, u32[]{:S(2)}) copy-start(bf16[2624,256]{1,0:T(8,128)(2,1)} %get-tuple-element.56.x_ref) | copy-start | bytes 4030468
  82.3 0.8 copy-start.14
  83.1 5.8 %collective-permute-start.6 = (bf16[224,256]{1,0:T(8,128)(2,1)S(1)}, bf16[224,256]{1,0:T(8,128)(2,1)}, u32[]{:S(2)}, u32[]{:S(2)}) collective-permute-start(bf16[224,256]{1,0:T(8,128)(2,1)S(1)} %fusion.1), channel_id=1, source_target_pairs={{0,8},{4,12},{8,0},{12,4},{16,24},{20,28},{24,16},{28,20},{1,9},{5... | collective-permute-start | bytes 344072 | tf_op jit(solution)/shard_map/ppermute | solution.py:383
  86.0 14.3 %collective-permute-start.8 = (bf16[588,512]{1,0:T(8,128)(2,1)}, bf16[588,512]{1,0:T(8,128)(2,1)S(1)}, u32[]{:S(2)}, u32[]{:S(2)}) collective-permute-start(bf16[588,512]{1,0:T(8,128)(2,1)} %copy-done.11), channel_id=1, source_target_pairs={{0,2},{1,3},{2,0},{3,1},{4,6},{5,7},{6,4},{7,5},{8,10},{9,11},{10,... | collective-permute-start | bytes 1806344 | tf_op jit(solution)/shard_map/ppermute | solution.py:383
  90.6 5.5 %collective-permute-start.7 = (bf16[112,256]{1,0:T(8,128)(2,1)}, bf16[112,256]{1,0:T(8,128)(2,1)}, u32[]{:S(2)}, u32[]{:S(2)}) collective-permute-start(bf16[112,256]{1,0:T(8,128)(2,1)} %fusion.3), channel_id=1, source_target_pairs={{0,16},{4,20},{8,24},{12,28},{16,0},{20,4},{24,8},{28,12},{1,17},{... | collective-permute-start | bytes 172040 | tf_op jit(solution)/shard_map/ppermute | solution.py:383
  100.4 5.7 %collective-permute-start.9 = (bf16[112,256]{1,0:T(8,128)(2,1)}, bf16[112,256]{1,0:T(8,128)(2,1)S(1)}, u32[]{:S(2)}, u32[]{:S(2)}) collective-permute-start(bf16[112,256]{1,0:T(8,128)(2,1)} %fusion.2), channel_id=1, source_target_pairs={{0,16},{4,20},{8,24},{12,28},{16,0},{20,4},{24,8},{28,12},{1,17},{... | collective-permute-start | bytes 172040 | tf_op jit(solution)/shard_map/ppermute | solution.py:383
  103.0 17.6 %collective-permute-start.12 = (bf16[588,512]{1,0:T(8,128)(2,1)}, bf16[588,512]{1,0:T(8,128)(2,1)}, u32[]{:S(2)}, u32[]{:S(2)}) collective-permute-start(bf16[588,512]{1,0:T(8,128)(2,1)} %copy-done.10), channel_id=1, source_target_pairs={{0,3},{1,2},{2,1},{3,0},{4,7},{5,6},{6,5},{7,4},{8,11},{9,10},{10,... | collective-permute-start | bytes 1806344 | tf_op jit(solution)/shard_map/ppermute | solution.py:383
  107.0 0.6 copy-start.15
  107.1 5.0 %collective-permute-start.10 = (bf16[224,256]{1,0:T(8,128)(2,1)S(1)}, bf16[224,256]{1,0:T(8,128)(2,1)}, u32[]{:S(2)}, u32[]{:S(2)}) collective-permute-start(bf16[224,256]{1,0:T(8,128)(2,1)S(1)} %maximum_select_fusion.2), channel_id=1, source_target_pairs={{0,8},{4,12},{8,0},{12,4},{16,24},{20,28},{24,16},{28,20},{1,9},{5... | collective-permute-start | bytes 344072 | tf_op jit(solution)/shard_map/ppermute | solution.py:383
  113.1 6.2 %collective-permute-start.11 = (bf16[448,256]{1,0:T(8,128)(2,1)S(1)}, bf16[448,256]{1,0:T(8,128)(2,1)}, u32[]{:S(2)}, u32[]{:S(2)}) collective-permute-start(bf16[448,256]{1,0:T(8,128)(2,1)S(1)} %maximum_select_fusion.1), channel_id=1, source_target_pairs={{0,4},{4,0},{8,12},{12,8},{16,20},{20,16},{24,28},{28,24},{1,5},{5... | collective-permute-start | bytes 688136 | tf_op jit(solution)/shard_map/ppermute | solution.py:383
  118.5 0.8 copy-start.6
  119.3 3.0 %collective-permute-start.15 = (bf16[588,512]{1,0:T(8,128)(2,1)}, bf16[588,512]{1,0:T(8,128)(2,1)S(1)}, u32[]{:S(2)}, u32[]{:S(2)}) collective-permute-start(bf16[588,512]{1,0:T(8,128)(2,1)} %get-tuple-element.58), channel_id=1, source_target_pairs={{0,1},{1,0},{2,3},{3,2},{4,5},{5,4},{6,7},{7,6},{8,9},{9,8},{10,11... | collective-permute-start | bytes 1806344 | tf_op jit(solution)/shard_map/ppermute | solution.py:383
  120.6 13.0 %collective-permute-start.14 = (bf16[896,256]{1,0:T(8,128)(2,1)S(1)}, bf16[896,256]{1,0:T(8,128)(2,1)S(1)}, u32[]{:S(2)}, u32[]{:S(2)}) collective-permute-start(bf16[896,256]{1,0:T(8,128)(2,1)S(1)} %maximum_select_fusion.q0_ref), channel_id=1, source_target_pairs={{0,2},{1,3},{2,0},{3,1},{4,6},{5,7},{6,4},{7,5},{8,10},{9,11},{10,... | collective-permute-start | bytes 1376264 | tf_op jit(solution)/shard_map/ppermute | solution.py:383
  122.1 11.4 %collective-permute-start.13 = (bf16[896,256]{1,0:T(8,128)(2,1)S(1)}, bf16[896,256]{1,0:T(8,128)(2,1)S(1)}, u32[]{:S(2)}, u32[]{:S(2)}) collective-permute-start(bf16[896,256]{1,0:T(8,128)(2,1)S(1)} %maximum_select_fusion.q0_ref), channel_id=1, source_target_pairs={{0,1},{1,0},{2,3},{3,2},{4,5},{5,4},{6,7},{7,6},{8,9},{9,8},{10,11... | collective-permute-start | bytes 1376264 | tf_op jit(solution)/shard_map/ppermute | solution.py:383
  133.5 1.8 %collective-permute-start.16 = (bf16[896,256]{1,0:T(8,128)(2,1)S(1)}, bf16[896,256]{1,0:T(8,128)(2,1)S(1)}, u32[]{:S(2)}, u32[]{:S(2)}) collective-permute-start(bf16[896,256]{1,0:T(8,128)(2,1)S(1)} %collective-permute-done.14.q2_ref), channel_id=1, source_target_pairs={{0,1},{1,0},{2,3},{3,2},{4,5},{5,4},{6,7},{7,6},{8,9},{9,8},{10,11... | collective-permute-start | bytes 1376264 | tf_op jit(solution)/shard_map/ppermute | solution.py:383
  135.4 1.1 copy-start.7

commit v7 on v6

--- a/solution.py
+++ b/solution.py
@@ -256,7 +256,7 @@
 
 def forced_kernel(
     fp, place_ref, v_ref, ghost_ref, first_ref, own_ref, fromleft_ref, fromright_ref, h_ref, pot_ref,
-    x_ref, image_ref, w_ref, slab_ref, a_ref, b_ref, c_ref,
+    x_ref, face_image_ref, slab_ref, a_ref, b_ref, c_ref,
 ):
     cells, cp = h_ref.shape[:2]
     stride = cp - fp
@@ -265,67 +265,52 @@
     half = cells // 2
     extra = own_ref.shape[1] - DEGREE - 1
     potg = to_col(jnp.sum(ghost_ref[fp:].astype(F32), axis=0, keepdims=True)[:, :fp], fp)
-    histories = []
-    last_image = None
+    nothing = jnp.zeros((fp, width), BF16)
+    sides = []
     for side, (got_ref, pot, start) in enumerate(
         ((fromleft_ref, pot_ref[:fp], v_ref[:fp]), (fromright_ref, potg, ghost_ref[:fp]))
     ):
         theirs = load_matrices(got_ref, got_ref.shape[0] - extra, DEGREE, fp, width)
         ours = load_matrices(own_ref.at[side], DEGREE + 1, DEGREE, fp, width)
         mats = [a + b for a, b in zip(theirs, ours)]
-        mats = [split(m) for m in mats]
-        values = [start]
-        for k in range(DEGREE + 1 if side == 0 else DEGREE):
+        line = jnp.concatenate(mats[::-1], axis=1)
+        sides.append((got_ref, pot, jnp.concatenate(split(line), axis=0), [start]))
+    for k in range(DEGREE + 1):
+        for side, (got_ref, pot, line, values) in enumerate(sides):
+            if side == 1 and k == DEGREE:
+                continue
             h = own_ref[side, k] + got_ref[k].astype(F32)
-            for m in range(1, k + 1):
-                h = h + mul(mats[k - m][0], values[m]) + mul(mats[k - m][1], values[m])
+            if k > 0:
+                past = [values[m] if m >= 1 else nothing for m in range(k - DEGREE + 1, k + 1)]
+                both = mul(line, jnp.concatenate(past, axis=0))
+                h = h + both[:fp] + both[fp:]
             now = values[k].astype(F32)
             h = h + pot * now
             if k == DEGREE:
-                last_image = h
-                break
+                face_image_ref[...] = h
+                continue
             value = advance(h, now, None if k == 0 else values[k - 1].astype(F32))
             if side == 1:
                 value = jnp.where(place_ref[0] == 1, 0.0, value)
             values.append(value.astype(BF16))
-        histories.append(values)
-    low, high = histories
+    low, high = sides[0][3], sides[1][3]
     a_ref[:fp] = low[1]
     a_ref[fp:total] = first_ref[fp:]
     a_ref[total:] = high[1]
-    refs = [None, a_ref, b_ref, c_ref, a_ref]
-    for k in range(1, DEGREE + 1):
+    refs = [v_ref, a_ref, b_ref, c_ref, x_ref]
+    for k in range(1, DEGREE):
         now_ref = refs[k]
 
         def emit(c, rows, lower, carry, k=k, now_ref=now_ref):
             at = slice(c * stride, (c + 1) * stride)
             now = now_ref[at].astype(F32)
-            image = rows + pot_ref[at] * now
-            if k == DEGREE:
-                out = image.astype(BF16)
-                part, at_w = divmod(c, half)
-                w_ref[part, at_w * stride : (at_w + 1) * stride] = out
-                if c == half:
-                    w_ref[0, half * stride :] = carry.astype(BF16)
-                    w_ref[1, :fp] = (lower + pot_ref[c * stride : c * stride + fp] * now[:fp]).astype(BF16)
-                if c == 0:
-                    out = jnp.concatenate([last_image.astype(BF16), out[fp:]], axis=0)
-                image_ref[at] = out
-                return
-            before = (v_ref if k == 1 else refs[k - 1])[at].astype(F32)
-            value = advance(image, now, before).astype(BF16)
+            value = advance(rows + pot_ref[at] * now, now, refs[k - 1][at].astype(F32)).astype(BF16)
             if c == 0:
                 value = jnp.concatenate([low[k + 1], value[fp:]], axis=0)
             refs[k + 1][at] = value
-            if k + 1 == DEGREE:
-                x_ref[at] = value
-
-        end = sweep(h_ref, now_ref, fp, emit)
-        if k < DEGREE:
-            refs[k + 1][total:] = high[k + 1]
-        else:
-            w_ref[1, half * stride :] = end.astype(BF16)
-    x_ref[total:] = high[DEGREE]
+
+        sweep(h_ref, now_ref, fp, emit)
+        refs[k + 1][total:] = high[k + 1]
 
     @pl.when(place_ref[1] == 0)
     def _():
@@ -334,6 +319,30 @@
     @pl.when(place_ref[1] == 1)
     def _():
         slab_ref[...] = x_ref[: half * stride + fp]
+
+
+def image_kernel(fp, place_ref, x_ref, face_image_ref, h_ref, pot_ref, image_ref, w_ref, first_ref, second_ref):
+    cells, cp = h_ref.shape[:2]
+    stride = cp - fp
+    half = cells // 2
+
+    def emit(c, rows, lower, carry):
+        at = slice(c * stride, (c + 1) * stride)
+        now = x_ref[at].astype(F32)
+        out = (rows + pot_ref[at] * now).astype(BF16)
+        part, at_w = divmod(c, half)
+        w_ref[part, at_w * stride : (at_w + 1) * stride] = out
+        if c == half:
+            w_ref[0, half * stride :] = carry.astype(BF16)
+            w_ref[1, :fp] = (lower + pot_ref[c * stride : c * stride + fp] * now[:fp]).astype(BF16)
+        if c == 0:
+            out = jnp.concatenate([face_image_ref[...].astype(BF16), out[fp:]], axis=0)
+        image_ref[at] = out
+
+    w_ref[1, half * stride :] = sweep(h_ref, x_ref, fp, emit).astype(BF16)
+    n = first_ref.shape[0]
+    first_ref[...] = w_ref[place_ref[1], :n]
+    second_ref[...] = w_ref[place_ref[1], n:]
 
 
 def back_kernel(node_ref, x_ref, image_ref, out_ref):
@@ -401,14 +410,37 @@
 
     @pl.when(core_ref[0] == 0)
     def _():
-        out_ref[width:] = sum(tmul(own[i][:, :half], other_ref[i]) for i in range(2)) * scale
+        out_ref[width:] = sum(tmul(w_ref[i, :, :half], other_ref[at[i]]) for i in range(2)) * scale
 
     @pl.when(core_ref[0] == 1)
     def _():
-        out_ref[width:] = sum(tmul(other_ref[i, :, half:], own[i]) for i in range(2)) * scale
-
-
-def far_gram_kernel(scale, place_ref, w_ref, other_ref, far_ref, near_ref, out_ref):
+        out_ref[width:] = sum(tmul(other_ref[at[i], half:], w_ref[i]) for i in range(2)) * scale
+
+
+def part_ways(sum_ref, mine, keep_ref, give_ref):
+    n = keep_ref.shape[0]
+    keep_ref[...] = sum_ref[pl.ds(pl.multiple_of(mine * n, 16), n)]
+    give_ref[...] = sum_ref[pl.ds(pl.multiple_of((1 - mine) * n, 16), n)].astype(BF16)
+
+
+def halve_kernel(step, bits_ref, keep_ref, got_ref, *refs):
+    total = keep_ref[...] + got_ref[...].astype(F32)
+    if len(refs) == 1:
+        refs[0][...] = total.astype(BF16)
+        return
+    *outs, sum_ref = refs
+    sum_ref[...] = total
+    part_ways(sum_ref, bits_ref[step], *outs)
+
+
+def join_kernel(step, bits_ref, own_ref, got_ref, out_ref):
+    n = own_ref.shape[0]
+    mine = bits_ref[step]
+    out_ref[pl.ds(pl.multiple_of(mine * n, 16), n)] = own_ref[...]
+    out_ref[pl.ds(pl.multiple_of((1 - mine) * n, 16), n)] = got_ref[...]
+
+
+def far_gram_kernel(scale, bits_ref, place_ref, w_ref, first_ref, second_ref, far_ref, near_ref, keep_ref, give_ref, out_ref):
     width = w_ref.shape[2]
     near = near_ref.shape[0]
     side, core = place_ref[0], place_ref[1]
@@ -417,7 +449,9 @@
     mine = pl.multiple_of(near + core * width, width // 2)
     other = pl.multiple_of(near + (1 - core) * width, width // 2)
     out_ref[pl.ds(mine, width)] = tmul(w_ref[side], far) * scale
-    out_ref[pl.ds(other, width)] = tmul(other_ref[side], far) * scale
+    n = first_ref.shape[0]
+    out_ref[pl.ds(other, width)] = (tmul(first_ref[...], far[:n]) + tmul(second_ref[...], far[n:])) * scale
+    part_ways(out_ref, bits_ref[0], keep_ref, give_ref)
 
 
 def paired_residual_kernel(place_ref, q0_ref, q1_ref, q2_ref, q3_ref, *refs):
@@ -463,7 +497,7 @@
         out_ref[:, at] = row_refs[k][:, width:].astype(F32) - mul(x, p)
 
 
-def paired_tail(x_own, image, w_own, give, node_row, o, d, dom, nodes):
+def paired_tail(x_own, image, w_own, w_side, give, node_row, o, d, dom, nodes):
     slab, width = w_own.shape[1:]
     orb = 4
     rows = nodes // orb
@@ -488,7 +522,8 @@
         )(jnp.stack([jnp.bitwise_xor(o, first), jnp.bitwise_xor(o, second)]), node_row, x_own, image)
 
     cuts = back(2, 3, x_own, image)
-    w_other = swap(w_own, "orb", 1)
+    x_other = swap(x_own, "orb", 1)
+    w_other = [swap(w, "orb", 1) for w in w_side]
     top = width + width // 2
     near = pl.pallas_call(
         functools.partial(near_gram_kernel, scale),
@@ -496,38 +531,57 @@
         out_shape=sds((top, width), F32),
         compiler_params=params(),
         cost_estimate=pl.CostEstimate(flops=1 << 20, bytes_accessed=1 << 10, transcendentals=0),
-    )(core.reshape(1), x_own, w_own, w_other)
-    far, near, *cuts = lax.optimization_barrier((far, near, *cuts))
+    )(core.reshape(1), x_own, w_own, x_other)
+    far, near, *cuts, w_other[0], w_other[1] = lax.optimization_barrier((far, near, *cuts, *w_other))
     row2 = swap(cuts[0], "orb", 2)
     cut3 = cuts[1]
-    share = pl.pallas_call(
+    steps = (dom - 1).bit_length()
+    bits = jnp.stack([(d // (1 << i)) % 2 for i in range(steps)])
+    little = pl.CostEstimate(flops=1 << 10, bytes_accessed=1 << 10, transcendentals=0)
+    count = top + 2 * width
+    keep, give = pl.pallas_call(
         functools.partial(far_gram_kernel, scale),
-        in_specs=[smem] + [vmem] * 4,
-        out_shape=sds((top + 2 * width, width), F32),
+        in_specs=[smem] * 2 + [vmem] * 5,
+        out_shape=[sds((count // 2, width), F32), sds((count // 2, width), BF16)],
+        scratch_shapes=[pltpu.VMEM((count, width), F32)],
         compiler_params=params(),
         cost_estimate=pl.CostEstimate(flops=8 * slab * width * width, bytes_accessed=4 << 20, transcendentals=0),
-    )(jnp.stack([side, core]), w_own, w_other, far, near)
-
-    bits = []
-    bit = 1
-    while bit < dom:
-        mine = (d // bit) % 2
-        share = share.reshape(2, share.shape[0] // 2, width)
-        keep = lax.dynamic_index_in_dim(share, mine, 0, keepdims=False)
-        give = lax.dynamic_index_in_dim(share, 1 - mine, 0, keepdims=False)
-        give = give.astype(BF16)
-        if bit == 1:
+    )(bits, jnp.stack([side, core]), w_own, *w_other, far, near)
+    row0 = cut1 = row3 = None
+    for i in range(steps):
+        if i == 0:
             x_own, image, give = lax.optimization_barrier((x_own, image, give))
             row0, cut1 = back(0, 1, x_own, image)
-        share = keep + swap(give, "dom", bit).astype(F32)
-        bits.append((bit, mine))
-        bit *= 2
-    share, row2, cut3 = lax.optimization_barrier((share.astype(BF16), row2, cut3))
-    row3 = swap(cut3, "orb", 3)
-    for bit, mine in reversed(bits):
-        got = swap(share, "dom", bit)
-        share = jnp.where(mine == 0, jnp.concatenate([share, got], axis=0), jnp.concatenate([got, share], axis=0))
-    share, row2, row3 = lax.optimization_barrier((share, row2, row3))
+        got = swap(give, "dom", 1 << i)
+        n = keep.shape[0]
+        last = i == steps - 1
+        outs = pl.pallas_call(
+            functools.partial(halve_kernel, i + 1),
+            in_specs=[smem] + [vmem] * 2,
+            out_shape=[sds((n, width), BF16)] if last else [sds((n // 2, width), F32), sds((n // 2, width), BF16)],
+            scratch_shapes=[] if last else [pltpu.VMEM((n, width), F32)],
+            compiler_params=params(),
+            cost_estimate=little,
+        )(bits, keep, got)
+        outs = list(outs)
+        if i == 1:
+            outs[-1], row2, cut3 = lax.optimization_barrier((outs[-1], row2, cut3))
+            row3 = swap(cut3, "orb", 3)
+        if last:
+            share = outs[0]
+        else:
+            keep, give = outs
+    for i in reversed(range(steps)):
+        got = swap(share, "dom", 1 << i)
+        share = pl.pallas_call(
+            functools.partial(join_kernel, i),
+            in_specs=[smem] + [vmem] * 2,
+            out_shape=sds((2 * share.shape[0], width), BF16),
+            compiler_params=params(),
+            cost_estimate=little,
+        )(bits, share, got)
+        if i == 1:
+            share, row3 = lax.optimization_barrier((share, row3))
     q2 = swap(share, "orb", 2)
     q1 = swap(share, "orb", 1)
     row1 = swap(cut1, "orb", 1)
@@ -591,22 +645,28 @@
     vmem = pl.BlockSpec(memory_space=pltpu.VMEM)
     slab = cells // 2 * stride + fp
     place = jnp.stack([(d == dom - 1).astype(jnp.int32), (o // 2) % 2])
-    x_own, image, w_own, give = pl.pallas_call(
+    x_own, face_image, give = pl.pallas_call(
         functools.partial(forced_kernel, fp),
         in_specs=[pl.BlockSpec(memory_space=pltpu.SMEM)] + [vmem] * 8,
         out_shape=[
             sds((total + fp, width), BF16),
-            sds((total, width), BF16),
-            sds((2, slab, width), BF16),
+            sds((fp, width), F32),
             sds((slab, width), BF16),
         ],
         scratch_shapes=[ext, ext, ext],
         compiler_params=params(),
         cost_estimate=cost,
     )(place, y, ghost, first, own, from_left, from_right, hcan, pot)
+    image, w_own, *w_side = pl.pallas_call(
+        functools.partial(image_kernel, fp),
+        in_specs=[pl.BlockSpec(memory_space=pltpu.SMEM)] + [vmem] * 4,
+        out_shape=[sds((total, width), BF16), sds((2, slab, width), BF16)] + [sds((slab // 2, width), BF16)] * 2,
+        compiler_params=params(),
+        cost_estimate=pl.CostEstimate(flops=1 << 20, bytes_accessed=1 << 10, transcendentals=0),
+    )(place, x_own, face_image, hcan, pot)
 
     if orb == 4 and dom % 8 == 0:
-        return paired_tail(x_own, image, w_own, give, node_row, o, d, dom, nodes)
+        return paired_tail(x_own, image, w_own, w_side, give, node_row, o, d, dom, nodes)
     cut = pl.pallas_call(
         back_kernel,
         grid=(orb,),

time: 142 us -> 132 us (0.930)
  other arithmetic: 7.05 us -> 0.41 us
  Pallas kernels: 47.4 us -> 54 us
  local copies, waits for them, and re-layouts: 13.2 us -> 6.79 us
  starting transfers between devices: 23.8 us -> 21.4 us
    pallas_call x0 -> x7, Pallas kernels: none -> 7.96 us  [the longest x1 4.52 us: body(): pl.pallas_call(functools.partial(image_kernel, fp), in_specs=[pl.BlockSpe...]
    unnamed x33 -> x17, local copies, waits for them, and re-layouts: 11.7 us -> 5.99 us
    select_n x3 -> x0, other arithmetic: 3.26 us -> none  [paired_tail(): jnp.where(mine == 0, jnp.concatenate([share, got], axis=0), jnp.concatena...]
    ppermute x14 -> x16, starting transfers between devices: 16.3 us -> 14 us  [swap(): lax.ppermute(block, axis, [(i, i ^ bit) for i in range(lax.axis_size(axis...]
    add x2 -> x0, other arithmetic: 2.08 us -> none  [paired_tail(): share = keep + swap(give, 'dom', bit).astype(F32)]
    pallas_call x1, Pallas kernels: 9.64 us -> 8.12 us  [body(): pl.pallas_call(functools.partial(forced_kernel, fp), in_specs=[pl.BlockSp...]
    convert_element_type x1 -> x0, other arithmetic: 1.45 us -> none  [paired_tail(): share.astype(BF16)]
    ppermute x14 -> x16, waiting for transfers between devices: 40.9 us -> 39.9 us  [swap(): lax.ppermute(block, axis, [(i, i ^ bit) for i in range(lax.axis_size(axis...]
  transfers between devices with their start and end apart: 17 -> 19, of which waited for: 11 -> 11; matrix products, arithmetic and copies ran while one was open for 7% -> 3% of each run, Pallas kernels for 8% -> 16%
where the time goes in v7:
time: 132 us; the launch traced here: 131 us
  Pallas kernels  54 us (41%)
  waiting for transfers between devices  48 us (36%)
  starting transfers between devices  21.4 us (16%)
  local copies, waits for them, and re-layouts  6.79 us (5%)
    ppermute x16, waiting for transfers between devices, swap(): lax.ppermute(block, axis, [(i, i ^ bit) for i in range(lax.axis_size(axis...  39.9 us
    pallas_call x1, Pallas kernels, body(): pl.pallas_call(functools.partial(free_kernel, fp, ip), out_shape=[sds((ce...  19.3 us
    ppermute x16, starting transfers between devices, swap(): lax.ppermute(block, axis, [(i, i ^ bit) for i in range(lax.axis_size(axis...  14 us
    pallas_call x2, Pallas kernels, back(): pl.pallas_call(back_pair_kernel, grid=(1,), in_specs=[smem, whole(1, tota...  8.47 us
    ppermute x3, waiting for transfers between devices, shift(): lax.ppermute(block, axis, [(i, i + distance) for i in range(n) if 0 <= i...  8.13 us
    pallas_call x1, Pallas kernels, body(): pl.pallas_call(functools.partial(forced_kernel, fp), in_specs=[pl.BlockSp...  8.12 us
    ppermute x3, starting transfers between devices, shift(): lax.ppermute(block, axis, [(i, i + distance) for i in range(n) if 0 <= i...  7.42 us
    unnamed x17, local copies, waits for them, and re-layouts  5.99 us
  transfers between devices with their start and end apart: 19, of which 11 were waited for; matrix products, arithmetic and copies ran while one was open for 3% of the time, Pallas kernels for 16%

profile of v7, /device:TPU:0, one launch (start us, length us, event | category | flops | bytes accessed | tf_op | source)
XLA Modules:
  0.0 131.5 jit_solution(12728118192329134967)
XLA Ops:
  0.6 0.7 reshape.19.pot_ref.potraw_ref
  1.3 1.3 copy-done.3
  2.6 0.7 copy-done.6
  3.3 0.5 shard_map.68
  3.8 0.0 copy-start.7
  3.8 1.3 collective-permute-start
  5.1 3.2 %copy.7.hraw_ref = bf16[8,343,343]{2,1,0:T(8,128)(2,1)} copy(bf16[8,343,343]{2,0,1:T(8,128)(2,1)} %param.7) | data formatting | bytes 3764768 | tf_op args[2]
  8.3 2.3 %collective-permute-done.ghost_ref = bf16[80,256]{1,0:T(8,128)(2,1)S(1)} collective-permute-done((bf16[80,256]{1,0:T(8,128)(2,1)S(1)}, bf16[80,256]{1,0:T(8,128)(2,1)S(1)}, u32[]{:S(2)}, u32[]{:S(2)}) %collective-permute-start) | collective-permute-done | bytes 40992 | tf_op jit(solution)/shard_map/ppermute | solution.py:397
  10.6 19.3 %shard_map.69 = (bf16[8,384,384]{2,1,0:T(8,128)(2,1)}, bf16[2560,256]{1,0:T(8,128)(2,1)S(1)}, f32[2560,1]{1,0:T(8,128)}, f32[8,1,320]{2,1,0:T(1,128)S(1)}, bf16[...) custom-call(s32[8,343]{1,0:T(8,128)S(1)} %copy-done.7, ...), custom_call_target="tpu_custom_call" | custom-call | flops 2415919104 | bytes 8388608 | tf_op jit(solution)/shard_map/pallas_call | solution.py:626
  30.0 4.8 %collective-permute-start.1 = (bf16[6,64,256]{2,1,0:T(8,128)(2,1)S(1)}, bf16[6,64,256]{2,1,0:T(8,128)(2,1)S(1)}, u32[]{:S(2)}, u32[]{:S(2)}) collective-permute-start(bf16[6,64,256]{2,1,0:T(8,128)(2,1)S(1)} %get-tuple-element.46), channel_id=1, source_target_pairs={{0,4},{4,8},{8,12},{12,16},{16,20},{20,24},{24,28},{1,5},{5,9},{9,... | collective-permute-start | bytes 589832 | tf_op jit(solution)/shard_map/ppermute | solution.py:397
  34.8 1.3 collective-permute-start.2
  36.2 0.1 pad_add_fusion.2.place_ref
  36.2 5.8 %collective-permute-done.2.fromright_ref = bf16[5,64,256]{2,1,0:T(8,128)(2,1)S(1)} collective-permute-done((bf16[5,64,256]{2,1,0:T(8,128)(2,1)S(1)}, bf16[5,64,256]{2,1,0:T(8,128)(2,1)S(1)}, u32[]{:S(2)}, u32[]{:S(2)}) %collective-permute-start.2) | collective-permute-done | bytes 163872 | tf_op jit(solution)/shard_map/ppermute | solution.py:397
  42.0 0.0 collective-permute-done.1.fromleft_ref
  42.0 8.1 %shard_map.70 = (bf16[2624,256]{1,0:T(8,128)(2,1)}, f32[64,256]{1,0:T(8,128)S(1)}, bf16[1344,256]{1,0:T(8,128)(2,1)}) custom-call(s32[2]{0:T(128)S(1)} %pad_add_fusion.2.place_ref, bf16[2560,256]{1,0:T(8,128)(2,1)S(1)} %get-tuple-element.43.v_ref, bf16[80,256]{1,0:T(8,128)(2,1)S(1)} %collective-permute-done.ghost_ref, ...), custom_call_target="tpu_custom_call" | custom-call | flops 2415919104 | bytes 8388608 | tf_op jit(solution)/shard_map/pallas_call | solution.py:648
  50.2 0.0 collective-permute-start.4
  50.2 1.5 %collective-permute-start.3 = (bf16[1344,256]{1,0:T(8,128)(2,1)}, bf16[1344,256]{1,0:T(8,128)(2,1)S(1)}, u32[]{:S(2)}, u32[]{:S(2)}) collective-permute-start(bf16[1344,256]{1,0:T(8,128)(2,1)} %get-tuple-element.53), channel_id=1, source_target_pairs={{0,2},{1,3},{2,0},{3,1},{4,6},{5,7},{6,4},{7,5},{8,10},{9,11},{10,... | collective-permute-start | bytes 2064392 | tf_op jit(solution)/shard_map/ppermute | solution.py:392
  51.7 4.5 %shard_map.71 = (bf16[2560,256]{1,0:T(8,128)(2,1)S(1)}, bf16[2,1344,256]{2,1,0:T(8,128)(2,1)}, bf16[672,256]{1,0:T(8,128)(2,1)}, bf16[672,256]{1,0:T(8,128)(2,1)}) custom-call(s32[2]{0:T(128)S(1)} %pad_add_fusion.2.place_ref, bf16[2624,256]{1,0:T(8,128)(2,1)} %get-tuple-element.76.x_ref, f32[64,256]{1,0:T(8,128)S(1)} %get-tuple-element.51.face_image_ref, ...), custom_call_target="tpu_custom_call" | custom-call | flops 1048576 | bytes 1024 | tf_op jit(solution)/shard_map/pallas_call | solution.py:660
  56.2 0.2 collective-permute-start.5
  56.4 0.3 collective-permute-start.6
  56.7 0.1 pad_add_fusion.3.at_ref
  56.8 0.1 reshape.20.node_ref
  56.9 4.6 %shard_map.73 = (bf16[588,512]{1,0:T(8,128)(2,1)S(1)}, bf16[588,512]{1,0:T(8,128)(2,1)}) custom-call(s32[2]{0:T(128)S(1)} %pad_add_fusion.3.at_ref, f32[1,2560]{1,0:T(1,128)S(1)} %reshape.20.node_ref, bf16[2624,256]{1,0:T(8,128)(2,1)S(1)} %copy-done, bf16[2560,256]{1,0:T(8,128)(2,1)S(1)} %get-tuple-element.77.image_ref), custom_call_target="tpu_custom_call" | custom-call | flops 1048576 | bytes 1024 | tf_op jit(solution)/shard_map/pallas_call | solution.py:514
  61.5 0.0 collective-permute-done.4.other_ref
  61.6 2.9 %shard_map.72.near_ref = f32[384,256]{1,0:T(8,128)S(1)} custom-call(s32[1]{0:T(128)} %bitcast.5.core_ref, bf16[2624,256]{1,0:T(8,128)(2,1)S(1)} %copy-done, bf16[2,1344,256]{2,1,0:T(8,128)(2,1)} %get-tuple-element.52.w_ref, bf16[2624,256]{1,0:T(8,128)(2,1)} %collective-permute-done.4.other_ref), custom_call_target="tpu_custom_call" | custom-call | flops 1048576 | bytes 1024 | tf_op jit(solution)/shard_map/pallas_call | solution.py:528
  64.4 0.0 collective-permute-done.5.first_ref
  64.4 0.0 collective-permute-done.6.second_ref
  64.5 3.8 %collective-permute-done.3.far_ref = bf16[1344,256]{1,0:T(8,128)(2,1)S(1)} collective-permute-done((bf16[1344,256]{1,0:T(8,128)(2,1)}, bf16[1344,256]{1,0:T(8,128)(2,1)S(1)}, u32[]{:S(2)}, u32[]{:S(2)}) %collective-permute-start.3) | collective-permute-done | bytes 688160 | tf_op jit(solution)/shard_map/ppermute | solution.py:392
  68.2 1.5 %collective-permute-start.9 = (bf16[588,512]{1,0:T(8,128)(2,1)S(1)}, bf16[588,512]{1,0:T(8,128)(2,1)S(1)}, u32[]{:S(2)}, u32[]{:S(2)}) collective-permute-start(bf16[588,512]{1,0:T(8,128)(2,1)S(1)} %get-tuple-element.71), channel_id=1, source_target_pairs={{0,2},{1,3},{2,0},{3,1},{4,6},{5,7},{6,4},{7,5},{8,10},{9,11},{10,... | collective-permute-start | bytes 1806344 | tf_op jit(solution)/shard_map/ppermute | solution.py:392
  69.7 0.1 pad_add_fusion.1.place_ref
  69.8 0.1 pad_add_fusion.bits_ref
  69.9 1.8 %shard_map.74 = (f32[448,256]{1,0:T(8,128)S(1)}, bf16[448,256]{1,0:T(8,128)(2,1)S(1)}) custom-call(s32[3]{0:T(128)S(1)} %pad_add_fusion.bits_ref, s32[2]{0:T(128)S(1)} %pad_add_fusion.1.place_ref, bf16[2,1344,256]{2,1,0:T(8,128)(2,1)S(1)} %copy-done.1, bf16[672,256]{1,0:T(8,128)(2,1)} %collective-permute-done.5.first_ref, ...), custom_call_target="tpu_custom_call" | custom-call | flops 704643072 | bytes 4194304 | tf_op jit(solution)/shard_map/pallas_call | solution.py:542
  71.6 2.3 %collective-permute-start.7 = (bf16[448,256]{1,0:T(8,128)(2,1)S(1)}, bf16[448,256]{1,0:T(8,128)(2,1)S(1)}, u32[]{:S(2)}, u32[]{:S(2)}) collective-permute-start(bf16[448,256]{1,0:T(8,128)(2,1)S(1)} %get-tuple-element.66), channel_id=1, source_target_pairs={{0,4},{4,0},{8,12},{12,8},{16,20},{20,16},{24,28},{28,24},{1,5},{5... | collective-permute-start | bytes 688136 | tf_op jit(solution)/shard_map/ppermute | solution.py:392
  73.9 5.2 %collective-permute-done.7.got_ref = bf16[448,256]{1,0:T(8,128)(2,1)S(1)} collective-permute-done((bf16[448,256]{1,0:T(8,128)(2,1)S(1)}, bf16[448,256]{1,0:T(8,128)(2,1)S(1)}, u32[]{:S(2)}, u32[]{:S(2)}) %collective-permute-start.7) | collective-permute-done | bytes 229408 | tf_op jit(solution)/shard_map/ppermute | solution.py:392
  79.2 0.6 shard_map.75
  79.8 2.9 %collective-permute-start.8 = (bf16[224,256]{1,0:T(8,128)(2,1)S(1)}, bf16[224,256]{1,0:T(8,128)(2,1)S(1)}, u32[]{:S(2)}, u32[]{:S(2)}) collective-permute-start(bf16[224,256]{1,0:T(8,128)(2,1)S(1)} %get-tuple-element.68), channel_id=1, source_target_pairs={{0,8},{4,12},{8,0},{12,4},{16,24},{20,28},{24,16},{28,20},{1,9},{5... | collective-permute-start | bytes 344072 | tf_op jit(solution)/shard_map/ppermute | solution.py:392
  82.7 2.8 %collective-permute-done.8.got_ref = bf16[224,256]{1,0:T(8,128)(2,1)S(1)} collective-permute-done((bf16[224,256]{1,0:T(8,128)(2,1)S(1)}, bf16[224,256]{1,0:T(8,128)(2,1)S(1)}, u32[]{:S(2)}, u32[]{:S(2)}) %collective-permute-start.8) | collective-permute-done | bytes 114720 | tf_op jit(solution)/shard_map/ppermute | solution.py:392
  85.5 0.6 shard_map.76
  86.0 0.0 collective-permute-done.9.refs_2_
  86.1 0.0 copy-start.4
  86.1 0.8 copy-done.4
  86.9 0.0 collective-permute-start.13
  86.9 3.0 %collective-permute-start.10 = (bf16[112,256]{1,0:T(8,128)(2,1)S(1)}, bf16[112,256]{1,0:T(8,128)(2,1)S(1)}, u32[]{:S(2)}, u32[]{:S(2)}) collective-permute-start(bf16[112,256]{1,0:T(8,128)(2,1)S(1)} %get-tuple-element.73), channel_id=1, source_target_pairs={{0,16},{4,20},{8,24},{12,28},{16,0},{20,4},{24,8},{28,12},{1,17},{... | collective-permute-start | bytes 172040 | tf_op jit(solution)/shard_map/ppermute | solution.py:392
  89.9 3.9 %collective-permute-done.10.got_ref = bf16[112,256]{1,0:T(8,128)(2,1)S(1)} collective-permute-done((bf16[112,256]{1,0:T(8,128)(2,1)S(1)}, bf16[112,256]{1,0:T(8,128)(2,1)S(1)}, u32[]{:S(2)}, u32[]{:S(2)}) %collective-permute-start.10) | collective-permute-done | bytes 57376 | tf_op jit(solution)/shard_map/ppermute | solution.py:392
  93.9 0.6 shard_map.77.own_ref
  94.4 1.6 %collective-permute-start.11 = (bf16[112,256]{1,0:T(8,128)(2,1)S(1)}, bf16[112,256]{1,0:T(8,128)(2,1)S(1)}, u32[]{:S(2)}, u32[]{:S(2)}) collective-permute-start(bf16[112,256]{1,0:T(8,128)(2,1)S(1)} %shard_map.77.own_ref), channel_id=1, source_target_pairs={{0,16},{4,20},{8,24},{12,28},{16,0},{20,4},{24,8},{28,12},{1,17},{... | collective-permute-start | bytes 172040 | tf_op jit(solution)/shard_map/ppermute | solution.py:392
  96.0 4.8 %collective-permute-done.11.got_ref = bf16[112,256]{1,0:T(8,128)(2,1)S(1)} collective-permute-done((bf16[112,256]{1,0:T(8,128)(2,1)S(1)}, bf16[112,256]{1,0:T(8,128)(2,1)S(1)}, u32[]{:S(2)}, u32[]{:S(2)}) %collective-permute-start.11) | collective-permute-done | bytes 57376 | tf_op jit(solution)/shard_map/ppermute | solution.py:392
  100.8 0.6 shard_map.78.own_ref
  101.3 0.1 collective-permute-start.12
  101.5 4.7 %collective-permute-done.12.got_ref = bf16[224,256]{1,0:T(8,128)(2,1)S(1)} collective-permute-done((bf16[224,256]{1,0:T(8,128)(2,1)S(1)}, bf16[224,256]{1,0:T(8,128)(2,1)S(1)}, u32[]{:S(2)}, u32[]{:S(2)}) %collective-permute-start.12) | collective-permute-done | bytes 114720 | tf_op jit(solution)/shard_map/ppermute | solution.py:392
  106.2 0.6 shard_map.79.own_ref
  106.8 0.0 collective-permute-done.13.refs_3_
  106.8 0.3 collective-permute-start.14
  107.1 0.1 pad_add_fusion.4.at_ref
  107.2 3.8 %shard_map.81 = (bf16[588,512]{1,0:T(8,128)(2,1)S(1)}, bf16[588,512]{1,0:T(8,128)(2,1)S(1)}) custom-call(s32[2]{0:T(128)S(1)} %pad_add_fusion.4.at_ref, f32[1,2560]{1,0:T(1,128)S(1)} %reshape.20.node_ref, bf16[2624,256]{1,0:T(8,128)(2,1)S(1)} %copy-done, bf16[2560,256]{1,0:T(8,128)(2,1)S(1)} %get-tuple-element.77.image_ref), custom_call_target="tpu_custom_call" | custom-call | flops 1048576 | bytes 1024 | tf_op jit(solution)/shard_map/pallas_call | solution.py:514
  111.0 0.1 collective-permute-start.17
  111.1 1.8 %collective-permute-done.14.got_ref = bf16[448,256]{1,0:T(8,128)(2,1)S(1)} collective-permute-done((bf16[448,256]{1,0:T(8,128)(2,1)S(1)}, bf16[448,256]{1,0:T(8,128)(2,1)S(1)}, u32[]{:S(2)}, u32[]{:S(2)}) %collective-permute-start.14) | collective-permute-done | bytes 229408 | tf_op jit(solution)/shard_map/ppermute | solution.py:392
  112.9 0.6 shard_map.80.q0_ref
  113.5 0.1 collective-permute-start.16
  113.5 0.1 collective-permute-start.15
  113.6 0.0 collective-permute-done.17.refs_1_
  113.6 11.1 %collective-permute-done.16.q2_ref = bf16[896,256]{1,0:T(8,128)(2,1)S(1)} collective-permute-done((bf16[896,256]{1,0:T(8,128)(2,1)S(1)}, bf16[896,256]{1,0:T(8,128)(2,1)S(1)}, u32[]{:S(2)}, u32[]{:S(2)}) %collective-permute-start.16) | collective-permute-done | bytes 458784 | tf_op jit(solution)/shard_map/ppermute | solution.py:392
  124.7 1.8 %collective-permute-done.18.q3_ref = bf16[896,256]{1,0:T(8,128)(2,1)S(1)} collective-permute-done((bf16[896,256]{1,0:T(8,128)(2,1)S(1)}, bf16[896,256]{1,0:T(8,128)(2,1)S(1)}, u32[]{:S(2)}, u32[]{:S(2)}) %collective-permute-start.18) | collective-permute-done | bytes 458784 | tf_op jit(solution)/shard_map/ppermute | solution.py:392
  126.5 5.0 %shard_map.82 = (f32[588,1024]{1,0:T(8,128)}, bf16[1024,1024]{1,0:T(8,128)(2,1)}) custom-call(s32[1]{0:T(128)} %bitcast.place_ref, bf16[896,256]{1,0:T(8,128)(2,1)S(1)} %shard_map.80.q0_ref, bf16[896,256]{1,0:T(8,128)(2,1)S(1)} %collective-permute-done.15.q1_ref, bf16[896,256]{1,0:T(8,128)(2,1)S(1)} %collective-permute-done.16.q2_ref, ...), custom_call_target="tpu_custom_call" | custom-call | tf_op jit(solution)/shard_map/pallas_call | solution.py:591
  (14 shorter events, 0.1 us)
Async XLA Ops:
  1.3 1.3 copy-start.3
  2.6 0.7 copy-start.6
  3.8 6.9 %copy-start.7 = (s32[8,343]{1,0:T(8,128)S(1)}, s32[8,343]{1,0:T(8,128)}, u32[]{:S(2)}) copy-start(s32[8,343]{1,0:T(8,128)} %conn_ref.1) | copy-start | bytes 32932
  3.8 6.8 %collective-permute-start = (bf16[80,256]{1,0:T(8,128)(2,1)S(1)}, bf16[80,256]{1,0:T(8,128)(2,1)S(1)}, u32[]{:S(2)}, u32[]{:S(2)}) collective-permute-start(bf16[80,256]{1,0:T(8,128)(2,1)S(1)} %shard_map.68), channel_id=1, source_target_pairs={{4,0},{8,4},{12,8},{16,12},{20,16},{24,20},{28,24},{5,1},{9,5},{13... | collective-permute-start | bytes 122888 | tf_op jit(solution)/shard_map/ppermute | solution.py:397
  30.0 12.1 %collective-permute-start.1 = (bf16[6,64,256]{2,1,0:T(8,128)(2,1)S(1)}, bf16[6,64,256]{2,1,0:T(8,128)(2,1)S(1)}, u32[]{:S(2)}, u32[]{:S(2)}) collective-permute-start(bf16[6,64,256]{2,1,0:T(8,128)(2,1)S(1)} %get-tuple-element.46), channel_id=1, source_target_pairs={{0,4},{4,8},{8,12},{12,16},{16,20},{20,24},{24,28},{1,5},{5,9},{9,... | collective-permute-start | bytes 589832 | tf_op jit(solution)/shard_map/ppermute | solution.py:397
  34.8 7.2 %collective-permute-start.2 = (bf16[5,64,256]{2,1,0:T(8,128)(2,1)S(1)}, bf16[5,64,256]{2,1,0:T(8,128)(2,1)S(1)}, u32[]{:S(2)}, u32[]{:S(2)}) collective-permute-start(bf16[5,64,256]{2,1,0:T(8,128)(2,1)S(1)} %get-tuple-element.47), channel_id=1, source_target_pairs={{4,0},{8,4},{12,8},{16,12},{20,16},{24,20},{28,24},{5,1},{9,5},{13... | collective-permute-start | bytes 491528 | tf_op jit(solution)/shard_map/ppermute | solution.py:397
  42.0 9.6 %copy-start.2 = (f32[2560,1]{1,0:T(8,128)S(1)}, f32[2560,1]{1,0:T(8,128)}, u32[]{:S(2)}) copy-start(f32[2560,1]{1,0:T(8,128)} %get-tuple-element.49.pot_ref) | copy-start | bytes 30724
  50.2 11.4 %collective-permute-start.4 = (bf16[2624,256]{1,0:T(8,128)(2,1)}, bf16[2624,256]{1,0:T(8,128)(2,1)}, u32[]{:S(2)}, u32[]{:S(2)}) collective-permute-start(bf16[2624,256]{1,0:T(8,128)(2,1)} %get-tuple-element.76.x_ref), channel_id=1, source_target_pairs={{0,1},{1,0},{2,3},{3,2},{4,5},{5,4},{6,7},{7,6},{8,9},{9,8},{10,11... | collective-permute-start | bytes 4030472 | tf_op jit(solution)/shard_map/ppermute | solution.py:392
  50.2 18.1 %collective-permute-start.3 = (bf16[1344,256]{1,0:T(8,128)(2,1)}, bf16[1344,256]{1,0:T(8,128)(2,1)S(1)}, u32[]{:S(2)}, u32[]{:S(2)}) collective-permute-start(bf16[1344,256]{1,0:T(8,128)(2,1)} %get-tuple-element.53), channel_id=1, source_target_pairs={{0,2},{1,3},{2,0},{3,1},{4,6},{5,7},{6,4},{7,5},{8,10},{9,11},{10,... | collective-permute-start | bytes 2064392 | tf_op jit(solution)/shard_map/ppermute | solution.py:392
  51.7 5.2 %copy-start = (bf16[2624,256]{1,0:T(8,128)(2,1)S(1)}, bf16[2624,256]{1,0:T(8,128)(2,1)}, u32[]{:S(2)}) copy-start(bf16[2624,256]{1,0:T(8,128)(2,1)} %get-tuple-element.76.x_ref) | copy-start | bytes 4030468
  56.2 8.2 %collective-permute-start.5 = (bf16[672,256]{1,0:T(8,128)(2,1)}, bf16[672,256]{1,0:T(8,128)(2,1)}, u32[]{:S(2)}, u32[]{:S(2)}) collective-permute-start(bf16[672,256]{1,0:T(8,128)(2,1)} %get-tuple-element.58), channel_id=1, source_target_pairs={{0,1},{1,0},{2,3},{3,2},{4,5},{5,4},{6,7},{7,6},{8,9},{9,8},{10,11... | collective-permute-start | bytes 1032200 | tf_op jit(solution)/shard_map/ppermute | solution.py:392
  56.4 8.0 %collective-permute-start.6 = (bf16[672,256]{1,0:T(8,128)(2,1)}, bf16[672,256]{1,0:T(8,128)(2,1)}, u32[]{:S(2)}, u32[]{:S(2)}) collective-permute-start(bf16[672,256]{1,0:T(8,128)(2,1)} %get-tuple-element.59), channel_id=1, source_target_pairs={{0,1},{1,0},{2,3},{3,2},{4,5},{5,4},{6,7},{7,6},{8,9},{9,8},{10,11... | collective-permute-start | bytes 1032200 | tf_op jit(solution)/shard_map/ppermute | solution.py:392
  61.5 8.3 %copy-start.1 = (bf16[2,1344,256]{2,1,0:T(8,128)(2,1)S(1)}, bf16[2,1344,256]{2,1,0:T(8,128)(2,1)}, u32[]{:S(2)}) copy-start(bf16[2,1344,256]{2,1,0:T(8,128)(2,1)} %get-tuple-element.52.w_ref) | copy-start | bytes 4128772
  68.2 17.8 %collective-permute-start.9 = (bf16[588,512]{1,0:T(8,128)(2,1)S(1)}, bf16[588,512]{1,0:T(8,128)(2,1)S(1)}, u32[]{:S(2)}, u32[]{:S(2)}) collective-permute-start(bf16[588,512]{1,0:T(8,128)(2,1)S(1)} %get-tuple-element.71), channel_id=1, source_target_pairs={{0,2},{1,3},{2,0},{3,1},{4,6},{5,7},{6,4},{7,5},{8,10},{9,11},{10,... | collective-permute-start | bytes 1806344 | tf_op jit(solution)/shard_map/ppermute | solution.py:392
  71.6 7.5 %collective-permute-start.7 = (bf16[448,256]{1,0:T(8,128)(2,1)S(1)}, bf16[448,256]{1,0:T(8,128)(2,1)S(1)}, u32[]{:S(2)}, u32[]{:S(2)}) collective-permute-start(bf16[448,256]{1,0:T(8,128)(2,1)S(1)} %get-tuple-element.66), channel_id=1, source_target_pairs={{0,4},{4,0},{8,12},{12,8},{16,20},{20,16},{24,28},{28,24},{1,5},{5... | collective-permute-start | bytes 688136 | tf_op jit(solution)/shard_map/ppermute | solution.py:392
  79.8 5.7 %collective-permute-start.8 = (bf16[224,256]{1,0:T(8,128)(2,1)S(1)}, bf16[224,256]{1,0:T(8,128)(2,1)S(1)}, u32[]{:S(2)}, u32[]{:S(2)}) collective-permute-start(bf16[224,256]{1,0:T(8,128)(2,1)S(1)} %get-tuple-element.68), channel_id=1, source_target_pairs={{0,8},{4,12},{8,0},{12,4},{16,24},{20,28},{24,16},{28,20},{1,9},{5... | collective-permute-start | bytes 344072 | tf_op jit(solution)/shard_map/ppermute | solution.py:392
  86.1 0.8 copy-start.4
  86.9 19.9 %collective-permute-start.13 = (bf16[588,512]{1,0:T(8,128)(2,1)}, bf16[588,512]{1,0:T(8,128)(2,1)}, u32[]{:S(2)}, u32[]{:S(2)}) collective-permute-start(bf16[588,512]{1,0:T(8,128)(2,1)} %get-tuple-element.74), channel_id=1, source_target_pairs={{0,3},{1,2},{2,1},{3,0},{4,7},{5,6},{6,5},{7,4},{8,11},{9,10},{10,... | collective-permute-start | bytes 1806344 | tf_op jit(solution)/shard_map/ppermute | solution.py:392
  86.9 7.0 %collective-permute-start.10 = (bf16[112,256]{1,0:T(8,128)(2,1)S(1)}, bf16[112,256]{1,0:T(8,128)(2,1)S(1)}, u32[]{:S(2)}, u32[]{:S(2)}) collective-permute-start(bf16[112,256]{1,0:T(8,128)(2,1)S(1)} %get-tuple-element.73), channel_id=1, source_target_pairs={{0,16},{4,20},{8,24},{12,28},{16,0},{20,4},{24,8},{28,12},{1,17},{... | collective-permute-start | bytes 172040 | tf_op jit(solution)/shard_map/ppermute | solution.py:392
  94.4 6.4 %collective-permute-start.11 = (bf16[112,256]{1,0:T(8,128)(2,1)S(1)}, bf16[112,256]{1,0:T(8,128)(2,1)S(1)}, u32[]{:S(2)}, u32[]{:S(2)}) collective-permute-start(bf16[112,256]{1,0:T(8,128)(2,1)S(1)} %shard_map.77.own_ref), channel_id=1, source_target_pairs={{0,16},{4,20},{8,24},{12,28},{16,0},{20,4},{24,8},{28,12},{1,17},{... | collective-permute-start | bytes 172040 | tf_op jit(solution)/shard_map/ppermute | solution.py:392
  101.3 4.9 %collective-permute-start.12 = (bf16[224,256]{1,0:T(8,128)(2,1)S(1)}, bf16[224,256]{1,0:T(8,128)(2,1)S(1)}, u32[]{:S(2)}, u32[]{:S(2)}) collective-permute-start(bf16[224,256]{1,0:T(8,128)(2,1)S(1)} %shard_map.78.own_ref), channel_id=1, source_target_pairs={{0,8},{4,12},{8,0},{12,4},{16,24},{20,28},{24,16},{28,20},{1,9},{5... | collective-permute-start | bytes 344072 | tf_op jit(solution)/shard_map/ppermute | solution.py:392
  106.8 6.1 %collective-permute-start.14 = (bf16[448,256]{1,0:T(8,128)(2,1)S(1)}, bf16[448,256]{1,0:T(8,128)(2,1)S(1)}, u32[]{:S(2)}, u32[]{:S(2)}) collective-permute-start(bf16[448,256]{1,0:T(8,128)(2,1)S(1)} %shard_map.79.own_ref), channel_id=1, source_target_pairs={{0,4},{4,0},{8,12},{12,8},{16,20},{20,16},{24,28},{28,24},{1,5},{5... | collective-permute-start | bytes 688136 | tf_op jit(solution)/shard_map/ppermute | solution.py:392
  107.2 19.3 %copy-start.5 = (bf16[588,512]{1,0:T(8,128)(2,1)S(1)}, bf16[588,512]{1,0:T(8,128)(2,1)}, u32[]{:S(2)}) copy-start(bf16[588,512]{1,0:T(8,128)(2,1)} %copy-done.4) | copy-start | bytes 1806340
  111.0 2.6 %collective-permute-start.17 = (bf16[588,512]{1,0:T(8,128)(2,1)S(1)}, bf16[588,512]{1,0:T(8,128)(2,1)S(1)}, u32[]{:S(2)}, u32[]{:S(2)}) collective-permute-start(bf16[588,512]{1,0:T(8,128)(2,1)S(1)} %get-tuple-element.78), channel_id=1, source_target_pairs={{0,1},{1,0},{2,3},{3,2},{4,5},{5,4},{6,7},{7,6},{8,9},{9,8},{10,11... | collective-permute-start | bytes 1806344 | tf_op jit(solution)/shard_map/ppermute | solution.py:392
  113.5 11.2 %collective-permute-start.16 = (bf16[896,256]{1,0:T(8,128)(2,1)S(1)}, bf16[896,256]{1,0:T(8,128)(2,1)S(1)}, u32[]{:S(2)}, u32[]{:S(2)}) collective-permute-start(bf16[896,256]{1,0:T(8,128)(2,1)S(1)} %shard_map.80.q0_ref), channel_id=1, source_target_pairs={{0,2},{1,3},{2,0},{3,1},{4,6},{5,7},{6,4},{7,5},{8,10},{9,11},{10,... | collective-permute-start | bytes 1376264 | tf_op jit(solution)/shard_map/ppermute | solution.py:392
  113.5 11.2 %collective-permute-start.15 = (bf16[896,256]{1,0:T(8,128)(2,1)S(1)}, bf16[896,256]{1,0:T(8,128)(2,1)S(1)}, u32[]{:S(2)}, u32[]{:S(2)}) collective-permute-start(bf16[896,256]{1,0:T(8,128)(2,1)S(1)} %shard_map.80.q0_ref), channel_id=1, source_target_pairs={{0,1},{1,0},{2,3},{3,2},{4,5},{5,4},{6,7},{7,6},{8,9},{9,8},{10,11... | collective-permute-start | bytes 1376264 | tf_op jit(solution)/shard_map/ppermute | solution.py:392
  124.7 1.8 %collective-permute-start.18 = (bf16[896,256]{1,0:T(8,128)(2,1)S(1)}, bf16[896,256]{1,0:T(8,128)(2,1)S(1)}, u32[]{:S(2)}, u32[]{:S(2)}) collective-permute-start(bf16[896,256]{1,0:T(8,128)(2,1)S(1)} %collective-permute-done.16.q2_ref), channel_id=1, source_target_pairs={{0,1},{1,0},{2,3},{3,2},{4,5},{5,4},{6,7},{7,6},{8,9},{9,8},{10,11... | collective-permute-start | bytes 1376264 | tf_op jit(solution)/shard_map/ppermute | solution.py:392

commit v8 on v7

--- a/solution.py
+++ b/solution.py
@@ -135,8 +135,9 @@
 
 
 def mul_r(a, b):
-    high, low = split(b)
-    return mul(a, high) + mul(a, low)
+    n = b.shape[1]
+    both = mul(a, jnp.concatenate(split(b), axis=1))
+    return both[:, :n] + both[:, n:]
 
 
 def sweep(h_ref, y_ref, fp, emit):
@@ -417,30 +418,36 @@
         out_ref[width:] = sum(tmul(other_ref[at[i], half:], w_ref[i]) for i in range(2)) * scale
 
 
-def part_ways(sum_ref, mine, keep_ref, give_ref):
+def part_ways(sum_ref, mine, keep_ref, give_refs):
     n = keep_ref.shape[0]
     keep_ref[...] = sum_ref[pl.ds(pl.multiple_of(mine * n, 16), n)]
-    give_ref[...] = sum_ref[pl.ds(pl.multiple_of((1 - mine) * n, 16), n)].astype(BF16)
-
-
-def halve_kernel(step, bits_ref, keep_ref, got_ref, *refs):
-    total = keep_ref[...] + got_ref[...].astype(F32)
+    for j, give_ref in enumerate(give_refs):
+        give_ref[...] = sum_ref[pl.ds(pl.multiple_of(jnp.bitwise_xor(mine, j + 1) * n, 16), n)].astype(BF16)
+
+
+def reduce_kernel(step, ways, bits_ref, keep_ref, *refs):
+    total = keep_ref[...]
+    for got_ref in refs[: ways - 1]:
+        total = total + got_ref[...].astype(F32)
+    refs = refs[ways - 1 :]
     if len(refs) == 1:
         refs[0][...] = total.astype(BF16)
         return
-    *outs, sum_ref = refs
+    keep_out, *gives, sum_ref = refs
     sum_ref[...] = total
-    part_ways(sum_ref, bits_ref[step], *outs)
-
-
-def join_kernel(step, bits_ref, own_ref, got_ref, out_ref):
+    part_ways(sum_ref, bits_ref[step], keep_out, gives)
+
+
+def join_kernel(step, bits_ref, own_ref, *refs):
+    *got_refs, out_ref = refs
     n = own_ref.shape[0]
     mine = bits_ref[step]
-    out_ref[pl.ds(pl.multiple_of(mine * n, 16), n)] = own_ref[...]
-    out_ref[pl.ds(pl.multiple_of((1 - mine) * n, 16), n)] = got_ref[...]
-
-
-def far_gram_kernel(scale, bits_ref, place_ref, w_ref, first_ref, second_ref, far_ref, near_ref, keep_ref, give_ref, out_ref):
+    for j, ref in enumerate([own_ref] + got_refs):
+        out_ref[pl.ds(pl.multiple_of(jnp.bitwise_xor(mine, j) * n, 16), n)] = ref[...]
+
+
+def far_gram_kernel(scale, bits_ref, place_ref, w_ref, first_ref, second_ref, far_ref, near_ref, keep_ref, *refs):
+    *give_refs, out_ref = refs
     width = w_ref.shape[2]
     near = near_ref.shape[0]
     side, core = place_ref[0], place_ref[1]
@@ -451,17 +458,20 @@
     out_ref[pl.ds(mine, width)] = tmul(w_ref[side], far) * scale
     n = first_ref.shape[0]
     out_ref[pl.ds(other, width)] = (tmul(first_ref[...], far[:n]) + tmul(second_ref[...], far[n:])) * scale
-    part_ways(out_ref, bits_ref[0], keep_ref, give_ref)
-
-
-def paired_residual_kernel(place_ref, q0_ref, q1_ref, q2_ref, q3_ref, *refs):
+    part_ways(out_ref, bits_ref[0], keep_ref, give_refs)
+
+
+def paired_residual_kernel(place_ref, *refs):
+    q_refs, refs = refs[:8], refs[8:]
     parts = 4
     row_refs, (out_ref, p_ref, q_ref) = refs[:parts], refs[parts:]
     width = row_refs[0].shape[1] // 2
     half = width // 2
-    for k, ref in enumerate((q0_ref, q1_ref, q2_ref, q3_ref)):
-        q_ref[k] = ref[...]
-    me = place_ref[0]
+    me, mine = place_ref[0], place_ref[1]
+    n = q_refs[0].shape[0]
+    for k in range(parts):
+        for j in range(2):
+            q_ref[k, pl.ds(pl.multiple_of(jnp.bitwise_xor(mine, j) * n, 16), n)] = q_refs[2 * k + j][...]
     eye = (lax.broadcasted_iota(jnp.int32, (width, width), 0) == lax.broadcasted_iota(jnp.int32, (width, width), 1)).astype(
         F32
     ).astype(BF16)
@@ -533,68 +543,77 @@
         cost_estimate=pl.CostEstimate(flops=1 << 20, bytes_accessed=1 << 10, transcendentals=0),
     )(core.reshape(1), x_own, w_own, x_other)
     far, near, *cuts, w_other[0], w_other[1] = lax.optimization_barrier((far, near, *cuts, *w_other))
-    row2 = swap(cuts[0], "orb", 2)
-    cut3 = cuts[1]
-    steps = (dom - 1).bit_length()
-    bits = jnp.stack([(d // (1 << i)) % 2 for i in range(steps)])
+    row2, row3 = swap(cuts[0], "orb", 2), swap(cuts[1], "orb", 3)
+    groups, base = [], 1
+    while base < dom:
+        ways = 2 if base == 1 or base * 4 > dom else 4
+        groups.append((base, ways))
+        base *= ways
+    bits = jnp.stack([(d // base) % ways for base, ways in groups])
     little = pl.CostEstimate(flops=1 << 10, bytes_accessed=1 << 10, transcendentals=0)
     count = top + 2 * width
-    keep, give = pl.pallas_call(
+
+    def parts_of(n, ways):
+        return [sds((n // ways, width), F32)] + [sds((n // ways, width), BF16)] * (ways - 1)
+
+    keep, *gives = pl.pallas_call(
         functools.partial(far_gram_kernel, scale),
         in_specs=[smem] * 2 + [vmem] * 5,
-        out_shape=[sds((count // 2, width), F32), sds((count // 2, width), BF16)],
+        out_shape=parts_of(count, 2),
         scratch_shapes=[pltpu.VMEM((count, width), F32)],
         compiler_params=params(),
         cost_estimate=pl.CostEstimate(flops=8 * slab * width * width, bytes_accessed=4 << 20, transcendentals=0),
     )(bits, jnp.stack([side, core]), w_own, *w_other, far, near)
-    row0 = cut1 = row3 = None
-    for i in range(steps):
+    row0 = cut1 = None
+    for i, (base, ways) in enumerate(groups):
         if i == 0:
-            x_own, image, give = lax.optimization_barrier((x_own, image, give))
+            x_own, image, gives[0] = lax.optimization_barrier((x_own, image, gives[0]))
             row0, cut1 = back(0, 1, x_own, image)
-        got = swap(give, "dom", 1 << i)
+        gots = [swap(give, "dom", base * (j + 1)) for j, give in enumerate(gives)]
         n = keep.shape[0]
-        last = i == steps - 1
+        last = i == len(groups) - 1
         outs = pl.pallas_call(
-            functools.partial(halve_kernel, i + 1),
-            in_specs=[smem] + [vmem] * 2,
-            out_shape=[sds((n, width), BF16)] if last else [sds((n // 2, width), F32), sds((n // 2, width), BF16)],
+            functools.partial(reduce_kernel, i + 1, ways),
+            in_specs=[smem] + [vmem] * ways,
+            out_shape=[sds((n, width), BF16)] if last else parts_of(n, groups[i + 1][1]),
             scratch_shapes=[] if last else [pltpu.VMEM((n, width), F32)],
             compiler_params=params(),
             cost_estimate=little,
-        )(bits, keep, got)
+        )(bits, keep, *gots)
         outs = list(outs)
-        if i == 1:
-            outs[-1], row2, cut3 = lax.optimization_barrier((outs[-1], row2, cut3))
-            row3 = swap(cut3, "orb", 3)
+        if i == 0:
+            outs[-1], row0, cut1 = lax.optimization_barrier((outs[-1], row0, cut1))
         if last:
+            outs[-1], row2 = lax.optimization_barrier((outs[-1], row2))
             share = outs[0]
         else:
-            keep, give = outs
-    for i in reversed(range(steps)):
-        got = swap(share, "dom", 1 << i)
+            keep, *gives = outs
+    for i in reversed(range(1, len(groups))):
+        base, ways = groups[i]
+        gots = [swap(share, "dom", base * j) for j in range(1, ways)]
         share = pl.pallas_call(
             functools.partial(join_kernel, i),
-            in_specs=[smem] + [vmem] * 2,
-            out_shape=sds((2 * share.shape[0], width), BF16),
+            in_specs=[smem] + [vmem] * ways,
+            out_shape=sds((ways * share.shape[0], width), BF16),
             compiler_params=params(),
             cost_estimate=little,
-        )(bits, share, got)
-        if i == 1:
-            share, row3 = lax.optimization_barrier((share, row3))
-    q2 = swap(share, "orb", 2)
-    q1 = swap(share, "orb", 1)
+        )(bits, share, *gots)
     row1 = swap(cut1, "orb", 1)
-    q2, row1 = lax.optimization_barrier((q2, row1))
-    q3 = swap(q2, "orb", 1)
+    got = swap(share, "dom", 1)
+    got, row3 = lax.optimization_barrier((got, row3))
+    q2 = [swap(share, "orb", 2), swap(got, "orb", 2)]
+    q1 = [swap(share, "orb", 1), swap(got, "orb", 1)]
+    q3a = swap(q2[0], "orb", 1)
+    q2[1], q1[0], q1[1], q3a, row1 = lax.optimization_barrier((q2[1], q1[0], q1[1], q3a, row1))
+    q3 = [q3a, swap(q2[1], "orb", 1)]
     cols = orb * width
     return pl.pallas_call(
         paired_residual_kernel,
-        in_specs=[smem] + [vmem] * 8,
+        in_specs=[smem] + [vmem] * 12,
         out_shape=(sds((rows, cols), F32), sds((cols, cols), BF16)),
-        scratch_shapes=[pltpu.VMEM((orb,) + share.shape, BF16)],
+        scratch_shapes=[pltpu.VMEM((orb, count, width), BF16)],
         compiler_params=params(),
-    )(o.reshape(1), share, q1, q2, q3, row0, row1, row2, row3)
+    )(jnp.stack([o, d % 2]), share, got, *q1, *q2, *q3, row0, row1, row2, row3)
 
 
 def body(orbitals, potential, cell_hamiltonian, connectivity, face_nodes):

time: 132 us -> 128 us (0.970)
  waiting for transfers between devices: 48 us -> 38.3 us
  starting transfers between devices: 21.4 us -> 25.1 us
  Pallas kernels: 54 us -> 55.8 us
    ppermute x16 -> x21, waiting for transfers between devices: 39.9 us -> 30.1 us  [swap(): lax.ppermute(block, axis, [(i, i ^ bit) for i in range(lax.axis_size(axis...]
    ppermute x16 -> x21, starting transfers between devices: 14 us -> 17.7 us  [swap(): lax.ppermute(block, axis, [(i, i ^ bit) for i in range(lax.axis_size(axis...]
    pallas_call x1, Pallas kernels: 19.3 us -> 21.8 us  [body(): pl.pallas_call(functools.partial(free_kernel, fp, ip), out_shape=[sds((ce...]
    pallas_call x4 -> x3, Pallas kernels: 6.7 us -> 6.54 us  [the longest x1 5.35 us: paired_tail(): pl.pallas_call(paired_residual_kernel, in_specs=[smem] + [vmem] * 12, out...]
  transfers between devices with their start and end apart: 19 -> 24, of which waited for: 11 -> 13; matrix products, arithmetic and copies ran while one was open for 3% -> 3% of each run, Pallas kernels for 16% -> 16%
where the time goes in v8:
time: 128 us; the launch traced here: 127 us
  Pallas kernels  55.8 us (44%)
  waiting for transfers between devices  38.3 us (30%)
  starting transfers between devices  25.1 us (20%)
  local copies, waits for them, and re-layouts  6.74 us (5%)
    ppermute x21, waiting for transfers between devices, swap(): lax.ppermute(block, axis, [(i, i ^ bit) for i in range(lax.axis_size(axis...  30.1 us
    pallas_call x1, Pallas kernels, body(): pl.pallas_call(functools.partial(free_kernel, fp, ip), out_shape=[sds((ce...  21.8 us
    ppermute x21, starting transfers between devices, swap(): lax.ppermute(block, axis, [(i, i ^ bit) for i in range(lax.axis_size(axis...  17.7 us
    pallas_call x2, Pallas kernels, back(): pl.pallas_call(back_pair_kernel, grid=(1,), in_specs=[smem, whole(1, tota...  8.48 us
    ppermute x3, waiting for transfers between devices, shift(): lax.ppermute(block, axis, [(i, i + distance) for i in range(n) if 0 <= i...  8.13 us
    pallas_call x1, Pallas kernels, body(): pl.pallas_call(functools.partial(forced_kernel, fp), in_specs=[pl.BlockSp...  8.09 us
    ppermute x3, starting transfers between devices, shift(): lax.ppermute(block, axis, [(i, i + distance) for i in range(n) if 0 <= i...  7.4 us
    unnamed x17, local copies, waits for them, and re-layouts  5.94 us
  transfers between devices with their start and end apart: 24, of which 13 were waited for; matrix products, arithmetic and copies ran while one was open for 3% of the time, Pallas kernels for 16%

profile of v8, /device:TPU:0, one launch (start us, length us, event | category | flops | bytes accessed | tf_op | source)
XLA Modules:
  0.0 127.2 jit_solution(4394914473583924428)
XLA Ops:
  0.6 0.7 reshape.15.pot_ref.potraw_ref
  1.3 1.3 %copy-done.3 = bf16[2352,256]{1,0:T(8,128)(2,1)S(1)} copy-done((bf16[2352,256]{1,0:T(8,128)(2,1)S(1)}, bf16[2352,256]{1,0:T(8,128)(2,1)}, u32[]{:S(2)}) %copy-start.3) | copy-done | bytes 1204248
  2.6 0.7 copy-done.6
  3.3 0.5 shard_map.68
  3.8 0.0 copy-start.7
  3.8 1.3 %collective-permute-start = (bf16[80,256]{1,0:T(8,128)(2,1)S(1)}, bf16[80,256]{1,0:T(8,128)(2,1)S(1)}, u32[]{:S(2)}, u32[]{:S(2)}) collective-permute-start(bf16[80,256]{1,0:T(8,128)(2,1)S(1)} %shard_map.68), channel_id=1, source_target_pairs={{4,0},{8,4},{12,8},{16,12},{20,16},{24,20},{28,24},{5,1},{9,5},{13... | collective-permute-start | bytes 122888 | tf_op jit(solution)/shard_map/ppermute | solution.py:398
  5.1 3.2 %copy.7.hraw_ref = bf16[8,343,343]{2,1,0:T(8,128)(2,1)} copy(bf16[8,343,343]{2,0,1:T(8,128)(2,1)} %param.7) | data formatting | bytes 3764768 | tf_op args[2]
  8.3 2.3 %collective-permute-done.ghost_ref = bf16[80,256]{1,0:T(8,128)(2,1)S(1)} collective-permute-done((bf16[80,256]{1,0:T(8,128)(2,1)S(1)}, bf16[80,256]{1,0:T(8,128)(2,1)S(1)}, u32[]{:S(2)}, u32[]{:S(2)}) %collective-permute-start) | collective-permute-done | bytes 40992 | tf_op jit(solution)/shard_map/ppermute | solution.py:398
  10.6 21.8 %shard_map.69 = (bf16[8,384,384]{2,1,0:T(8,128)(2,1)}, bf16[2560,256]{1,0:T(8,128)(2,1)S(1)}, f32[2560,1]{1,0:T(8,128)}, f32[8,1,320]{2,1,0:T(1,128)S(1)}, bf16[...) custom-call(s32[8,343]{1,0:T(8,128)S(1)} %copy-done.7, ...), custom_call_target="tpu_custom_call" | custom-call | flops 2415919104 | bytes 8388608 | tf_op jit(solution)/shard_map/pallas_call | solution.py:645
  32.4 4.8 %collective-permute-start.1 = (bf16[6,64,256]{2,1,0:T(8,128)(2,1)S(1)}, bf16[6,64,256]{2,1,0:T(8,128)(2,1)S(1)}, u32[]{:S(2)}, u32[]{:S(2)}) collective-permute-start(bf16[6,64,256]{2,1,0:T(8,128)(2,1)S(1)} %get-tuple-element.51), channel_id=1, source_target_pairs={{0,4},{4,8},{8,12},{12,16},{16,20},{20,24},{24,28},{1,5},{5,9},{9,... | collective-permute-start | bytes 589832 | tf_op jit(solution)/shard_map/ppermute | solution.py:398
  37.2 1.3 %collective-permute-start.2 = (bf16[5,64,256]{2,1,0:T(8,128)(2,1)S(1)}, bf16[5,64,256]{2,1,0:T(8,128)(2,1)S(1)}, u32[]{:S(2)}, u32[]{:S(2)}) collective-permute-start(bf16[5,64,256]{2,1,0:T(8,128)(2,1)S(1)} %get-tuple-element.52), channel_id=1, source_target_pairs={{4,0},{8,4},{12,8},{16,12},{20,16},{24,20},{28,24},{5,1},{9,5},{13... | collective-permute-start | bytes 491528 | tf_op jit(solution)/shard_map/ppermute | solution.py:398
  38.6 0.1 pad_add_fusion.3.place_ref
  38.7 5.8 %collective-permute-done.2.fromright_ref = bf16[5,64,256]{2,1,0:T(8,128)(2,1)S(1)} collective-permute-done((bf16[5,64,256]{2,1,0:T(8,128)(2,1)S(1)}, bf16[5,64,256]{2,1,0:T(8,128)(2,1)S(1)}, u32[]{:S(2)}, u32[]{:S(2)}) %collective-permute-start.2) | collective-permute-done | bytes 163872 | tf_op jit(solution)/shard_map/ppermute | solution.py:398
  44.5 0.0 collective-permute-done.1.fromleft_ref
  44.5 8.1 %shard_map.70 = (bf16[2624,256]{1,0:T(8,128)(2,1)}, f32[64,256]{1,0:T(8,128)S(1)}, bf16[1344,256]{1,0:T(8,128)(2,1)}) custom-call(s32[2]{0:T(128)S(1)} %pad_add_fusion.3.place_ref, bf16[2560,256]{1,0:T(8,128)(2,1)S(1)} %get-tuple-element.48.v_ref, bf16[80,256]{1,0:T(8,128)(2,1)S(1)} %collective-permute-done.ghost_ref, ...), custom_call_target="tpu_custom_call" | custom-call | flops 2415919104 | bytes 8388608 | tf_op jit(solution)/shard_map/pallas_call | solution.py:667
  52.6 0.0 collective-permute-start.4
  52.6 1.5 %collective-permute-start.3 = (bf16[1344,256]{1,0:T(8,128)(2,1)}, bf16[1344,256]{1,0:T(8,128)(2,1)S(1)}, u32[]{:S(2)}, u32[]{:S(2)}) collective-permute-start(bf16[1344,256]{1,0:T(8,128)(2,1)} %get-tuple-element.58), channel_id=1, source_target_pairs={{0,2},{1,3},{2,0},{3,1},{4,6},{5,7},{6,4},{7,5},{8,10},{9,11},{10,... | collective-permute-start | bytes 2064392 | tf_op jit(solution)/shard_map/ppermute | solution.py:393
  54.1 4.5 %shard_map.71 = (bf16[2560,256]{1,0:T(8,128)(2,1)S(1)}, bf16[2,1344,256]{2,1,0:T(8,128)(2,1)}, bf16[672,256]{1,0:T(8,128)(2,1)}, bf16[672,256]{1,0:T(8,128)(2,1)}) custom-call(s32[2]{0:T(128)S(1)} %pad_add_fusion.3.place_ref, bf16[2624,256]{1,0:T(8,128)(2,1)} %get-tuple-element.76.x_ref, f32[64,256]{1,0:T(8,128)S(1)} %get-tuple-element.56.face_image_ref, ...), custom_call_target="tpu_custom_call" | custom-call | flops 1048576 | bytes 1024 | tf_op jit(solution)/shard_map/pallas_call | solution.py:679
  58.6 0.2 collective-permute-start.5
  58.8 0.3 collective-permute-start.6
  59.1 0.1 pad_add_fusion.4.at_ref
  59.2 0.1 reshape.16.node_ref
  59.3 4.7 %shard_map.73 = (bf16[588,512]{1,0:T(8,128)(2,1)}, bf16[588,512]{1,0:T(8,128)(2,1)}) custom-call(s32[2]{0:T(128)S(1)} %pad_add_fusion.4.at_ref, f32[1,2560]{1,0:T(1,128)S(1)} %reshape.16.node_ref, bf16[2624,256]{1,0:T(8,128)(2,1)S(1)} %copy-done, bf16[2560,256]{1,0:T(8,128)(2,1)S(1)} %get-tuple-element.77.image_ref), custom_call_target="tpu_custom_call" | custom-call | flops 1048576 | bytes 1024 | tf_op jit(solution)/shard_map/pallas_call | solution.py:524
  63.9 2.9 %shard_map.72.near_ref = f32[384,256]{1,0:T(8,128)S(1)} custom-call(s32[1]{0:T(128)} %bitcast.4.core_ref, bf16[2624,256]{1,0:T(8,128)(2,1)S(1)} %copy-done, bf16[2,1344,256]{2,1,0:T(8,128)(2,1)} %get-tuple-element.57.w_ref, bf16[2624,256]{1,0:T(8,128)(2,1)} %collective-permute-done.4.other_ref), custom_call_target="tpu_custom_call" | custom-call | flops 1048576 | bytes 1024 | tf_op jit(solution)/shard_map/pallas_call | solution.py:538
  66.8 0.0 collective-permute-done.6.second_ref
  66.8 3.8 %collective-permute-done.3.far_ref = bf16[1344,256]{1,0:T(8,128)(2,1)S(1)} collective-permute-done((bf16[1344,256]{1,0:T(8,128)(2,1)}, bf16[1344,256]{1,0:T(8,128)(2,1)S(1)}, u32[]{:S(2)}, u32[]{:S(2)}) %collective-permute-start.3) | collective-permute-done | bytes 688160 | tf_op jit(solution)/shard_map/ppermute | solution.py:393
  70.6 1.5 %collective-permute-start.11 = (bf16[588,512]{1,0:T(8,128)(2,1)}, bf16[588,512]{1,0:T(8,128)(2,1)}, u32[]{:S(2)}, u32[]{:S(2)}) collective-permute-start(bf16[588,512]{1,0:T(8,128)(2,1)} %get-tuple-element.81), channel_id=1, source_target_pairs={{0,2},{1,3},{2,0},{3,1},{4,6},{5,7},{6,4},{7,5},{8,10},{9,11},{10,... | collective-permute-start | bytes 1806344 | tf_op jit(solution)/shard_map/ppermute | solution.py:393
  72.1 0.1 pad_add_fusion.2.place_ref
  72.2 0.1 pad_add_fusion.1.bits_ref
  72.3 2.5 %shard_map.74 = (f32[448,256]{1,0:T(8,128)S(1)}, bf16[448,256]{1,0:T(8,128)(2,1)}) custom-call(s32[2]{0:T(128)S(1)} %pad_add_fusion.1.bits_ref, s32[2]{0:T(128)S(1)} %pad_add_fusion.2.place_ref, bf16[2,1344,256]{2,1,0:T(8,128)(2,1)S(1)} %copy-done.1, bf16[672,256]{1,0:T(8,128)(2,1)} %collective-permute-done.5.first_ref, ...), custom_call_target="tpu_custom_call" | custom-call | flops 704643072 | bytes 4194304 | tf_op jit(solution)/shard_map/pallas_call | solution.py:559
  74.7 0.8 copy-done.4
  75.5 2.2 %collective-permute-start.7 = (bf16[448,256]{1,0:T(8,128)(2,1)}, bf16[448,256]{1,0:T(8,128)(2,1)S(1)}, u32[]{:S(2)}, u32[]{:S(2)}) collective-permute-start(bf16[448,256]{1,0:T(8,128)(2,1)} %get-tuple-element.71), channel_id=1, source_target_pairs={{0,4},{4,0},{8,12},{12,8},{16,20},{20,16},{24,28},{28,24},{1,5},{5... | collective-permute-start | bytes 688136 | tf_op jit(solution)/shard_map/ppermute | solution.py:393
  77.7 0.0 collective-permute-start.16
  77.7 0.1 pad_add_fusion.5.at_ref
  77.8 3.8 %shard_map.76 = (bf16[588,512]{1,0:T(8,128)(2,1)S(1)}, bf16[588,512]{1,0:T(8,128)(2,1)S(1)}) custom-call(s32[2]{0:T(128)S(1)} %pad_add_fusion.5.at_ref, f32[1,2560]{1,0:T(1,128)S(1)} %reshape.16.node_ref, bf16[2624,256]{1,0:T(8,128)(2,1)S(1)} %copy-done, bf16[2560,256]{1,0:T(8,128)(2,1)S(1)} %get-tuple-element.77.image_ref), custom_call_target="tpu_custom_call" | custom-call | flops 1048576 | bytes 1024 | tf_op jit(solution)/shard_map/pallas_call | solution.py:524
  81.6 1.5 %collective-permute-done.7.refs_0_ = bf16[448,256]{1,0:T(8,128)(2,1)S(1)} collective-permute-done((bf16[448,256]{1,0:T(8,128)(2,1)}, bf16[448,256]{1,0:T(8,128)(2,1)S(1)}, u32[]{:S(2)}, u32[]{:S(2)}) %collective-permute-start.7) | collective-permute-done | bytes 229408 | tf_op jit(solution)/shard_map/ppermute | solution.py:393
  83.1 0.6 shard_map.75
  83.8 4.9 %collective-permute-start.10 = (bf16[112,256]{1,0:T(8,128)(2,1)S(1)}, bf16[112,256]{1,0:T(8,128)(2,1)S(1)}, u32[]{:S(2)}, u32[]{:S(2)}) collective-permute-start(bf16[112,256]{1,0:T(8,128)(2,1)S(1)} %get-tuple-element.80), channel_id=1, source_target_pairs={{0,24},{4,28},{8,16},{12,20},{16,8},{20,12},{24,0},{28,4},{1,25},{... | collective-permute-start | bytes 172040 | tf_op jit(solution)/shard_map/ppermute | solution.py:393
  88.7 0.0 collective-permute-start.8
  88.7 2.4 %collective-permute-done.10.refs_2_ = bf16[112,256]{1,0:T(8,128)(2,1)S(1)} collective-permute-done((bf16[112,256]{1,0:T(8,128)(2,1)S(1)}, bf16[112,256]{1,0:T(8,128)(2,1)S(1)}, u32[]{:S(2)}, u32[]{:S(2)}) %collective-permute-start.10) | collective-permute-done | bytes 57376 | tf_op jit(solution)/shard_map/ppermute | solution.py:393
  91.1 0.9 collective-permute-start.9
  92.0 1.6 %collective-permute-done.8.refs_0_ = bf16[112,256]{1,0:T(8,128)(2,1)S(1)} collective-permute-done((bf16[112,256]{1,0:T(8,128)(2,1)S(1)}, bf16[112,256]{1,0:T(8,128)(2,1)S(1)}, u32[]{:S(2)}, u32[]{:S(2)}) %collective-permute-start.8) | collective-permute-done | bytes 57376 | tf_op jit(solution)/shard_map/ppermute | solution.py:393
  93.7 2.5 %collective-permute-done.9.refs_1_ = bf16[112,256]{1,0:T(8,128)(2,1)S(1)} collective-permute-done((bf16[112,256]{1,0:T(8,128)(2,1)S(1)}, bf16[112,256]{1,0:T(8,128)(2,1)S(1)}, u32[]{:S(2)}, u32[]{:S(2)}) %collective-permute-start.9) | collective-permute-done | bytes 57376 | tf_op jit(solution)/shard_map/ppermute | solution.py:393
  96.2 0.6 shard_map.77.own_ref
  96.8 1.9 %collective-permute-start.12 = (bf16[112,256]{1,0:T(8,128)(2,1)S(1)}, bf16[112,256]{1,0:T(8,128)(2,1)S(1)}, u32[]{:S(2)}, u32[]{:S(2)}) collective-permute-start(bf16[112,256]{1,0:T(8,128)(2,1)S(1)} %shard_map.77.own_ref), channel_id=1, source_target_pairs={{0,8},{4,12},{8,0},{12,4},{16,24},{20,28},{24,16},{28,20},{1,9},{5... | collective-permute-start | bytes 172040 | tf_op jit(solution)/shard_map/ppermute | solution.py:393
  98.7 3.0 %collective-permute-start.13 = (bf16[112,256]{1,0:T(8,128)(2,1)S(1)}, bf16[112,256]{1,0:T(8,128)(2,1)S(1)}, u32[]{:S(2)}, u32[]{:S(2)}) collective-permute-start(bf16[112,256]{1,0:T(8,128)(2,1)S(1)} %shard_map.77.own_ref), channel_id=1, source_target_pairs={{0,16},{4,20},{8,24},{12,28},{16,0},{20,4},{24,8},{28,12},{1,17},{... | collective-permute-start | bytes 172040 | tf_op jit(solution)/shard_map/ppermute | solution.py:393
  101.7 0.0 collective-permute-start.14
  101.7 0.0 collective-permute-done.12.refs_0_
  101.7 2.8 %collective-permute-done.13.refs_1_ = bf16[112,256]{1,0:T(8,128)(2,1)S(1)} collective-permute-done((bf16[112,256]{1,0:T(8,128)(2,1)S(1)}, bf16[112,256]{1,0:T(8,128)(2,1)S(1)}, u32[]{:S(2)}, u32[]{:S(2)}) %collective-permute-start.13) | collective-permute-done | bytes 57376 | tf_op jit(solution)/shard_map/ppermute | solution.py:393
  104.5 3.2 %collective-permute-done.14.refs_2_ = bf16[112,256]{1,0:T(8,128)(2,1)S(1)} collective-permute-done((bf16[112,256]{1,0:T(8,128)(2,1)S(1)}, bf16[112,256]{1,0:T(8,128)(2,1)S(1)}, u32[]{:S(2)}, u32[]{:S(2)}) %collective-permute-start.14) | collective-permute-done | bytes 57376 | tf_op jit(solution)/shard_map/ppermute | solution.py:393
  107.7 0.6 shard_map.78.refs_0_
  108.2 0.3 collective-permute-start.15
  108.5 0.4 collective-permute-start.20
  108.9 5.4 %collective-permute-done.15.refs_1_ = bf16[448,256]{1,0:T(8,128)(2,1)S(1)} collective-permute-done((bf16[448,256]{1,0:T(8,128)(2,1)S(1)}, bf16[448,256]{1,0:T(8,128)(2,1)S(1)}, u32[]{:S(2)}, u32[]{:S(2)}) %collective-permute-start.15) | collective-permute-done | bytes 229408 | tf_op jit(solution)/shard_map/ppermute | solution.py:393
  114.3 0.5 collective-permute-start.17
  114.9 0.0 collective-permute-start.19
  114.9 2.1 %collective-permute-done.20.refs_4_ = bf16[448,256]{1,0:T(8,128)(2,1)S(1)} collective-permute-done((bf16[448,256]{1,0:T(8,128)(2,1)S(1)}, bf16[448,256]{1,0:T(8,128)(2,1)S(1)}, u32[]{:S(2)}, u32[]{:S(2)}) %collective-permute-start.20) | collective-permute-done | bytes 229408 | tf_op jit(solution)/shard_map/ppermute | solution.py:393
  117.0 0.0 collective-permute-start.21
  117.0 0.0 collective-permute-done.22.refs_9_
  117.0 0.0 collective-permute-done.18.refs_2_
  117.0 3.4 %collective-permute-done.17.refs_5_ = bf16[448,256]{1,0:T(8,128)(2,1)S(1)} collective-permute-done((bf16[448,256]{1,0:T(8,128)(2,1)S(1)}, bf16[448,256]{1,0:T(8,128)(2,1)S(1)}, u32[]{:S(2)}, u32[]{:S(2)}) %collective-permute-start.17) | collective-permute-done | bytes 229408 | tf_op jit(solution)/shard_map/ppermute | solution.py:393
  120.4 0.1 pad_add_fusion.place_ref
  120.4 1.4 %collective-permute-done.23.refs_7_ = bf16[448,256]{1,0:T(8,128)(2,1)S(1)} collective-permute-done((bf16[448,256]{1,0:T(8,128)(2,1)S(1)}, bf16[448,256]{1,0:T(8,128)(2,1)S(1)}, u32[]{:S(2)}, u32[]{:S(2)}) %collective-permute-start.23) | collective-permute-done | bytes 229408 | tf_op jit(solution)/shard_map/ppermute | solution.py:393
  121.8 5.4 %shard_map.79 = (f32[588,1024]{1,0:T(8,128)}, bf16[1024,1024]{1,0:T(8,128)(2,1)}) custom-call(s32[2]{0:T(128)S(1)} %pad_add_fusion.place_ref, bf16[448,256]{1,0:T(8,128)(2,1)S(1)} %shard_map.78.refs_0_, bf16[448,256]{1,0:T(8,128)(2,1)S(1)} %collective-permute-done.15.refs_1_, bf16[448,256]{1,0:T(8,128)(2,1)S(1)} %collective-permute-done.18.refs_2_, ...), custom_call_target="tpu_custom_call" | custom-call | tf_op jit(solution)/shard_map/pallas_call | solution.py:610
  (22 shorter events, 0.1 us)
Async XLA Ops:
  1.3 1.3 %copy-start.3 = (bf16[2352,256]{1,0:T(8,128)(2,1)S(1)}, bf16[2352,256]{1,0:T(8,128)(2,1)}, u32[]{:S(2)}) copy-start(bf16[2352,256]{1,0:T(8,128)(2,1)} %raw_ref.1) | copy-start | bytes 3612676
  2.6 0.7 copy-start.6
  3.8 6.9 %copy-start.7 = (s32[8,343]{1,0:T(8,128)S(1)}, s32[8,343]{1,0:T(8,128)}, u32[]{:S(2)}) copy-start(s32[8,343]{1,0:T(8,128)} %conn_ref.1) | copy-start | bytes 32932
  3.8 6.8 %collective-permute-start = (bf16[80,256]{1,0:T(8,128)(2,1)S(1)}, bf16[80,256]{1,0:T(8,128)(2,1)S(1)}, u32[]{:S(2)}, u32[]{:S(2)}) collective-permute-start(bf16[80,256]{1,0:T(8,128)(2,1)S(1)} %shard_map.68), channel_id=1, source_target_pairs={{4,0},{8,4},{12,8},{16,12},{20,16},{24,20},{28,24},{5,1},{9,5},{13... | collective-permute-start | bytes 122888 | tf_op jit(solution)/shard_map/ppermute | solution.py:398
  32.4 12.0 %collective-permute-start.1 = (bf16[6,64,256]{2,1,0:T(8,128)(2,1)S(1)}, bf16[6,64,256]{2,1,0:T(8,128)(2,1)S(1)}, u32[]{:S(2)}, u32[]{:S(2)}) collective-permute-start(bf16[6,64,256]{2,1,0:T(8,128)(2,1)S(1)} %get-tuple-element.51), channel_id=1, source_target_pairs={{0,4},{4,8},{8,12},{12,16},{16,20},{20,24},{24,28},{1,5},{5,9},{9,... | collective-permute-start | bytes 589832 | tf_op jit(solution)/shard_map/ppermute | solution.py:398
  37.2 7.2 %collective-permute-start.2 = (bf16[5,64,256]{2,1,0:T(8,128)(2,1)S(1)}, bf16[5,64,256]{2,1,0:T(8,128)(2,1)S(1)}, u32[]{:S(2)}, u32[]{:S(2)}) collective-permute-start(bf16[5,64,256]{2,1,0:T(8,128)(2,1)S(1)} %get-tuple-element.52), channel_id=1, source_target_pairs={{4,0},{8,4},{12,8},{16,12},{20,16},{24,20},{28,24},{5,1},{9,5},{13... | collective-permute-start | bytes 491528 | tf_op jit(solution)/shard_map/ppermute | solution.py:398
  44.5 9.6 %copy-start.2 = (f32[2560,1]{1,0:T(8,128)S(1)}, f32[2560,1]{1,0:T(8,128)}, u32[]{:S(2)}) copy-start(f32[2560,1]{1,0:T(8,128)} %get-tuple-element.54.pot_ref) | copy-start | bytes 30724
  52.6 11.4 %collective-permute-start.4 = (bf16[2624,256]{1,0:T(8,128)(2,1)}, bf16[2624,256]{1,0:T(8,128)(2,1)}, u32[]{:S(2)}, u32[]{:S(2)}) collective-permute-start(bf16[2624,256]{1,0:T(8,128)(2,1)} %get-tuple-element.76.x_ref), channel_id=1, source_target_pairs={{0,1},{1,0},{2,3},{3,2},{4,5},{5,4},{6,7},{7,6},{8,9},{9,8},{10,11... | collective-permute-start | bytes 4030472 | tf_op jit(solution)/shard_map/ppermute | solution.py:393
  52.6 18.1 %collective-permute-start.3 = (bf16[1344,256]{1,0:T(8,128)(2,1)}, bf16[1344,256]{1,0:T(8,128)(2,1)S(1)}, u32[]{:S(2)}, u32[]{:S(2)}) collective-permute-start(bf16[1344,256]{1,0:T(8,128)(2,1)} %get-tuple-element.58), channel_id=1, source_target_pairs={{0,2},{1,3},{2,0},{3,1},{4,6},{5,7},{6,4},{7,5},{8,10},{9,11},{10,... | collective-permute-start | bytes 2064392 | tf_op jit(solution)/shard_map/ppermute | solution.py:393
  54.1 5.2 %copy-start = (bf16[2624,256]{1,0:T(8,128)(2,1)S(1)}, bf16[2624,256]{1,0:T(8,128)(2,1)}, u32[]{:S(2)}) copy-start(bf16[2624,256]{1,0:T(8,128)(2,1)} %get-tuple-element.76.x_ref) | copy-start | bytes 4030468
  58.6 8.3 %collective-permute-start.5 = (bf16[672,256]{1,0:T(8,128)(2,1)}, bf16[672,256]{1,0:T(8,128)(2,1)}, u32[]{:S(2)}, u32[]{:S(2)}) collective-permute-start(bf16[672,256]{1,0:T(8,128)(2,1)} %get-tuple-element.63), channel_id=1, source_target_pairs={{0,1},{1,0},{2,3},{3,2},{4,5},{5,4},{6,7},{7,6},{8,9},{9,8},{10,11... | collective-permute-start | bytes 1032200 | tf_op jit(solution)/shard_map/ppermute | solution.py:393
  58.8 8.0 %collective-permute-start.6 = (bf16[672,256]{1,0:T(8,128)(2,1)}, bf16[672,256]{1,0:T(8,128)(2,1)}, u32[]{:S(2)}, u32[]{:S(2)}) collective-permute-start(bf16[672,256]{1,0:T(8,128)(2,1)} %get-tuple-element.64), channel_id=1, source_target_pairs={{0,1},{1,0},{2,3},{3,2},{4,5},{5,4},{6,7},{7,6},{8,9},{9,8},{10,11... | collective-permute-start | bytes 1032200 | tf_op jit(solution)/shard_map/ppermute | solution.py:393
  63.9 8.3 %copy-start.1 = (bf16[2,1344,256]{2,1,0:T(8,128)(2,1)S(1)}, bf16[2,1344,256]{2,1,0:T(8,128)(2,1)}, u32[]{:S(2)}) copy-start(bf16[2,1344,256]{2,1,0:T(8,128)(2,1)} %get-tuple-element.57.w_ref) | copy-start | bytes 4128772
  70.6 26.2 %collective-permute-start.11 = (bf16[588,512]{1,0:T(8,128)(2,1)}, bf16[588,512]{1,0:T(8,128)(2,1)}, u32[]{:S(2)}, u32[]{:S(2)}) collective-permute-start(bf16[588,512]{1,0:T(8,128)(2,1)} %get-tuple-element.81), channel_id=1, source_target_pairs={{0,2},{1,3},{2,0},{3,1},{4,6},{5,7},{6,4},{7,5},{8,10},{9,11},{10,... | collective-permute-start | bytes 1806344 | tf_op jit(solution)/shard_map/ppermute | solution.py:393
  74.7 0.8 copy-start.4
  75.5 7.6 %copy-start.5 = (f32[448,256]{1,0:T(8,128)S(1)}, f32[448,256]{1,0:T(8,128)}, u32[]{:S(2)}) copy-start(f32[448,256]{1,0:T(8,128)} %copy-done.4) | copy-start | bytes 1376260
  75.5 7.6 %collective-permute-start.7 = (bf16[448,256]{1,0:T(8,128)(2,1)}, bf16[448,256]{1,0:T(8,128)(2,1)S(1)}, u32[]{:S(2)}, u32[]{:S(2)}) collective-permute-start(bf16[448,256]{1,0:T(8,128)(2,1)} %get-tuple-element.71), channel_id=1, source_target_pairs={{0,4},{4,0},{8,12},{12,8},{16,20},{20,16},{24,28},{28,24},{1,5},{5... | collective-permute-start | bytes 688136 | tf_op jit(solution)/shard_map/ppermute | solution.py:393
  77.7 31.2 %collective-permute-start.16 = (bf16[588,512]{1,0:T(8,128)(2,1)}, bf16[588,512]{1,0:T(8,128)(2,1)}, u32[]{:S(2)}, u32[]{:S(2)}) collective-permute-start(bf16[588,512]{1,0:T(8,128)(2,1)} %get-tuple-element.83), channel_id=1, source_target_pairs={{0,3},{1,2},{2,1},{3,0},{4,7},{5,6},{6,5},{7,4},{8,11},{9,10},{10,... | collective-permute-start | bytes 1806344 | tf_op jit(solution)/shard_map/ppermute | solution.py:393
  83.8 7.4 %collective-permute-start.10 = (bf16[112,256]{1,0:T(8,128)(2,1)S(1)}, bf16[112,256]{1,0:T(8,128)(2,1)S(1)}, u32[]{:S(2)}, u32[]{:S(2)}) collective-permute-start(bf16[112,256]{1,0:T(8,128)(2,1)S(1)} %get-tuple-element.80), channel_id=1, source_target_pairs={{0,24},{4,28},{8,16},{12,20},{16,8},{20,12},{24,0},{28,4},{1,25},{... | collective-permute-start | bytes 172040 | tf_op jit(solution)/shard_map/ppermute | solution.py:393
  88.7 28.2 %collective-permute-start.22 = (bf16[588,512]{1,0:T(8,128)(2,1)S(1)}, bf16[588,512]{1,0:T(8,128)(2,1)S(1)}, u32[]{:S(2)}, u32[]{:S(2)}) collective-permute-start(bf16[588,512]{1,0:T(8,128)(2,1)S(1)} %get-tuple-element.85), channel_id=1, source_target_pairs={{0,1},{1,0},{2,3},{3,2},{4,5},{5,4},{6,7},{7,6},{8,9},{9,8},{10,11... | collective-permute-start | bytes 1806344 | tf_op jit(solution)/shard_map/ppermute | solution.py:393
  88.7 4.9 %collective-permute-start.8 = (bf16[112,256]{1,0:T(8,128)(2,1)S(1)}, bf16[112,256]{1,0:T(8,128)(2,1)S(1)}, u32[]{:S(2)}, u32[]{:S(2)}) collective-permute-start(bf16[112,256]{1,0:T(8,128)(2,1)S(1)} %get-tuple-element.73), channel_id=1, source_target_pairs={{0,8},{4,12},{8,0},{12,4},{16,24},{20,28},{24,16},{28,20},{1,9},{5... | collective-permute-start | bytes 172040 | tf_op jit(solution)/shard_map/ppermute | solution.py:393
  91.1 5.1 %collective-permute-start.9 = (bf16[112,256]{1,0:T(8,128)(2,1)S(1)}, bf16[112,256]{1,0:T(8,128)(2,1)S(1)}, u32[]{:S(2)}, u32[]{:S(2)}) collective-permute-start(bf16[112,256]{1,0:T(8,128)(2,1)S(1)} %get-tuple-element.74), channel_id=1, source_target_pairs={{0,16},{4,20},{8,24},{12,28},{16,0},{20,4},{24,8},{28,12},{1,17},{... | collective-permute-start | bytes 172040 | tf_op jit(solution)/shard_map/ppermute | solution.py:393
  96.8 4.9 %collective-permute-start.12 = (bf16[112,256]{1,0:T(8,128)(2,1)S(1)}, bf16[112,256]{1,0:T(8,128)(2,1)S(1)}, u32[]{:S(2)}, u32[]{:S(2)}) collective-permute-start(bf16[112,256]{1,0:T(8,128)(2,1)S(1)} %shard_map.77.own_ref), channel_id=1, source_target_pairs={{0,8},{4,12},{8,0},{12,4},{16,24},{20,28},{24,16},{28,20},{1,9},{5... | collective-permute-start | bytes 172040 | tf_op jit(solution)/shard_map/ppermute | solution.py:393
  98.7 5.8 %collective-permute-start.13 = (bf16[112,256]{1,0:T(8,128)(2,1)S(1)}, bf16[112,256]{1,0:T(8,128)(2,1)S(1)}, u32[]{:S(2)}, u32[]{:S(2)}) collective-permute-start(bf16[112,256]{1,0:T(8,128)(2,1)S(1)} %shard_map.77.own_ref), channel_id=1, source_target_pairs={{0,16},{4,20},{8,24},{12,28},{16,0},{20,4},{24,8},{28,12},{1,17},{... | collective-permute-start | bytes 172040 | tf_op jit(solution)/shard_map/ppermute | solution.py:393
  101.7 6.0 %collective-permute-start.14 = (bf16[112,256]{1,0:T(8,128)(2,1)S(1)}, bf16[112,256]{1,0:T(8,128)(2,1)S(1)}, u32[]{:S(2)}, u32[]{:S(2)}) collective-permute-start(bf16[112,256]{1,0:T(8,128)(2,1)S(1)} %shard_map.77.own_ref), channel_id=1, source_target_pairs={{0,24},{4,28},{8,16},{12,20},{16,8},{20,12},{24,0},{28,4},{1,25},{... | collective-permute-start | bytes 172040 | tf_op jit(solution)/shard_map/ppermute | solution.py:393
  108.2 6.1 %collective-permute-start.15 = (bf16[448,256]{1,0:T(8,128)(2,1)S(1)}, bf16[448,256]{1,0:T(8,128)(2,1)S(1)}, u32[]{:S(2)}, u32[]{:S(2)}) collective-permute-start(bf16[448,256]{1,0:T(8,128)(2,1)S(1)} %shard_map.78.refs_0_), channel_id=1, source_target_pairs={{0,4},{4,0},{8,12},{12,8},{16,20},{20,16},{24,28},{28,24},{1,5},{5... | collective-permute-start | bytes 688136 | tf_op jit(solution)/shard_map/ppermute | solution.py:393
  108.5 8.4 %collective-permute-start.20 = (bf16[448,256]{1,0:T(8,128)(2,1)S(1)}, bf16[448,256]{1,0:T(8,128)(2,1)S(1)}, u32[]{:S(2)}, u32[]{:S(2)}) collective-permute-start(bf16[448,256]{1,0:T(8,128)(2,1)S(1)} %shard_map.78.refs_0_), channel_id=1, source_target_pairs={{0,2},{1,3},{2,0},{3,1},{4,6},{5,7},{6,4},{7,5},{8,10},{9,11},{10,... | collective-permute-start | bytes 688136 | tf_op jit(solution)/shard_map/ppermute | solution.py:393
  108.9 8.0 %collective-permute-start.18 = (bf16[448,256]{1,0:T(8,128)(2,1)S(1)}, bf16[448,256]{1,0:T(8,128)(2,1)S(1)}, u32[]{:S(2)}, u32[]{:S(2)}) collective-permute-start(bf16[448,256]{1,0:T(8,128)(2,1)S(1)} %shard_map.78.refs_0_), channel_id=1, source_target_pairs={{0,1},{1,0},{2,3},{3,2},{4,5},{5,4},{6,7},{7,6},{8,9},{9,8},{10,11... | collective-permute-start | bytes 688136 | tf_op jit(solution)/shard_map/ppermute | solution.py:393
  114.3 6.0 %collective-permute-start.17 = (bf16[448,256]{1,0:T(8,128)(2,1)S(1)}, bf16[448,256]{1,0:T(8,128)(2,1)S(1)}, u32[]{:S(2)}, u32[]{:S(2)}) collective-permute-start(bf16[448,256]{1,0:T(8,128)(2,1)S(1)} %collective-permute-done.15.refs_1_), channel_id=1, source_target_pairs={{0,2},{1,3},{2,0},{3,1},{4,6},{5,7},{6,4},{7,5},{8,10},{9,11},{10,... | collective-permute-start | bytes 688136 | tf_op jit(solution)/shard_map/ppermute | solution.py:393
  114.9 5.5 %collective-permute-start.19 = (bf16[448,256]{1,0:T(8,128)(2,1)S(1)}, bf16[448,256]{1,0:T(8,128)(2,1)S(1)}, u32[]{:S(2)}, u32[]{:S(2)}) collective-permute-start(bf16[448,256]{1,0:T(8,128)(2,1)S(1)} %collective-permute-done.15.refs_1_), channel_id=1, source_target_pairs={{0,1},{1,0},{2,3},{3,2},{4,5},{5,4},{6,7},{7,6},{8,9},{9,8},{10,11... | collective-permute-start | bytes 688136 | tf_op jit(solution)/shard_map/ppermute | solution.py:393
  117.0 3.4 %collective-permute-start.21 = (bf16[448,256]{1,0:T(8,128)(2,1)S(1)}, bf16[448,256]{1,0:T(8,128)(2,1)S(1)}, u32[]{:S(2)}, u32[]{:S(2)}) collective-permute-start(bf16[448,256]{1,0:T(8,128)(2,1)S(1)} %collective-permute-done.20.refs_4_), channel_id=1, source_target_pairs={{0,1},{1,0},{2,3},{3,2},{4,5},{5,4},{6,7},{7,6},{8,9},{9,8},{10,11... | collective-permute-start | bytes 688136 | tf_op jit(solution)/shard_map/ppermute | solution.py:393
  120.4 1.5 %collective-permute-start.23 = (bf16[448,256]{1,0:T(8,128)(2,1)S(1)}, bf16[448,256]{1,0:T(8,128)(2,1)S(1)}, u32[]{:S(2)}, u32[]{:S(2)}) collective-permute-start(bf16[448,256]{1,0:T(8,128)(2,1)S(1)} %collective-permute-done.17.refs_5_), channel_id=1, source_target_pairs={{0,1},{1,0},{2,3},{3,2},{4,5},{5,4},{6,7},{7,6},{8,9},{9,8},{10,11... | collective-permute-start | bytes 688136 | tf_op jit(solution)/shard_map/ppermute | solution.py:393

commit v9 on v8

--- a/solution.py
+++ b/solution.py
@@ -73,7 +73,7 @@
     return jnp.where(mask, 1.0, 0.0).astype(BF16)
 
 
-def order(fp, ip, conn_ref, face_ref, h_ref, x_ref, pot_ref, hcan_ref, v_ref, potc_ref, node_ref):
+def order(fp, ip, arrived, conn_ref, face_ref, h_ref, x_ref, pot_ref, hcan_ref, v_ref, potc_ref, node_ref):
     cells, npc = conn_ref.shape
     nodes = x_ref.shape[0]
     face = face_ref.shape[1]
@@ -106,6 +106,7 @@
     slot = jnp.where(top > 0.5, top_slot + float(stride), jnp.where(bot > 0.5, bot_slot, mid_rank + float(fp)))
     high, low = halves(conn + 1.0)
     number = iota((8, nodes), 1)[:1]
+    arrived()
     for c in range(cells):
         perm = flat(iota((cp, npc), 0) == slot[c : c + 1])
         half = mul(perm, h_ref[c]).astype(BF16)
@@ -135,9 +136,7 @@
 
 
 def mul_r(a, b):
-    n = b.shape[1]
-    both = mul(a, jnp.concatenate(split(b), axis=1))
-    return both[:, :n] + both[:, n:]
+    return mul(a, b.astype(BF16))
 
 
 def sweep(h_ref, y_ref, fp, emit):
@@ -204,9 +203,11 @@
 
 def free_kernel(
     fp, ip, conn_ref, face_ref, hraw_ref, raw_ref, potraw_ref, ghost_ref,
-    h_ref, v_ref, pot_ref, node_ref, first_ref, own_ref, up_ref, down_ref, a_ref, b_ref,
+    h_ref, v_ref, pot_ref, node_ref, first_ref, own_ref, up_ref, down_ref, a_ref, b_ref, hin_ref, sem,
 ):
-    order(fp, ip, conn_ref, face_ref, hraw_ref, raw_ref, potraw_ref, h_ref, v_ref, pot_ref, node_ref)
+    copy = pltpu.make_async_copy(hraw_ref, hin_ref, sem)
+    copy.start()
+    order(fp, ip, copy.wait, conn_ref, face_ref, hin_ref, raw_ref, potraw_ref, h_ref, v_ref, pot_ref, node_ref)
     cells, cp = h_ref.shape[:2]
     stride = cp - fp
     total = cells * stride
@@ -464,7 +465,7 @@
 def paired_residual_kernel(place_ref, *refs):
     q_refs, refs = refs[:8], refs[8:]
     parts = 4
-    row_refs, (out_ref, p_ref, q_ref) = refs[:parts], refs[parts:]
+    row_refs, (out_hbm, p_hbm, out_ref, p_ref, q_ref, sems) = refs[:parts], refs[parts:]
     width = row_refs[0].shape[1] // 2
     half = width // 2
     me, mine = place_ref[0], place_ref[1]
@@ -499,12 +500,18 @@
             block = (one.astype(F32) + turned(two)).astype(BF16)
             put(i, j, block)
             put(j, i, turned(block).astype(BF16))
+    copies = [pltpu.make_async_copy(p_ref, p_hbm, sems.at[parts])]
+    copies[0].start()
     x = jnp.concatenate([ref[:, :width] for ref in row_refs], axis=1)
     spots = [pl.ds(pl.multiple_of(jnp.bitwise_xor(me, k) * width, width), width) for k in range(parts)]
     for k in range(parts):
         at = spots[k]
         p = jnp.concatenate([p_ref[spots[m], at] for m in range(parts)], axis=0)
-        out_ref[:, at] = row_refs[k][:, width:].astype(F32) - mul(x, p)
+        out_ref[k] = row_refs[k][:, width:].astype(F32) - mul(x, p)
+        copies.append(pltpu.make_async_copy(out_ref.at[k], out_hbm.at[:, at], sems.at[k]))
+        copies[-1].start()
+    for copy in copies:
+        copy.wait()
 
 
 def paired_tail(x_own, image, w_own, w_side, give, node_row, o, d, dom, nodes):
@@ -604,14 +611,20 @@
     q2 = [swap(share, "orb", 2), swap(got, "orb", 2)]
     q1 = [swap(share, "orb", 1), swap(got, "orb", 1)]
     q3a = swap(q2[0], "orb", 1)
-    q2[1], q1[0], q1[1], q3a, row1 = lax.optimization_barrier((q2[1], q1[0], q1[1], q3a, row1))
+    q2[1], row1 = lax.optimization_barrier((q2[1], row1))
     q3 = [q3a, swap(q2[1], "orb", 1)]
     cols = orb * width
     return pl.pallas_call(
         paired_residual_kernel,
         in_specs=[smem] + [vmem] * 12,
         out_shape=(sds((rows, cols), F32), sds((cols, cols), BF16)),
-        scratch_shapes=[pltpu.VMEM((orb, count, width), BF16)],
+        out_specs=[pl.BlockSpec(memory_space=pl.ANY)] * 2,
+        scratch_shapes=[
+            pltpu.VMEM((orb, rows, width), F32),
+            pltpu.VMEM((cols, cols), BF16),
+            pltpu.VMEM((orb, count, width), BF16),
+            pltpu.SemaphoreType.DMA((orb + 1,)),
+        ],
         compiler_params=params(),
     )(jnp.stack([o, d % 2]), share, got, *q1, *q2, *q3, row0, row1, row2, row3)
 
@@ -642,8 +655,10 @@
     cost = pl.CostEstimate(
         flops=2 * DEGREE * cells * cp * cp * width, bytes_accessed=8 << 20, transcendentals=0
     )
+    vmem = pl.BlockSpec(memory_space=pltpu.VMEM)
     hcan, y, pot, node, first, own, up, down = pl.pallas_call(
         functools.partial(free_kernel, fp, ip),
+        in_specs=[vmem] * 2 + [pl.BlockSpec(memory_space=pl.ANY)] + [vmem] * 3,
         out_shape=[
             sds((cells, cp, cp), BF16),
             sds((total, width), BF16),
@@ -654,7 +669,7 @@
             sds((DEGREE + 1 + extra, fp, width), BF16),
             sds((DEGREE + extra, fp, width), BF16),
         ],
-        scratch_shapes=[ext, ext],
+        scratch_shapes=[ext, ext, pltpu.VMEM((cells, npc, npc), BF16), pltpu.SemaphoreType.DMA],
         compiler_params=params(),
         cost_estimate=cost,
     )(connectivity, face_row, cell_hamiltonian, orbitals, pot_row, ghost)

time: 128 us -> 125 us (0.977)
  Pallas kernels: 55.8 us -> 52.7 us
    pallas_call x1, Pallas kernels: 21.8 us -> 19.3 us  [body(): pl.pallas_call(functools.partial(free_kernel, fp, ip), in_specs=[vmem] *...]
  transfers between devices with their start and end apart: 24 -> 24, of which waited for: 13 -> 12; matrix products, arithmetic and copies ran while one was open for 3% -> 3% of each run, Pallas kernels for 16% -> 16%
where the time goes in v9:
time: 125 us; the launch traced here: 124 us
  Pallas kernels  52.7 us (42%)
  waiting for transfers between devices  37.8 us (30%)
  starting transfers between devices  25.6 us (20%)
  local copies, waits for them, and re-layouts  6.74 us (5%)
    ppermute x21, waiting for transfers between devices, swap(): lax.ppermute(block, axis, [(i, i ^ bit) for i in range(lax.axis_size(axis...  29.6 us
    pallas_call x1, Pallas kernels, body(): pl.pallas_call(functools.partial(free_kernel, fp, ip), in_specs=[vmem] *...  19.3 us
    ppermute x21, starting transfers between devices, swap(): lax.ppermute(block, axis, [(i, i ^ bit) for i in range(lax.axis_size(axis...  18.2 us
    pallas_call x2, Pallas kernels, back(): pl.pallas_call(back_pair_kernel, grid=(1,), in_specs=[smem, whole(1, tota...  8.48 us
    ppermute x3, waiting for transfers between devices, shift(): lax.ppermute(block, axis, [(i, i + distance) for i in range(n) if 0 <= i...  8.13 us
    pallas_call x1, Pallas kernels, body(): pl.pallas_call(functools.partial(forced_kernel, fp), in_specs=[pl.BlockSp...  8.09 us
    ppermute x3, starting transfers between devices, shift(): lax.ppermute(block, axis, [(i, i + distance) for i in range(n) if 0 <= i...  7.42 us
    unnamed x17, local copies, waits for them, and re-layouts  5.94 us
  transfers between devices with their start and end apart: 24, of which 12 were waited for; matrix products, arithmetic and copies ran while one was open for 3% of the time, Pallas kernels for 16%

profile of v9, /device:TPU:0, one launch (start us, length us, event | category | flops | bytes accessed | tf_op | source)
XLA Modules:
  0.0 124.3 jit_solution(14129666237229895662)
XLA Ops:
  0.6 0.7 reshape.15.pot_ref.potraw_ref
  1.3 1.3 %copy-done.3 = bf16[2352,256]{1,0:T(8,128)(2,1)S(1)} copy-done((bf16[2352,256]{1,0:T(8,128)(2,1)S(1)}, bf16[2352,256]{1,0:T(8,128)(2,1)}, u32[]{:S(2)}) %copy-start.3) | copy-done | bytes 1204248
  2.6 0.7 copy-done.6
  3.3 0.5 shard_map.68
  3.8 0.0 copy-start.7
  3.8 1.3 %collective-permute-start = (bf16[80,256]{1,0:T(8,128)(2,1)S(1)}, bf16[80,256]{1,0:T(8,128)(2,1)S(1)}, u32[]{:S(2)}, u32[]{:S(2)}) collective-permute-start(bf16[80,256]{1,0:T(8,128)(2,1)S(1)} %shard_map.68), channel_id=1, source_target_pairs={{4,0},{8,4},{12,8},{16,12},{20,16},{24,20},{28,24},{5,1},{9,5},{13... | collective-permute-start | bytes 122888 | tf_op jit(solution)/shard_map/ppermute | solution.py:399
  5.1 3.2 %copy.7.hraw_ref = bf16[8,343,343]{2,1,0:T(8,128)(2,1)} copy(bf16[8,343,343]{2,0,1:T(8,128)(2,1)} %param.7) | data formatting | bytes 3764768 | tf_op args[2]
  8.3 2.3 %collective-permute-done.ghost_ref = bf16[80,256]{1,0:T(8,128)(2,1)S(1)} collective-permute-done((bf16[80,256]{1,0:T(8,128)(2,1)S(1)}, bf16[80,256]{1,0:T(8,128)(2,1)S(1)}, u32[]{:S(2)}, u32[]{:S(2)}) %collective-permute-start) | collective-permute-done | bytes 40992 | tf_op jit(solution)/shard_map/ppermute | solution.py:399
  10.6 19.3 %shard_map.69 = (bf16[8,384,384]{2,1,0:T(8,128)(2,1)}, bf16[2560,256]{1,0:T(8,128)(2,1)S(1)}, f32[2560,1]{1,0:T(8,128)}, f32[8,1,320]{2,1,0:T(1,128)S(1)}, bf16[...) custom-call(s32[8,343]{1,0:T(8,128)S(1)} %copy-done.7, ...), custom_call_target="tpu_custom_call" | custom-call | flops 2415919104 | bytes 8388608 | tf_op jit(solution)/shard_map/pallas_call | solution.py:659
  30.0 4.8 %collective-permute-start.1 = (bf16[6,64,256]{2,1,0:T(8,128)(2,1)S(1)}, bf16[6,64,256]{2,1,0:T(8,128)(2,1)S(1)}, u32[]{:S(2)}, u32[]{:S(2)}) collective-permute-start(bf16[6,64,256]{2,1,0:T(8,128)(2,1)S(1)} %get-tuple-element.48), channel_id=1, source_target_pairs={{0,4},{4,8},{8,12},{12,16},{16,20},{20,24},{24,28},{1,5},{5,9},{9,... | collective-permute-start | bytes 589832 | tf_op jit(solution)/shard_map/ppermute | solution.py:399
  34.8 1.3 %collective-permute-start.2 = (bf16[5,64,256]{2,1,0:T(8,128)(2,1)S(1)}, bf16[5,64,256]{2,1,0:T(8,128)(2,1)S(1)}, u32[]{:S(2)}, u32[]{:S(2)}) collective-permute-start(bf16[5,64,256]{2,1,0:T(8,128)(2,1)S(1)} %get-tuple-element.49), channel_id=1, source_target_pairs={{4,0},{8,4},{12,8},{16,12},{20,16},{24,20},{28,24},{5,1},{9,5},{13... | collective-permute-start | bytes 491528 | tf_op jit(solution)/shard_map/ppermute | solution.py:399
  36.2 0.1 pad_add_fusion.3.place_ref
  36.2 5.8 %collective-permute-done.2.fromright_ref = bf16[5,64,256]{2,1,0:T(8,128)(2,1)S(1)} collective-permute-done((bf16[5,64,256]{2,1,0:T(8,128)(2,1)S(1)}, bf16[5,64,256]{2,1,0:T(8,128)(2,1)S(1)}, u32[]{:S(2)}, u32[]{:S(2)}) %collective-permute-start.2) | collective-permute-done | bytes 163872 | tf_op jit(solution)/shard_map/ppermute | solution.py:399
  42.0 0.0 collective-permute-done.1.fromleft_ref
  42.0 8.1 %shard_map.70 = (bf16[2624,256]{1,0:T(8,128)(2,1)}, f32[64,256]{1,0:T(8,128)S(1)}, bf16[1344,256]{1,0:T(8,128)(2,1)}) custom-call(s32[2]{0:T(128)S(1)} %pad_add_fusion.3.place_ref, bf16[2560,256]{1,0:T(8,128)(2,1)S(1)} %get-tuple-element.45.v_ref, bf16[80,256]{1,0:T(8,128)(2,1)S(1)} %collective-permute-done.ghost_ref, ...), custom_call_target="tpu_custom_call" | custom-call | flops 2415919104 | bytes 8388608 | tf_op jit(solution)/shard_map/pallas_call | solution.py:682
  50.1 0.0 collective-permute-start.4
  50.1 1.5 %collective-permute-start.3 = (bf16[1344,256]{1,0:T(8,128)(2,1)}, bf16[1344,256]{1,0:T(8,128)(2,1)S(1)}, u32[]{:S(2)}, u32[]{:S(2)}) collective-permute-start(bf16[1344,256]{1,0:T(8,128)(2,1)} %get-tuple-element.55), channel_id=1, source_target_pairs={{0,2},{1,3},{2,0},{3,1},{4,6},{5,7},{6,4},{7,5},{8,10},{9,11},{10,... | collective-permute-start | bytes 2064392 | tf_op jit(solution)/shard_map/ppermute | solution.py:394
  51.6 4.5 %shard_map.71 = (bf16[2560,256]{1,0:T(8,128)(2,1)S(1)}, bf16[2,1344,256]{2,1,0:T(8,128)(2,1)}, bf16[672,256]{1,0:T(8,128)(2,1)}, bf16[672,256]{1,0:T(8,128)(2,1)}) custom-call(s32[2]{0:T(128)S(1)} %pad_add_fusion.3.place_ref, bf16[2624,256]{1,0:T(8,128)(2,1)} %get-tuple-element.73.x_ref, f32[64,256]{1,0:T(8,128)S(1)} %get-tuple-element.53.face_image_ref, ...), custom_call_target="tpu_custom_call" | custom-call | flops 1048576 | bytes 1024 | tf_op jit(solution)/shard_map/pallas_call | solution.py:694
  56.2 0.2 collective-permute-start.5
  56.4 0.3 collective-permute-start.6
  56.7 0.1 pad_add_fusion.4.at_ref
  56.8 0.1 reshape.16.node_ref
  56.9 4.7 %shard_map.73 = (bf16[588,512]{1,0:T(8,128)(2,1)}, bf16[588,512]{1,0:T(8,128)(2,1)}) custom-call(s32[2]{0:T(128)S(1)} %pad_add_fusion.4.at_ref, f32[1,2560]{1,0:T(1,128)S(1)} %reshape.16.node_ref, bf16[2624,256]{1,0:T(8,128)(2,1)S(1)} %copy-done, bf16[2560,256]{1,0:T(8,128)(2,1)S(1)} %get-tuple-element.74.image_ref), custom_call_target="tpu_custom_call" | custom-call | flops 1048576 | bytes 1024 | tf_op jit(solution)/shard_map/pallas_call | solution.py:531
  61.5 0.0 collective-permute-done.4.other_ref
  61.5 2.9 %shard_map.72.near_ref = f32[384,256]{1,0:T(8,128)S(1)} custom-call(s32[1]{0:T(128)} %bitcast.4.core_ref, bf16[2624,256]{1,0:T(8,128)(2,1)S(1)} %copy-done, bf16[2,1344,256]{2,1,0:T(8,128)(2,1)} %get-tuple-element.54.w_ref, bf16[2624,256]{1,0:T(8,128)(2,1)} %collective-permute-done.4.other_ref), custom_call_target="tpu_custom_call" | custom-call | flops 1048576 | bytes 1024 | tf_op jit(solution)/shard_map/pallas_call | solution.py:545
  64.4 0.0 collective-permute-done.6.second_ref
  64.4 3.8 %collective-permute-done.3.far_ref = bf16[1344,256]{1,0:T(8,128)(2,1)S(1)} collective-permute-done((bf16[1344,256]{1,0:T(8,128)(2,1)}, bf16[1344,256]{1,0:T(8,128)(2,1)S(1)}, u32[]{:S(2)}, u32[]{:S(2)}) %collective-permute-start.3) | collective-permute-done | bytes 688160 | tf_op jit(solution)/shard_map/ppermute | solution.py:394
  68.2 1.5 %collective-permute-start.11 = (bf16[588,512]{1,0:T(8,128)(2,1)}, bf16[588,512]{1,0:T(8,128)(2,1)}, u32[]{:S(2)}, u32[]{:S(2)}) collective-permute-start(bf16[588,512]{1,0:T(8,128)(2,1)} %get-tuple-element.78), channel_id=1, source_target_pairs={{0,2},{1,3},{2,0},{3,1},{4,6},{5,7},{6,4},{7,5},{8,10},{9,11},{10,... | collective-permute-start | bytes 1806344 | tf_op jit(solution)/shard_map/ppermute | solution.py:394
  69.7 0.1 pad_add_fusion.2.place_ref
  69.8 0.1 pad_add_fusion.1.bits_ref
  69.8 2.5 %shard_map.74 = (f32[448,256]{1,0:T(8,128)S(1)}, bf16[448,256]{1,0:T(8,128)(2,1)}) custom-call(s32[2]{0:T(128)S(1)} %pad_add_fusion.1.bits_ref, s32[2]{0:T(128)S(1)} %pad_add_fusion.2.place_ref, bf16[2,1344,256]{2,1,0:T(8,128)(2,1)S(1)} %copy-done.1, bf16[672,256]{1,0:T(8,128)(2,1)} %collective-permute-done.5.first_ref, ...), custom_call_target="tpu_custom_call" | custom-call | flops 704643072 | bytes 4194304 | tf_op jit(solution)/shard_map/pallas_call | solution.py:566
  72.3 0.8 copy-done.4
  73.1 2.2 %collective-permute-start.7 = (bf16[448,256]{1,0:T(8,128)(2,1)}, bf16[448,256]{1,0:T(8,128)(2,1)S(1)}, u32[]{:S(2)}, u32[]{:S(2)}) collective-permute-start(bf16[448,256]{1,0:T(8,128)(2,1)} %get-tuple-element.68), channel_id=1, source_target_pairs={{0,4},{4,0},{8,12},{12,8},{16,20},{20,16},{24,28},{28,24},{1,5},{5... | collective-permute-start | bytes 688136 | tf_op jit(solution)/shard_map/ppermute | solution.py:394
  75.3 0.0 collective-permute-start.16
  75.3 0.1 pad_add_fusion.5.at_ref
  75.4 3.8 %shard_map.76 = (bf16[588,512]{1,0:T(8,128)(2,1)S(1)}, bf16[588,512]{1,0:T(8,128)(2,1)S(1)}) custom-call(s32[2]{0:T(128)S(1)} %pad_add_fusion.5.at_ref, f32[1,2560]{1,0:T(1,128)S(1)} %reshape.16.node_ref, bf16[2624,256]{1,0:T(8,128)(2,1)S(1)} %copy-done, bf16[2560,256]{1,0:T(8,128)(2,1)S(1)} %get-tuple-element.74.image_ref), custom_call_target="tpu_custom_call" | custom-call | flops 1048576 | bytes 1024 | tf_op jit(solution)/shard_map/pallas_call | solution.py:531
  79.2 1.5 %collective-permute-done.7.refs_0_ = bf16[448,256]{1,0:T(8,128)(2,1)S(1)} collective-permute-done((bf16[448,256]{1,0:T(8,128)(2,1)}, bf16[448,256]{1,0:T(8,128)(2,1)S(1)}, u32[]{:S(2)}, u32[]{:S(2)}) %collective-permute-start.7) | collective-permute-done | bytes 229408 | tf_op jit(solution)/shard_map/ppermute | solution.py:394
  80.7 0.6 shard_map.75
  81.4 4.9 %collective-permute-start.10 = (bf16[112,256]{1,0:T(8,128)(2,1)S(1)}, bf16[112,256]{1,0:T(8,128)(2,1)S(1)}, u32[]{:S(2)}, u32[]{:S(2)}) collective-permute-start(bf16[112,256]{1,0:T(8,128)(2,1)S(1)} %get-tuple-element.77), channel_id=1, source_target_pairs={{0,24},{4,28},{8,16},{12,20},{16,8},{20,12},{24,0},{28,4},{1,25},{... | collective-permute-start | bytes 172040 | tf_op jit(solution)/shard_map/ppermute | solution.py:394
  86.3 0.0 collective-permute-start.21
  86.3 0.0 collective-permute-start.8
  86.3 2.4 %collective-permute-done.10.refs_2_ = bf16[112,256]{1,0:T(8,128)(2,1)S(1)} collective-permute-done((bf16[112,256]{1,0:T(8,128)(2,1)S(1)}, bf16[112,256]{1,0:T(8,128)(2,1)S(1)}, u32[]{:S(2)}, u32[]{:S(2)}) %collective-permute-start.10) | collective-permute-done | bytes 57376 | tf_op jit(solution)/shard_map/ppermute | solution.py:394
  88.7 0.9 collective-permute-start.9
  89.6 1.6 %collective-permute-done.8.refs_0_ = bf16[112,256]{1,0:T(8,128)(2,1)S(1)} collective-permute-done((bf16[112,256]{1,0:T(8,128)(2,1)S(1)}, bf16[112,256]{1,0:T(8,128)(2,1)S(1)}, u32[]{:S(2)}, u32[]{:S(2)}) %collective-permute-start.8) | collective-permute-done | bytes 57376 | tf_op jit(solution)/shard_map/ppermute | solution.py:394
  91.2 2.5 %collective-permute-done.9.refs_1_ = bf16[112,256]{1,0:T(8,128)(2,1)S(1)} collective-permute-done((bf16[112,256]{1,0:T(8,128)(2,1)S(1)}, bf16[112,256]{1,0:T(8,128)(2,1)S(1)}, u32[]{:S(2)}, u32[]{:S(2)}) %collective-permute-start.9) | collective-permute-done | bytes 57376 | tf_op jit(solution)/shard_map/ppermute | solution.py:394
  93.8 0.6 shard_map.77.own_ref
  94.4 1.9 %collective-permute-start.12 = (bf16[112,256]{1,0:T(8,128)(2,1)S(1)}, bf16[112,256]{1,0:T(8,128)(2,1)S(1)}, u32[]{:S(2)}, u32[]{:S(2)}) collective-permute-start(bf16[112,256]{1,0:T(8,128)(2,1)S(1)} %shard_map.77.own_ref), channel_id=1, source_target_pairs={{0,8},{4,12},{8,0},{12,4},{16,24},{20,28},{24,16},{28,20},{1,9},{5... | collective-permute-start | bytes 172040 | tf_op jit(solution)/shard_map/ppermute | solution.py:394
  96.3 3.0 %collective-permute-start.13 = (bf16[112,256]{1,0:T(8,128)(2,1)S(1)}, bf16[112,256]{1,0:T(8,128)(2,1)S(1)}, u32[]{:S(2)}, u32[]{:S(2)}) collective-permute-start(bf16[112,256]{1,0:T(8,128)(2,1)S(1)} %shard_map.77.own_ref), channel_id=1, source_target_pairs={{0,16},{4,20},{8,24},{12,28},{16,0},{20,4},{24,8},{28,12},{1,17},{... | collective-permute-start | bytes 172040 | tf_op jit(solution)/shard_map/ppermute | solution.py:394
  99.3 0.0 collective-permute-start.14
  99.3 2.8 %collective-permute-done.13.refs_1_ = bf16[112,256]{1,0:T(8,128)(2,1)S(1)} collective-permute-done((bf16[112,256]{1,0:T(8,128)(2,1)S(1)}, bf16[112,256]{1,0:T(8,128)(2,1)S(1)}, u32[]{:S(2)}, u32[]{:S(2)}) %collective-permute-start.13) | collective-permute-done | bytes 57376 | tf_op jit(solution)/shard_map/ppermute | solution.py:394
  102.1 3.2 %collective-permute-done.14.refs_2_ = bf16[112,256]{1,0:T(8,128)(2,1)S(1)} collective-permute-done((bf16[112,256]{1,0:T(8,128)(2,1)S(1)}, bf16[112,256]{1,0:T(8,128)(2,1)S(1)}, u32[]{:S(2)}, u32[]{:S(2)}) %collective-permute-start.14) | collective-permute-done | bytes 57376 | tf_op jit(solution)/shard_map/ppermute | solution.py:394
  105.3 0.6 shard_map.78.refs_0_
  105.8 0.3 collective-permute-start.15
  106.1 0.4 collective-permute-start.19
  106.5 0.0 collective-permute-done.16.refs_11_
  106.5 5.4 %collective-permute-done.15.refs_1_ = bf16[448,256]{1,0:T(8,128)(2,1)S(1)} collective-permute-done((bf16[448,256]{1,0:T(8,128)(2,1)S(1)}, bf16[448,256]{1,0:T(8,128)(2,1)S(1)}, u32[]{:S(2)}, u32[]{:S(2)}) %collective-permute-start.15) | collective-permute-done | bytes 229408 | tf_op jit(solution)/shard_map/ppermute | solution.py:394
  111.9 0.5 collective-permute-start.20
  112.4 0.5 collective-permute-start.18
  112.9 0.0 collective-permute-done.19.refs_4_
  113.0 0.0 collective-permute-start.22
  113.0 5.0 %collective-permute-done.20.refs_5_ = bf16[448,256]{1,0:T(8,128)(2,1)S(1)} collective-permute-done((bf16[448,256]{1,0:T(8,128)(2,1)S(1)}, bf16[448,256]{1,0:T(8,128)(2,1)S(1)}, u32[]{:S(2)}, u32[]{:S(2)}) %collective-permute-start.20) | collective-permute-done | bytes 229408 | tf_op jit(solution)/shard_map/ppermute | solution.py:394
  117.9 0.1 pad_add_fusion.place_ref
  118.0 1.4 %collective-permute-done.23.refs_7_ = bf16[448,256]{1,0:T(8,128)(2,1)S(1)} collective-permute-done((bf16[448,256]{1,0:T(8,128)(2,1)S(1)}, bf16[448,256]{1,0:T(8,128)(2,1)S(1)}, u32[]{:S(2)}, u32[]{:S(2)}) %collective-permute-start.23) | collective-permute-done | bytes 229408 | tf_op jit(solution)/shard_map/ppermute | solution.py:394
  119.4 4.7 %shard_map.79 = (f32[588,1024]{1,0:T(8,128)}, bf16[1024,1024]{1,0:T(8,128)(2,1)}) custom-call(s32[2]{0:T(128)S(1)} %pad_add_fusion.place_ref, bf16[448,256]{1,0:T(8,128)(2,1)S(1)} %shard_map.78.refs_0_, bf16[448,256]{1,0:T(8,128)(2,1)S(1)} %collective-permute-done.15.refs_1_, bf16[448,256]{1,0:T(8,128)(2,1)S(1)} %collective-permute-done.17.refs_2_, ...), custom_call_target="tpu_custom_call" | custom-call | tf_op jit(solution)/shard_map/pallas_call | solution.py:617
  (22 shorter events, 0.1 us)
Async XLA Ops:
  1.3 1.3 %copy-start.3 = (bf16[2352,256]{1,0:T(8,128)(2,1)S(1)}, bf16[2352,256]{1,0:T(8,128)(2,1)}, u32[]{:S(2)}) copy-start(bf16[2352,256]{1,0:T(8,128)(2,1)} %raw_ref.1) | copy-start | bytes 3612676
  2.6 0.7 copy-start.6
  3.8 6.9 %copy-start.7 = (s32[8,343]{1,0:T(8,128)S(1)}, s32[8,343]{1,0:T(8,128)}, u32[]{:S(2)}) copy-start(s32[8,343]{1,0:T(8,128)} %conn_ref.1) | copy-start | bytes 32932
  3.8 6.8 %collective-permute-start = (bf16[80,256]{1,0:T(8,128)(2,1)S(1)}, bf16[80,256]{1,0:T(8,128)(2,1)S(1)}, u32[]{:S(2)}, u32[]{:S(2)}) collective-permute-start(bf16[80,256]{1,0:T(8,128)(2,1)S(1)} %shard_map.68), channel_id=1, source_target_pairs={{4,0},{8,4},{12,8},{16,12},{20,16},{24,20},{28,24},{5,1},{9,5},{13... | collective-permute-start | bytes 122888 | tf_op jit(solution)/shard_map/ppermute | solution.py:399
  30.0 12.1 %collective-permute-start.1 = (bf16[6,64,256]{2,1,0:T(8,128)(2,1)S(1)}, bf16[6,64,256]{2,1,0:T(8,128)(2,1)S(1)}, u32[]{:S(2)}, u32[]{:S(2)}) collective-permute-start(bf16[6,64,256]{2,1,0:T(8,128)(2,1)S(1)} %get-tuple-element.48), channel_id=1, source_target_pairs={{0,4},{4,8},{8,12},{12,16},{16,20},{20,24},{24,28},{1,5},{5,9},{9,... | collective-permute-start | bytes 589832 | tf_op jit(solution)/shard_map/ppermute | solution.py:399
  34.8 7.2 %collective-permute-start.2 = (bf16[5,64,256]{2,1,0:T(8,128)(2,1)S(1)}, bf16[5,64,256]{2,1,0:T(8,128)(2,1)S(1)}, u32[]{:S(2)}, u32[]{:S(2)}) collective-permute-start(bf16[5,64,256]{2,1,0:T(8,128)(2,1)S(1)} %get-tuple-element.49), channel_id=1, source_target_pairs={{4,0},{8,4},{12,8},{16,12},{20,16},{24,20},{28,24},{5,1},{9,5},{13... | collective-permute-start | bytes 491528 | tf_op jit(solution)/shard_map/ppermute | solution.py:399
  42.0 9.6 %copy-start.2 = (f32[2560,1]{1,0:T(8,128)S(1)}, f32[2560,1]{1,0:T(8,128)}, u32[]{:S(2)}) copy-start(f32[2560,1]{1,0:T(8,128)} %get-tuple-element.51.pot_ref) | copy-start | bytes 30724
  50.1 11.4 %collective-permute-start.4 = (bf16[2624,256]{1,0:T(8,128)(2,1)}, bf16[2624,256]{1,0:T(8,128)(2,1)}, u32[]{:S(2)}, u32[]{:S(2)}) collective-permute-start(bf16[2624,256]{1,0:T(8,128)(2,1)} %get-tuple-element.73.x_ref), channel_id=1, source_target_pairs={{0,1},{1,0},{2,3},{3,2},{4,5},{5,4},{6,7},{7,6},{8,9},{9,8},{10,11... | collective-permute-start | bytes 4030472 | tf_op jit(solution)/shard_map/ppermute | solution.py:394
  50.1 18.1 %collective-permute-start.3 = (bf16[1344,256]{1,0:T(8,128)(2,1)}, bf16[1344,256]{1,0:T(8,128)(2,1)S(1)}, u32[]{:S(2)}, u32[]{:S(2)}) collective-permute-start(bf16[1344,256]{1,0:T(8,128)(2,1)} %get-tuple-element.55), channel_id=1, source_target_pairs={{0,2},{1,3},{2,0},{3,1},{4,6},{5,7},{6,4},{7,5},{8,10},{9,11},{10,... | collective-permute-start | bytes 2064392 | tf_op jit(solution)/shard_map/ppermute | solution.py:394
  51.6 5.2 %copy-start = (bf16[2624,256]{1,0:T(8,128)(2,1)S(1)}, bf16[2624,256]{1,0:T(8,128)(2,1)}, u32[]{:S(2)}) copy-start(bf16[2624,256]{1,0:T(8,128)(2,1)} %get-tuple-element.73.x_ref) | copy-start | bytes 4030468
  56.2 8.3 %collective-permute-start.5 = (bf16[672,256]{1,0:T(8,128)(2,1)}, bf16[672,256]{1,0:T(8,128)(2,1)}, u32[]{:S(2)}, u32[]{:S(2)}) collective-permute-start(bf16[672,256]{1,0:T(8,128)(2,1)} %get-tuple-element.60), channel_id=1, source_target_pairs={{0,1},{1,0},{2,3},{3,2},{4,5},{5,4},{6,7},{7,6},{8,9},{9,8},{10,11... | collective-permute-start | bytes 1032200 | tf_op jit(solution)/shard_map/ppermute | solution.py:394
  56.4 8.0 %collective-permute-start.6 = (bf16[672,256]{1,0:T(8,128)(2,1)}, bf16[672,256]{1,0:T(8,128)(2,1)}, u32[]{:S(2)}, u32[]{:S(2)}) collective-permute-start(bf16[672,256]{1,0:T(8,128)(2,1)} %get-tuple-element.61), channel_id=1, source_target_pairs={{0,1},{1,0},{2,3},{3,2},{4,5},{5,4},{6,7},{7,6},{8,9},{9,8},{10,11... | collective-permute-start | bytes 1032200 | tf_op jit(solution)/shard_map/ppermute | solution.py:394
  61.5 8.3 %copy-start.1 = (bf16[2,1344,256]{2,1,0:T(8,128)(2,1)S(1)}, bf16[2,1344,256]{2,1,0:T(8,128)(2,1)}, u32[]{:S(2)}) copy-start(bf16[2,1344,256]{2,1,0:T(8,128)(2,1)} %get-tuple-element.54.w_ref) | copy-start | bytes 4128772
  68.2 26.2 %collective-permute-start.11 = (bf16[588,512]{1,0:T(8,128)(2,1)}, bf16[588,512]{1,0:T(8,128)(2,1)}, u32[]{:S(2)}, u32[]{:S(2)}) collective-permute-start(bf16[588,512]{1,0:T(8,128)(2,1)} %get-tuple-element.78), channel_id=1, source_target_pairs={{0,2},{1,3},{2,0},{3,1},{4,6},{5,7},{6,4},{7,5},{8,10},{9,11},{10,... | collective-permute-start | bytes 1806344 | tf_op jit(solution)/shard_map/ppermute | solution.py:394
  72.3 0.8 copy-start.4
  73.1 7.7 %copy-start.5 = (f32[448,256]{1,0:T(8,128)S(1)}, f32[448,256]{1,0:T(8,128)}, u32[]{:S(2)}) copy-start(f32[448,256]{1,0:T(8,128)} %copy-done.4) | copy-start | bytes 1376260
  73.1 7.6 %collective-permute-start.7 = (bf16[448,256]{1,0:T(8,128)(2,1)}, bf16[448,256]{1,0:T(8,128)(2,1)S(1)}, u32[]{:S(2)}, u32[]{:S(2)}) collective-permute-start(bf16[448,256]{1,0:T(8,128)(2,1)} %get-tuple-element.68), channel_id=1, source_target_pairs={{0,4},{4,0},{8,12},{12,8},{16,20},{20,16},{24,28},{28,24},{1,5},{5... | collective-permute-start | bytes 688136 | tf_op jit(solution)/shard_map/ppermute | solution.py:394
  75.3 31.2 %collective-permute-start.16 = (bf16[588,512]{1,0:T(8,128)(2,1)}, bf16[588,512]{1,0:T(8,128)(2,1)}, u32[]{:S(2)}, u32[]{:S(2)}) collective-permute-start(bf16[588,512]{1,0:T(8,128)(2,1)} %get-tuple-element.80), channel_id=1, source_target_pairs={{0,3},{1,2},{2,1},{3,0},{4,7},{5,6},{6,5},{7,4},{8,11},{9,10},{10,... | collective-permute-start | bytes 1806344 | tf_op jit(solution)/shard_map/ppermute | solution.py:394
  81.4 7.4 %collective-permute-start.10 = (bf16[112,256]{1,0:T(8,128)(2,1)S(1)}, bf16[112,256]{1,0:T(8,128)(2,1)S(1)}, u32[]{:S(2)}, u32[]{:S(2)}) collective-permute-start(bf16[112,256]{1,0:T(8,128)(2,1)S(1)} %get-tuple-element.77), channel_id=1, source_target_pairs={{0,24},{4,28},{8,16},{12,20},{16,8},{20,12},{24,0},{28,4},{1,25},{... | collective-permute-start | bytes 172040 | tf_op jit(solution)/shard_map/ppermute | solution.py:394
  86.3 26.7 %collective-permute-start.21 = (bf16[588,512]{1,0:T(8,128)(2,1)S(1)}, bf16[588,512]{1,0:T(8,128)(2,1)S(1)}, u32[]{:S(2)}, u32[]{:S(2)}) collective-permute-start(bf16[588,512]{1,0:T(8,128)(2,1)S(1)} %get-tuple-element.82), channel_id=1, source_target_pairs={{0,1},{1,0},{2,3},{3,2},{4,5},{5,4},{6,7},{7,6},{8,9},{9,8},{10,11... | collective-permute-start | bytes 1806344 | tf_op jit(solution)/shard_map/ppermute | solution.py:394
  86.3 4.9 %collective-permute-start.8 = (bf16[112,256]{1,0:T(8,128)(2,1)S(1)}, bf16[112,256]{1,0:T(8,128)(2,1)S(1)}, u32[]{:S(2)}, u32[]{:S(2)}) collective-permute-start(bf16[112,256]{1,0:T(8,128)(2,1)S(1)} %get-tuple-element.70), channel_id=1, source_target_pairs={{0,8},{4,12},{8,0},{12,4},{16,24},{20,28},{24,16},{28,20},{1,9},{5... | collective-permute-start | bytes 172040 | tf_op jit(solution)/shard_map/ppermute | solution.py:394
  88.7 5.1 %collective-permute-start.9 = (bf16[112,256]{1,0:T(8,128)(2,1)S(1)}, bf16[112,256]{1,0:T(8,128)(2,1)S(1)}, u32[]{:S(2)}, u32[]{:S(2)}) collective-permute-start(bf16[112,256]{1,0:T(8,128)(2,1)S(1)} %get-tuple-element.71), channel_id=1, source_target_pairs={{0,16},{4,20},{8,24},{12,28},{16,0},{20,4},{24,8},{28,12},{1,17},{... | collective-permute-start | bytes 172040 | tf_op jit(solution)/shard_map/ppermute | solution.py:394
  94.4 4.9 %collective-permute-start.12 = (bf16[112,256]{1,0:T(8,128)(2,1)S(1)}, bf16[112,256]{1,0:T(8,128)(2,1)S(1)}, u32[]{:S(2)}, u32[]{:S(2)}) collective-permute-start(bf16[112,256]{1,0:T(8,128)(2,1)S(1)} %shard_map.77.own_ref), channel_id=1, source_target_pairs={{0,8},{4,12},{8,0},{12,4},{16,24},{20,28},{24,16},{28,20},{1,9},{5... | collective-permute-start | bytes 172040 | tf_op jit(solution)/shard_map/ppermute | solution.py:394
  96.3 5.8 %collective-permute-start.13 = (bf16[112,256]{1,0:T(8,128)(2,1)S(1)}, bf16[112,256]{1,0:T(8,128)(2,1)S(1)}, u32[]{:S(2)}, u32[]{:S(2)}) collective-permute-start(bf16[112,256]{1,0:T(8,128)(2,1)S(1)} %shard_map.77.own_ref), channel_id=1, source_target_pairs={{0,16},{4,20},{8,24},{12,28},{16,0},{20,4},{24,8},{28,12},{1,17},{... | collective-permute-start | bytes 172040 | tf_op jit(solution)/shard_map/ppermute | solution.py:394
  99.3 6.0 %collective-permute-start.14 = (bf16[112,256]{1,0:T(8,128)(2,1)S(1)}, bf16[112,256]{1,0:T(8,128)(2,1)S(1)}, u32[]{:S(2)}, u32[]{:S(2)}) collective-permute-start(bf16[112,256]{1,0:T(8,128)(2,1)S(1)} %shard_map.77.own_ref), channel_id=1, source_target_pairs={{0,24},{4,28},{8,16},{12,20},{16,8},{20,12},{24,0},{28,4},{1,25},{... | collective-permute-start | bytes 172040 | tf_op jit(solution)/shard_map/ppermute | solution.py:394
  105.8 6.1 %collective-permute-start.15 = (bf16[448,256]{1,0:T(8,128)(2,1)S(1)}, bf16[448,256]{1,0:T(8,128)(2,1)S(1)}, u32[]{:S(2)}, u32[]{:S(2)}) collective-permute-start(bf16[448,256]{1,0:T(8,128)(2,1)S(1)} %shard_map.78.refs_0_), channel_id=1, source_target_pairs={{0,4},{4,0},{8,12},{12,8},{16,20},{20,16},{24,28},{28,24},{1,5},{5... | collective-permute-start | bytes 688136 | tf_op jit(solution)/shard_map/ppermute | solution.py:394
  106.1 6.8 %collective-permute-start.19 = (bf16[448,256]{1,0:T(8,128)(2,1)S(1)}, bf16[448,256]{1,0:T(8,128)(2,1)S(1)}, u32[]{:S(2)}, u32[]{:S(2)}) collective-permute-start(bf16[448,256]{1,0:T(8,128)(2,1)S(1)} %shard_map.78.refs_0_), channel_id=1, source_target_pairs={{0,2},{1,3},{2,0},{3,1},{4,6},{5,7},{6,4},{7,5},{8,10},{9,11},{10,... | collective-permute-start | bytes 688136 | tf_op jit(solution)/shard_map/ppermute | solution.py:394
  111.9 6.0 %collective-permute-start.20 = (bf16[448,256]{1,0:T(8,128)(2,1)S(1)}, bf16[448,256]{1,0:T(8,128)(2,1)S(1)}, u32[]{:S(2)}, u32[]{:S(2)}) collective-permute-start(bf16[448,256]{1,0:T(8,128)(2,1)S(1)} %collective-permute-done.15.refs_1_), channel_id=1, source_target_pairs={{0,2},{1,3},{2,0},{3,1},{4,6},{5,7},{6,4},{7,5},{8,10},{9,11},{10,... | collective-permute-start | bytes 688136 | tf_op jit(solution)/shard_map/ppermute | solution.py:394
  112.4 5.6 %collective-permute-start.17 = (bf16[448,256]{1,0:T(8,128)(2,1)S(1)}, bf16[448,256]{1,0:T(8,128)(2,1)S(1)}, u32[]{:S(2)}, u32[]{:S(2)}) collective-permute-start(bf16[448,256]{1,0:T(8,128)(2,1)S(1)} %shard_map.78.refs_0_), channel_id=1, source_target_pairs={{0,1},{1,0},{2,3},{3,2},{4,5},{5,4},{6,7},{7,6},{8,9},{9,8},{10,11... | collective-permute-start | bytes 688136 | tf_op jit(solution)/shard_map/ppermute | solution.py:394
  112.4 5.6 %collective-permute-start.18 = (bf16[448,256]{1,0:T(8,128)(2,1)S(1)}, bf16[448,256]{1,0:T(8,128)(2,1)S(1)}, u32[]{:S(2)}, u32[]{:S(2)}) collective-permute-start(bf16[448,256]{1,0:T(8,128)(2,1)S(1)} %collective-permute-done.15.refs_1_), channel_id=1, source_target_pairs={{0,1},{1,0},{2,3},{3,2},{4,5},{5,4},{6,7},{7,6},{8,9},{9,8},{10,11... | collective-permute-start | bytes 688136 | tf_op jit(solution)/shard_map/ppermute | solution.py:394
  113.0 5.1 %collective-permute-start.22 = (bf16[448,256]{1,0:T(8,128)(2,1)S(1)}, bf16[448,256]{1,0:T(8,128)(2,1)S(1)}, u32[]{:S(2)}, u32[]{:S(2)}) collective-permute-start(bf16[448,256]{1,0:T(8,128)(2,1)S(1)} %collective-permute-done.19.refs_4_), channel_id=1, source_target_pairs={{0,1},{1,0},{2,3},{3,2},{4,5},{5,4},{6,7},{7,6},{8,9},{9,8},{10,11... | collective-permute-start | bytes 688136 | tf_op jit(solution)/shard_map/ppermute | solution.py:394
  117.9 1.5 %collective-permute-start.23 = (bf16[448,256]{1,0:T(8,128)(2,1)S(1)}, bf16[448,256]{1,0:T(8,128)(2,1)S(1)}, u32[]{:S(2)}, u32[]{:S(2)}) collective-permute-start(bf16[448,256]{1,0:T(8,128)(2,1)S(1)} %collective-permute-done.20.refs_5_), channel_id=1, source_target_pairs={{0,1},{1,0},{2,3},{3,2},{4,5},{5,4},{6,7},{7,6},{8,9},{9,8},{10,11... | collective-permute-start | bytes 688136 | tf_op jit(solution)/shard_map/ppermute | solution.py:394

commit v10 on v9

--- a/solution.py
+++ b/solution.py
@@ -203,11 +203,18 @@
 
 def free_kernel(
     fp, ip, conn_ref, face_ref, hraw_ref, raw_ref, potraw_ref, ghost_ref,
-    h_ref, v_ref, pot_ref, node_ref, first_ref, own_ref, up_ref, down_ref, a_ref, b_ref, hin_ref, sem,
+    h_hbm, v_ref, pot_hbm, node_ref, first_hbm, own_ref, up_ref, down_ref,
+    h_ref, pot_ref, first_ref, a_ref, b_ref, hin_ref, sem, sems,
 ):
     copy = pltpu.make_async_copy(hraw_ref, hin_ref, sem)
     copy.start()
     order(fp, ip, copy.wait, conn_ref, face_ref, hin_ref, raw_ref, potraw_ref, h_ref, v_ref, pot_ref, node_ref)
+    leaving = [
+        pltpu.make_async_copy(src, dst, sems.at[i])
+        for i, (src, dst) in enumerate(((h_ref, h_hbm), (pot_ref, pot_hbm), (first_ref, first_hbm)))
+    ]
+    leaving[0].start()
+    leaving[1].start()
     cells, cp = h_ref.shape[:2]
     stride = cp - fp
     total = cells * stride
@@ -245,6 +252,7 @@
         high = sweep(h_ref, now_ref, fp, emit)
         keep(k, ends["low"], high)
         if k == 0:
+            leaving[2].start()
             a_ref[total:] = jnp.zeros((fp, width), BF16)
         now_ref, other_ref = other_ref, now_ref
     keep(DEGREE, mul(h_ref[0, :fp], now_ref[:cp]), mul(h_ref[cells - 1, stride:], now_ref[total - stride :]))
@@ -254,16 +262,33 @@
     store_matrices(high, up_ref, DEGREE + 1, fp, width)
     for side, mats in enumerate((low, high)):
         store_matrices(mats, own_ref.at[side], DEGREE + 1, fp, width)
+    for copy in leaving:
+        copy.wait()
 
 
 def forced_kernel(
-    fp, place_ref, v_ref, ghost_ref, first_ref, own_ref, fromleft_ref, fromright_ref, h_ref, pot_ref,
-    x_ref, face_image_ref, slab_ref, a_ref, b_ref, c_ref,
+    fp, place_ref, v_ref, ghost_ref, first_hbm, own_ref, fromleft_ref, fromright_ref, h_hbm, pot_hbm,
+    x_ref, face_image_ref, slab_ref, a_ref, b_ref, c_ref, h_ref, pot_ref, sems,
 ):
     cells, cp = h_ref.shape[:2]
     stride = cp - fp
     total = cells * stride
     width = v_ref.shape[1]
+    rest = pl.ds(fp, total - fp)
+    coming = [
+        pltpu.make_async_copy(src, dst, sems.at[i])
+        for i, (src, dst) in enumerate(
+            (
+                (pot_hbm.at[pl.ds(0, fp)], pot_ref.at[pl.ds(0, fp)]),
+                (first_hbm, a_ref.at[pl.ds(0, total)]),
+                (pot_hbm.at[rest], pot_ref.at[rest]),
+                (h_hbm, h_ref),
+            )
+        )
+    ]
+    for copy in coming:
+        copy.start()
+    coming[0].wait()
     half = cells // 2
     extra = own_ref.shape[1] - DEGREE - 1
     potg = to_col(jnp.sum(ghost_ref[fp:].astype(F32), axis=0, keepdims=True)[:, :fp], fp)
@@ -296,8 +321,9 @@
                 value = jnp.where(place_ref[0] == 1, 0.0, value)
             values.append(value.astype(BF16))
     low, high = sides[0][3], sides[1][3]
+    for copy in coming[1:]:
+        copy.wait()
     a_ref[:fp] = low[1]
-    a_ref[fp:total] = first_ref[fp:]
     a_ref[total:] = high[1]
     refs = [v_ref, a_ref, b_ref, c_ref, x_ref]
     for k in range(1, DEGREE):
@@ -655,7 +681,7 @@
     cost = pl.CostEstimate(
         flops=2 * DEGREE * cells * cp * cp * width, bytes_accessed=8 << 20, transcendentals=0
     )
-    vmem = pl.BlockSpec(memory_space=pltpu.VMEM)
+    vmem, hbm = pl.BlockSpec(memory_space=pltpu.VMEM), pl.BlockSpec(memory_space=pl.ANY)
     hcan, y, pot, node, first, own, up, down = pl.pallas_call(
         functools.partial(free_kernel, fp, ip),
         in_specs=[vmem] * 2 + [pl.BlockSpec(memory_space=pl.ANY)] + [vmem] * 3,
@@ -669,25 +695,41 @@
             sds((DEGREE + 1 + extra, fp, width), BF16),
             sds((DEGREE + extra, fp, width), BF16),
         ],
-        scratch_shapes=[ext, ext, pltpu.VMEM((cells, npc, npc), BF16), pltpu.SemaphoreType.DMA],
+        out_specs=[hbm, vmem, hbm, vmem, hbm, vmem, vmem, vmem],
+        scratch_shapes=[
+            pltpu.VMEM((cells, cp, cp), BF16),
+            pltpu.VMEM((total, 1), F32),
+            pltpu.VMEM((total, width), BF16),
+            ext,
+            ext,
+            pltpu.VMEM((cells, npc, npc), BF16),
+            pltpu.SemaphoreType.DMA,
+            pltpu.SemaphoreType.DMA((3,)),
+        ],
         compiler_params=params(),
         cost_estimate=cost,
     )(connectivity, face_row, cell_hamiltonian, orbitals, pot_row, ghost)
     node_row = node.reshape(1, total)
     from_left = shift(up, "dom", 1)
     from_right = shift(down, "dom", -1)
-    vmem = pl.BlockSpec(memory_space=pltpu.VMEM)
     slab = cells // 2 * stride + fp
     place = jnp.stack([(d == dom - 1).astype(jnp.int32), (o // 2) % 2])
     x_own, face_image, give = pl.pallas_call(
         functools.partial(forced_kernel, fp),
-        in_specs=[pl.BlockSpec(memory_space=pltpu.SMEM)] + [vmem] * 8,
+        in_specs=[pl.BlockSpec(memory_space=pltpu.SMEM), vmem, vmem, hbm, vmem, vmem, vmem, hbm, hbm],
         out_shape=[
             sds((total + fp, width), BF16),
             sds((fp, width), F32),
             sds((slab, width), BF16),
         ],
-        scratch_shapes=[ext, ext, ext],
+        scratch_shapes=[
+            ext,
+            ext,
+            ext,
+            pltpu.VMEM((cells, cp, cp), BF16),
+            pltpu.VMEM((total, 1), F32),
+            pltpu.SemaphoreType.DMA((4,)),
+        ],
         compiler_params=params(),
         cost_estimate=cost,
     )(place, y, ghost, first, own, from_left, from_right, hcan, pot)

time: 125 us -> 124 us (level)
  no operation moved by 1% of the time
where the time goes in v10:
time: 124 us
  Pallas kernels  51.9 us (42%)
  waiting for transfers between devices  37.7 us (30%)
  starting transfers between devices  25.7 us (21%)
  local copies, waits for them, and re-layouts  6.74 us (5%)
    ppermute x21, waiting for transfers between devices, swap(): lax.ppermute(block, axis, [(i, i ^ bit) for i in range(lax.axis_size(axis...  29.6 us
    pallas_call x1, Pallas kernels, body(): pl.pallas_call(functools.partial(free_kernel, fp, ip), in_specs=[vmem] *...  18.3 us
    ppermute x21, starting transfers between devices, swap(): lax.ppermute(block, axis, [(i, i ^ bit) for i in range(lax.axis_size(axis...  18.3 us
    pallas_call x2, Pallas kernels, back(): pl.pallas_call(back_pair_kernel, grid=(1,), in_specs=[smem, whole(1, tota...  8.48 us
    pallas_call x1, Pallas kernels, body(): pl.pallas_call(functools.partial(forced_kernel, fp), in_specs=[pl.BlockSp...  8.3 us
    ppermute x3, waiting for transfers between devices, shift(): lax.ppermute(block, axis, [(i, i + distance) for i in range(n) if 0 <= i...  8.13 us
    ppermute x3, starting transfers between devices, shift(): lax.ppermute(block, axis, [(i, i + distance) for i in range(n) if 0 <= i...  7.42 us
    unnamed x17, local copies, waits for them, and re-layouts  5.94 us
  transfers between devices with their start and end apart: 24, of which 12 were waited for; matrix products, arithmetic and copies ran while one was open for 3% of the time, Pallas kernels for 16%

profile of v10, /device:TPU:0, one launch (start us, length us, event | category | flops | bytes accessed | tf_op | source)
XLA Modules:
  0.0 123.6 jit_solution(1271244683880837358)
XLA Ops:
  0.6 0.7 reshape.15.pot_ref.potraw_ref
  1.3 1.3 %copy-done.3 = bf16[2352,256]{1,0:T(8,128)(2,1)S(1)} copy-done((bf16[2352,256]{1,0:T(8,128)(2,1)S(1)}, bf16[2352,256]{1,0:T(8,128)(2,1)}, u32[]{:S(2)}) %copy-start.3) | copy-done | bytes 1204248
  2.6 0.7 copy-done.6
  3.3 0.5 shard_map.68
  3.8 0.0 copy-start.7
  3.8 1.3 %collective-permute-start = (bf16[80,256]{1,0:T(8,128)(2,1)S(1)}, bf16[80,256]{1,0:T(8,128)(2,1)S(1)}, u32[]{:S(2)}, u32[]{:S(2)}) collective-permute-start(bf16[80,256]{1,0:T(8,128)(2,1)S(1)} %shard_map.68), channel_id=1, source_target_pairs={{4,0},{8,4},{12,8},{16,12},{20,16},{24,20},{28,24},{5,1},{9,5},{13... | collective-permute-start | bytes 122888 | tf_op jit(solution)/shard_map/ppermute | solution.py:425
  5.1 3.2 %copy.7.hraw_ref = bf16[8,343,343]{2,1,0:T(8,128)(2,1)} copy(bf16[8,343,343]{2,0,1:T(8,128)(2,1)} %param.7) | data formatting | bytes 3764768 | tf_op args[2]
  8.3 2.3 %collective-permute-done.ghost_ref = bf16[80,256]{1,0:T(8,128)(2,1)S(1)} collective-permute-done((bf16[80,256]{1,0:T(8,128)(2,1)S(1)}, bf16[80,256]{1,0:T(8,128)(2,1)S(1)}, u32[]{:S(2)}, u32[]{:S(2)}) %collective-permute-start) | collective-permute-done | bytes 40992 | tf_op jit(solution)/shard_map/ppermute | solution.py:425
  10.6 18.3 %shard_map.69 = (bf16[8,384,384]{2,1,0:T(8,128)(2,1)}, bf16[2560,256]{1,0:T(8,128)(2,1)S(1)}, f32[2560,1]{1,0:T(8,128)}, f32[8,1,320]{2,1,0:T(1,128)S(1)}, bf16[...) custom-call(s32[8,343]{1,0:T(8,128)S(1)} %copy-done.7, ...), custom_call_target="tpu_custom_call" | custom-call | flops 2415919104 | bytes 8388608 | tf_op jit(solution)/shard_map/pallas_call | solution.py:685
  29.0 4.8 %collective-permute-start.1 = (bf16[6,64,256]{2,1,0:T(8,128)(2,1)S(1)}, bf16[6,64,256]{2,1,0:T(8,128)(2,1)S(1)}, u32[]{:S(2)}, u32[]{:S(2)}) collective-permute-start(bf16[6,64,256]{2,1,0:T(8,128)(2,1)S(1)} %get-tuple-element.48), channel_id=1, source_target_pairs={{0,4},{4,8},{8,12},{12,16},{16,20},{20,24},{24,28},{1,5},{5,9},{9,... | collective-permute-start | bytes 589832 | tf_op jit(solution)/shard_map/ppermute | solution.py:425
  33.8 1.3 %collective-permute-start.2 = (bf16[5,64,256]{2,1,0:T(8,128)(2,1)S(1)}, bf16[5,64,256]{2,1,0:T(8,128)(2,1)S(1)}, u32[]{:S(2)}, u32[]{:S(2)}) collective-permute-start(bf16[5,64,256]{2,1,0:T(8,128)(2,1)S(1)} %get-tuple-element.49), channel_id=1, source_target_pairs={{4,0},{8,4},{12,8},{16,12},{20,16},{24,20},{28,24},{5,1},{9,5},{13... | collective-permute-start | bytes 491528 | tf_op jit(solution)/shard_map/ppermute | solution.py:425
  35.2 0.1 pad_add_fusion.3.place_ref
  35.2 5.8 %collective-permute-done.2.fromright_ref = bf16[5,64,256]{2,1,0:T(8,128)(2,1)S(1)} collective-permute-done((bf16[5,64,256]{2,1,0:T(8,128)(2,1)S(1)}, bf16[5,64,256]{2,1,0:T(8,128)(2,1)S(1)}, u32[]{:S(2)}, u32[]{:S(2)}) %collective-permute-start.2) | collective-permute-done | bytes 163872 | tf_op jit(solution)/shard_map/ppermute | solution.py:425
  41.0 8.3 %shard_map.70 = (bf16[2624,256]{1,0:T(8,128)(2,1)}, f32[64,256]{1,0:T(8,128)S(1)}, bf16[1344,256]{1,0:T(8,128)(2,1)}) custom-call(s32[2]{0:T(128)S(1)} %pad_add_fusion.3.place_ref, bf16[2560,256]{1,0:T(8,128)(2,1)S(1)} %get-tuple-element.45.v_ref, bf16[80,256]{1,0:T(8,128)(2,1)S(1)} %collective-permute-done.ghost_ref, ...), custom_call_target="tpu_custom_call" | custom-call | flops 2415919104 | bytes 8388608 | tf_op jit(solution)/shard_map/pallas_call | solution.py:717
  49.4 0.1 collective-permute-start.4
  49.4 1.6 %collective-permute-start.3 = (bf16[1344,256]{1,0:T(8,128)(2,1)}, bf16[1344,256]{1,0:T(8,128)(2,1)S(1)}, u32[]{:S(2)}, u32[]{:S(2)}) collective-permute-start(bf16[1344,256]{1,0:T(8,128)(2,1)} %get-tuple-element.55), channel_id=1, source_target_pairs={{0,2},{1,3},{2,0},{3,1},{4,6},{5,7},{6,4},{7,5},{8,10},{9,11},{10,... | collective-permute-start | bytes 2064392 | tf_op jit(solution)/shard_map/ppermute | solution.py:420
  51.0 4.5 %shard_map.71 = (bf16[2560,256]{1,0:T(8,128)(2,1)S(1)}, bf16[2,1344,256]{2,1,0:T(8,128)(2,1)}, bf16[672,256]{1,0:T(8,128)(2,1)}, bf16[672,256]{1,0:T(8,128)(2,1)}) custom-call(s32[2]{0:T(128)S(1)} %pad_add_fusion.3.place_ref, bf16[2624,256]{1,0:T(8,128)(2,1)} %get-tuple-element.73.x_ref, f32[64,256]{1,0:T(8,128)S(1)} %get-tuple-element.53.face_image_ref, ...), custom_call_target="tpu_custom_call" | custom-call | flops 1048576 | bytes 1024 | tf_op jit(solution)/shard_map/pallas_call | solution.py:736
  55.5 0.2 collective-permute-start.5
  55.7 0.3 collective-permute-start.6
  56.0 0.1 pad_add_fusion.4.at_ref
  56.1 0.1 reshape.16.node_ref
  56.2 4.7 %shard_map.73 = (bf16[588,512]{1,0:T(8,128)(2,1)}, bf16[588,512]{1,0:T(8,128)(2,1)}) custom-call(s32[2]{0:T(128)S(1)} %pad_add_fusion.4.at_ref, f32[1,2560]{1,0:T(1,128)S(1)} %reshape.16.node_ref, bf16[2624,256]{1,0:T(8,128)(2,1)S(1)} %copy-done, bf16[2560,256]{1,0:T(8,128)(2,1)S(1)} %get-tuple-element.74.image_ref), custom_call_target="tpu_custom_call" | custom-call | flops 1048576 | bytes 1024 | tf_op jit(solution)/shard_map/pallas_call | solution.py:557
  60.9 0.0 collective-permute-done.4.other_ref
  60.9 2.9 %shard_map.72.near_ref = f32[384,256]{1,0:T(8,128)S(1)} custom-call(s32[1]{0:T(128)} %bitcast.4.core_ref, bf16[2624,256]{1,0:T(8,128)(2,1)S(1)} %copy-done, bf16[2,1344,256]{2,1,0:T(8,128)(2,1)} %get-tuple-element.54.w_ref, bf16[2624,256]{1,0:T(8,128)(2,1)} %collective-permute-done.4.other_ref), custom_call_target="tpu_custom_call" | custom-call | flops 1048576 | bytes 1024 | tf_op jit(solution)/shard_map/pallas_call | solution.py:571
  63.8 0.0 collective-permute-done.5.first_ref
  63.8 3.7 %collective-permute-done.3.far_ref = bf16[1344,256]{1,0:T(8,128)(2,1)S(1)} collective-permute-done((bf16[1344,256]{1,0:T(8,128)(2,1)}, bf16[1344,256]{1,0:T(8,128)(2,1)S(1)}, u32[]{:S(2)}, u32[]{:S(2)}) %collective-permute-start.3) | collective-permute-done | bytes 688160 | tf_op jit(solution)/shard_map/ppermute | solution.py:420
  67.5 1.5 %collective-permute-start.11 = (bf16[588,512]{1,0:T(8,128)(2,1)}, bf16[588,512]{1,0:T(8,128)(2,1)}, u32[]{:S(2)}, u32[]{:S(2)}) collective-permute-start(bf16[588,512]{1,0:T(8,128)(2,1)} %get-tuple-element.78), channel_id=1, source_target_pairs={{0,2},{1,3},{2,0},{3,1},{4,6},{5,7},{6,4},{7,5},{8,10},{9,11},{10,... | collective-permute-start | bytes 1806344 | tf_op jit(solution)/shard_map/ppermute | solution.py:420
  69.0 0.1 pad_add_fusion.2.place_ref
  69.1 0.1 pad_add_fusion.1.bits_ref
  69.1 2.5 %shard_map.74 = (f32[448,256]{1,0:T(8,128)S(1)}, bf16[448,256]{1,0:T(8,128)(2,1)}) custom-call(s32[2]{0:T(128)S(1)} %pad_add_fusion.1.bits_ref, s32[2]{0:T(128)S(1)} %pad_add_fusion.2.place_ref, bf16[2,1344,256]{2,1,0:T(8,128)(2,1)S(1)} %copy-done.1, bf16[672,256]{1,0:T(8,128)(2,1)} %collective-permute-done.5.first_ref, ...), custom_call_target="tpu_custom_call" | custom-call | flops 704643072 | bytes 4194304 | tf_op jit(solution)/shard_map/pallas_call | solution.py:592
  71.6 0.8 copy-done.4
  72.4 2.2 %collective-permute-start.7 = (bf16[448,256]{1,0:T(8,128)(2,1)}, bf16[448,256]{1,0:T(8,128)(2,1)S(1)}, u32[]{:S(2)}, u32[]{:S(2)}) collective-permute-start(bf16[448,256]{1,0:T(8,128)(2,1)} %get-tuple-element.68), channel_id=1, source_target_pairs={{0,4},{4,0},{8,12},{12,8},{16,20},{20,16},{24,28},{28,24},{1,5},{5... | collective-permute-start | bytes 688136 | tf_op jit(solution)/shard_map/ppermute | solution.py:420
  74.6 0.0 collective-permute-start.16
  74.6 0.1 pad_add_fusion.5.at_ref
  74.7 3.8 %shard_map.76 = (bf16[588,512]{1,0:T(8,128)(2,1)S(1)}, bf16[588,512]{1,0:T(8,128)(2,1)S(1)}) custom-call(s32[2]{0:T(128)S(1)} %pad_add_fusion.5.at_ref, f32[1,2560]{1,0:T(1,128)S(1)} %reshape.16.node_ref, bf16[2624,256]{1,0:T(8,128)(2,1)S(1)} %copy-done, bf16[2560,256]{1,0:T(8,128)(2,1)S(1)} %get-tuple-element.74.image_ref), custom_call_target="tpu_custom_call" | custom-call | flops 1048576 | bytes 1024 | tf_op jit(solution)/shard_map/pallas_call | solution.py:557
  78.5 1.4 %collective-permute-done.7.refs_0_ = bf16[448,256]{1,0:T(8,128)(2,1)S(1)} collective-permute-done((bf16[448,256]{1,0:T(8,128)(2,1)}, bf16[448,256]{1,0:T(8,128)(2,1)S(1)}, u32[]{:S(2)}, u32[]{:S(2)}) %collective-permute-start.7) | collective-permute-done | bytes 229408 | tf_op jit(solution)/shard_map/ppermute | solution.py:420
  80.0 0.6 shard_map.75
  80.6 4.9 %collective-permute-start.10 = (bf16[112,256]{1,0:T(8,128)(2,1)S(1)}, bf16[112,256]{1,0:T(8,128)(2,1)S(1)}, u32[]{:S(2)}, u32[]{:S(2)}) collective-permute-start(bf16[112,256]{1,0:T(8,128)(2,1)S(1)} %get-tuple-element.77), channel_id=1, source_target_pairs={{0,24},{4,28},{8,16},{12,20},{16,8},{20,12},{24,0},{28,4},{1,25},{... | collective-permute-start | bytes 172040 | tf_op jit(solution)/shard_map/ppermute | solution.py:420
  85.5 0.0 collective-permute-start.21
  85.5 0.0 collective-permute-start.8
  85.5 2.4 %collective-permute-done.10.refs_2_ = bf16[112,256]{1,0:T(8,128)(2,1)S(1)} collective-permute-done((bf16[112,256]{1,0:T(8,128)(2,1)S(1)}, bf16[112,256]{1,0:T(8,128)(2,1)S(1)}, u32[]{:S(2)}, u32[]{:S(2)}) %collective-permute-start.10) | collective-permute-done | bytes 57376 | tf_op jit(solution)/shard_map/ppermute | solution.py:420
  88.0 0.9 collective-permute-start.9
  88.8 1.7 %collective-permute-done.8.refs_0_ = bf16[112,256]{1,0:T(8,128)(2,1)S(1)} collective-permute-done((bf16[112,256]{1,0:T(8,128)(2,1)S(1)}, bf16[112,256]{1,0:T(8,128)(2,1)S(1)}, u32[]{:S(2)}, u32[]{:S(2)}) %collective-permute-start.8) | collective-permute-done | bytes 57376 | tf_op jit(solution)/shard_map/ppermute | solution.py:420
  90.5 2.5 %collective-permute-done.9.refs_1_ = bf16[112,256]{1,0:T(8,128)(2,1)S(1)} collective-permute-done((bf16[112,256]{1,0:T(8,128)(2,1)S(1)}, bf16[112,256]{1,0:T(8,128)(2,1)S(1)}, u32[]{:S(2)}, u32[]{:S(2)}) %collective-permute-start.9) | collective-permute-done | bytes 57376 | tf_op jit(solution)/shard_map/ppermute | solution.py:420
  93.0 0.6 shard_map.77.own_ref
  93.6 1.9 %collective-permute-start.12 = (bf16[112,256]{1,0:T(8,128)(2,1)S(1)}, bf16[112,256]{1,0:T(8,128)(2,1)S(1)}, u32[]{:S(2)}, u32[]{:S(2)}) collective-permute-start(bf16[112,256]{1,0:T(8,128)(2,1)S(1)} %shard_map.77.own_ref), channel_id=1, source_target_pairs={{0,8},{4,12},{8,0},{12,4},{16,24},{20,28},{24,16},{28,20},{1,9},{5... | collective-permute-start | bytes 172040 | tf_op jit(solution)/shard_map/ppermute | solution.py:420
  95.5 3.0 %collective-permute-start.13 = (bf16[112,256]{1,0:T(8,128)(2,1)S(1)}, bf16[112,256]{1,0:T(8,128)(2,1)S(1)}, u32[]{:S(2)}, u32[]{:S(2)}) collective-permute-start(bf16[112,256]{1,0:T(8,128)(2,1)S(1)} %shard_map.77.own_ref), channel_id=1, source_target_pairs={{0,16},{4,20},{8,24},{12,28},{16,0},{20,4},{24,8},{28,12},{1,17},{... | collective-permute-start | bytes 172040 | tf_op jit(solution)/shard_map/ppermute | solution.py:420
  98.5 0.0 collective-permute-start.14
  98.5 0.0 collective-permute-done.12.refs_0_
  98.5 2.8 %collective-permute-done.13.refs_1_ = bf16[112,256]{1,0:T(8,128)(2,1)S(1)} collective-permute-done((bf16[112,256]{1,0:T(8,128)(2,1)S(1)}, bf16[112,256]{1,0:T(8,128)(2,1)S(1)}, u32[]{:S(2)}, u32[]{:S(2)}) %collective-permute-start.13) | collective-permute-done | bytes 57376 | tf_op jit(solution)/shard_map/ppermute | solution.py:420
  101.3 3.2 %collective-permute-done.14.refs_2_ = bf16[112,256]{1,0:T(8,128)(2,1)S(1)} collective-permute-done((bf16[112,256]{1,0:T(8,128)(2,1)S(1)}, bf16[112,256]{1,0:T(8,128)(2,1)S(1)}, u32[]{:S(2)}, u32[]{:S(2)}) %collective-permute-start.14) | collective-permute-done | bytes 57376 | tf_op jit(solution)/shard_map/ppermute | solution.py:420
  104.5 0.6 shard_map.78.refs_0_
  105.1 0.3 collective-permute-start.15
  105.3 0.4 collective-permute-start.19
  105.7 5.4 %collective-permute-done.15.refs_1_ = bf16[448,256]{1,0:T(8,128)(2,1)S(1)} collective-permute-done((bf16[448,256]{1,0:T(8,128)(2,1)S(1)}, bf16[448,256]{1,0:T(8,128)(2,1)S(1)}, u32[]{:S(2)}, u32[]{:S(2)}) %collective-permute-start.15) | collective-permute-done | bytes 229408 | tf_op jit(solution)/shard_map/ppermute | solution.py:420
  111.2 0.5 collective-permute-start.20
  111.7 0.0 collective-permute-start.17
  111.7 0.5 collective-permute-start.18
  112.2 0.0 collective-permute-done.19.refs_4_
  112.2 0.0 collective-permute-start.22
  112.2 5.0 %collective-permute-done.20.refs_5_ = bf16[448,256]{1,0:T(8,128)(2,1)S(1)} collective-permute-done((bf16[448,256]{1,0:T(8,128)(2,1)S(1)}, bf16[448,256]{1,0:T(8,128)(2,1)S(1)}, u32[]{:S(2)}, u32[]{:S(2)}) %collective-permute-start.20) | collective-permute-done | bytes 229408 | tf_op jit(solution)/shard_map/ppermute | solution.py:420
  117.2 0.1 pad_add_fusion.place_ref
  117.3 1.4 %collective-permute-done.23.refs_7_ = bf16[448,256]{1,0:T(8,128)(2,1)S(1)} collective-permute-done((bf16[448,256]{1,0:T(8,128)(2,1)S(1)}, bf16[448,256]{1,0:T(8,128)(2,1)S(1)}, u32[]{:S(2)}, u32[]{:S(2)}) %collective-permute-start.23) | collective-permute-done | bytes 229408 | tf_op jit(solution)/shard_map/ppermute | solution.py:420
  118.7 4.7 %shard_map.79 = (f32[588,1024]{1,0:T(8,128)}, bf16[1024,1024]{1,0:T(8,128)(2,1)}) custom-call(s32[2]{0:T(128)S(1)} %pad_add_fusion.place_ref, bf16[448,256]{1,0:T(8,128)(2,1)S(1)} %shard_map.78.refs_0_, bf16[448,256]{1,0:T(8,128)(2,1)S(1)} %collective-permute-done.15.refs_1_, bf16[448,256]{1,0:T(8,128)(2,1)S(1)} %collective-permute-done.17.refs_2_, ...), custom_call_target="tpu_custom_call" | custom-call | tf_op jit(solution)/shard_map/pallas_call | solution.py:643
  (22 shorter events, 0.1 us)
Async XLA Ops:
  1.3 1.3 %copy-start.3 = (bf16[2352,256]{1,0:T(8,128)(2,1)S(1)}, bf16[2352,256]{1,0:T(8,128)(2,1)}, u32[]{:S(2)}) copy-start(bf16[2352,256]{1,0:T(8,128)(2,1)} %raw_ref.1) | copy-start | bytes 3612676
  2.6 0.7 copy-start.6
  3.8 6.9 %copy-start.7 = (s32[8,343]{1,0:T(8,128)S(1)}, s32[8,343]{1,0:T(8,128)}, u32[]{:S(2)}) copy-start(s32[8,343]{1,0:T(8,128)} %conn_ref.1) | copy-start | bytes 32932
  3.8 6.8 %collective-permute-start = (bf16[80,256]{1,0:T(8,128)(2,1)S(1)}, bf16[80,256]{1,0:T(8,128)(2,1)S(1)}, u32[]{:S(2)}, u32[]{:S(2)}) collective-permute-start(bf16[80,256]{1,0:T(8,128)(2,1)S(1)} %shard_map.68), channel_id=1, source_target_pairs={{4,0},{8,4},{12,8},{16,12},{20,16},{24,20},{28,24},{5,1},{9,5},{13... | collective-permute-start | bytes 122888 | tf_op jit(solution)/shard_map/ppermute | solution.py:425
  29.0 12.1 %collective-permute-start.1 = (bf16[6,64,256]{2,1,0:T(8,128)(2,1)S(1)}, bf16[6,64,256]{2,1,0:T(8,128)(2,1)S(1)}, u32[]{:S(2)}, u32[]{:S(2)}) collective-permute-start(bf16[6,64,256]{2,1,0:T(8,128)(2,1)S(1)} %get-tuple-element.48), channel_id=1, source_target_pairs={{0,4},{4,8},{8,12},{12,16},{16,20},{20,24},{24,28},{1,5},{5,9},{9,... | collective-permute-start | bytes 589832 | tf_op jit(solution)/shard_map/ppermute | solution.py:425
  33.8 7.2 %collective-permute-start.2 = (bf16[5,64,256]{2,1,0:T(8,128)(2,1)S(1)}, bf16[5,64,256]{2,1,0:T(8,128)(2,1)S(1)}, u32[]{:S(2)}, u32[]{:S(2)}) collective-permute-start(bf16[5,64,256]{2,1,0:T(8,128)(2,1)S(1)} %get-tuple-element.49), channel_id=1, source_target_pairs={{4,0},{8,4},{12,8},{16,12},{20,16},{24,20},{28,24},{5,1},{9,5},{13... | collective-permute-start | bytes 491528 | tf_op jit(solution)/shard_map/ppermute | solution.py:425
  41.0 10.0 %copy-start.2 = (f32[2560,1]{1,0:T(8,128)S(1)}, f32[2560,1]{1,0:T(8,128)}, u32[]{:S(2)}) copy-start(f32[2560,1]{1,0:T(8,128)} %get-tuple-element.51.pot_hbm.pot_ref) | copy-start | bytes 30724
  49.4 11.5 %collective-permute-start.4 = (bf16[2624,256]{1,0:T(8,128)(2,1)}, bf16[2624,256]{1,0:T(8,128)(2,1)}, u32[]{:S(2)}, u32[]{:S(2)}) collective-permute-start(bf16[2624,256]{1,0:T(8,128)(2,1)} %get-tuple-element.73.x_ref), channel_id=1, source_target_pairs={{0,1},{1,0},{2,3},{3,2},{4,5},{5,4},{6,7},{7,6},{8,9},{9,8},{10,11... | collective-permute-start | bytes 4030472 | tf_op jit(solution)/shard_map/ppermute | solution.py:420
  49.4 18.1 %collective-permute-start.3 = (bf16[1344,256]{1,0:T(8,128)(2,1)}, bf16[1344,256]{1,0:T(8,128)(2,1)S(1)}, u32[]{:S(2)}, u32[]{:S(2)}) collective-permute-start(bf16[1344,256]{1,0:T(8,128)(2,1)} %get-tuple-element.55), channel_id=1, source_target_pairs={{0,2},{1,3},{2,0},{3,1},{4,6},{5,7},{6,4},{7,5},{8,10},{9,11},{10,... | collective-permute-start | bytes 2064392 | tf_op jit(solution)/shard_map/ppermute | solution.py:420
  51.0 5.2 %copy-start = (bf16[2624,256]{1,0:T(8,128)(2,1)S(1)}, bf16[2624,256]{1,0:T(8,128)(2,1)}, u32[]{:S(2)}) copy-start(bf16[2624,256]{1,0:T(8,128)(2,1)} %get-tuple-element.73.x_ref) | copy-start | bytes 4030468
  55.5 8.2 %collective-permute-start.5 = (bf16[672,256]{1,0:T(8,128)(2,1)}, bf16[672,256]{1,0:T(8,128)(2,1)}, u32[]{:S(2)}, u32[]{:S(2)}) collective-permute-start(bf16[672,256]{1,0:T(8,128)(2,1)} %get-tuple-element.60), channel_id=1, source_target_pairs={{0,1},{1,0},{2,3},{3,2},{4,5},{5,4},{6,7},{7,6},{8,9},{9,8},{10,11... | collective-permute-start | bytes 1032200 | tf_op jit(solution)/shard_map/ppermute | solution.py:420
  55.7 8.1 %collective-permute-start.6 = (bf16[672,256]{1,0:T(8,128)(2,1)}, bf16[672,256]{1,0:T(8,128)(2,1)}, u32[]{:S(2)}, u32[]{:S(2)}) collective-permute-start(bf16[672,256]{1,0:T(8,128)(2,1)} %get-tuple-element.61), channel_id=1, source_target_pairs={{0,1},{1,0},{2,3},{3,2},{4,5},{5,4},{6,7},{7,6},{8,9},{9,8},{10,11... | collective-permute-start | bytes 1032200 | tf_op jit(solution)/shard_map/ppermute | solution.py:420
  60.9 8.3 %copy-start.1 = (bf16[2,1344,256]{2,1,0:T(8,128)(2,1)S(1)}, bf16[2,1344,256]{2,1,0:T(8,128)(2,1)}, u32[]{:S(2)}) copy-start(bf16[2,1344,256]{2,1,0:T(8,128)(2,1)} %get-tuple-element.54.w_ref) | copy-start | bytes 4128772
  67.5 26.1 %collective-permute-start.11 = (bf16[588,512]{1,0:T(8,128)(2,1)}, bf16[588,512]{1,0:T(8,128)(2,1)}, u32[]{:S(2)}, u32[]{:S(2)}) collective-permute-start(bf16[588,512]{1,0:T(8,128)(2,1)} %get-tuple-element.78), channel_id=1, source_target_pairs={{0,2},{1,3},{2,0},{3,1},{4,6},{5,7},{6,4},{7,5},{8,10},{9,11},{10,... | collective-permute-start | bytes 1806344 | tf_op jit(solution)/shard_map/ppermute | solution.py:420
  71.6 0.8 copy-start.4
  72.4 7.6 %copy-start.5 = (f32[448,256]{1,0:T(8,128)S(1)}, f32[448,256]{1,0:T(8,128)}, u32[]{:S(2)}) copy-start(f32[448,256]{1,0:T(8,128)} %copy-done.4) | copy-start | bytes 1376260
  72.4 7.6 %collective-permute-start.7 = (bf16[448,256]{1,0:T(8,128)(2,1)}, bf16[448,256]{1,0:T(8,128)(2,1)S(1)}, u32[]{:S(2)}, u32[]{:S(2)}) collective-permute-start(bf16[448,256]{1,0:T(8,128)(2,1)} %get-tuple-element.68), channel_id=1, source_target_pairs={{0,4},{4,0},{8,12},{12,8},{16,20},{20,16},{24,28},{28,24},{1,5},{5... | collective-permute-start | bytes 688136 | tf_op jit(solution)/shard_map/ppermute | solution.py:420
  74.6 31.1 %collective-permute-start.16 = (bf16[588,512]{1,0:T(8,128)(2,1)}, bf16[588,512]{1,0:T(8,128)(2,1)}, u32[]{:S(2)}, u32[]{:S(2)}) collective-permute-start(bf16[588,512]{1,0:T(8,128)(2,1)} %get-tuple-element.80), channel_id=1, source_target_pairs={{0,3},{1,2},{2,1},{3,0},{4,7},{5,6},{6,5},{7,4},{8,11},{9,10},{10,... | collective-permute-start | bytes 1806344 | tf_op jit(solution)/shard_map/ppermute | solution.py:420
  80.6 7.4 %collective-permute-start.10 = (bf16[112,256]{1,0:T(8,128)(2,1)S(1)}, bf16[112,256]{1,0:T(8,128)(2,1)S(1)}, u32[]{:S(2)}, u32[]{:S(2)}) collective-permute-start(bf16[112,256]{1,0:T(8,128)(2,1)S(1)} %get-tuple-element.77), channel_id=1, source_target_pairs={{0,24},{4,28},{8,16},{12,20},{16,8},{20,12},{24,0},{28,4},{1,25},{... | collective-permute-start | bytes 172040 | tf_op jit(solution)/shard_map/ppermute | solution.py:420
  85.5 26.7 %collective-permute-start.21 = (bf16[588,512]{1,0:T(8,128)(2,1)S(1)}, bf16[588,512]{1,0:T(8,128)(2,1)S(1)}, u32[]{:S(2)}, u32[]{:S(2)}) collective-permute-start(bf16[588,512]{1,0:T(8,128)(2,1)S(1)} %get-tuple-element.82), channel_id=1, source_target_pairs={{0,1},{1,0},{2,3},{3,2},{4,5},{5,4},{6,7},{7,6},{8,9},{9,8},{10,11... | collective-permute-start | bytes 1806344 | tf_op jit(solution)/shard_map/ppermute | solution.py:420
  85.5 4.9 %collective-permute-start.8 = (bf16[112,256]{1,0:T(8,128)(2,1)S(1)}, bf16[112,256]{1,0:T(8,128)(2,1)S(1)}, u32[]{:S(2)}, u32[]{:S(2)}) collective-permute-start(bf16[112,256]{1,0:T(8,128)(2,1)S(1)} %get-tuple-element.70), channel_id=1, source_target_pairs={{0,8},{4,12},{8,0},{12,4},{16,24},{20,28},{24,16},{28,20},{1,9},{5... | collective-permute-start | bytes 172040 | tf_op jit(solution)/shard_map/ppermute | solution.py:420
  88.0 5.1 %collective-permute-start.9 = (bf16[112,256]{1,0:T(8,128)(2,1)S(1)}, bf16[112,256]{1,0:T(8,128)(2,1)S(1)}, u32[]{:S(2)}, u32[]{:S(2)}) collective-permute-start(bf16[112,256]{1,0:T(8,128)(2,1)S(1)} %get-tuple-element.71), channel_id=1, source_target_pairs={{0,16},{4,20},{8,24},{12,28},{16,0},{20,4},{24,8},{28,12},{1,17},{... | collective-permute-start | bytes 172040 | tf_op jit(solution)/shard_map/ppermute | solution.py:420
  93.6 4.9 %collective-permute-start.12 = (bf16[112,256]{1,0:T(8,128)(2,1)S(1)}, bf16[112,256]{1,0:T(8,128)(2,1)S(1)}, u32[]{:S(2)}, u32[]{:S(2)}) collective-permute-start(bf16[112,256]{1,0:T(8,128)(2,1)S(1)} %shard_map.77.own_ref), channel_id=1, source_target_pairs={{0,8},{4,12},{8,0},{12,4},{16,24},{20,28},{24,16},{28,20},{1,9},{5... | collective-permute-start | bytes 172040 | tf_op jit(solution)/shard_map/ppermute | solution.py:420
  95.5 5.8 %collective-permute-start.13 = (bf16[112,256]{1,0:T(8,128)(2,1)S(1)}, bf16[112,256]{1,0:T(8,128)(2,1)S(1)}, u32[]{:S(2)}, u32[]{:S(2)}) collective-permute-start(bf16[112,256]{1,0:T(8,128)(2,1)S(1)} %shard_map.77.own_ref), channel_id=1, source_target_pairs={{0,16},{4,20},{8,24},{12,28},{16,0},{20,4},{24,8},{28,12},{1,17},{... | collective-permute-start | bytes 172040 | tf_op jit(solution)/shard_map/ppermute | solution.py:420
  98.5 6.0 %collective-permute-start.14 = (bf16[112,256]{1,0:T(8,128)(2,1)S(1)}, bf16[112,256]{1,0:T(8,128)(2,1)S(1)}, u32[]{:S(2)}, u32[]{:S(2)}) collective-permute-start(bf16[112,256]{1,0:T(8,128)(2,1)S(1)} %shard_map.77.own_ref), channel_id=1, source_target_pairs={{0,24},{4,28},{8,16},{12,20},{16,8},{20,12},{24,0},{28,4},{1,25},{... | collective-permute-start | bytes 172040 | tf_op jit(solution)/shard_map/ppermute | solution.py:420
  105.1 6.1 %collective-permute-start.15 = (bf16[448,256]{1,0:T(8,128)(2,1)S(1)}, bf16[448,256]{1,0:T(8,128)(2,1)S(1)}, u32[]{:S(2)}, u32[]{:S(2)}) collective-permute-start(bf16[448,256]{1,0:T(8,128)(2,1)S(1)} %shard_map.78.refs_0_), channel_id=1, source_target_pairs={{0,4},{4,0},{8,12},{12,8},{16,20},{20,16},{24,28},{28,24},{1,5},{5... | collective-permute-start | bytes 688136 | tf_op jit(solution)/shard_map/ppermute | solution.py:420
  105.3 6.8 %collective-permute-start.19 = (bf16[448,256]{1,0:T(8,128)(2,1)S(1)}, bf16[448,256]{1,0:T(8,128)(2,1)S(1)}, u32[]{:S(2)}, u32[]{:S(2)}) collective-permute-start(bf16[448,256]{1,0:T(8,128)(2,1)S(1)} %shard_map.78.refs_0_), channel_id=1, source_target_pairs={{0,2},{1,3},{2,0},{3,1},{4,6},{5,7},{6,4},{7,5},{8,10},{9,11},{10,... | collective-permute-start | bytes 688136 | tf_op jit(solution)/shard_map/ppermute | solution.py:420
  111.2 6.0 %collective-permute-start.20 = (bf16[448,256]{1,0:T(8,128)(2,1)S(1)}, bf16[448,256]{1,0:T(8,128)(2,1)S(1)}, u32[]{:S(2)}, u32[]{:S(2)}) collective-permute-start(bf16[448,256]{1,0:T(8,128)(2,1)S(1)} %collective-permute-done.15.refs_1_), channel_id=1, source_target_pairs={{0,2},{1,3},{2,0},{3,1},{4,6},{5,7},{6,4},{7,5},{8,10},{9,11},{10,... | collective-permute-start | bytes 688136 | tf_op jit(solution)/shard_map/ppermute | solution.py:420
  111.7 5.6 %collective-permute-start.17 = (bf16[448,256]{1,0:T(8,128)(2,1)S(1)}, bf16[448,256]{1,0:T(8,128)(2,1)S(1)}, u32[]{:S(2)}, u32[]{:S(2)}) collective-permute-start(bf16[448,256]{1,0:T(8,128)(2,1)S(1)} %shard_map.78.refs_0_), channel_id=1, source_target_pairs={{0,1},{1,0},{2,3},{3,2},{4,5},{5,4},{6,7},{7,6},{8,9},{9,8},{10,11... | collective-permute-start | bytes 688136 | tf_op jit(solution)/shard_map/ppermute | solution.py:420
  111.7 5.6 %collective-permute-start.18 = (bf16[448,256]{1,0:T(8,128)(2,1)S(1)}, bf16[448,256]{1,0:T(8,128)(2,1)S(1)}, u32[]{:S(2)}, u32[]{:S(2)}) collective-permute-start(bf16[448,256]{1,0:T(8,128)(2,1)S(1)} %collective-permute-done.15.refs_1_), channel_id=1, source_target_pairs={{0,1},{1,0},{2,3},{3,2},{4,5},{5,4},{6,7},{7,6},{8,9},{9,8},{10,11... | collective-permute-start | bytes 688136 | tf_op jit(solution)/shard_map/ppermute | solution.py:420
  112.2 5.1 %collective-permute-start.22 = (bf16[448,256]{1,0:T(8,128)(2,1)S(1)}, bf16[448,256]{1,0:T(8,128)(2,1)S(1)}, u32[]{:S(2)}, u32[]{:S(2)}) collective-permute-start(bf16[448,256]{1,0:T(8,128)(2,1)S(1)} %collective-permute-done.19.refs_4_), channel_id=1, source_target_pairs={{0,1},{1,0},{2,3},{3,2},{4,5},{5,4},{6,7},{7,6},{8,9},{9,8},{10,11... | collective-permute-start | bytes 688136 | tf_op jit(solution)/shard_map/ppermute | solution.py:420
  117.2 1.5 %collective-permute-start.23 = (bf16[448,256]{1,0:T(8,128)(2,1)S(1)}, bf16[448,256]{1,0:T(8,128)(2,1)S(1)}, u32[]{:S(2)}, u32[]{:S(2)}) collective-permute-start(bf16[448,256]{1,0:T(8,128)(2,1)S(1)} %collective-permute-done.20.refs_5_), channel_id=1, source_target_pairs={{0,1},{1,0},{2,3},{3,2},{4,5},{5,4},{6,7},{7,6},{8,9},{9,8},{10,11... | collective-permute-start | bytes 688136 | tf_op jit(solution)/shard_map/ppermute | solution.py:420

commit v11 on v10

--- a/solution.py
+++ b/solution.py
@@ -12,6 +12,7 @@
 HALF = 2.0
 F32 = jnp.float32
 BF16 = jnp.bfloat16
+LANES = 128
 VMEM_LIMIT = 50 * 1024 * 1024
 
 
@@ -117,7 +118,14 @@
         at = slice(c * stride, (c + 1) * stride)
         hit = node == number
         v_ref[at] = mul(flat(hit), x_ref[...]).astype(BF16)
-        potc_ref[at] = jnp.sum(jnp.where(hit, pot_ref[...], 0.0), axis=1, keepdims=True)
+        column = jnp.sum(jnp.where(hit, pot_ref[...], 0.0), axis=1, keepdims=True)
+        potc_ref[at] = jnp.broadcast_to(column, (stride, LANES))
+
+
+def spread(column, width):
+    if width <= LANES:
+        return column[:, :width]
+    return jnp.concatenate([column] * (width // LANES), axis=1)
 
 
 def advance(image, now, before):
@@ -162,6 +170,7 @@
     else:
         f, r, s, g = slice(0, fp), slice(fp, cp), slice(stride - fp, stride), slice(0, fp)
         rest = slice(fp, cp)
+    potc = spread(potc, fp)
     gain = 2.0 / HALF
     out = [hc[f, f].astype(F32)]
     one = gain * hc[r, f].astype(F32)
@@ -242,7 +251,7 @@
             before = None if k == 0 else other_ref[at].astype(F32)
             if k == 1:
                 before = v_ref[at].astype(F32)
-            value = advance(rows + pot_ref[at] * now, now, before).astype(BF16)
+            value = advance(rows + spread(pot_ref[at], now.shape[1]) * now, now, before).astype(BF16)
             if c == 0:
                 value = jnp.concatenate([jnp.zeros((fp, width), BF16), value[fp:]], axis=0)
             if k == 0:
@@ -295,7 +304,7 @@
     nothing = jnp.zeros((fp, width), BF16)
     sides = []
     for side, (got_ref, pot, start) in enumerate(
-        ((fromleft_ref, pot_ref[:fp], v_ref[:fp]), (fromright_ref, potg, ghost_ref[:fp]))
+        ((fromleft_ref, spread(pot_ref[:fp], width), v_ref[:fp]), (fromright_ref, potg, ghost_ref[:fp]))
     ):
         theirs = load_matrices(got_ref, got_ref.shape[0] - extra, DEGREE, fp, width)
         ours = load_matrices(own_ref.at[side], DEGREE + 1, DEGREE, fp, width)
@@ -332,7 +341,7 @@
         def emit(c, rows, lower, carry, k=k, now_ref=now_ref):
             at = slice(c * stride, (c + 1) * stride)
             now = now_ref[at].astype(F32)
-            value = advance(rows + pot_ref[at] * now, now, refs[k - 1][at].astype(F32)).astype(BF16)
+            value = advance(rows + spread(pot_ref[at], now.shape[1]) * now, now, refs[k - 1][at].astype(F32)).astype(BF16)
             if c == 0:
                 value = jnp.concatenate([low[k + 1], value[fp:]], axis=0)
             refs[k + 1][at] = value
@@ -357,12 +366,12 @@
     def emit(c, rows, lower, carry):
         at = slice(c * stride, (c + 1) * stride)
         now = x_ref[at].astype(F32)
-        out = (rows + pot_ref[at] * now).astype(BF16)
+        out = (rows + spread(pot_ref[at], now.shape[1]) * now).astype(BF16)
         part, at_w = divmod(c, half)
         w_ref[part, at_w * stride : (at_w + 1) * stride] = out
         if c == half:
             w_ref[0, half * stride :] = carry.astype(BF16)
-            w_ref[1, :fp] = (lower + pot_ref[c * stride : c * stride + fp] * now[:fp]).astype(BF16)
+            w_ref[1, :fp] = (lower + spread(pot_ref[c * stride : c * stride + fp], now.shape[1]) * now[:fp]).astype(BF16)
         if c == 0:
             out = jnp.concatenate([face_image_ref[...].astype(BF16), out[fp:]], axis=0)
         image_ref[at] = out
@@ -688,7 +697,7 @@
         out_shape=[
             sds((cells, cp, cp), BF16),
             sds((total, width), BF16),
-            sds((total, 1), F32),
+            sds((total, LANES), F32),
             sds((cells, 1, stride), F32),
             sds((total, width), BF16),
             sds((2, DEGREE + 1 + extra, fp, width), F32),
@@ -698,7 +707,7 @@
         out_specs=[hbm, vmem, hbm, vmem, hbm, vmem, vmem, vmem],
         scratch_shapes=[
             pltpu.VMEM((cells, cp, cp), BF16),
-            pltpu.VMEM((total, 1), F32),
+            pltpu.VMEM((total, LANES), F32),
             pltpu.VMEM((total, width), BF16),
             ext,
             ext,
@@ -727,7 +736,7 @@
             ext,
             ext,
             pltpu.VMEM((cells, cp, cp), BF16),
-            pltpu.VMEM((total, 1), F32),
+            pltpu.VMEM((total, LANES), F32),
             pltpu.SemaphoreType.DMA((4,)),
         ],
         compiler_params=params(),

time: 124 us -> 123 us (level)
  transfers between devices with their start and end apart: 24 -> 24, of which waited for: 12 -> 12; matrix products, arithmetic and copies ran while one was open for 3% -> 3% of each run, Pallas kernels for 16% -> 17%
where the time goes in v11:
time: 123 us
  Pallas kernels  51.1 us (42%)
  waiting for transfers between devices  37.5 us (30%)
  starting transfers between devices  25.7 us (21%)
  local copies, waits for them, and re-layouts  6.74 us (5%)
    ppermute x21, waiting for transfers between devices, swap(): lax.ppermute(block, axis, [(i, i ^ bit) for i in range(lax.axis_size(axis...  29.3 us
    ppermute x21, starting transfers between devices, swap(): lax.ppermute(block, axis, [(i, i ^ bit) for i in range(lax.axis_size(axis...  18.3 us
    pallas_call x1, Pallas kernels, body(): pl.pallas_call(functools.partial(free_kernel, fp, ip), in_specs=[vmem] *...  17.9 us
    pallas_call x2, Pallas kernels, back(): pl.pallas_call(back_pair_kernel, grid=(1,), in_specs=[smem, whole(1, tota...  8.48 us
    ppermute x3, waiting for transfers between devices, shift(): lax.ppermute(block, axis, [(i, i + distance) for i in range(n) if 0 <= i...  8.13 us
    pallas_call x1, Pallas kernels, body(): pl.pallas_call(functools.partial(forced_kernel, fp), in_specs=[pl.BlockSp...  7.75 us
    ppermute x3, starting transfers between devices, shift(): lax.ppermute(block, axis, [(i, i + distance) for i in range(n) if 0 <= i...  7.42 us
    unnamed x17, local copies, waits for them, and re-layouts  5.94 us
  transfers between devices with their start and end apart: 24, of which 12 were waited for; matrix products, arithmetic and copies ran while one was open for 3% of the time, Pallas kernels for 17%

profile of v11, /device:TPU:0, one launch (start us, length us, event | category | flops | bytes accessed | tf_op | source)
XLA Modules:
  0.0 122.5 jit_solution(2603128527789494213)
XLA Ops:
  0.6 0.7 reshape.15.pot_ref.potraw_ref
  1.3 1.3 %copy-done.3 = bf16[2352,256]{1,0:T(8,128)(2,1)S(1)} copy-done((bf16[2352,256]{1,0:T(8,128)(2,1)S(1)}, bf16[2352,256]{1,0:T(8,128)(2,1)}, u32[]{:S(2)}) %copy-start.3) | copy-done | bytes 1204248
  2.6 0.7 copy-done.6
  3.3 0.5 shard_map.68
  3.8 0.0 copy-start.7
  3.8 1.3 %collective-permute-start = (bf16[80,256]{1,0:T(8,128)(2,1)S(1)}, bf16[80,256]{1,0:T(8,128)(2,1)S(1)}, u32[]{:S(2)}, u32[]{:S(2)}) collective-permute-start(bf16[80,256]{1,0:T(8,128)(2,1)S(1)} %shard_map.68), channel_id=1, source_target_pairs={{4,0},{8,4},{12,8},{16,12},{20,16},{24,20},{28,24},{5,1},{9,5},{13... | collective-permute-start | bytes 122888 | tf_op jit(solution)/shard_map/ppermute | solution.py:434
  5.1 3.2 %copy.7.hraw_ref = bf16[8,343,343]{2,1,0:T(8,128)(2,1)} copy(bf16[8,343,343]{2,0,1:T(8,128)(2,1)} %param.7) | data formatting | bytes 3764768 | tf_op args[2]
  8.3 2.3 %collective-permute-done.ghost_ref = bf16[80,256]{1,0:T(8,128)(2,1)S(1)} collective-permute-done((bf16[80,256]{1,0:T(8,128)(2,1)S(1)}, bf16[80,256]{1,0:T(8,128)(2,1)S(1)}, u32[]{:S(2)}, u32[]{:S(2)}) %collective-permute-start) | collective-permute-done | bytes 40992 | tf_op jit(solution)/shard_map/ppermute | solution.py:434
  10.6 17.9 %shard_map.69 = (bf16[8,384,384]{2,1,0:T(8,128)(2,1)}, bf16[2560,256]{1,0:T(8,128)(2,1)S(1)}, f32[2560,128]{1,0:T(8,128)}, f32[8,1,320]{2,1,0:T(1,128)S(1)}, bf1...) custom-call(s32[8,343]{1,0:T(8,128)S(1)} %copy-done.7, ...), custom_call_target="tpu_custom_call" | custom-call | flops 2415919104 | bytes 8388608 | tf_op jit(solution)/shard_map/pallas_call | solution.py:694
  28.5 4.8 %collective-permute-start.1 = (bf16[6,64,256]{2,1,0:T(8,128)(2,1)S(1)}, bf16[6,64,256]{2,1,0:T(8,128)(2,1)S(1)}, u32[]{:S(2)}, u32[]{:S(2)}) collective-permute-start(bf16[6,64,256]{2,1,0:T(8,128)(2,1)S(1)} %get-tuple-element.48), channel_id=1, source_target_pairs={{0,4},{4,8},{8,12},{12,16},{16,20},{20,24},{24,28},{1,5},{5,9},{9,... | collective-permute-start | bytes 589832 | tf_op jit(solution)/shard_map/ppermute | solution.py:434
  33.3 1.3 %collective-permute-start.2 = (bf16[5,64,256]{2,1,0:T(8,128)(2,1)S(1)}, bf16[5,64,256]{2,1,0:T(8,128)(2,1)S(1)}, u32[]{:S(2)}, u32[]{:S(2)}) collective-permute-start(bf16[5,64,256]{2,1,0:T(8,128)(2,1)S(1)} %get-tuple-element.49), channel_id=1, source_target_pairs={{4,0},{8,4},{12,8},{16,12},{20,16},{24,20},{28,24},{5,1},{9,5},{13... | collective-permute-start | bytes 491528 | tf_op jit(solution)/shard_map/ppermute | solution.py:434
  34.7 0.1 pad_add_fusion.3.place_ref
  34.8 5.8 %collective-permute-done.2.fromright_ref = bf16[5,64,256]{2,1,0:T(8,128)(2,1)S(1)} collective-permute-done((bf16[5,64,256]{2,1,0:T(8,128)(2,1)S(1)}, bf16[5,64,256]{2,1,0:T(8,128)(2,1)S(1)}, u32[]{:S(2)}, u32[]{:S(2)}) %collective-permute-start.2) | collective-permute-done | bytes 163872 | tf_op jit(solution)/shard_map/ppermute | solution.py:434
  40.6 0.0 collective-permute-done.1.fromleft_ref
  40.6 7.8 %shard_map.70 = (bf16[2624,256]{1,0:T(8,128)(2,1)}, f32[64,256]{1,0:T(8,128)S(1)}, bf16[1344,256]{1,0:T(8,128)(2,1)}) custom-call(s32[2]{0:T(128)S(1)} %pad_add_fusion.3.place_ref, bf16[2560,256]{1,0:T(8,128)(2,1)S(1)} %get-tuple-element.45.v_ref, bf16[80,256]{1,0:T(8,128)(2,1)S(1)} %collective-permute-done.ghost_ref, ...), custom_call_target="tpu_custom_call" | custom-call | flops 2415919104 | bytes 8388608 | tf_op jit(solution)/shard_map/pallas_call | solution.py:726
  48.3 0.1 collective-permute-start.4
  48.4 1.6 %collective-permute-start.3 = (bf16[1344,256]{1,0:T(8,128)(2,1)}, bf16[1344,256]{1,0:T(8,128)(2,1)S(1)}, u32[]{:S(2)}, u32[]{:S(2)}) collective-permute-start(bf16[1344,256]{1,0:T(8,128)(2,1)} %get-tuple-element.55), channel_id=1, source_target_pairs={{0,2},{1,3},{2,0},{3,1},{4,6},{5,7},{6,4},{7,5},{8,10},{9,11},{10,... | collective-permute-start | bytes 2064392 | tf_op jit(solution)/shard_map/ppermute | solution.py:429
  50.0 4.5 %shard_map.71 = (bf16[2560,256]{1,0:T(8,128)(2,1)S(1)}, bf16[2,1344,256]{2,1,0:T(8,128)(2,1)}, bf16[672,256]{1,0:T(8,128)(2,1)}, bf16[672,256]{1,0:T(8,128)(2,1)}) custom-call(s32[2]{0:T(128)S(1)} %pad_add_fusion.3.place_ref, bf16[2624,256]{1,0:T(8,128)(2,1)} %get-tuple-element.73.x_ref, f32[64,256]{1,0:T(8,128)S(1)} %get-tuple-element.53.face_image_ref, ...), custom_call_target="tpu_custom_call" | custom-call | flops 1048576 | bytes 1024 | tf_op jit(solution)/shard_map/pallas_call | solution.py:745
  54.5 0.2 collective-permute-start.5
  54.7 0.3 collective-permute-start.6
  55.0 0.1 pad_add_fusion.4.at_ref
  55.1 0.1 reshape.16.node_ref
  55.2 4.7 %shard_map.73 = (bf16[588,512]{1,0:T(8,128)(2,1)}, bf16[588,512]{1,0:T(8,128)(2,1)}) custom-call(s32[2]{0:T(128)S(1)} %pad_add_fusion.4.at_ref, f32[1,2560]{1,0:T(1,128)S(1)} %reshape.16.node_ref, bf16[2624,256]{1,0:T(8,128)(2,1)S(1)} %copy-done, bf16[2560,256]{1,0:T(8,128)(2,1)S(1)} %get-tuple-element.74.image_ref), custom_call_target="tpu_custom_call" | custom-call | flops 1048576 | bytes 1024 | tf_op jit(solution)/shard_map/pallas_call | solution.py:566
  59.9 3.1 %shard_map.72.near_ref = f32[384,256]{1,0:T(8,128)S(1)} custom-call(s32[1]{0:T(128)} %bitcast.4.core_ref, bf16[2624,256]{1,0:T(8,128)(2,1)S(1)} %copy-done, bf16[2,1344,256]{2,1,0:T(8,128)(2,1)} %get-tuple-element.54.w_ref, bf16[2624,256]{1,0:T(8,128)(2,1)} %collective-permute-done.4.other_ref), custom_call_target="tpu_custom_call" | custom-call | flops 1048576 | bytes 1024 | tf_op jit(solution)/shard_map/pallas_call | solution.py:580
  63.0 3.5 %collective-permute-done.3.far_ref = bf16[1344,256]{1,0:T(8,128)(2,1)S(1)} collective-permute-done((bf16[1344,256]{1,0:T(8,128)(2,1)}, bf16[1344,256]{1,0:T(8,128)(2,1)S(1)}, u32[]{:S(2)}, u32[]{:S(2)}) %collective-permute-start.3) | collective-permute-done | bytes 688160 | tf_op jit(solution)/shard_map/ppermute | solution.py:429
  66.5 1.5 %collective-permute-start.11 = (bf16[588,512]{1,0:T(8,128)(2,1)}, bf16[588,512]{1,0:T(8,128)(2,1)}, u32[]{:S(2)}, u32[]{:S(2)}) collective-permute-start(bf16[588,512]{1,0:T(8,128)(2,1)} %get-tuple-element.78), channel_id=1, source_target_pairs={{0,2},{1,3},{2,0},{3,1},{4,6},{5,7},{6,4},{7,5},{8,10},{9,11},{10,... | collective-permute-start | bytes 1806344 | tf_op jit(solution)/shard_map/ppermute | solution.py:429
  68.0 0.1 pad_add_fusion.2.place_ref
  68.0 0.1 pad_add_fusion.1.bits_ref
  68.1 2.5 %shard_map.74 = (f32[448,256]{1,0:T(8,128)S(1)}, bf16[448,256]{1,0:T(8,128)(2,1)}) custom-call(s32[2]{0:T(128)S(1)} %pad_add_fusion.1.bits_ref, s32[2]{0:T(128)S(1)} %pad_add_fusion.2.place_ref, bf16[2,1344,256]{2,1,0:T(8,128)(2,1)S(1)} %copy-done.1, bf16[672,256]{1,0:T(8,128)(2,1)} %collective-permute-done.5.first_ref, ...), custom_call_target="tpu_custom_call" | custom-call | flops 704643072 | bytes 4194304 | tf_op jit(solution)/shard_map/pallas_call | solution.py:601
  70.6 0.8 copy-done.4
  71.3 2.2 %collective-permute-start.7 = (bf16[448,256]{1,0:T(8,128)(2,1)}, bf16[448,256]{1,0:T(8,128)(2,1)S(1)}, u32[]{:S(2)}, u32[]{:S(2)}) collective-permute-start(bf16[448,256]{1,0:T(8,128)(2,1)} %get-tuple-element.68), channel_id=1, source_target_pairs={{0,4},{4,0},{8,12},{12,8},{16,20},{20,16},{24,28},{28,24},{1,5},{5... | collective-permute-start | bytes 688136 | tf_op jit(solution)/shard_map/ppermute | solution.py:429
  73.6 0.0 collective-permute-start.16
  73.6 0.1 pad_add_fusion.5.at_ref
  73.6 3.8 %shard_map.76 = (bf16[588,512]{1,0:T(8,128)(2,1)S(1)}, bf16[588,512]{1,0:T(8,128)(2,1)S(1)}) custom-call(s32[2]{0:T(128)S(1)} %pad_add_fusion.5.at_ref, f32[1,2560]{1,0:T(1,128)S(1)} %reshape.16.node_ref, bf16[2624,256]{1,0:T(8,128)(2,1)S(1)} %copy-done, bf16[2560,256]{1,0:T(8,128)(2,1)S(1)} %get-tuple-element.74.image_ref), custom_call_target="tpu_custom_call" | custom-call | flops 1048576 | bytes 1024 | tf_op jit(solution)/shard_map/pallas_call | solution.py:566
  77.5 1.4 %collective-permute-done.7.refs_0_ = bf16[448,256]{1,0:T(8,128)(2,1)S(1)} collective-permute-done((bf16[448,256]{1,0:T(8,128)(2,1)}, bf16[448,256]{1,0:T(8,128)(2,1)S(1)}, u32[]{:S(2)}, u32[]{:S(2)}) %collective-permute-start.7) | collective-permute-done | bytes 229408 | tf_op jit(solution)/shard_map/ppermute | solution.py:429
  78.9 0.6 shard_map.75
  79.6 4.9 %collective-permute-start.10 = (bf16[112,256]{1,0:T(8,128)(2,1)S(1)}, bf16[112,256]{1,0:T(8,128)(2,1)S(1)}, u32[]{:S(2)}, u32[]{:S(2)}) collective-permute-start(bf16[112,256]{1,0:T(8,128)(2,1)S(1)} %get-tuple-element.77), channel_id=1, source_target_pairs={{0,24},{4,28},{8,16},{12,20},{16,8},{20,12},{24,0},{28,4},{1,25},{... | collective-permute-start | bytes 172040 | tf_op jit(solution)/shard_map/ppermute | solution.py:429
  84.5 0.0 collective-permute-start.21
  84.5 0.0 collective-permute-start.8
  84.5 2.4 %collective-permute-done.10.refs_2_ = bf16[112,256]{1,0:T(8,128)(2,1)S(1)} collective-permute-done((bf16[112,256]{1,0:T(8,128)(2,1)S(1)}, bf16[112,256]{1,0:T(8,128)(2,1)S(1)}, u32[]{:S(2)}, u32[]{:S(2)}) %collective-permute-start.10) | collective-permute-done | bytes 57376 | tf_op jit(solution)/shard_map/ppermute | solution.py:429
  86.9 0.9 collective-permute-start.9
  87.8 1.7 %collective-permute-done.8.refs_0_ = bf16[112,256]{1,0:T(8,128)(2,1)S(1)} collective-permute-done((bf16[112,256]{1,0:T(8,128)(2,1)S(1)}, bf16[112,256]{1,0:T(8,128)(2,1)S(1)}, u32[]{:S(2)}, u32[]{:S(2)}) %collective-permute-start.8) | collective-permute-done | bytes 57376 | tf_op jit(solution)/shard_map/ppermute | solution.py:429
  89.4 2.5 %collective-permute-done.9.refs_1_ = bf16[112,256]{1,0:T(8,128)(2,1)S(1)} collective-permute-done((bf16[112,256]{1,0:T(8,128)(2,1)S(1)}, bf16[112,256]{1,0:T(8,128)(2,1)S(1)}, u32[]{:S(2)}, u32[]{:S(2)}) %collective-permute-start.9) | collective-permute-done | bytes 57376 | tf_op jit(solution)/shard_map/ppermute | solution.py:429
  92.0 0.6 shard_map.77.own_ref
  92.6 0.0 collective-permute-done.11.refs_10_
  92.6 1.9 %collective-permute-start.12 = (bf16[112,256]{1,0:T(8,128)(2,1)S(1)}, bf16[112,256]{1,0:T(8,128)(2,1)S(1)}, u32[]{:S(2)}, u32[]{:S(2)}) collective-permute-start(bf16[112,256]{1,0:T(8,128)(2,1)S(1)} %shard_map.77.own_ref), channel_id=1, source_target_pairs={{0,8},{4,12},{8,0},{12,4},{16,24},{20,28},{24,16},{28,20},{1,9},{5... | collective-permute-start | bytes 172040 | tf_op jit(solution)/shard_map/ppermute | solution.py:429
  94.5 3.0 %collective-permute-start.13 = (bf16[112,256]{1,0:T(8,128)(2,1)S(1)}, bf16[112,256]{1,0:T(8,128)(2,1)S(1)}, u32[]{:S(2)}, u32[]{:S(2)}) collective-permute-start(bf16[112,256]{1,0:T(8,128)(2,1)S(1)} %shard_map.77.own_ref), channel_id=1, source_target_pairs={{0,16},{4,20},{8,24},{12,28},{16,0},{20,4},{24,8},{28,12},{1,17},{... | collective-permute-start | bytes 172040 | tf_op jit(solution)/shard_map/ppermute | solution.py:429
  97.5 0.0 collective-permute-start.14
  97.5 0.0 collective-permute-done.12.refs_0_
  97.5 2.8 %collective-permute-done.13.refs_1_ = bf16[112,256]{1,0:T(8,128)(2,1)S(1)} collective-permute-done((bf16[112,256]{1,0:T(8,128)(2,1)S(1)}, bf16[112,256]{1,0:T(8,128)(2,1)S(1)}, u32[]{:S(2)}, u32[]{:S(2)}) %collective-permute-start.13) | collective-permute-done | bytes 57376 | tf_op jit(solution)/shard_map/ppermute | solution.py:429
  100.3 3.2 %collective-permute-done.14.refs_2_ = bf16[112,256]{1,0:T(8,128)(2,1)S(1)} collective-permute-done((bf16[112,256]{1,0:T(8,128)(2,1)S(1)}, bf16[112,256]{1,0:T(8,128)(2,1)S(1)}, u32[]{:S(2)}, u32[]{:S(2)}) %collective-permute-start.14) | collective-permute-done | bytes 57376 | tf_op jit(solution)/shard_map/ppermute | solution.py:429
  103.5 0.6 shard_map.78.refs_0_
  104.0 0.3 collective-permute-start.15
  104.3 0.4 collective-permute-start.19
  104.7 5.4 %collective-permute-done.15.refs_1_ = bf16[448,256]{1,0:T(8,128)(2,1)S(1)} collective-permute-done((bf16[448,256]{1,0:T(8,128)(2,1)S(1)}, bf16[448,256]{1,0:T(8,128)(2,1)S(1)}, u32[]{:S(2)}, u32[]{:S(2)}) %collective-permute-start.15) | collective-permute-done | bytes 229408 | tf_op jit(solution)/shard_map/ppermute | solution.py:429
  110.1 0.5 collective-permute-start.20
  110.6 0.0 collective-permute-start.17
  110.7 0.5 collective-permute-start.18
  111.2 0.0 collective-permute-start.22
  111.2 0.0 collective-permute-done.21.refs_9_
  111.2 5.0 %collective-permute-done.20.refs_5_ = bf16[448,256]{1,0:T(8,128)(2,1)S(1)} collective-permute-done((bf16[448,256]{1,0:T(8,128)(2,1)S(1)}, bf16[448,256]{1,0:T(8,128)(2,1)S(1)}, u32[]{:S(2)}, u32[]{:S(2)}) %collective-permute-start.20) | collective-permute-done | bytes 229408 | tf_op jit(solution)/shard_map/ppermute | solution.py:429
  116.1 0.1 pad_add_fusion.place_ref
  116.2 1.4 %collective-permute-done.23.refs_7_ = bf16[448,256]{1,0:T(8,128)(2,1)S(1)} collective-permute-done((bf16[448,256]{1,0:T(8,128)(2,1)S(1)}, bf16[448,256]{1,0:T(8,128)(2,1)S(1)}, u32[]{:S(2)}, u32[]{:S(2)}) %collective-permute-start.23) | collective-permute-done | bytes 229408 | tf_op jit(solution)/shard_map/ppermute | solution.py:429
  117.6 4.7 %shard_map.79 = (f32[588,1024]{1,0:T(8,128)}, bf16[1024,1024]{1,0:T(8,128)(2,1)}) custom-call(s32[2]{0:T(128)S(1)} %pad_add_fusion.place_ref, bf16[448,256]{1,0:T(8,128)(2,1)S(1)} %shard_map.78.refs_0_, bf16[448,256]{1,0:T(8,128)(2,1)S(1)} %collective-permute-done.15.refs_1_, bf16[448,256]{1,0:T(8,128)(2,1)S(1)} %collective-permute-done.17.refs_2_, ...), custom_call_target="tpu_custom_call" | custom-call | tf_op jit(solution)/shard_map/pallas_call | solution.py:652
  (22 shorter events, 0.1 us)
Async XLA Ops:
  1.3 1.3 %copy-start.3 = (bf16[2352,256]{1,0:T(8,128)(2,1)S(1)}, bf16[2352,256]{1,0:T(8,128)(2,1)}, u32[]{:S(2)}) copy-start(bf16[2352,256]{1,0:T(8,128)(2,1)} %raw_ref.1) | copy-start | bytes 3612676
  2.6 0.7 copy-start.6
  3.8 6.9 %copy-start.7 = (s32[8,343]{1,0:T(8,128)S(1)}, s32[8,343]{1,0:T(8,128)}, u32[]{:S(2)}) copy-start(s32[8,343]{1,0:T(8,128)} %conn_ref.1) | copy-start | bytes 32932
  3.8 6.8 %collective-permute-start = (bf16[80,256]{1,0:T(8,128)(2,1)S(1)}, bf16[80,256]{1,0:T(8,128)(2,1)S(1)}, u32[]{:S(2)}, u32[]{:S(2)}) collective-permute-start(bf16[80,256]{1,0:T(8,128)(2,1)S(1)} %shard_map.68), channel_id=1, source_target_pairs={{4,0},{8,4},{12,8},{16,12},{20,16},{24,20},{28,24},{5,1},{9,5},{13... | collective-permute-start | bytes 122888 | tf_op jit(solution)/shard_map/ppermute | solution.py:434
  28.5 12.1 %collective-permute-start.1 = (bf16[6,64,256]{2,1,0:T(8,128)(2,1)S(1)}, bf16[6,64,256]{2,1,0:T(8,128)(2,1)S(1)}, u32[]{:S(2)}, u32[]{:S(2)}) collective-permute-start(bf16[6,64,256]{2,1,0:T(8,128)(2,1)S(1)} %get-tuple-element.48), channel_id=1, source_target_pairs={{0,4},{4,8},{8,12},{12,16},{16,20},{20,24},{24,28},{1,5},{5,9},{9,... | collective-permute-start | bytes 589832 | tf_op jit(solution)/shard_map/ppermute | solution.py:434
  33.3 7.2 %collective-permute-start.2 = (bf16[5,64,256]{2,1,0:T(8,128)(2,1)S(1)}, bf16[5,64,256]{2,1,0:T(8,128)(2,1)S(1)}, u32[]{:S(2)}, u32[]{:S(2)}) collective-permute-start(bf16[5,64,256]{2,1,0:T(8,128)(2,1)S(1)} %get-tuple-element.49), channel_id=1, source_target_pairs={{4,0},{8,4},{12,8},{16,12},{20,16},{24,20},{28,24},{5,1},{9,5},{13... | collective-permute-start | bytes 491528 | tf_op jit(solution)/shard_map/ppermute | solution.py:434
  40.6 9.4 %copy-start.2 = (f32[2560,128]{1,0:T(8,128)S(1)}, f32[2560,128]{1,0:T(8,128)}, u32[]{:S(2)}) copy-start(f32[2560,128]{1,0:T(8,128)} %get-tuple-element.51.pot_hbm.pot_ref) | copy-start | bytes 3932164
  48.3 11.5 %collective-permute-start.4 = (bf16[2624,256]{1,0:T(8,128)(2,1)}, bf16[2624,256]{1,0:T(8,128)(2,1)}, u32[]{:S(2)}, u32[]{:S(2)}) collective-permute-start(bf16[2624,256]{1,0:T(8,128)(2,1)} %get-tuple-element.73.x_ref), channel_id=1, source_target_pairs={{0,1},{1,0},{2,3},{3,2},{4,5},{5,4},{6,7},{7,6},{8,9},{9,8},{10,11... | collective-permute-start | bytes 4030472 | tf_op jit(solution)/shard_map/ppermute | solution.py:429
  48.4 18.1 %collective-permute-start.3 = (bf16[1344,256]{1,0:T(8,128)(2,1)}, bf16[1344,256]{1,0:T(8,128)(2,1)S(1)}, u32[]{:S(2)}, u32[]{:S(2)}) collective-permute-start(bf16[1344,256]{1,0:T(8,128)(2,1)} %get-tuple-element.55), channel_id=1, source_target_pairs={{0,2},{1,3},{2,0},{3,1},{4,6},{5,7},{6,4},{7,5},{8,10},{9,11},{10,... | collective-permute-start | bytes 2064392 | tf_op jit(solution)/shard_map/ppermute | solution.py:429
  50.0 5.2 %copy-start = (bf16[2624,256]{1,0:T(8,128)(2,1)S(1)}, bf16[2624,256]{1,0:T(8,128)(2,1)}, u32[]{:S(2)}) copy-start(bf16[2624,256]{1,0:T(8,128)(2,1)} %get-tuple-element.73.x_ref) | copy-start | bytes 4030468
  54.5 8.5 %collective-permute-start.5 = (bf16[672,256]{1,0:T(8,128)(2,1)}, bf16[672,256]{1,0:T(8,128)(2,1)}, u32[]{:S(2)}, u32[]{:S(2)}) collective-permute-start(bf16[672,256]{1,0:T(8,128)(2,1)} %get-tuple-element.60), channel_id=1, source_target_pairs={{0,1},{1,0},{2,3},{3,2},{4,5},{5,4},{6,7},{7,6},{8,9},{9,8},{10,11... | collective-permute-start | bytes 1032200 | tf_op jit(solution)/shard_map/ppermute | solution.py:429
  54.7 8.3 %collective-permute-start.6 = (bf16[672,256]{1,0:T(8,128)(2,1)}, bf16[672,256]{1,0:T(8,128)(2,1)}, u32[]{:S(2)}, u32[]{:S(2)}) collective-permute-start(bf16[672,256]{1,0:T(8,128)(2,1)} %get-tuple-element.61), channel_id=1, source_target_pairs={{0,1},{1,0},{2,3},{3,2},{4,5},{5,4},{6,7},{7,6},{8,9},{9,8},{10,11... | collective-permute-start | bytes 1032200 | tf_op jit(solution)/shard_map/ppermute | solution.py:429
  59.9 8.3 %copy-start.1 = (bf16[2,1344,256]{2,1,0:T(8,128)(2,1)S(1)}, bf16[2,1344,256]{2,1,0:T(8,128)(2,1)}, u32[]{:S(2)}) copy-start(bf16[2,1344,256]{2,1,0:T(8,128)(2,1)} %get-tuple-element.54.w_ref) | copy-start | bytes 4128772
  66.5 26.1 %collective-permute-start.11 = (bf16[588,512]{1,0:T(8,128)(2,1)}, bf16[588,512]{1,0:T(8,128)(2,1)}, u32[]{:S(2)}, u32[]{:S(2)}) collective-permute-start(bf16[588,512]{1,0:T(8,128)(2,1)} %get-tuple-element.78), channel_id=1, source_target_pairs={{0,2},{1,3},{2,0},{3,1},{4,6},{5,7},{6,4},{7,5},{8,10},{9,11},{10,... | collective-permute-start | bytes 1806344 | tf_op jit(solution)/shard_map/ppermute | solution.py:429
  70.6 0.8 copy-start.4
  71.3 7.6 %copy-start.5 = (f32[448,256]{1,0:T(8,128)S(1)}, f32[448,256]{1,0:T(8,128)}, u32[]{:S(2)}) copy-start(f32[448,256]{1,0:T(8,128)} %copy-done.4) | copy-start | bytes 1376260
  71.3 7.6 %collective-permute-start.7 = (bf16[448,256]{1,0:T(8,128)(2,1)}, bf16[448,256]{1,0:T(8,128)(2,1)S(1)}, u32[]{:S(2)}, u32[]{:S(2)}) collective-permute-start(bf16[448,256]{1,0:T(8,128)(2,1)} %get-tuple-element.68), channel_id=1, source_target_pairs={{0,4},{4,0},{8,12},{12,8},{16,20},{20,16},{24,28},{28,24},{1,5},{5... | collective-permute-start | bytes 688136 | tf_op jit(solution)/shard_map/ppermute | solution.py:429
  73.6 31.1 %collective-permute-start.16 = (bf16[588,512]{1,0:T(8,128)(2,1)}, bf16[588,512]{1,0:T(8,128)(2,1)}, u32[]{:S(2)}, u32[]{:S(2)}) collective-permute-start(bf16[588,512]{1,0:T(8,128)(2,1)} %get-tuple-element.80), channel_id=1, source_target_pairs={{0,3},{1,2},{2,1},{3,0},{4,7},{5,6},{6,5},{7,4},{8,11},{9,10},{10,... | collective-permute-start | bytes 1806344 | tf_op jit(solution)/shard_map/ppermute | solution.py:429
  79.6 7.4 %collective-permute-start.10 = (bf16[112,256]{1,0:T(8,128)(2,1)S(1)}, bf16[112,256]{1,0:T(8,128)(2,1)S(1)}, u32[]{:S(2)}, u32[]{:S(2)}) collective-permute-start(bf16[112,256]{1,0:T(8,128)(2,1)S(1)} %get-tuple-element.77), channel_id=1, source_target_pairs={{0,24},{4,28},{8,16},{12,20},{16,8},{20,12},{24,0},{28,4},{1,25},{... | collective-permute-start | bytes 172040 | tf_op jit(solution)/shard_map/ppermute | solution.py:429
  84.5 26.7 %collective-permute-start.21 = (bf16[588,512]{1,0:T(8,128)(2,1)S(1)}, bf16[588,512]{1,0:T(8,128)(2,1)S(1)}, u32[]{:S(2)}, u32[]{:S(2)}) collective-permute-start(bf16[588,512]{1,0:T(8,128)(2,1)S(1)} %get-tuple-element.82), channel_id=1, source_target_pairs={{0,1},{1,0},{2,3},{3,2},{4,5},{5,4},{6,7},{7,6},{8,9},{9,8},{10,11... | collective-permute-start | bytes 1806344 | tf_op jit(solution)/shard_map/ppermute | solution.py:429
  84.5 4.9 %collective-permute-start.8 = (bf16[112,256]{1,0:T(8,128)(2,1)S(1)}, bf16[112,256]{1,0:T(8,128)(2,1)S(1)}, u32[]{:S(2)}, u32[]{:S(2)}) collective-permute-start(bf16[112,256]{1,0:T(8,128)(2,1)S(1)} %get-tuple-element.70), channel_id=1, source_target_pairs={{0,8},{4,12},{8,0},{12,4},{16,24},{20,28},{24,16},{28,20},{1,9},{5... | collective-permute-start | bytes 172040 | tf_op jit(solution)/shard_map/ppermute | solution.py:429
  86.9 5.1 %collective-permute-start.9 = (bf16[112,256]{1,0:T(8,128)(2,1)S(1)}, bf16[112,256]{1,0:T(8,128)(2,1)S(1)}, u32[]{:S(2)}, u32[]{:S(2)}) collective-permute-start(bf16[112,256]{1,0:T(8,128)(2,1)S(1)} %get-tuple-element.71), channel_id=1, source_target_pairs={{0,16},{4,20},{8,24},{12,28},{16,0},{20,4},{24,8},{28,12},{1,17},{... | collective-permute-start | bytes 172040 | tf_op jit(solution)/shard_map/ppermute | solution.py:429
  92.6 4.9 %collective-permute-start.12 = (bf16[112,256]{1,0:T(8,128)(2,1)S(1)}, bf16[112,256]{1,0:T(8,128)(2,1)S(1)}, u32[]{:S(2)}, u32[]{:S(2)}) collective-permute-start(bf16[112,256]{1,0:T(8,128)(2,1)S(1)} %shard_map.77.own_ref), channel_id=1, source_target_pairs={{0,8},{4,12},{8,0},{12,4},{16,24},{20,28},{24,16},{28,20},{1,9},{5... | collective-permute-start | bytes 172040 | tf_op jit(solution)/shard_map/ppermute | solution.py:429
  94.5 5.8 %collective-permute-start.13 = (bf16[112,256]{1,0:T(8,128)(2,1)S(1)}, bf16[112,256]{1,0:T(8,128)(2,1)S(1)}, u32[]{:S(2)}, u32[]{:S(2)}) collective-permute-start(bf16[112,256]{1,0:T(8,128)(2,1)S(1)} %shard_map.77.own_ref), channel_id=1, source_target_pairs={{0,16},{4,20},{8,24},{12,28},{16,0},{20,4},{24,8},{28,12},{1,17},{... | collective-permute-start | bytes 172040 | tf_op jit(solution)/shard_map/ppermute | solution.py:429
  97.5 6.0 %collective-permute-start.14 = (bf16[112,256]{1,0:T(8,128)(2,1)S(1)}, bf16[112,256]{1,0:T(8,128)(2,1)S(1)}, u32[]{:S(2)}, u32[]{:S(2)}) collective-permute-start(bf16[112,256]{1,0:T(8,128)(2,1)S(1)} %shard_map.77.own_ref), channel_id=1, source_target_pairs={{0,24},{4,28},{8,16},{12,20},{16,8},{20,12},{24,0},{28,4},{1,25},{... | collective-permute-start | bytes 172040 | tf_op jit(solution)/shard_map/ppermute | solution.py:429
  104.0 6.1 %collective-permute-start.15 = (bf16[448,256]{1,0:T(8,128)(2,1)S(1)}, bf16[448,256]{1,0:T(8,128)(2,1)S(1)}, u32[]{:S(2)}, u32[]{:S(2)}) collective-permute-start(bf16[448,256]{1,0:T(8,128)(2,1)S(1)} %shard_map.78.refs_0_), channel_id=1, source_target_pairs={{0,4},{4,0},{8,12},{12,8},{16,20},{20,16},{24,28},{28,24},{1,5},{5... | collective-permute-start | bytes 688136 | tf_op jit(solution)/shard_map/ppermute | solution.py:429
  104.3 6.9 %collective-permute-start.19 = (bf16[448,256]{1,0:T(8,128)(2,1)S(1)}, bf16[448,256]{1,0:T(8,128)(2,1)S(1)}, u32[]{:S(2)}, u32[]{:S(2)}) collective-permute-start(bf16[448,256]{1,0:T(8,128)(2,1)S(1)} %shard_map.78.refs_0_), channel_id=1, source_target_pairs={{0,2},{1,3},{2,0},{3,1},{4,6},{5,7},{6,4},{7,5},{8,10},{9,11},{10,... | collective-permute-start | bytes 688136 | tf_op jit(solution)/shard_map/ppermute | solution.py:429
  110.1 6.0 %collective-permute-start.20 = (bf16[448,256]{1,0:T(8,128)(2,1)S(1)}, bf16[448,256]{1,0:T(8,128)(2,1)S(1)}, u32[]{:S(2)}, u32[]{:S(2)}) collective-permute-start(bf16[448,256]{1,0:T(8,128)(2,1)S(1)} %collective-permute-done.15.refs_1_), channel_id=1, source_target_pairs={{0,2},{1,3},{2,0},{3,1},{4,6},{5,7},{6,4},{7,5},{8,10},{9,11},{10,... | collective-permute-start | bytes 688136 | tf_op jit(solution)/shard_map/ppermute | solution.py:429
  110.6 5.6 %collective-permute-start.17 = (bf16[448,256]{1,0:T(8,128)(2,1)S(1)}, bf16[448,256]{1,0:T(8,128)(2,1)S(1)}, u32[]{:S(2)}, u32[]{:S(2)}) collective-permute-start(bf16[448,256]{1,0:T(8,128)(2,1)S(1)} %shard_map.78.refs_0_), channel_id=1, source_target_pairs={{0,1},{1,0},{2,3},{3,2},{4,5},{5,4},{6,7},{7,6},{8,9},{9,8},{10,11... | collective-permute-start | bytes 688136 | tf_op jit(solution)/shard_map/ppermute | solution.py:429
  110.7 5.6 %collective-permute-start.18 = (bf16[448,256]{1,0:T(8,128)(2,1)S(1)}, bf16[448,256]{1,0:T(8,128)(2,1)S(1)}, u32[]{:S(2)}, u32[]{:S(2)}) collective-permute-start(bf16[448,256]{1,0:T(8,128)(2,1)S(1)} %collective-permute-done.15.refs_1_), channel_id=1, source_target_pairs={{0,1},{1,0},{2,3},{3,2},{4,5},{5,4},{6,7},{7,6},{8,9},{9,8},{10,11... | collective-permute-start | bytes 688136 | tf_op jit(solution)/shard_map/ppermute | solution.py:429
  111.2 5.1 %collective-permute-start.22 = (bf16[448,256]{1,0:T(8,128)(2,1)S(1)}, bf16[448,256]{1,0:T(8,128)(2,1)S(1)}, u32[]{:S(2)}, u32[]{:S(2)}) collective-permute-start(bf16[448,256]{1,0:T(8,128)(2,1)S(1)} %collective-permute-done.19.refs_4_), channel_id=1, source_target_pairs={{0,1},{1,0},{2,3},{3,2},{4,5},{5,4},{6,7},{7,6},{8,9},{9,8},{10,11... | collective-permute-start | bytes 688136 | tf_op jit(solution)/shard_map/ppermute | solution.py:429
  116.1 1.5 %collective-permute-start.23 = (bf16[448,256]{1,0:T(8,128)(2,1)S(1)}, bf16[448,256]{1,0:T(8,128)(2,1)S(1)}, u32[]{:S(2)}, u32[]{:S(2)}) collective-permute-start(bf16[448,256]{1,0:T(8,128)(2,1)S(1)} %collective-permute-done.20.refs_5_), channel_id=1, source_target_pairs={{0,1},{1,0},{2,3},{3,2},{4,5},{5,4},{6,7},{7,6},{8,9},{9,8},{10,11... | collective-permute-start | bytes 688136 | tf_op jit(solution)/shard_map/ppermute | solution.py:429

commit v12 on v11

--- a/solution.py
+++ b/solution.py
@@ -482,18 +482,19 @@
         out_ref[pl.ds(pl.multiple_of(jnp.bitwise_xor(mine, j) * n, 16), n)] = ref[...]
 
 
-def far_gram_kernel(scale, bits_ref, place_ref, w_ref, first_ref, second_ref, far_ref, near_ref, keep_ref, *refs):
+def far_gram_kernel(scale, bits_ref, place_ref, *refs):
+    *pair_refs, far_ref, near_ref, keep_ref = refs[:7]
+    refs = refs[7:]
     *give_refs, out_ref = refs
-    width = w_ref.shape[2]
+    n, width = pair_refs[0].shape
     near = near_ref.shape[0]
-    side, core = place_ref[0], place_ref[1]
+    core = place_ref[1]
     out_ref[:near] = near_ref[...]
     far = far_ref[...]
-    mine = pl.multiple_of(near + core * width, width // 2)
-    other = pl.multiple_of(near + (1 - core) * width, width // 2)
-    out_ref[pl.ds(mine, width)] = tmul(w_ref[side], far) * scale
-    n = first_ref.shape[0]
-    out_ref[pl.ds(other, width)] = (tmul(first_ref[...], far[:n]) + tmul(second_ref[...], far[n:])) * scale
+    for i, at in enumerate((core, 1 - core)):
+        first_ref, second_ref = pair_refs[2 * i : 2 * i + 2]
+        block = (tmul(first_ref[...], far[:n]) + tmul(second_ref[...], far[n:])) * scale
+        out_ref[pl.ds(pl.multiple_of(near + at * width, width // 2), width)] = block
     part_ways(out_ref, bits_ref[0], keep_ref, give_refs)
 
 
@@ -600,12 +601,12 @@
 
     keep, *gives = pl.pallas_call(
         functools.partial(far_gram_kernel, scale),
-        in_specs=[smem] * 2 + [vmem] * 5,
+        in_specs=[smem] * 2 + [vmem] * 6,
         out_shape=parts_of(count, 2),
         scratch_shapes=[pltpu.VMEM((count, width), F32)],
         compiler_params=params(),
         cost_estimate=pl.CostEstimate(flops=8 * slab * width * width, bytes_accessed=4 << 20, transcendentals=0),
-    )(bits, jnp.stack([side, core]), w_own, *w_other, far, near)
+    )(bits, jnp.stack([side, core]), *w_side, *w_other, far, near)
     row0 = cut1 = None
     for i, (base, ways) in enumerate(groups):
         if i == 0:
@@ -626,7 +627,6 @@
         if i == 0:
             outs[-1], row0, cut1 = lax.optimization_barrier((outs[-1], row0, cut1))
         if last:
-            outs[-1], row2 = lax.optimization_barrier((outs[-1], row2))
             share = outs[0]
         else:
             keep, *gives = outs
@@ -640,6 +640,7 @@
             compiler_params=params(),
             cost_estimate=little,
         )(bits, share, *gots)
+    share, row2 = lax.optimization_barrier((share, row2))
     row1 = swap(cut1, "orb", 1)
     got = swap(share, "dom", 1)
     got, row3 = lax.optimization_barrier((got, row3))

time: 123 us -> 122 us (level)
  waiting for transfers between devices: 37.5 us -> 35.2 us
  local copies, waits for them, and re-layouts: 6.74 us -> 8.76 us
    ppermute x21, waiting for transfers between devices: 29.3 us -> 27.1 us  [swap(): lax.ppermute(block, axis, [(i, i ^ bit) for i in range(lax.axis_size(axis...]
    unnamed x17 -> x19, local copies, waits for them, and re-layouts: 5.94 us -> 7.96 us
  transfers between devices with their start and end apart: 24 -> 24, of which waited for: 12 -> 14; matrix products, arithmetic and copies ran while one was open for 3% -> 3% of each run, Pallas kernels for 17% -> 17%
where the time goes in v12:
time: 122 us
  Pallas kernels  51.1 us (42%)
  waiting for transfers between devices  35.2 us (29%)
  starting transfers between devices  25.1 us (21%)
  local copies, waits for them, and re-layouts  8.76 us (7%)
    ppermute x21, waiting for transfers between devices, swap(): lax.ppermute(block, axis, [(i, i ^ bit) for i in range(lax.axis_size(axis...  27.1 us
    pallas_call x1, Pallas kernels, body(): pl.pallas_call(functools.partial(free_kernel, fp, ip), in_specs=[vmem] *...  17.8 us
    ppermute x21, starting transfers between devices, swap(): lax.ppermute(block, axis, [(i, i ^ bit) for i in range(lax.axis_size(axis...  17.7 us
    pallas_call x2, Pallas kernels, back(): pl.pallas_call(back_pair_kernel, grid=(1,), in_specs=[smem, whole(1, tota...  8.47 us
    ppermute x3, waiting for transfers between devices, shift(): lax.ppermute(block, axis, [(i, i + distance) for i in range(n) if 0 <= i...  8.11 us
    unnamed x19, local copies, waits for them, and re-layouts  7.96 us
    pallas_call x1, Pallas kernels, body(): pl.pallas_call(functools.partial(forced_kernel, fp), in_specs=[pl.BlockSp...  7.52 us
    ppermute x3, starting transfers between devices, shift(): lax.ppermute(block, axis, [(i, i + distance) for i in range(n) if 0 <= i...  7.4 us
  transfers between devices with their start and end apart: 24, of which 14 were waited for; matrix products, arithmetic and copies ran while one was open for 3% of the time, Pallas kernels for 17%

profile of v12, /device:TPU:0, one launch (start us, length us, event | category | flops | bytes accessed | tf_op | source)
XLA Modules:
  0.0 121.6 jit_solution(2707452284005939400)
XLA Ops:
  0.6 0.7 reshape.15.pot_ref.potraw_ref
  1.3 1.3 %copy-done.2 = bf16[2352,256]{1,0:T(8,128)(2,1)S(1)} copy-done((bf16[2352,256]{1,0:T(8,128)(2,1)S(1)}, bf16[2352,256]{1,0:T(8,128)(2,1)}, u32[]{:S(2)}) %copy-start.2) | copy-done | bytes 1204248
  2.6 0.7 copy-done.5
  3.3 0.5 shard_map.68
  3.8 0.0 copy-start.6
  3.8 1.3 %collective-permute-start = (bf16[80,256]{1,0:T(8,128)(2,1)S(1)}, bf16[80,256]{1,0:T(8,128)(2,1)S(1)}, u32[]{:S(2)}, u32[]{:S(2)}) collective-permute-start(bf16[80,256]{1,0:T(8,128)(2,1)S(1)} %shard_map.68), channel_id=1, source_target_pairs={{4,0},{8,4},{12,8},{16,12},{20,16},{24,20},{28,24},{5,1},{9,5},{13... | collective-permute-start | bytes 122888 | tf_op jit(solution)/shard_map/ppermute | solution.py:434
  5.1 3.2 %copy.7.hraw_ref = bf16[8,343,343]{2,1,0:T(8,128)(2,1)} copy(bf16[8,343,343]{2,0,1:T(8,128)(2,1)} %param.7) | data formatting | bytes 3764768 | tf_op args[2]
  8.3 2.3 %collective-permute-done.ghost_ref = bf16[80,256]{1,0:T(8,128)(2,1)S(1)} collective-permute-done((bf16[80,256]{1,0:T(8,128)(2,1)S(1)}, bf16[80,256]{1,0:T(8,128)(2,1)S(1)}, u32[]{:S(2)}, u32[]{:S(2)}) %collective-permute-start) | collective-permute-done | bytes 40992 | tf_op jit(solution)/shard_map/ppermute | solution.py:434
  10.6 17.8 %shard_map.69 = (bf16[8,384,384]{2,1,0:T(8,128)(2,1)}, bf16[2560,256]{1,0:T(8,128)(2,1)S(1)}, f32[2560,128]{1,0:T(8,128)}, f32[8,1,320]{2,1,0:T(1,128)S(1)}, bf1...) custom-call(s32[8,343]{1,0:T(8,128)S(1)} %copy-done.6, ...), custom_call_target="tpu_custom_call" | custom-call | flops 2415919104 | bytes 8388608 | tf_op jit(solution)/shard_map/pallas_call | solution.py:695
  28.5 0.9 copy-done.7
  29.4 4.8 %collective-permute-start.1 = (bf16[6,64,256]{2,1,0:T(8,128)(2,1)S(1)}, bf16[6,64,256]{2,1,0:T(8,128)(2,1)S(1)}, u32[]{:S(2)}, u32[]{:S(2)}) collective-permute-start(bf16[6,64,256]{2,1,0:T(8,128)(2,1)S(1)} %get-tuple-element.48), channel_id=1, source_target_pairs={{0,4},{4,8},{8,12},{12,16},{16,20},{20,24},{24,28},{1,5},{5,9},{9,... | collective-permute-start | bytes 589832 | tf_op jit(solution)/shard_map/ppermute | solution.py:434
  34.2 1.3 %collective-permute-start.2 = (bf16[5,64,256]{2,1,0:T(8,128)(2,1)S(1)}, bf16[5,64,256]{2,1,0:T(8,128)(2,1)S(1)}, u32[]{:S(2)}, u32[]{:S(2)}) collective-permute-start(bf16[5,64,256]{2,1,0:T(8,128)(2,1)S(1)} %get-tuple-element.49), channel_id=1, source_target_pairs={{4,0},{8,4},{12,8},{16,12},{20,16},{24,20},{28,24},{5,1},{9,5},{13... | collective-permute-start | bytes 491528 | tf_op jit(solution)/shard_map/ppermute | solution.py:434
  35.5 0.1 pad_add_fusion.3.place_ref
  35.6 5.8 %collective-permute-done.2.fromright_ref = bf16[5,64,256]{2,1,0:T(8,128)(2,1)S(1)} collective-permute-done((bf16[5,64,256]{2,1,0:T(8,128)(2,1)S(1)}, bf16[5,64,256]{2,1,0:T(8,128)(2,1)S(1)}, u32[]{:S(2)}, u32[]{:S(2)}) %collective-permute-start.2) | collective-permute-done | bytes 163872 | tf_op jit(solution)/shard_map/ppermute | solution.py:434
  41.4 0.0 collective-permute-done.1.fromleft_ref
  41.4 1.1 copy-done.8
  42.6 7.5 %shard_map.70 = (bf16[2624,256]{1,0:T(8,128)(2,1)}, f32[64,256]{1,0:T(8,128)S(1)}, bf16[1344,256]{1,0:T(8,128)(2,1)S(1)}) custom-call(s32[2]{0:T(128)S(1)} %pad_add_fusion.3.place_ref, bf16[2560,256]{1,0:T(8,128)(2,1)S(1)} %get-tuple-element.45.v_ref, bf16[80,256]{1,0:T(8,128)(2,1)S(1)} %collective-permute-done.ghost_ref, ...), custom_call_target="tpu_custom_call" | custom-call | flops 2415919104 | bytes 8388608 | tf_op jit(solution)/shard_map/pallas_call | solution.py:727
  50.1 0.1 collective-permute-start.4
  50.2 1.6 %collective-permute-start.3 = (bf16[1344,256]{1,0:T(8,128)(2,1)S(1)}, bf16[1344,256]{1,0:T(8,128)(2,1)}, u32[]{:S(2)}, u32[]{:S(2)}) collective-permute-start(bf16[1344,256]{1,0:T(8,128)(2,1)S(1)} %get-tuple-element.56), channel_id=1, source_target_pairs={{0,2},{1,3},{2,0},{3,1},{4,6},{5,7},{6,4},{7,5},{8,10},{9,11},{10,... | collective-permute-start | bytes 2064392 | tf_op jit(solution)/shard_map/ppermute | solution.py:429
  51.7 4.5 %shard_map.71 = (bf16[2560,256]{1,0:T(8,128)(2,1)S(1)}, bf16[2,1344,256]{2,1,0:T(8,128)(2,1)}, bf16[672,256]{1,0:T(8,128)(2,1)}, bf16[672,256]{1,0:T(8,128)(2,1)}) custom-call(s32[2]{0:T(128)S(1)} %pad_add_fusion.3.place_ref, bf16[2624,256]{1,0:T(8,128)(2,1)} %get-tuple-element.73.x_ref, f32[64,256]{1,0:T(8,128)S(1)} %get-tuple-element.53.face_image_ref, ...), custom_call_target="tpu_custom_call" | custom-call | flops 1048576 | bytes 1024 | tf_op jit(solution)/shard_map/pallas_call | solution.py:746
  56.3 0.2 collective-permute-start.5
  56.4 0.3 collective-permute-start.6
  56.8 0.1 pad_add_fusion.4.at_ref
  56.9 0.1 pad_add_fusion.2.place_ref
  57.0 0.1 reshape.16.node_ref
  57.1 4.6 %shard_map.73 = (bf16[588,512]{1,0:T(8,128)(2,1)}, bf16[588,512]{1,0:T(8,128)(2,1)}) custom-call(s32[2]{0:T(128)S(1)} %pad_add_fusion.4.at_ref, f32[1,2560]{1,0:T(1,128)S(1)} %reshape.16.node_ref, bf16[2624,256]{1,0:T(8,128)(2,1)S(1)} %copy-done, bf16[2560,256]{1,0:T(8,128)(2,1)S(1)} %get-tuple-element.74.image_ref), custom_call_target="tpu_custom_call" | custom-call | flops 1048576 | bytes 1024 | tf_op jit(solution)/shard_map/pallas_call | solution.py:567
  61.7 0.0 collective-permute-done.4.other_ref
  61.7 3.0 %shard_map.72.refs_5_ = f32[384,256]{1,0:T(8,128)S(1)} custom-call(s32[1]{0:T(128)} %bitcast.4.core_ref, bf16[2624,256]{1,0:T(8,128)(2,1)S(1)} %copy-done, bf16[2,1344,256]{2,1,0:T(8,128)(2,1)} %get-tuple-element.57.w_ref, bf16[2624,256]{1,0:T(8,128)(2,1)} %collective-permute-done.4.other_ref), custom_call_target="tpu_custom_call" | custom-call | flops 1048576 | bytes 1024 | tf_op jit(solution)/shard_map/pallas_call | solution.py:581
  64.7 0.0 collective-permute-done.6.refs_3_
  64.7 3.4 %collective-permute-done.3.refs_4_ = bf16[1344,256]{1,0:T(8,128)(2,1)} collective-permute-done((bf16[1344,256]{1,0:T(8,128)(2,1)S(1)}, bf16[1344,256]{1,0:T(8,128)(2,1)}, u32[]{:S(2)}, u32[]{:S(2)}) %collective-permute-start.3) | collective-permute-done | bytes 688160 | tf_op jit(solution)/shard_map/ppermute | solution.py:429
  68.1 1.5 %collective-permute-start.14 = (bf16[588,512]{1,0:T(8,128)(2,1)}, bf16[588,512]{1,0:T(8,128)(2,1)S(1)}, u32[]{:S(2)}, u32[]{:S(2)}) collective-permute-start(bf16[588,512]{1,0:T(8,128)(2,1)} %get-tuple-element.78), channel_id=1, source_target_pairs={{0,2},{1,3},{2,0},{3,1},{4,6},{5,7},{6,4},{7,5},{8,10},{9,11},{10,... | collective-permute-start | bytes 1806344 | tf_op jit(solution)/shard_map/ppermute | solution.py:429
  69.6 0.1 pad_add_fusion.1.bits_ref
  69.7 2.9 %shard_map.74 = (f32[448,256]{1,0:T(8,128)S(1)}, bf16[448,256]{1,0:T(8,128)(2,1)}) custom-call(s32[2]{0:T(128)S(1)} %pad_add_fusion.1.bits_ref, s32[2]{0:T(128)S(1)} %pad_add_fusion.2.place_ref, bf16[672,256]{1,0:T(8,128)(2,1)} %get-tuple-element.54.refs_0_, bf16[672,256]{1,0:T(8,128)(2,1)} %get-tuple-element.55.refs_1_, ...), custom_call_target="tpu_custom_call" | custom-call | flops 704643072 | bytes 4194304 | tf_op jit(solution)/shard_map/pallas_call | solution.py:602
  72.6 0.8 copy-done.3
  73.4 2.2 %collective-permute-start.7 = (bf16[448,256]{1,0:T(8,128)(2,1)}, bf16[448,256]{1,0:T(8,128)(2,1)S(1)}, u32[]{:S(2)}, u32[]{:S(2)}) collective-permute-start(bf16[448,256]{1,0:T(8,128)(2,1)} %get-tuple-element.68), channel_id=1, source_target_pairs={{0,4},{4,0},{8,12},{12,8},{16,20},{20,16},{24,28},{28,24},{1,5},{5... | collective-permute-start | bytes 688136 | tf_op jit(solution)/shard_map/ppermute | solution.py:429
  75.6 0.0 collective-permute-start.16
  75.6 0.1 pad_add_fusion.5.at_ref
  75.7 3.8 %shard_map.76 = (bf16[588,512]{1,0:T(8,128)(2,1)S(1)}, bf16[588,512]{1,0:T(8,128)(2,1)S(1)}) custom-call(s32[2]{0:T(128)S(1)} %pad_add_fusion.5.at_ref, f32[1,2560]{1,0:T(1,128)S(1)} %reshape.16.node_ref, bf16[2624,256]{1,0:T(8,128)(2,1)S(1)} %copy-done, bf16[2560,256]{1,0:T(8,128)(2,1)S(1)} %get-tuple-element.74.image_ref), custom_call_target="tpu_custom_call" | custom-call | flops 1048576 | bytes 1024 | tf_op jit(solution)/shard_map/pallas_call | solution.py:567
  79.6 1.4 %collective-permute-done.7.refs_0_ = bf16[448,256]{1,0:T(8,128)(2,1)S(1)} collective-permute-done((bf16[448,256]{1,0:T(8,128)(2,1)}, bf16[448,256]{1,0:T(8,128)(2,1)S(1)}, u32[]{:S(2)}, u32[]{:S(2)}) %collective-permute-start.7) | collective-permute-done | bytes 229408 | tf_op jit(solution)/shard_map/ppermute | solution.py:429
  81.0 0.6 shard_map.75
  81.6 4.9 %collective-permute-start.10 = (bf16[112,256]{1,0:T(8,128)(2,1)S(1)}, bf16[112,256]{1,0:T(8,128)(2,1)S(1)}, u32[]{:S(2)}, u32[]{:S(2)}) collective-permute-start(bf16[112,256]{1,0:T(8,128)(2,1)S(1)} %get-tuple-element.77), channel_id=1, source_target_pairs={{0,24},{4,28},{8,16},{12,20},{16,8},{20,12},{24,0},{28,4},{1,25},{... | collective-permute-start | bytes 172040 | tf_op jit(solution)/shard_map/ppermute | solution.py:429
  86.6 0.6 collective-permute-start.9
  87.2 1.6 %collective-permute-done.10.refs_2_ = bf16[112,256]{1,0:T(8,128)(2,1)S(1)} collective-permute-done((bf16[112,256]{1,0:T(8,128)(2,1)S(1)}, bf16[112,256]{1,0:T(8,128)(2,1)S(1)}, u32[]{:S(2)}, u32[]{:S(2)}) %collective-permute-start.10) | collective-permute-done | bytes 57376 | tf_op jit(solution)/shard_map/ppermute | solution.py:429
  88.8 0.0 collective-permute-start.21
  88.8 1.9 %collective-permute-done.8.refs_0_ = bf16[112,256]{1,0:T(8,128)(2,1)S(1)} collective-permute-done((bf16[112,256]{1,0:T(8,128)(2,1)S(1)}, bf16[112,256]{1,0:T(8,128)(2,1)S(1)}, u32[]{:S(2)}, u32[]{:S(2)}) %collective-permute-start.8) | collective-permute-done | bytes 57376 | tf_op jit(solution)/shard_map/ppermute | solution.py:429
  90.7 0.9 collective-permute-done.9.refs_1_
  91.7 0.6 shard_map.77.own_ref
  92.2 2.1 %collective-permute-start.11 = (bf16[112,256]{1,0:T(8,128)(2,1)S(1)}, bf16[112,256]{1,0:T(8,128)(2,1)S(1)}, u32[]{:S(2)}, u32[]{:S(2)}) collective-permute-start(bf16[112,256]{1,0:T(8,128)(2,1)S(1)} %shard_map.77.own_ref), channel_id=1, source_target_pairs={{0,8},{4,12},{8,0},{12,4},{16,24},{20,28},{24,16},{28,20},{1,9},{5... | collective-permute-start | bytes 172040 | tf_op jit(solution)/shard_map/ppermute | solution.py:429
  94.3 0.1 collective-permute-start.12
  94.4 2.3 %collective-permute-done.11.refs_0_ = bf16[112,256]{1,0:T(8,128)(2,1)S(1)} collective-permute-done((bf16[112,256]{1,0:T(8,128)(2,1)S(1)}, bf16[112,256]{1,0:T(8,128)(2,1)S(1)}, u32[]{:S(2)}, u32[]{:S(2)}) %collective-permute-start.11) | collective-permute-done | bytes 57376 | tf_op jit(solution)/shard_map/ppermute | solution.py:429
  96.7 1.9 %collective-permute-start.13 = (bf16[112,256]{1,0:T(8,128)(2,1)S(1)}, bf16[112,256]{1,0:T(8,128)(2,1)S(1)}, u32[]{:S(2)}, u32[]{:S(2)}) collective-permute-start(bf16[112,256]{1,0:T(8,128)(2,1)S(1)} %shard_map.77.own_ref), channel_id=1, source_target_pairs={{0,24},{4,28},{8,16},{12,20},{16,8},{20,12},{24,0},{28,4},{1,25},{... | collective-permute-start | bytes 172040 | tf_op jit(solution)/shard_map/ppermute | solution.py:429
  98.5 1.4 %collective-permute-done.12.refs_1_ = bf16[112,256]{1,0:T(8,128)(2,1)S(1)} collective-permute-done((bf16[112,256]{1,0:T(8,128)(2,1)S(1)}, bf16[112,256]{1,0:T(8,128)(2,1)S(1)}, u32[]{:S(2)}, u32[]{:S(2)}) %collective-permute-start.12) | collective-permute-done | bytes 57376 | tf_op jit(solution)/shard_map/ppermute | solution.py:429
  99.9 2.8 %collective-permute-done.13.refs_2_ = bf16[112,256]{1,0:T(8,128)(2,1)S(1)} collective-permute-done((bf16[112,256]{1,0:T(8,128)(2,1)S(1)}, bf16[112,256]{1,0:T(8,128)(2,1)S(1)}, u32[]{:S(2)}, u32[]{:S(2)}) %collective-permute-start.13) | collective-permute-done | bytes 57376 | tf_op jit(solution)/shard_map/ppermute | solution.py:429
  102.7 0.6 shard_map.78.refs_0_
  103.3 0.2 collective-permute-start.15
  103.5 1.0 collective-permute-start.19
  104.5 4.9 %collective-permute-done.15.refs_1_ = bf16[448,256]{1,0:T(8,128)(2,1)S(1)} collective-permute-done((bf16[448,256]{1,0:T(8,128)(2,1)S(1)}, bf16[448,256]{1,0:T(8,128)(2,1)S(1)}, u32[]{:S(2)}, u32[]{:S(2)}) %collective-permute-start.15) | collective-permute-done | bytes 229408 | tf_op jit(solution)/shard_map/ppermute | solution.py:429
  109.4 0.5 collective-permute-start.20
  109.9 0.5 collective-permute-start.18
  110.4 1.5 %collective-permute-done.19.refs_4_ = bf16[448,256]{1,0:T(8,128)(2,1)S(1)} collective-permute-done((bf16[448,256]{1,0:T(8,128)(2,1)S(1)}, bf16[448,256]{1,0:T(8,128)(2,1)S(1)}, u32[]{:S(2)}, u32[]{:S(2)}) %collective-permute-start.19) | collective-permute-done | bytes 229408 | tf_op jit(solution)/shard_map/ppermute | solution.py:429
  111.9 3.5 %collective-permute-done.20.refs_5_ = bf16[448,256]{1,0:T(8,128)(2,1)S(1)} collective-permute-done((bf16[448,256]{1,0:T(8,128)(2,1)S(1)}, bf16[448,256]{1,0:T(8,128)(2,1)S(1)}, u32[]{:S(2)}, u32[]{:S(2)}) %collective-permute-start.20) | collective-permute-done | bytes 229408 | tf_op jit(solution)/shard_map/ppermute | solution.py:429
  115.4 0.1 pad_add_fusion.place_ref
  115.5 1.4 %collective-permute-done.23.refs_7_ = bf16[448,256]{1,0:T(8,128)(2,1)S(1)} collective-permute-done((bf16[448,256]{1,0:T(8,128)(2,1)S(1)}, bf16[448,256]{1,0:T(8,128)(2,1)S(1)}, u32[]{:S(2)}, u32[]{:S(2)}) %collective-permute-start.23) | collective-permute-done | bytes 229408 | tf_op jit(solution)/shard_map/ppermute | solution.py:429
  116.9 4.5 %shard_map.79 = (f32[588,1024]{1,0:T(8,128)}, bf16[1024,1024]{1,0:T(8,128)(2,1)}) custom-call(s32[2]{0:T(128)S(1)} %pad_add_fusion.place_ref, bf16[448,256]{1,0:T(8,128)(2,1)S(1)} %shard_map.78.refs_0_, bf16[448,256]{1,0:T(8,128)(2,1)S(1)} %collective-permute-done.15.refs_1_, bf16[448,256]{1,0:T(8,128)(2,1)S(1)} %collective-permute-done.17.refs_2_, ...), custom_call_target="tpu_custom_call" | custom-call | tf_op jit(solution)/shard_map/pallas_call | solution.py:653
  (24 shorter events, 0.1 us)
Async XLA Ops:
  1.3 1.3 %copy-start.2 = (bf16[2352,256]{1,0:T(8,128)(2,1)S(1)}, bf16[2352,256]{1,0:T(8,128)(2,1)}, u32[]{:S(2)}) copy-start(bf16[2352,256]{1,0:T(8,128)(2,1)} %raw_ref.1) | copy-start | bytes 3612676
  2.6 0.7 copy-start.5
  3.8 6.9 %copy-start.6 = (s32[8,343]{1,0:T(8,128)S(1)}, s32[8,343]{1,0:T(8,128)}, u32[]{:S(2)}) copy-start(s32[8,343]{1,0:T(8,128)} %conn_ref.1) | copy-start | bytes 32932
  3.8 6.8 %collective-permute-start = (bf16[80,256]{1,0:T(8,128)(2,1)S(1)}, bf16[80,256]{1,0:T(8,128)(2,1)S(1)}, u32[]{:S(2)}, u32[]{:S(2)}) collective-permute-start(bf16[80,256]{1,0:T(8,128)(2,1)S(1)} %shard_map.68), channel_id=1, source_target_pairs={{4,0},{8,4},{12,8},{16,12},{20,16},{24,20},{28,24},{5,1},{9,5},{13... | collective-permute-start | bytes 122888 | tf_op jit(solution)/shard_map/ppermute | solution.py:434
  28.5 0.9 copy-start.7
  29.4 12.0 %collective-permute-start.1 = (bf16[6,64,256]{2,1,0:T(8,128)(2,1)S(1)}, bf16[6,64,256]{2,1,0:T(8,128)(2,1)S(1)}, u32[]{:S(2)}, u32[]{:S(2)}) collective-permute-start(bf16[6,64,256]{2,1,0:T(8,128)(2,1)S(1)} %get-tuple-element.48), channel_id=1, source_target_pairs={{0,4},{4,8},{8,12},{12,16},{16,20},{20,24},{24,28},{1,5},{5,9},{9,... | collective-permute-start | bytes 589832 | tf_op jit(solution)/shard_map/ppermute | solution.py:434
  34.2 7.2 %collective-permute-start.2 = (bf16[5,64,256]{2,1,0:T(8,128)(2,1)S(1)}, bf16[5,64,256]{2,1,0:T(8,128)(2,1)S(1)}, u32[]{:S(2)}, u32[]{:S(2)}) collective-permute-start(bf16[5,64,256]{2,1,0:T(8,128)(2,1)S(1)} %get-tuple-element.49), channel_id=1, source_target_pairs={{4,0},{8,4},{12,8},{16,12},{20,16},{24,20},{28,24},{5,1},{9,5},{13... | collective-permute-start | bytes 491528 | tf_op jit(solution)/shard_map/ppermute | solution.py:434
  41.4 1.1 copy-start.8
  42.6 9.2 %copy-start.1 = (f32[2560,128]{1,0:T(8,128)S(1)}, f32[2560,128]{1,0:T(8,128)}, u32[]{:S(2)}) copy-start(f32[2560,128]{1,0:T(8,128)} %get-tuple-element.51.pot_hbm.pot_ref) | copy-start | bytes 3932164
  50.1 11.6 %collective-permute-start.4 = (bf16[2624,256]{1,0:T(8,128)(2,1)}, bf16[2624,256]{1,0:T(8,128)(2,1)}, u32[]{:S(2)}, u32[]{:S(2)}) collective-permute-start(bf16[2624,256]{1,0:T(8,128)(2,1)} %get-tuple-element.73.x_ref), channel_id=1, source_target_pairs={{0,1},{1,0},{2,3},{3,2},{4,5},{5,4},{6,7},{7,6},{8,9},{9,8},{10,11... | collective-permute-start | bytes 4030472 | tf_op jit(solution)/shard_map/ppermute | solution.py:429
  50.2 18.0 %collective-permute-start.3 = (bf16[1344,256]{1,0:T(8,128)(2,1)S(1)}, bf16[1344,256]{1,0:T(8,128)(2,1)}, u32[]{:S(2)}, u32[]{:S(2)}) collective-permute-start(bf16[1344,256]{1,0:T(8,128)(2,1)S(1)} %get-tuple-element.56), channel_id=1, source_target_pairs={{0,2},{1,3},{2,0},{3,1},{4,6},{5,7},{6,4},{7,5},{8,10},{9,11},{10,... | collective-permute-start | bytes 2064392 | tf_op jit(solution)/shard_map/ppermute | solution.py:429
  51.7 5.3 %copy-start = (bf16[2624,256]{1,0:T(8,128)(2,1)S(1)}, bf16[2624,256]{1,0:T(8,128)(2,1)}, u32[]{:S(2)}) copy-start(bf16[2624,256]{1,0:T(8,128)(2,1)} %get-tuple-element.73.x_ref) | copy-start | bytes 4030468
  56.3 8.4 %collective-permute-start.5 = (bf16[672,256]{1,0:T(8,128)(2,1)}, bf16[672,256]{1,0:T(8,128)(2,1)}, u32[]{:S(2)}, u32[]{:S(2)}) collective-permute-start(bf16[672,256]{1,0:T(8,128)(2,1)} %get-tuple-element.54.refs_0_), channel_id=1, source_target_pairs={{0,1},{1,0},{2,3},{3,2},{4,5},{5,4},{6,7},{7,6},{8,9},{9,8},{10,11... | collective-permute-start | bytes 1032200 | tf_op jit(solution)/shard_map/ppermute | solution.py:429
  56.4 8.3 %collective-permute-start.6 = (bf16[672,256]{1,0:T(8,128)(2,1)}, bf16[672,256]{1,0:T(8,128)(2,1)}, u32[]{:S(2)}, u32[]{:S(2)}) collective-permute-start(bf16[672,256]{1,0:T(8,128)(2,1)} %get-tuple-element.55.refs_1_), channel_id=1, source_target_pairs={{0,1},{1,0},{2,3},{3,2},{4,5},{5,4},{6,7},{7,6},{8,9},{9,8},{10,11... | collective-permute-start | bytes 1032200 | tf_op jit(solution)/shard_map/ppermute | solution.py:429
  68.1 35.2 %collective-permute-start.14 = (bf16[588,512]{1,0:T(8,128)(2,1)}, bf16[588,512]{1,0:T(8,128)(2,1)S(1)}, u32[]{:S(2)}, u32[]{:S(2)}) collective-permute-start(bf16[588,512]{1,0:T(8,128)(2,1)} %get-tuple-element.78), channel_id=1, source_target_pairs={{0,2},{1,3},{2,0},{3,1},{4,6},{5,7},{6,4},{7,5},{8,10},{9,11},{10,... | collective-permute-start | bytes 1806344 | tf_op jit(solution)/shard_map/ppermute | solution.py:429
  72.6 0.8 copy-start.3
  73.4 7.6 %collective-permute-start.7 = (bf16[448,256]{1,0:T(8,128)(2,1)}, bf16[448,256]{1,0:T(8,128)(2,1)S(1)}, u32[]{:S(2)}, u32[]{:S(2)}) collective-permute-start(bf16[448,256]{1,0:T(8,128)(2,1)} %get-tuple-element.68), channel_id=1, source_target_pairs={{0,4},{4,0},{8,12},{12,8},{16,20},{20,16},{24,28},{28,24},{1,5},{5... | collective-permute-start | bytes 688136 | tf_op jit(solution)/shard_map/ppermute | solution.py:429
  75.6 28.9 %collective-permute-start.16 = (bf16[588,512]{1,0:T(8,128)(2,1)}, bf16[588,512]{1,0:T(8,128)(2,1)}, u32[]{:S(2)}, u32[]{:S(2)}) collective-permute-start(bf16[588,512]{1,0:T(8,128)(2,1)} %get-tuple-element.80), channel_id=1, source_target_pairs={{0,3},{1,2},{2,1},{3,0},{4,7},{5,6},{6,5},{7,4},{8,11},{9,10},{10,... | collective-permute-start | bytes 1806344 | tf_op jit(solution)/shard_map/ppermute | solution.py:429
  75.6 5.4 %copy-start.4 = (f32[448,256]{1,0:T(8,128)S(1)}, f32[448,256]{1,0:T(8,128)}, u32[]{:S(2)}) copy-start(f32[448,256]{1,0:T(8,128)} %copy-done.3) | copy-start | bytes 1376260
  81.6 7.2 %collective-permute-start.10 = (bf16[112,256]{1,0:T(8,128)(2,1)S(1)}, bf16[112,256]{1,0:T(8,128)(2,1)S(1)}, u32[]{:S(2)}, u32[]{:S(2)}) collective-permute-start(bf16[112,256]{1,0:T(8,128)(2,1)S(1)} %get-tuple-element.77), channel_id=1, source_target_pairs={{0,24},{4,28},{8,16},{12,20},{16,8},{20,12},{24,0},{28,4},{1,25},{... | collective-permute-start | bytes 172040 | tf_op jit(solution)/shard_map/ppermute | solution.py:429
  86.6 4.2 %collective-permute-start.8 = (bf16[112,256]{1,0:T(8,128)(2,1)S(1)}, bf16[112,256]{1,0:T(8,128)(2,1)S(1)}, u32[]{:S(2)}, u32[]{:S(2)}) collective-permute-start(bf16[112,256]{1,0:T(8,128)(2,1)S(1)} %get-tuple-element.70), channel_id=1, source_target_pairs={{0,8},{4,12},{8,0},{12,4},{16,24},{20,28},{24,16},{28,20},{1,9},{5... | collective-permute-start | bytes 172040 | tf_op jit(solution)/shard_map/ppermute | solution.py:429
  86.6 5.1 %collective-permute-start.9 = (bf16[112,256]{1,0:T(8,128)(2,1)S(1)}, bf16[112,256]{1,0:T(8,128)(2,1)S(1)}, u32[]{:S(2)}, u32[]{:S(2)}) collective-permute-start(bf16[112,256]{1,0:T(8,128)(2,1)S(1)} %get-tuple-element.71), channel_id=1, source_target_pairs={{0,16},{4,20},{8,24},{12,28},{16,0},{20,4},{24,8},{28,12},{1,17},{... | collective-permute-start | bytes 172040 | tf_op jit(solution)/shard_map/ppermute | solution.py:429
  88.8 23.1 %collective-permute-start.21 = (bf16[588,512]{1,0:T(8,128)(2,1)S(1)}, bf16[588,512]{1,0:T(8,128)(2,1)S(1)}, u32[]{:S(2)}, u32[]{:S(2)}) collective-permute-start(bf16[588,512]{1,0:T(8,128)(2,1)S(1)} %get-tuple-element.82), channel_id=1, source_target_pairs={{0,1},{1,0},{2,3},{3,2},{4,5},{5,4},{6,7},{7,6},{8,9},{9,8},{10,11... | collective-permute-start | bytes 1806344 | tf_op jit(solution)/shard_map/ppermute | solution.py:429
  92.2 4.4 %collective-permute-start.11 = (bf16[112,256]{1,0:T(8,128)(2,1)S(1)}, bf16[112,256]{1,0:T(8,128)(2,1)S(1)}, u32[]{:S(2)}, u32[]{:S(2)}) collective-permute-start(bf16[112,256]{1,0:T(8,128)(2,1)S(1)} %shard_map.77.own_ref), channel_id=1, source_target_pairs={{0,8},{4,12},{8,0},{12,4},{16,24},{20,28},{24,16},{28,20},{1,9},{5... | collective-permute-start | bytes 172040 | tf_op jit(solution)/shard_map/ppermute | solution.py:429
  94.3 5.6 %collective-permute-start.12 = (bf16[112,256]{1,0:T(8,128)(2,1)S(1)}, bf16[112,256]{1,0:T(8,128)(2,1)S(1)}, u32[]{:S(2)}, u32[]{:S(2)}) collective-permute-start(bf16[112,256]{1,0:T(8,128)(2,1)S(1)} %shard_map.77.own_ref), channel_id=1, source_target_pairs={{0,16},{4,20},{8,24},{12,28},{16,0},{20,4},{24,8},{28,12},{1,17},{... | collective-permute-start | bytes 172040 | tf_op jit(solution)/shard_map/ppermute | solution.py:429
  96.7 6.1 %collective-permute-start.13 = (bf16[112,256]{1,0:T(8,128)(2,1)S(1)}, bf16[112,256]{1,0:T(8,128)(2,1)S(1)}, u32[]{:S(2)}, u32[]{:S(2)}) collective-permute-start(bf16[112,256]{1,0:T(8,128)(2,1)S(1)} %shard_map.77.own_ref), channel_id=1, source_target_pairs={{0,24},{4,28},{8,16},{12,20},{16,8},{20,12},{24,0},{28,4},{1,25},{... | collective-permute-start | bytes 172040 | tf_op jit(solution)/shard_map/ppermute | solution.py:429
  103.3 6.1 %collective-permute-start.15 = (bf16[448,256]{1,0:T(8,128)(2,1)S(1)}, bf16[448,256]{1,0:T(8,128)(2,1)S(1)}, u32[]{:S(2)}, u32[]{:S(2)}) collective-permute-start(bf16[448,256]{1,0:T(8,128)(2,1)S(1)} %shard_map.78.refs_0_), channel_id=1, source_target_pairs={{0,4},{4,0},{8,12},{12,8},{16,20},{20,16},{24,28},{28,24},{1,5},{5... | collective-permute-start | bytes 688136 | tf_op jit(solution)/shard_map/ppermute | solution.py:429
  103.5 8.4 %collective-permute-start.19 = (bf16[448,256]{1,0:T(8,128)(2,1)S(1)}, bf16[448,256]{1,0:T(8,128)(2,1)S(1)}, u32[]{:S(2)}, u32[]{:S(2)}) collective-permute-start(bf16[448,256]{1,0:T(8,128)(2,1)S(1)} %shard_map.78.refs_0_), channel_id=1, source_target_pairs={{0,2},{1,3},{2,0},{3,1},{4,6},{5,7},{6,4},{7,5},{8,10},{9,11},{10,... | collective-permute-start | bytes 688136 | tf_op jit(solution)/shard_map/ppermute | solution.py:429
  109.4 6.0 %collective-permute-start.20 = (bf16[448,256]{1,0:T(8,128)(2,1)S(1)}, bf16[448,256]{1,0:T(8,128)(2,1)S(1)}, u32[]{:S(2)}, u32[]{:S(2)}) collective-permute-start(bf16[448,256]{1,0:T(8,128)(2,1)S(1)} %collective-permute-done.15.refs_1_), channel_id=1, source_target_pairs={{0,2},{1,3},{2,0},{3,1},{4,6},{5,7},{6,4},{7,5},{8,10},{9,11},{10,... | collective-permute-start | bytes 688136 | tf_op jit(solution)/shard_map/ppermute | solution.py:429
  109.9 5.6 %collective-permute-start.17 = (bf16[448,256]{1,0:T(8,128)(2,1)S(1)}, bf16[448,256]{1,0:T(8,128)(2,1)S(1)}, u32[]{:S(2)}, u32[]{:S(2)}) collective-permute-start(bf16[448,256]{1,0:T(8,128)(2,1)S(1)} %shard_map.78.refs_0_), channel_id=1, source_target_pairs={{0,1},{1,0},{2,3},{3,2},{4,5},{5,4},{6,7},{7,6},{8,9},{9,8},{10,11... | collective-permute-start | bytes 688136 | tf_op jit(solution)/shard_map/ppermute | solution.py:429
  109.9 5.6 %collective-permute-start.18 = (bf16[448,256]{1,0:T(8,128)(2,1)S(1)}, bf16[448,256]{1,0:T(8,128)(2,1)S(1)}, u32[]{:S(2)}, u32[]{:S(2)}) collective-permute-start(bf16[448,256]{1,0:T(8,128)(2,1)S(1)} %collective-permute-done.15.refs_1_), channel_id=1, source_target_pairs={{0,1},{1,0},{2,3},{3,2},{4,5},{5,4},{6,7},{7,6},{8,9},{9,8},{10,11... | collective-permute-start | bytes 688136 | tf_op jit(solution)/shard_map/ppermute | solution.py:429
  111.9 3.6 %collective-permute-start.22 = (bf16[448,256]{1,0:T(8,128)(2,1)S(1)}, bf16[448,256]{1,0:T(8,128)(2,1)S(1)}, u32[]{:S(2)}, u32[]{:S(2)}) collective-permute-start(bf16[448,256]{1,0:T(8,128)(2,1)S(1)} %collective-permute-done.19.refs_4_), channel_id=1, source_target_pairs={{0,1},{1,0},{2,3},{3,2},{4,5},{5,4},{6,7},{7,6},{8,9},{9,8},{10,11... | collective-permute-start | bytes 688136 | tf_op jit(solution)/shard_map/ppermute | solution.py:429
  115.4 1.5 %collective-permute-start.23 = (bf16[448,256]{1,0:T(8,128)(2,1)S(1)}, bf16[448,256]{1,0:T(8,128)(2,1)S(1)}, u32[]{:S(2)}, u32[]{:S(2)}) collective-permute-start(bf16[448,256]{1,0:T(8,128)(2,1)S(1)} %collective-permute-done.20.refs_5_), channel_id=1, source_target_pairs={{0,1},{1,0},{2,3},{3,2},{4,5},{5,4},{6,7},{7,6},{8,9},{9,8},{10,11... | collective-permute-start | bytes 688136 | tf_op jit(solution)/shard_map/ppermute | solution.py:429

commit v13 on v12

--- a/solution.py
+++ b/solution.py
@@ -647,7 +647,6 @@
     q2 = [swap(share, "orb", 2), swap(got, "orb", 2)]
     q1 = [swap(share, "orb", 1), swap(got, "orb", 1)]
     q3a = swap(q2[0], "orb", 1)
-    q2[1], row1 = lax.optimization_barrier((q2[1], row1))
     q3 = [q3a, swap(q2[1], "orb", 1)]
     cols = orb * width
     return pl.pallas_call(

time: 122 us -> 123 us (level)
  starting transfers between devices: 25.1 us -> 27.5 us
    ppermute x21, starting transfers between devices: 17.7 us -> 20.1 us  [swap(): lax.ppermute(block, axis, [(i, i ^ bit) for i in range(lax.axis_size(axis...]
where the time goes in v13:
time: 123 us
  Pallas kernels  51.1 us (42%)
  waiting for transfers between devices  34.2 us (28%)
  starting transfers between devices  27.5 us (22%)
  local copies, waits for them, and re-layouts  8.63 us (7%)
    ppermute x21, waiting for transfers between devices, swap(): lax.ppermute(block, axis, [(i, i ^ bit) for i in range(lax.axis_size(axis...  26 us
    ppermute x21, starting transfers between devices, swap(): lax.ppermute(block, axis, [(i, i ^ bit) for i in range(lax.axis_size(axis...  20.1 us
    pallas_call x1, Pallas kernels, body(): pl.pallas_call(functools.partial(free_kernel, fp, ip), in_specs=[vmem] *...  17.8 us
    pallas_call x2, Pallas kernels, back(): pl.pallas_call(back_pair_kernel, grid=(1,), in_specs=[smem, whole(1, tota...  8.48 us
    ppermute x3, waiting for transfers between devices, shift(): lax.ppermute(block, axis, [(i, i + distance) for i in range(n) if 0 <= i...  8.17 us
    unnamed x19, local copies, waits for them, and re-layouts  7.84 us
    pallas_call x1, Pallas kernels, body(): pl.pallas_call(functools.partial(forced_kernel, fp), in_specs=[pl.BlockSp...  7.74 us
    ppermute x3, starting transfers between devices, shift(): lax.ppermute(block, axis, [(i, i + distance) for i in range(n) if 0 <= i...  7.42 us
  transfers between devices with their start and end apart: 24, of which 14 were waited for; matrix products, arithmetic and copies ran while one was open for 3% of the time, Pallas kernels for 17%

profile of v13, /device:TPU:0, one launch (start us, length us, event | category | flops | bytes accessed | tf_op | source)
XLA Modules:
  0.0 122.9 jit_solution(16823525009234959844)
XLA Ops:
  0.6 0.7 reshape.15.pot_ref.potraw_ref
  1.3 1.3 %copy-done.2 = bf16[2352,256]{1,0:T(8,128)(2,1)S(1)} copy-done((bf16[2352,256]{1,0:T(8,128)(2,1)S(1)}, bf16[2352,256]{1,0:T(8,128)(2,1)}, u32[]{:S(2)}) %copy-start.2) | copy-done | bytes 1204248
  2.6 0.7 copy-done.5
  3.3 0.5 shard_map.68
  3.8 0.0 copy-start.8
  3.8 1.3 %collective-permute-start = (bf16[80,256]{1,0:T(8,128)(2,1)S(1)}, bf16[80,256]{1,0:T(8,128)(2,1)S(1)}, u32[]{:S(2)}, u32[]{:S(2)}) collective-permute-start(bf16[80,256]{1,0:T(8,128)(2,1)S(1)} %shard_map.68), channel_id=1, source_target_pairs={{4,0},{8,4},{12,8},{16,12},{20,16},{24,20},{28,24},{5,1},{9,5},{13... | collective-permute-start | bytes 122888 | tf_op jit(solution)/shard_map/ppermute | solution.py:434
  5.1 3.2 %copy.7.hraw_ref = bf16[8,343,343]{2,1,0:T(8,128)(2,1)} copy(bf16[8,343,343]{2,0,1:T(8,128)(2,1)} %param.7) | data formatting | bytes 3764768 | tf_op args[2]
  8.3 2.4 %collective-permute-done.ghost_ref = bf16[80,256]{1,0:T(8,128)(2,1)S(1)} collective-permute-done((bf16[80,256]{1,0:T(8,128)(2,1)S(1)}, bf16[80,256]{1,0:T(8,128)(2,1)S(1)}, u32[]{:S(2)}, u32[]{:S(2)}) %collective-permute-start) | collective-permute-done | bytes 40992 | tf_op jit(solution)/shard_map/ppermute | solution.py:434
  10.6 17.8 %shard_map.69 = (bf16[8,384,384]{2,1,0:T(8,128)(2,1)}, bf16[2560,256]{1,0:T(8,128)(2,1)S(1)}, f32[2560,128]{1,0:T(8,128)}, f32[8,1,320]{2,1,0:T(1,128)S(1)}, bf1...) custom-call(s32[8,343]{1,0:T(8,128)S(1)} %copy-done.8, ...), custom_call_target="tpu_custom_call" | custom-call | flops 2415919104 | bytes 8388608 | tf_op jit(solution)/shard_map/pallas_call | solution.py:694
  28.5 4.8 %collective-permute-start.1 = (bf16[6,64,256]{2,1,0:T(8,128)(2,1)S(1)}, bf16[6,64,256]{2,1,0:T(8,128)(2,1)S(1)}, u32[]{:S(2)}, u32[]{:S(2)}) collective-permute-start(bf16[6,64,256]{2,1,0:T(8,128)(2,1)S(1)} %get-tuple-element.46), channel_id=1, source_target_pairs={{0,4},{4,8},{8,12},{12,16},{16,20},{20,24},{24,28},{1,5},{5,9},{9,... | collective-permute-start | bytes 589832 | tf_op jit(solution)/shard_map/ppermute | solution.py:434
  33.3 1.3 %collective-permute-start.2 = (bf16[5,64,256]{2,1,0:T(8,128)(2,1)S(1)}, bf16[5,64,256]{2,1,0:T(8,128)(2,1)S(1)}, u32[]{:S(2)}, u32[]{:S(2)}) collective-permute-start(bf16[5,64,256]{2,1,0:T(8,128)(2,1)S(1)} %get-tuple-element.47), channel_id=1, source_target_pairs={{4,0},{8,4},{12,8},{16,12},{20,16},{24,20},{28,24},{5,1},{9,5},{13... | collective-permute-start | bytes 491528 | tf_op jit(solution)/shard_map/ppermute | solution.py:434
  34.7 0.1 pad_add_fusion.3.place_ref
  34.7 5.8 %collective-permute-done.2.fromright_ref = bf16[5,64,256]{2,1,0:T(8,128)(2,1)S(1)} collective-permute-done((bf16[5,64,256]{2,1,0:T(8,128)(2,1)S(1)}, bf16[5,64,256]{2,1,0:T(8,128)(2,1)S(1)}, u32[]{:S(2)}, u32[]{:S(2)}) %collective-permute-start.2) | collective-permute-done | bytes 163872 | tf_op jit(solution)/shard_map/ppermute | solution.py:434
  40.6 0.0 collective-permute-done.1.fromleft_ref
  40.6 7.7 %shard_map.70 = (bf16[2624,256]{1,0:T(8,128)(2,1)}, f32[64,256]{1,0:T(8,128)S(1)}, bf16[1344,256]{1,0:T(8,128)(2,1)}) custom-call(s32[2]{0:T(128)S(1)} %pad_add_fusion.3.place_ref, bf16[2560,256]{1,0:T(8,128)(2,1)S(1)} %get-tuple-element.43.v_ref, bf16[80,256]{1,0:T(8,128)(2,1)S(1)} %collective-permute-done.ghost_ref, ...), custom_call_target="tpu_custom_call" | custom-call | flops 2415919104 | bytes 8388608 | tf_op jit(solution)/shard_map/pallas_call | solution.py:726
  48.3 0.1 collective-permute-start.4
  48.4 1.6 %collective-permute-start.3 = (bf16[1344,256]{1,0:T(8,128)(2,1)}, bf16[1344,256]{1,0:T(8,128)(2,1)S(1)}, u32[]{:S(2)}, u32[]{:S(2)}) collective-permute-start(bf16[1344,256]{1,0:T(8,128)(2,1)} %get-tuple-element.54), channel_id=1, source_target_pairs={{0,2},{1,3},{2,0},{3,1},{4,6},{5,7},{6,4},{7,5},{8,10},{9,11},{10,... | collective-permute-start | bytes 2064392 | tf_op jit(solution)/shard_map/ppermute | solution.py:429
  50.0 4.5 %shard_map.71 = (bf16[2560,256]{1,0:T(8,128)(2,1)S(1)}, bf16[2,1344,256]{2,1,0:T(8,128)(2,1)}, bf16[672,256]{1,0:T(8,128)(2,1)}, bf16[672,256]{1,0:T(8,128)(2,1)}) custom-call(s32[2]{0:T(128)S(1)} %pad_add_fusion.3.place_ref, bf16[2624,256]{1,0:T(8,128)(2,1)} %get-tuple-element.71.x_ref, f32[64,256]{1,0:T(8,128)S(1)} %get-tuple-element.51.face_image_ref, ...), custom_call_target="tpu_custom_call" | custom-call | flops 1048576 | bytes 1024 | tf_op jit(solution)/shard_map/pallas_call | solution.py:745
  54.5 0.2 collective-permute-start.5
  54.7 0.3 collective-permute-start.6
  55.0 0.1 pad_add_fusion.4.at_ref
  55.1 0.1 reshape.16.node_ref
  55.2 4.7 %shard_map.73 = (bf16[588,512]{1,0:T(8,128)(2,1)}, bf16[588,512]{1,0:T(8,128)(2,1)}) custom-call(s32[2]{0:T(128)S(1)} %pad_add_fusion.4.at_ref, f32[1,2560]{1,0:T(1,128)S(1)} %reshape.16.node_ref, bf16[2624,256]{1,0:T(8,128)(2,1)S(1)} %copy-done, bf16[2560,256]{1,0:T(8,128)(2,1)S(1)} %get-tuple-element.72.image_ref), custom_call_target="tpu_custom_call" | custom-call | flops 1048576 | bytes 1024 | tf_op jit(solution)/shard_map/pallas_call | solution.py:567
  59.9 0.0 collective-permute-done.4.other_ref
  59.9 3.0 %shard_map.72.refs_5_ = f32[384,256]{1,0:T(8,128)S(1)} custom-call(s32[1]{0:T(128)} %bitcast.4.core_ref, bf16[2624,256]{1,0:T(8,128)(2,1)S(1)} %copy-done, bf16[2,1344,256]{2,1,0:T(8,128)(2,1)} %get-tuple-element.55.w_ref, bf16[2624,256]{1,0:T(8,128)(2,1)} %collective-permute-done.4.other_ref), custom_call_target="tpu_custom_call" | custom-call | flops 1048576 | bytes 1024 | tf_op jit(solution)/shard_map/pallas_call | solution.py:581
  62.9 0.0 collective-permute-done.6.refs_3_
  62.9 3.6 %collective-permute-done.3.refs_4_ = bf16[1344,256]{1,0:T(8,128)(2,1)S(1)} collective-permute-done((bf16[1344,256]{1,0:T(8,128)(2,1)}, bf16[1344,256]{1,0:T(8,128)(2,1)S(1)}, u32[]{:S(2)}, u32[]{:S(2)}) %collective-permute-start.3) | collective-permute-done | bytes 688160 | tf_op jit(solution)/shard_map/ppermute | solution.py:429
  66.4 0.8 copy-done.6
  67.3 1.5 %collective-permute-start.14 = (bf16[588,512]{1,0:T(8,128)(2,1)}, bf16[588,512]{1,0:T(8,128)(2,1)S(1)}, u32[]{:S(2)}, u32[]{:S(2)}) collective-permute-start(bf16[588,512]{1,0:T(8,128)(2,1)} %get-tuple-element.76), channel_id=1, source_target_pairs={{0,2},{1,3},{2,0},{3,1},{4,6},{5,7},{6,4},{7,5},{8,10},{9,11},{10,... | collective-permute-start | bytes 1806344 | tf_op jit(solution)/shard_map/ppermute | solution.py:429
  68.8 0.1 pad_add_fusion.2.place_ref
  68.9 0.1 pad_add_fusion.1.bits_ref
  69.0 0.0 copy-start.7
  69.0 1.1 copy-done.7
  70.1 2.7 %shard_map.74 = (f32[448,256]{1,0:T(8,128)S(1)}, bf16[448,256]{1,0:T(8,128)(2,1)}) custom-call(s32[2]{0:T(128)S(1)} %pad_add_fusion.1.bits_ref, s32[2]{0:T(128)S(1)} %pad_add_fusion.2.place_ref, bf16[672,256]{1,0:T(8,128)(2,1)} %get-tuple-element.52.refs_0_, bf16[672,256]{1,0:T(8,128)(2,1)} %get-tuple-element.53.refs_1_, ...), custom_call_target="tpu_custom_call" | custom-call | flops 704643072 | bytes 4194304 | tf_op jit(solution)/shard_map/pallas_call | solution.py:602
  72.7 0.8 copy-done.3
  73.5 2.2 %collective-permute-start.7 = (bf16[448,256]{1,0:T(8,128)(2,1)}, bf16[448,256]{1,0:T(8,128)(2,1)S(1)}, u32[]{:S(2)}, u32[]{:S(2)}) collective-permute-start(bf16[448,256]{1,0:T(8,128)(2,1)} %get-tuple-element.66), channel_id=1, source_target_pairs={{0,4},{4,0},{8,12},{12,8},{16,20},{20,16},{24,28},{28,24},{1,5},{5... | collective-permute-start | bytes 688136 | tf_op jit(solution)/shard_map/ppermute | solution.py:429
  75.7 0.1 pad_add_fusion.5.at_ref
  75.8 3.8 %shard_map.76 = (bf16[588,512]{1,0:T(8,128)(2,1)S(1)}, bf16[588,512]{1,0:T(8,128)(2,1)S(1)}) custom-call(s32[2]{0:T(128)S(1)} %pad_add_fusion.5.at_ref, f32[1,2560]{1,0:T(1,128)S(1)} %reshape.16.node_ref, bf16[2624,256]{1,0:T(8,128)(2,1)S(1)} %copy-done, bf16[2560,256]{1,0:T(8,128)(2,1)S(1)} %get-tuple-element.72.image_ref), custom_call_target="tpu_custom_call" | custom-call | flops 1048576 | bytes 1024 | tf_op jit(solution)/shard_map/pallas_call | solution.py:567
  79.6 2.7 %collective-permute-done.7.refs_0_ = bf16[448,256]{1,0:T(8,128)(2,1)S(1)} collective-permute-done((bf16[448,256]{1,0:T(8,128)(2,1)}, bf16[448,256]{1,0:T(8,128)(2,1)S(1)}, u32[]{:S(2)}, u32[]{:S(2)}) %collective-permute-start.7) | collective-permute-done | bytes 229408 | tf_op jit(solution)/shard_map/ppermute | solution.py:429
  82.3 0.6 shard_map.75
  82.9 5.0 %collective-permute-start.10 = (bf16[112,256]{1,0:T(8,128)(2,1)S(1)}, bf16[112,256]{1,0:T(8,128)(2,1)S(1)}, u32[]{:S(2)}, u32[]{:S(2)}) collective-permute-start(bf16[112,256]{1,0:T(8,128)(2,1)S(1)} %get-tuple-element.75), channel_id=1, source_target_pairs={{0,24},{4,28},{8,16},{12,20},{16,8},{20,12},{24,0},{28,4},{1,25},{... | collective-permute-start | bytes 172040 | tf_op jit(solution)/shard_map/ppermute | solution.py:429
  87.9 0.0 collective-permute-start.8
  87.9 0.6 collective-permute-start.9
  88.5 2.0 %collective-permute-done.10.refs_2_ = bf16[112,256]{1,0:T(8,128)(2,1)S(1)} collective-permute-done((bf16[112,256]{1,0:T(8,128)(2,1)S(1)}, bf16[112,256]{1,0:T(8,128)(2,1)S(1)}, u32[]{:S(2)}, u32[]{:S(2)}) %collective-permute-start.10) | collective-permute-done | bytes 57376 | tf_op jit(solution)/shard_map/ppermute | solution.py:429
  90.6 1.6 %collective-permute-done.8.refs_0_ = bf16[112,256]{1,0:T(8,128)(2,1)S(1)} collective-permute-done((bf16[112,256]{1,0:T(8,128)(2,1)S(1)}, bf16[112,256]{1,0:T(8,128)(2,1)S(1)}, u32[]{:S(2)}, u32[]{:S(2)}) %collective-permute-start.8) | collective-permute-done | bytes 57376 | tf_op jit(solution)/shard_map/ppermute | solution.py:429
  92.2 1.2 collective-permute-done.9.refs_1_
  93.4 0.6 shard_map.77.own_ref
  94.0 1.7 %collective-permute-start.11 = (bf16[112,256]{1,0:T(8,128)(2,1)S(1)}, bf16[112,256]{1,0:T(8,128)(2,1)S(1)}, u32[]{:S(2)}, u32[]{:S(2)}) collective-permute-start(bf16[112,256]{1,0:T(8,128)(2,1)S(1)} %shard_map.77.own_ref), channel_id=1, source_target_pairs={{0,8},{4,12},{8,0},{12,4},{16,24},{20,28},{24,16},{28,20},{1,9},{5... | collective-permute-start | bytes 172040 | tf_op jit(solution)/shard_map/ppermute | solution.py:429
  95.6 0.8 collective-permute-start.12
  96.4 2.0 %collective-permute-start.13 = (bf16[112,256]{1,0:T(8,128)(2,1)S(1)}, bf16[112,256]{1,0:T(8,128)(2,1)S(1)}, u32[]{:S(2)}, u32[]{:S(2)}) collective-permute-start(bf16[112,256]{1,0:T(8,128)(2,1)S(1)} %shard_map.77.own_ref), channel_id=1, source_target_pairs={{0,24},{4,28},{8,16},{12,20},{16,8},{20,12},{24,0},{28,4},{1,25},{... | collective-permute-start | bytes 172040 | tf_op jit(solution)/shard_map/ppermute | solution.py:429
  98.4 0.5 collective-permute-done.11.refs_0_
  98.9 2.3 %collective-permute-done.12.refs_1_ = bf16[112,256]{1,0:T(8,128)(2,1)S(1)} collective-permute-done((bf16[112,256]{1,0:T(8,128)(2,1)S(1)}, bf16[112,256]{1,0:T(8,128)(2,1)S(1)}, u32[]{:S(2)}, u32[]{:S(2)}) %collective-permute-start.12) | collective-permute-done | bytes 57376 | tf_op jit(solution)/shard_map/ppermute | solution.py:429
  101.2 1.2 collective-permute-done.13.refs_2_
  102.4 0.6 shard_map.78.refs_0_
  103.0 0.7 collective-permute-start.15
  103.7 1.2 collective-permute-start.19
  104.9 4.1 %collective-permute-done.15.refs_1_ = bf16[448,256]{1,0:T(8,128)(2,1)S(1)} collective-permute-done((bf16[448,256]{1,0:T(8,128)(2,1)S(1)}, bf16[448,256]{1,0:T(8,128)(2,1)S(1)}, u32[]{:S(2)}, u32[]{:S(2)}) %collective-permute-start.15) | collective-permute-done | bytes 229408 | tf_op jit(solution)/shard_map/ppermute | solution.py:429
  109.1 1.7 %collective-permute-start.20 = (bf16[448,256]{1,0:T(8,128)(2,1)S(1)}, bf16[448,256]{1,0:T(8,128)(2,1)S(1)}, u32[]{:S(2)}, u32[]{:S(2)}) collective-permute-start(bf16[448,256]{1,0:T(8,128)(2,1)S(1)} %collective-permute-done.15.refs_1_), channel_id=1, source_target_pairs={{0,2},{1,3},{2,0},{3,1},{4,6},{5,7},{6,4},{7,5},{8,10},{9,11},{10,... | collective-permute-start | bytes 688136 | tf_op jit(solution)/shard_map/ppermute | solution.py:429
  110.8 0.5 collective-permute-start.18
  111.3 0.8 collective-permute-done.19.refs_4_
  112.1 4.5 %collective-permute-done.20.refs_5_ = bf16[448,256]{1,0:T(8,128)(2,1)S(1)} collective-permute-done((bf16[448,256]{1,0:T(8,128)(2,1)S(1)}, bf16[448,256]{1,0:T(8,128)(2,1)S(1)}, u32[]{:S(2)}, u32[]{:S(2)}) %collective-permute-start.20) | collective-permute-done | bytes 229408 | tf_op jit(solution)/shard_map/ppermute | solution.py:429
  116.6 0.1 pad_add_fusion.place_ref
  116.7 1.4 %collective-permute-done.22.refs_7_ = bf16[448,256]{1,0:T(8,128)(2,1)S(1)} collective-permute-done((bf16[448,256]{1,0:T(8,128)(2,1)S(1)}, bf16[448,256]{1,0:T(8,128)(2,1)S(1)}, u32[]{:S(2)}, u32[]{:S(2)}) %collective-permute-start.22) | collective-permute-done | bytes 229408 | tf_op jit(solution)/shard_map/ppermute | solution.py:429
  118.1 4.5 %shard_map.79 = (f32[588,1024]{1,0:T(8,128)}, bf16[1024,1024]{1,0:T(8,128)(2,1)}) custom-call(s32[2]{0:T(128)S(1)} %pad_add_fusion.place_ref, bf16[448,256]{1,0:T(8,128)(2,1)S(1)} %shard_map.78.refs_0_, bf16[448,256]{1,0:T(8,128)(2,1)S(1)} %collective-permute-done.15.refs_1_, bf16[448,256]{1,0:T(8,128)(2,1)S(1)} %collective-permute-done.17.refs_2_, ...), custom_call_target="tpu_custom_call" | custom-call | tf_op jit(solution)/shard_map/pallas_call | solution.py:652
  (24 shorter events, 0.1 us)
Async XLA Ops:
  1.3 1.3 %copy-start.2 = (bf16[2352,256]{1,0:T(8,128)(2,1)S(1)}, bf16[2352,256]{1,0:T(8,128)(2,1)}, u32[]{:S(2)}) copy-start(bf16[2352,256]{1,0:T(8,128)(2,1)} %raw_ref.1) | copy-start | bytes 3612676
  2.6 0.7 copy-start.5
  3.8 6.9 %copy-start.8 = (s32[8,343]{1,0:T(8,128)S(1)}, s32[8,343]{1,0:T(8,128)}, u32[]{:S(2)}) copy-start(s32[8,343]{1,0:T(8,128)} %conn_ref.1) | copy-start | bytes 32932
  3.8 6.8 %collective-permute-start = (bf16[80,256]{1,0:T(8,128)(2,1)S(1)}, bf16[80,256]{1,0:T(8,128)(2,1)S(1)}, u32[]{:S(2)}, u32[]{:S(2)}) collective-permute-start(bf16[80,256]{1,0:T(8,128)(2,1)S(1)} %shard_map.68), channel_id=1, source_target_pairs={{4,0},{8,4},{12,8},{16,12},{20,16},{24,20},{28,24},{5,1},{9,5},{13... | collective-permute-start | bytes 122888 | tf_op jit(solution)/shard_map/ppermute | solution.py:434
  28.5 12.1 %collective-permute-start.1 = (bf16[6,64,256]{2,1,0:T(8,128)(2,1)S(1)}, bf16[6,64,256]{2,1,0:T(8,128)(2,1)S(1)}, u32[]{:S(2)}, u32[]{:S(2)}) collective-permute-start(bf16[6,64,256]{2,1,0:T(8,128)(2,1)S(1)} %get-tuple-element.46), channel_id=1, source_target_pairs={{0,4},{4,8},{8,12},{12,16},{16,20},{20,24},{24,28},{1,5},{5,9},{9,... | collective-permute-start | bytes 589832 | tf_op jit(solution)/shard_map/ppermute | solution.py:434
  33.3 7.2 %collective-permute-start.2 = (bf16[5,64,256]{2,1,0:T(8,128)(2,1)S(1)}, bf16[5,64,256]{2,1,0:T(8,128)(2,1)S(1)}, u32[]{:S(2)}, u32[]{:S(2)}) collective-permute-start(bf16[5,64,256]{2,1,0:T(8,128)(2,1)S(1)} %get-tuple-element.47), channel_id=1, source_target_pairs={{4,0},{8,4},{12,8},{16,12},{20,16},{24,20},{28,24},{5,1},{9,5},{13... | collective-permute-start | bytes 491528 | tf_op jit(solution)/shard_map/ppermute | solution.py:434
  40.6 9.4 %copy-start.1 = (f32[2560,128]{1,0:T(8,128)S(1)}, f32[2560,128]{1,0:T(8,128)}, u32[]{:S(2)}) copy-start(f32[2560,128]{1,0:T(8,128)} %get-tuple-element.49.pot_hbm.pot_ref) | copy-start | bytes 3932164
  48.3 11.5 %collective-permute-start.4 = (bf16[2624,256]{1,0:T(8,128)(2,1)}, bf16[2624,256]{1,0:T(8,128)(2,1)}, u32[]{:S(2)}, u32[]{:S(2)}) collective-permute-start(bf16[2624,256]{1,0:T(8,128)(2,1)} %get-tuple-element.71.x_ref), channel_id=1, source_target_pairs={{0,1},{1,0},{2,3},{3,2},{4,5},{5,4},{6,7},{7,6},{8,9},{9,8},{10,11... | collective-permute-start | bytes 4030472 | tf_op jit(solution)/shard_map/ppermute | solution.py:429
  48.4 18.1 %collective-permute-start.3 = (bf16[1344,256]{1,0:T(8,128)(2,1)}, bf16[1344,256]{1,0:T(8,128)(2,1)S(1)}, u32[]{:S(2)}, u32[]{:S(2)}) collective-permute-start(bf16[1344,256]{1,0:T(8,128)(2,1)} %get-tuple-element.54), channel_id=1, source_target_pairs={{0,2},{1,3},{2,0},{3,1},{4,6},{5,7},{6,4},{7,5},{8,10},{9,11},{10,... | collective-permute-start | bytes 2064392 | tf_op jit(solution)/shard_map/ppermute | solution.py:429
  50.0 5.2 %copy-start = (bf16[2624,256]{1,0:T(8,128)(2,1)S(1)}, bf16[2624,256]{1,0:T(8,128)(2,1)}, u32[]{:S(2)}) copy-start(bf16[2624,256]{1,0:T(8,128)(2,1)} %get-tuple-element.71.x_ref) | copy-start | bytes 4030468
  54.5 8.4 %collective-permute-start.5 = (bf16[672,256]{1,0:T(8,128)(2,1)}, bf16[672,256]{1,0:T(8,128)(2,1)}, u32[]{:S(2)}, u32[]{:S(2)}) collective-permute-start(bf16[672,256]{1,0:T(8,128)(2,1)} %get-tuple-element.52.refs_0_), channel_id=1, source_target_pairs={{0,1},{1,0},{2,3},{3,2},{4,5},{5,4},{6,7},{7,6},{8,9},{9,8},{10,11... | collective-permute-start | bytes 1032200 | tf_op jit(solution)/shard_map/ppermute | solution.py:429
  54.7 8.2 %collective-permute-start.6 = (bf16[672,256]{1,0:T(8,128)(2,1)}, bf16[672,256]{1,0:T(8,128)(2,1)}, u32[]{:S(2)}, u32[]{:S(2)}) collective-permute-start(bf16[672,256]{1,0:T(8,128)(2,1)} %get-tuple-element.53.refs_1_), channel_id=1, source_target_pairs={{0,1},{1,0},{2,3},{3,2},{4,5},{5,4},{6,7},{7,6},{8,9},{9,8},{10,11... | collective-permute-start | bytes 1032200 | tf_op jit(solution)/shard_map/ppermute | solution.py:429
  66.4 0.8 copy-start.6
  67.3 35.7 %collective-permute-start.14 = (bf16[588,512]{1,0:T(8,128)(2,1)}, bf16[588,512]{1,0:T(8,128)(2,1)S(1)}, u32[]{:S(2)}, u32[]{:S(2)}) collective-permute-start(bf16[588,512]{1,0:T(8,128)(2,1)} %get-tuple-element.76), channel_id=1, source_target_pairs={{0,2},{1,3},{2,0},{3,1},{4,6},{5,7},{6,4},{7,5},{8,10},{9,11},{10,... | collective-permute-start | bytes 1806344 | tf_op jit(solution)/shard_map/ppermute | solution.py:429
  68.9 36.0 %collective-permute-start.16 = (bf16[588,512]{1,0:T(8,128)(2,1)}, bf16[588,512]{1,0:T(8,128)(2,1)}, u32[]{:S(2)}, u32[]{:S(2)}) collective-permute-start(bf16[588,512]{1,0:T(8,128)(2,1)} %get-tuple-element.78), channel_id=1, source_target_pairs={{0,3},{1,2},{2,1},{3,0},{4,7},{5,6},{6,5},{7,4},{8,11},{9,10},{10,... | collective-permute-start | bytes 1806344 | tf_op jit(solution)/shard_map/ppermute | solution.py:429
  69.0 1.1 copy-start.7
  72.7 0.8 copy-start.3
  73.5 8.8 %collective-permute-start.7 = (bf16[448,256]{1,0:T(8,128)(2,1)}, bf16[448,256]{1,0:T(8,128)(2,1)S(1)}, u32[]{:S(2)}, u32[]{:S(2)}) collective-permute-start(bf16[448,256]{1,0:T(8,128)(2,1)} %get-tuple-element.66), channel_id=1, source_target_pairs={{0,4},{4,0},{8,12},{12,8},{16,20},{20,16},{24,28},{28,24},{1,5},{5... | collective-permute-start | bytes 688136 | tf_op jit(solution)/shard_map/ppermute | solution.py:429
  75.7 6.6 %copy-start.4 = (f32[448,256]{1,0:T(8,128)S(1)}, f32[448,256]{1,0:T(8,128)}, u32[]{:S(2)}) copy-start(f32[448,256]{1,0:T(8,128)} %copy-done.3) | copy-start | bytes 1376260
  82.9 7.6 %collective-permute-start.10 = (bf16[112,256]{1,0:T(8,128)(2,1)S(1)}, bf16[112,256]{1,0:T(8,128)(2,1)S(1)}, u32[]{:S(2)}, u32[]{:S(2)}) collective-permute-start(bf16[112,256]{1,0:T(8,128)(2,1)S(1)} %get-tuple-element.75), channel_id=1, source_target_pairs={{0,24},{4,28},{8,16},{12,20},{16,8},{20,12},{24,0},{28,4},{1,25},{... | collective-permute-start | bytes 172040 | tf_op jit(solution)/shard_map/ppermute | solution.py:429
  87.9 4.3 %collective-permute-start.8 = (bf16[112,256]{1,0:T(8,128)(2,1)S(1)}, bf16[112,256]{1,0:T(8,128)(2,1)S(1)}, u32[]{:S(2)}, u32[]{:S(2)}) collective-permute-start(bf16[112,256]{1,0:T(8,128)(2,1)S(1)} %get-tuple-element.68), channel_id=1, source_target_pairs={{0,8},{4,12},{8,0},{12,4},{16,24},{20,28},{24,16},{28,20},{1,9},{5... | collective-permute-start | bytes 172040 | tf_op jit(solution)/shard_map/ppermute | solution.py:429
  87.9 5.5 %collective-permute-start.9 = (bf16[112,256]{1,0:T(8,128)(2,1)S(1)}, bf16[112,256]{1,0:T(8,128)(2,1)S(1)}, u32[]{:S(2)}, u32[]{:S(2)}) collective-permute-start(bf16[112,256]{1,0:T(8,128)(2,1)S(1)} %get-tuple-element.69), channel_id=1, source_target_pairs={{0,16},{4,20},{8,24},{12,28},{16,0},{20,4},{24,8},{28,12},{1,17},{... | collective-permute-start | bytes 172040 | tf_op jit(solution)/shard_map/ppermute | solution.py:429
  94.0 4.9 %collective-permute-start.11 = (bf16[112,256]{1,0:T(8,128)(2,1)S(1)}, bf16[112,256]{1,0:T(8,128)(2,1)S(1)}, u32[]{:S(2)}, u32[]{:S(2)}) collective-permute-start(bf16[112,256]{1,0:T(8,128)(2,1)S(1)} %shard_map.77.own_ref), channel_id=1, source_target_pairs={{0,8},{4,12},{8,0},{12,4},{16,24},{20,28},{24,16},{28,20},{1,9},{5... | collective-permute-start | bytes 172040 | tf_op jit(solution)/shard_map/ppermute | solution.py:429
  95.6 5.6 %collective-permute-start.12 = (bf16[112,256]{1,0:T(8,128)(2,1)S(1)}, bf16[112,256]{1,0:T(8,128)(2,1)S(1)}, u32[]{:S(2)}, u32[]{:S(2)}) collective-permute-start(bf16[112,256]{1,0:T(8,128)(2,1)S(1)} %shard_map.77.own_ref), channel_id=1, source_target_pairs={{0,16},{4,20},{8,24},{12,28},{16,0},{20,4},{24,8},{28,12},{1,17},{... | collective-permute-start | bytes 172040 | tf_op jit(solution)/shard_map/ppermute | solution.py:429
  96.4 6.0 %collective-permute-start.13 = (bf16[112,256]{1,0:T(8,128)(2,1)S(1)}, bf16[112,256]{1,0:T(8,128)(2,1)S(1)}, u32[]{:S(2)}, u32[]{:S(2)}) collective-permute-start(bf16[112,256]{1,0:T(8,128)(2,1)S(1)} %shard_map.77.own_ref), channel_id=1, source_target_pairs={{0,24},{4,28},{8,16},{12,20},{16,8},{20,12},{24,0},{28,4},{1,25},{... | collective-permute-start | bytes 172040 | tf_op jit(solution)/shard_map/ppermute | solution.py:429
  103.0 6.1 %collective-permute-start.15 = (bf16[448,256]{1,0:T(8,128)(2,1)S(1)}, bf16[448,256]{1,0:T(8,128)(2,1)S(1)}, u32[]{:S(2)}, u32[]{:S(2)}) collective-permute-start(bf16[448,256]{1,0:T(8,128)(2,1)S(1)} %shard_map.78.refs_0_), channel_id=1, source_target_pairs={{0,4},{4,0},{8,12},{12,8},{16,20},{20,16},{24,28},{28,24},{1,5},{5... | collective-permute-start | bytes 688136 | tf_op jit(solution)/shard_map/ppermute | solution.py:429
  103.7 13.0 %collective-permute-start.23 = (bf16[588,512]{1,0:T(8,128)(2,1)S(1)}, bf16[588,512]{1,0:T(8,128)(2,1)S(1)}, u32[]{:S(2)}, u32[]{:S(2)}) collective-permute-start(bf16[588,512]{1,0:T(8,128)(2,1)S(1)} %get-tuple-element.81), channel_id=1, source_target_pairs={{0,1},{1,0},{2,3},{3,2},{4,5},{5,4},{6,7},{7,6},{8,9},{9,8},{10,11... | collective-permute-start | bytes 1806344 | tf_op jit(solution)/shard_map/ppermute | solution.py:429
  103.7 8.4 %collective-permute-start.19 = (bf16[448,256]{1,0:T(8,128)(2,1)S(1)}, bf16[448,256]{1,0:T(8,128)(2,1)S(1)}, u32[]{:S(2)}, u32[]{:S(2)}) collective-permute-start(bf16[448,256]{1,0:T(8,128)(2,1)S(1)} %shard_map.78.refs_0_), channel_id=1, source_target_pairs={{0,2},{1,3},{2,0},{3,1},{4,6},{5,7},{6,4},{7,5},{8,10},{9,11},{10,... | collective-permute-start | bytes 688136 | tf_op jit(solution)/shard_map/ppermute | solution.py:429
  109.1 7.6 %collective-permute-start.20 = (bf16[448,256]{1,0:T(8,128)(2,1)S(1)}, bf16[448,256]{1,0:T(8,128)(2,1)S(1)}, u32[]{:S(2)}, u32[]{:S(2)}) collective-permute-start(bf16[448,256]{1,0:T(8,128)(2,1)S(1)} %collective-permute-done.15.refs_1_), channel_id=1, source_target_pairs={{0,2},{1,3},{2,0},{3,1},{4,6},{5,7},{6,4},{7,5},{8,10},{9,11},{10,... | collective-permute-start | bytes 688136 | tf_op jit(solution)/shard_map/ppermute | solution.py:429
  110.8 5.9 %collective-permute-start.17 = (bf16[448,256]{1,0:T(8,128)(2,1)S(1)}, bf16[448,256]{1,0:T(8,128)(2,1)S(1)}, u32[]{:S(2)}, u32[]{:S(2)}) collective-permute-start(bf16[448,256]{1,0:T(8,128)(2,1)S(1)} %shard_map.78.refs_0_), channel_id=1, source_target_pairs={{0,1},{1,0},{2,3},{3,2},{4,5},{5,4},{6,7},{7,6},{8,9},{9,8},{10,11... | collective-permute-start | bytes 688136 | tf_op jit(solution)/shard_map/ppermute | solution.py:429
  110.8 5.9 %collective-permute-start.18 = (bf16[448,256]{1,0:T(8,128)(2,1)S(1)}, bf16[448,256]{1,0:T(8,128)(2,1)S(1)}, u32[]{:S(2)}, u32[]{:S(2)}) collective-permute-start(bf16[448,256]{1,0:T(8,128)(2,1)S(1)} %collective-permute-done.15.refs_1_), channel_id=1, source_target_pairs={{0,1},{1,0},{2,3},{3,2},{4,5},{5,4},{6,7},{7,6},{8,9},{9,8},{10,11... | collective-permute-start | bytes 688136 | tf_op jit(solution)/shard_map/ppermute | solution.py:429
  112.1 4.6 %collective-permute-start.21 = (bf16[448,256]{1,0:T(8,128)(2,1)S(1)}, bf16[448,256]{1,0:T(8,128)(2,1)S(1)}, u32[]{:S(2)}, u32[]{:S(2)}) collective-permute-start(bf16[448,256]{1,0:T(8,128)(2,1)S(1)} %collective-permute-done.19.refs_4_), channel_id=1, source_target_pairs={{0,1},{1,0},{2,3},{3,2},{4,5},{5,4},{6,7},{7,6},{8,9},{9,8},{10,11... | collective-permute-start | bytes 688136 | tf_op jit(solution)/shard_map/ppermute | solution.py:429
  116.6 1.5 %collective-permute-start.22 = (bf16[448,256]{1,0:T(8,128)(2,1)S(1)}, bf16[448,256]{1,0:T(8,128)(2,1)S(1)}, u32[]{:S(2)}, u32[]{:S(2)}) collective-permute-start(bf16[448,256]{1,0:T(8,128)(2,1)S(1)} %collective-permute-done.20.refs_5_), channel_id=1, source_target_pairs={{0,1},{1,0},{2,3},{3,2},{4,5},{5,4},{6,7},{7,6},{8,9},{9,8},{10,11... | collective-permute-start | bytes 688136 | tf_op jit(solution)/shard_map/ppermute | solution.py:429
